TPU v7x, 32 devices: a whole 2x2x4 slice. The times are simulated.
32 devices in a mesh: groups: 2 (over x), gx: 16 (over z, y, core).
Axes of the slice: x: 2, y: 2, z: 4, core: 2. Of those that a mesh axis runs over, the one named last changes fastest.
Arguments:
- activations: bfloat16 [768, 8192], P('groups', 'gx'), parts along dimension 0, may hold values from -320 to 320, as said below
- norm_gain: bfloat16 [8192], P('gx'), may hold values from 0.25 to 1.75
- gate_weight: bfloat16 [8192, 26624], P(None, 'gx'), may hold values from -0.09375 to 0.09375
- up_weight: bfloat16 [8192, 26624], P(None, 'gx'), may hold values from -0.0625 to 0.0625
- down_weight: bfloat16 [26624, 8192], P('gx'), may hold values from -0.0546875 to 0.0546875
Outputs:
- updated: bfloat16 [768, 8192], P('groups', 'gx'), parts along dimension 0
There are 2 independent parts, one for each index of `groups`. A program takes and returns all parts, laid end to end along the dimension named above; an argument that names none is the same for every part. Nothing has to cross between parts.
Inputs may be any that keep to these rules, and one draw needn't show every extreme that they name: real-valued activations of each replica.
All inputs are finite; a program needn't handle non-finite values.
Results may differ from a plain program's by a relative error of at most 0.0015.
Values may be sent and summed in bfloat16 or wider, within the bound.
No kernel may reach another device: no remote copies, remote signals or barrier semaphores. Data moves between devices by JAX's collectives and lax.ppermute only.
A program may use at most 192 MiB of HBM per device.

v0:
```python
import jax
import jax.numpy as jnp
from jax import lax
from jax.sharding import PartitionSpec as P

epsilon = 1e-05


def per_device(activations, norm_gain, gate_weight, up_weight, down_weight):
    resident = activations.astype(jnp.float32)
    totals = lax.psum(jnp.sum(resident * resident, axis=1), "gx")
    factor = lax.rsqrt(totals / (resident.shape[1] * lax.axis_size("gx")) + epsilon)
    normed = (resident * factor[:, None] * norm_gain.astype(jnp.float32)[None, :]).astype(
        jnp.bfloat16
    )
    pieces = lax.all_gather(normed, "gx", axis=1, tiled=True)
    gate_sum = jnp.dot(pieces, gate_weight, preferred_element_type=jnp.float32)
    up_sum = jnp.dot(pieces, up_weight, preferred_element_type=jnp.float32)
    hidden = (jax.nn.silu(gate_sum) * up_sum).astype(jnp.bfloat16)
    summed = lax.psum_scatter(
        lax.dot_general(
            down_weight, hidden, (((0,), (1,)), ((), ())), preferred_element_type=jnp.float32
        ),
        "gx",
        scatter_dimension=0,
        tiled=True,
    )
    branch = summed.T
    return (resident + branch).astype(jnp.bfloat16)


def solution(mesh):
    in_specs = (P("groups", "gx"), P("gx"), P(None, "gx"), P(None, "gx"), P("gx", None))
    out_specs = P("groups", "gx")
    return jax.shard_map(
        per_device, mesh=mesh, in_specs=in_specs, out_specs=out_specs, check_vma=False
    )
```

profile of v0, /device:TPU:0, one launch (start us, length us, event | category | flops | bytes accessed | tf_op | source)
XLA Modules:
  0.0 302.8 jit_solution(2349535593904253351)
XLA Ops:
  6.5 0.0 all-gather.2.cloned.1.call-start
  6.5 0.7 convert_element_type.16
  7.2 1.2 fusion.1
  8.4 34.9 %psum.7 = f32[384]{0:T(512)S(1)} all-reduce(f32[384]{0:T(512)S(1)} %fusion.1), channel_id=1, replica_groups=mesh['groups'=2,'gx'=16] {'gx'}, use_global_device_ids=true, to_apply=%region_1.0 | all-reduce | flops 384 | bytes 3072 | tf_op jit(solution)/shard_map/psum | solution.py:11
  43.3 1.9 fusion.3
  45.2 0.0 all-gather.2.cloned.1.call-update
  45.2 0.0 reduce-scatter.2.cloned.1.call-start
  45.3 63.0 %all-gather.2.cloned.1.call-done = bf16[384,8192]{1,0:T(8,128)(2,1)} async-done(((bf16[384,512]{1,0:T(8,128)(2,1)}), bf16[384,8192]{1,0:T(8,128)(2,1)}) %all-gather.2.cloned.1.call-update) | async-done | bytes 6291472 | tf_op jit(solution)/shard_map/all_gather | solution.py:16
  108.3 0.0 copy-start.1
  108.3 17.7 %fusion.5 = f32[384,1664]{1,0:T(8,128)S(1)} fusion(bf16[384,8192]{1,0:T(8,128)(2,1)} %all-gather.2.cloned.1.call-done, bf16[8192,1664]{1,0:T(8,128)(2,1)} %param.7), kind=kOutput, calls=%fused_computation.11 | convolution fusion | flops 10468982784 | bytes 36110336 | tf_op jit(solution)/shard_map/dot_general | solution.py:17
  126.0 0.0 copy-done.1
  126.0 15.7 %fusion = bf16[384,1664]{1,0:T(8,128)(2,1)S(1)} fusion(bf16[384,8192]{1,0:T(8,128)(2,1)S(1)} %copy-done.1, bf16[8192,1664]{1,0:T(8,128)(2,1)} %param.8, f32[384,1664]{1,0:T(8,128)S(1)} %fusion.5), kind=kOutput, calls=%fused_computation.2 | convolution fusion | flops 10472816640 | bytes 37388288 | tf_op jit(solution)/shard_map/dot_general | solution.py:18
  141.7 19.2 %convolution_bitcast_fusion = f32[8192,384]{0,1:T(8,128)} fusion(bf16[384,1664]{1,0:T(8,128)(2,1)S(1)} %fusion, bf16[1664,8192]{1,0:T(8,128)(2,1)} %param.9), kind=kOutput, calls=%fused_computation | convolution fusion | flops 10468982784 | bytes 41123840 | tf_op jit(solution)/shard_map/dot_general | solution.py:21
  160.9 0.0 copy-start
  160.9 0.0 reduce-scatter.2.cloned.1.call-update
  160.9 133.0 %reduce-scatter.2.cloned.1.call-done = f32[512,384]{0,1:T(8,128)} async-done(((f32[8192,384]{0,1:T(8,128)}), f32[512,384]{0,1:T(8,128)}) %reduce-scatter.2.cloned.1.call-update) | async-done | bytes 786448 | tf_op jit(solution)/shard_map/reduce_scatter | solution.py:20
  294.0 0.0 copy-done
  294.0 2.0 fusion.4
  (1 shorter events, 0.0 us)
Async XLA Ops:
  6.5 101.8 %all-gather.2.cloned.1.call-start = ((), (), s32[]{:S(2)}) async-start(), calls=%async_computation.1 | async-start | bytes 6684672 | tf_op jit(solution)/shard_map/all_gather | solution.py:16
  45.2 248.7 %reduce-scatter.2.cloned.1.call-start = ((), (), s32[]{:S(2)}) async-start(), calls=%async_computation.2 | async-start | bytes 13369344 | tf_op jit(solution)/shard_map/reduce_scatter | solution.py:20
  108.3 17.7 %copy-start.1 = (bf16[384,8192]{1,0:T(8,128)(2,1)S(1)}, bf16[384,8192]{1,0:T(8,128)(2,1)}, u32[]{:S(2)}) copy-start(bf16[384,8192]{1,0:T(8,128)(2,1)} %all-gather.2.cloned.1.call-done) | copy-start | bytes 18874372
  160.9 133.1 %copy-start = (bf16[384,512]{1,0:T(8,128)(2,1)S(1)}, bf16[384,512]{1,0:T(8,128)(2,1)}, u32[]{:S(2)}) copy-start(bf16[384,512]{1,0:T(8,128)(2,1)} %param.5) | copy-start | bytes 1179652
Sparse Core Ops, SparseCore 0:
  45.4 62.9 all-gather.1
  161.1 132.8 reduce-scatter.1
where the time goes:
time: 303 us
  waiting for transfers between devices  196 us (65%)
  matrix products  52.6 us (17%)
  blocking collectives  34.9 us (12%)
  between operations  13.4 us (4%)
  other arithmetic  5.74 us (2%)
    reduce_scatter x1, waiting for transfers between devices, per_device(): lax.psum_scatter(lax.dot_general(down_weight, hidden, (((0,), (1,)), ((),...  133 us
    all_gather x1, waiting for transfers between devices, per_device(): pieces = lax.all_gather(normed, 'gx', axis=1, tiled=True)  63 us
    psum x1, blocking collectives, per_device(): totals = lax.psum(jnp.sum(resident * resident, axis=1), 'gx')  34.9 us
    dot_general x1, matrix products, per_device(): lax.dot_general(down_weight, hidden, (((0,), (1,)), ((), ())), preferred_...  19.2 us
    dot_general x1, matrix products, per_device(): gate_sum = jnp.dot(pieces, gate_weight, preferred_element_type=jnp.float32)  17.7 us
    dot_general x1, matrix products, per_device(): up_sum = jnp.dot(pieces, up_weight, preferred_element_type=jnp.float32)  15.7 us
  transfers between devices with their start and end apart: 2, of which 2 were waited for; matrix products, arithmetic and copies ran while one was open for 0% of the time, Pallas kernels for 0%

commit v1 on v0

--- a/solution.py
+++ b/solution.py
@@ -1,12 +1,173 @@
+import functools
+
 import jax
 import jax.numpy as jnp
 from jax import lax
+from jax.experimental import pallas as pl
+from jax.experimental.pallas import tpu as pltpu
 from jax.sharding import PartitionSpec as P
 
 epsilon = 1e-05
-
-
-def per_device(activations, norm_gain, gate_weight, up_weight, down_weight):
+INNER = 4
+GAIN_ROWS = 16
+VMEM_LIMIT = 56 * 1024 * 1024
+
+
+def swap(x, mask, n):
+    return lax.ppermute(x, "gx", [(i, i ^ mask) for i in range(n)])
+
+
+def gate_up_body(first, last, rows, idx_ref, *refs):
+    blocks = refs[:INNER]
+    factor_ref, gate_ref, up_ref = refs[INNER : INNER + 3]
+    rest = refs[INNER + 3 :]
+    if not first:
+        gate_in, up_in = rest[:2]
+        rest = rest[2:]
+    if last:
+        hidden_ref, gate_acc, up_acc = rest
+    else:
+        gate_acc, up_acc = rest
+    step = pl.program_id(0)
+
+    for s in range(INNER):
+
+        @pl.when(step == s)
+        def _(s=s):
+            x = blocks[s][:rows, :].astype(jnp.float32)
+            gain = blocks[s][rows : rows + GAIN_ROWS, :].astype(jnp.float32)[:1, :]
+            normed = (x * factor_ref[:, :1] * gain).astype(jnp.bfloat16)
+            g = jnp.dot(normed, gate_ref[...], preferred_element_type=jnp.float32)
+            u = jnp.dot(normed, up_ref[...], preferred_element_type=jnp.float32)
+            if s == 0:
+                if first:
+                    gate_acc[...] = g
+                    up_acc[...] = u
+                else:
+                    gate_acc[...] = gate_in[...] + g
+                    up_acc[...] = up_in[...] + u
+            elif s == INNER - 1 and last:
+                g = gate_acc[...] + g
+                u = up_acc[...] + u
+                hidden_ref[...] = (g / (1.0 + jnp.exp(-g)) * u).astype(jnp.bfloat16)
+            else:
+                gate_acc[...] += g
+                up_acc[...] += u
+
+
+def gate_up(idx, blocks, factor, gate_weight, up_weight, acc, last):
+    rows = factor.shape[0]
+    depth = blocks[0].shape[1]
+    ff = gate_weight.shape[1]
+    first = acc is None
+    whole = lambda shape: pl.BlockSpec(shape, lambda s, idx: (0, 0))
+    weight = pl.BlockSpec((depth, ff), lambda s, idx: (idx[s], 0))
+    in_specs = [whole(b.shape) for b in blocks] + [whole(factor.shape), weight, weight]
+    args = list(blocks) + [factor, gate_weight, up_weight]
+    if not first:
+        in_specs += [whole((rows, ff))] * 2
+        args += list(acc)
+    if last:
+        out_shape = [jax.ShapeDtypeStruct((rows, ff), jnp.bfloat16)]
+        out_specs = [whole((rows, ff))]
+        scratch = [pltpu.VMEM((rows, ff), jnp.float32)] * 2
+    else:
+        out_shape = [jax.ShapeDtypeStruct((rows, ff), jnp.float32)] * 2
+        out_specs = [whole((rows, ff))] * 2
+        scratch = []
+    return pl.pallas_call(
+        functools.partial(gate_up_body, first, last, rows),
+        grid_spec=pltpu.PrefetchScalarGridSpec(
+            num_scalar_prefetch=1,
+            grid=(INNER,),
+            in_specs=in_specs,
+            out_specs=out_specs,
+            scratch_shapes=scratch,
+        ),
+        out_shape=out_shape,
+        compiler_params=pltpu.CompilerParams(vmem_limit_bytes=VMEM_LIMIT),
+        cost_estimate=pl.CostEstimate(
+            flops=4 * rows * depth * INNER * ff,
+            bytes_accessed=4 * depth * INNER * ff + 8 * rows * ff,
+            transcendentals=0,
+        ),
+        name="gate_up",
+    )(idx, *args)
+
+
+def down_body(idx_ref, hidden_ref, weight_ref, out_ref):
+    out_ref[0] = jnp.dot(
+        hidden_ref[...], weight_ref[...], preferred_element_type=jnp.float32
+    ).astype(out_ref.dtype)
+
+
+def down(idx, hidden, down_weight, width, dtype):
+    rows, ff = hidden.shape
+    count = idx.shape[0]
+    return pl.pallas_call(
+        down_body,
+        grid_spec=pltpu.PrefetchScalarGridSpec(
+            num_scalar_prefetch=1,
+            grid=(count,),
+            in_specs=[
+                pl.BlockSpec((rows, ff), lambda s, idx: (0, 0)),
+                pl.BlockSpec((ff, width), lambda s, idx: (0, idx[s])),
+            ],
+            out_specs=pl.BlockSpec((1, rows, width), lambda s, idx: (s, 0, 0)),
+        ),
+        out_shape=jax.ShapeDtypeStruct((count, rows, width), dtype),
+        compiler_params=pltpu.CompilerParams(vmem_limit_bytes=VMEM_LIMIT),
+        cost_estimate=pl.CostEstimate(
+            flops=2 * rows * ff * width * count,
+            bytes_accessed=2 * ff * width * count + 4 * rows * width * count,
+            transcendentals=0,
+        ),
+        name="down",
+    )(idx, hidden, down_weight)
+
+
+def overlapped(n, activations, norm_gain, gate_weight, up_weight, down_weight):
+    rows, width = activations.shape
+    outer = n // INNER
+    me = lax.axis_index("gx")
+    resident = activations.astype(jnp.float32)
+
+    gains = jnp.broadcast_to(norm_gain[None, :], (GAIN_ROWS, width))
+    shard = jnp.concatenate([activations, gains], axis=0)
+
+    total = jnp.sum(resident * resident, axis=1)
+    total = total + sum(swap(total, INNER * k, n) for k in range(1, outer))
+    total = total + swap(total, 2, n)
+    total = total + swap(total, 1, n)
+    factor = lax.rsqrt(total / (width * n) + epsilon)
+    factor = jnp.broadcast_to(factor[:, None], (rows, 128))
+
+    acc = None
+    for k in range(outer):
+        a = shard if k == 0 else swap(shard, INNER * k, n)
+        b = swap(a, 2, n)
+        blocks = [a, b, swap(a, 1, n), swap(b, 1, n)]
+        idx = jnp.stack([me ^ (INNER * k + q) for q in (0, 2, 1, 3)]).astype(jnp.int32)
+        acc = gate_up(idx, blocks, factor, gate_weight, up_weight, acc, k == outer - 1)
+    hidden = acc[0]
+
+    branch = None
+    for k in reversed(range(outer)):
+        away = jnp.stack([me ^ (INNER * k + q) for q in (3, 1)]).astype(jnp.int32)
+        stay = jnp.stack([me ^ (INNER * k + q) for q in (2, 0)]).astype(jnp.int32)
+        sent = down(away, hidden, down_weight, width, jnp.bfloat16)
+        kept = down(stay, hidden, down_weight, width, jnp.float32)
+        got = swap(sent, 1, n).astype(jnp.float32)
+        far = (kept[0] + got[0]).astype(jnp.bfloat16)
+        near = kept[1] + got[1]
+        near = near + swap(far, 2, n).astype(jnp.float32)
+        if k:
+            near = swap(near.astype(jnp.bfloat16), INNER * k, n).astype(jnp.float32)
+        branch = near if branch is None else branch + near
+    return (resident + branch).astype(jnp.bfloat16)
+
+
+def plain(activations, norm_gain, gate_weight, up_weight, down_weight):
     resident = activations.astype(jnp.float32)
     totals = lax.psum(jnp.sum(resident * resident, axis=1), "gx")
     factor = lax.rsqrt(totals / (resident.shape[1] * lax.axis_size("gx")) + epsilon)
@@ -25,13 +186,25 @@
         scatter_dimension=0,
         tiled=True,
     )
-    branch = summed.T
-    return (resident + branch).astype(jnp.bfloat16)
+    return (resident + summed.T).astype(jnp.bfloat16)
+
+
+def per_device(n, activations, norm_gain, gate_weight, up_weight, down_weight):
+    args = (activations, norm_gain, gate_weight, up_weight, down_weight)
+    outer = n // INNER
+    aligned = activations.shape[1] % 128 == 0 and gate_weight.shape[1] % 128 == 0
+    if aligned and n == INNER * outer and outer & (outer - 1) == 0 and outer <= 8:
+        return overlapped(n, *args)
+    return plain(*args)
 
 
 def solution(mesh):
     in_specs = (P("groups", "gx"), P("gx"), P(None, "gx"), P(None, "gx"), P("gx", None))
     out_specs = P("groups", "gx")
     return jax.shard_map(
-        per_device, mesh=mesh, in_specs=in_specs, out_specs=out_specs, check_vma=False
+        functools.partial(per_device, mesh.shape["gx"]),
+        mesh=mesh,
+        in_specs=in_specs,
+        out_specs=out_specs,
+        check_vma=False,
     )

time: 303 us -> 206 us (0.68)
  waiting for transfers between devices: 196 us -> 50.7 us
  Pallas kernels: 0 us -> 95.1 us
  matrix products: 52.6 us -> 0 us
  starting transfers between devices: 0.04 us -> 40.1 us
  blocking collectives: 34.9 us -> 0 us
  between operations: 13.4 us -> 0.3 us
  other arithmetic: 5.74 us -> 13.1 us
  local copies, waits for them, and re-layouts: 0.01 us -> 6.56 us
    reduce_scatter x1 -> x0, waiting for transfers between devices: 133 us -> none  [per_device(): lax.psum_scatter(lax.dot_general(down_weight, hidden, (((0,), (1,)), ((),...]
    pallas_call x0 -> x12, Pallas kernels: none -> 95.1 us  [the longest x4 54 us: gate_up(): pl.pallas_call(functools.partial(gate_up_body, first, last, rows), grid_s...]
    all_gather x1 -> x0, waiting for transfers between devices: 63 us -> none  [per_device(): pieces = lax.all_gather(normed, 'gx', axis=1, tiled=True)]
    dot_general x3 -> x0, matrix products: 52.6 us -> none  [the longest x1 19.2 us: per_device(): lax.dot_general(down_weight, hidden, (((0,), (1,)), ((), ())), preferred_...]
    ppermute x0 -> x31, waiting for transfers between devices: none -> 50.7 us  [swap(): return lax.ppermute(x, 'gx', [(i, i ^ mask) for i in range(n)])]
    ppermute x0 -> x31, starting transfers between devices: none -> 40.1 us  [swap(): return lax.ppermute(x, 'gx', [(i, i ^ mask) for i in range(n)])]
    psum x1 -> x0, blocking collectives: 34.9 us -> none  [per_device(): totals = lax.psum(jnp.sum(resident * resident, axis=1), 'gx')]
    another operation x0 -> x12, other arithmetic: none -> 7.58 us  [the longest x4 2.57 us: overlapped(): away = jnp.stack([me ^ INNER * k + q for q in (3, 1)]).astype(jnp.int32)]
  transfers between devices with their start and end apart: 2 -> 31, of which waited for: 2 -> 11; matrix products, arithmetic and copies ran while one was open for 0% -> 6% of each run, Pallas kernels for 0% -> 37%
where the time goes in v1:
time: 206 us
  Pallas kernels  95.1 us (46%)
  waiting for transfers between devices  50.7 us (25%)
  starting transfers between devices  40.1 us (19%)
  other arithmetic  13.1 us (6%)
  local copies, waits for them, and re-layouts  6.56 us (3%)
    pallas_call x4, Pallas kernels, gate_up(): pl.pallas_call(functools.partial(gate_up_body, first, last, rows), grid_s...  54 us
    ppermute x31, waiting for transfers between devices, swap(): return lax.ppermute(x, 'gx', [(i, i ^ mask) for i in range(n)])  50.7 us
    pallas_call x8, Pallas kernels, down(): pl.pallas_call(down_body, grid_spec=pltpu.PrefetchScalarGridSpec(num_scal...  41.1 us
    ppermute x31, starting transfers between devices, swap(): return lax.ppermute(x, 'gx', [(i, i ^ mask) for i in range(n)])  40.1 us
    unnamed x42, local copies, waits for them, and re-layouts  5.08 us
  transfers between devices with their start and end apart: 31, of which 11 were waited for; matrix products, arithmetic and copies ran while one was open for 6% of the time, Pallas kernels for 37%

profile of v1, /device:TPU:0, one launch (start us, length us, event | category | flops | bytes accessed | tf_op | source)
XLA Modules:
  0.0 205.9 jit_solution(7577857084035601977)
XLA Ops:
  1.2 3.1 %collective-permute-start.4 = (f32[384]{0:T(512)S(1)}, f32[384]{0:T(512)S(1)}, u32[]{:S(2)}, u32[]{:S(2)}) collective-permute-start(f32[384]{0:T(512)S(1)} %fusion), channel_id=1, source_target_pairs={{0,4},{1,5},{2,6},{3,7},{4,0},{5,1},{6,2},{7,3},{8,12},{9,13},{10,... | collective-permute-start | bytes 4616 | tf_op jit(solution)/shard_map/ppermute | solution.py:17
  4.2 2.6 %collective-permute-start.5 = (f32[384]{0:T(512)S(1)}, f32[384]{0:T(512)S(1)}, u32[]{:S(2)}, u32[]{:S(2)}) collective-permute-start(f32[384]{0:T(512)S(1)} %fusion), channel_id=1, source_target_pairs={{0,8},{1,9},{2,10},{3,11},{4,12},{5,13},{6,14},{7,15},{8,0},{9,1},... | collective-permute-start | bytes 4616 | tf_op jit(solution)/shard_map/ppermute | solution.py:17
  16.1 3.5 %collective-permute-start.9 = (bf16[400,512]{1,0:T(8,128)(2,1)S(1)}, bf16[400,512]{1,0:T(8,128)(2,1)S(1)}, u32[]{:S(2)}, u32[]{:S(2)}) collective-permute-start(bf16[400,512]{1,0:T(8,128)(2,1)S(1)} %pad_maximum_fusion.refs_0_), channel_id=1, source_target_pairs={{0,8},{1,9},{2,10},{3,11},{4,12},{5,13},{6,14},{7,15},{8,0},{9,1},... | collective-permute-start | bytes 1228808 | tf_op jit(solution)/shard_map/ppermute | solution.py:17
  20.8 2.4 %collective-permute-done.7 = f32[384]{0:T(512)S(1)} collective-permute-done((f32[384]{0:T(512)S(1)}, f32[384]{0:T(512)S(1)}, u32[]{:S(2)}, u32[]{:S(2)}) %collective-permute-start.7) | collective-permute-done | bytes 1568 | tf_op jit(solution)/shard_map/ppermute | solution.py:17
  24.7 11.1 %collective-permute-done.13.refs_0_ = bf16[400,512]{1,0:T(8,128)(2,1)S(1)} collective-permute-done((bf16[400,512]{1,0:T(8,128)(2,1)S(1)}, bf16[400,512]{1,0:T(8,128)(2,1)S(1)}, u32[]{:S(2)}, u32[]{:S(2)}) %collective-permute-start.13) | collective-permute-done | bytes 409632 | tf_op jit(solution)/shard_map/ppermute | solution.py:17
  37.4 10.1 %collective-permute-done.9.refs_0_ = bf16[400,512]{1,0:T(8,128)(2,1)S(1)} collective-permute-done((bf16[400,512]{1,0:T(8,128)(2,1)S(1)}, bf16[400,512]{1,0:T(8,128)(2,1)S(1)}, u32[]{:S(2)}, u32[]{:S(2)}) %collective-permute-start.9) | collective-permute-done | bytes 409632 | tf_op jit(solution)/shard_map/ppermute | solution.py:17
  50.5 12.5 %gate_up.4 = (f32[384,1664]{1,0:T(8,128)}, f32[384,1664]{1,0:T(8,128)}) custom-call(s32[4]{0:T(128)} %pad_add_fusion.4.idx_ref, bf16[400,512]{1,0:T(8,128)(2,1)} %copy-done.5, bf16[400,512]{1,0:T(8,128)(2,1)} %copy-done.18, bf16[400,512]{1,0:T(8,128)(2,1)} %copy-done.19, bf16[400,512]{1,0:T(8,128)(2,1)} %copy-done.20, f32[384,128]{1,0:T(8,128)} %broadcast_in_dim.5.refs_4_, ...), custom_call_target="tpu_custom_call" | custom-call | flops 5234491392 | bytes 18743296 | tf_op jit(solution)/shard_map/gate_up/pallas_call | solution.py:78
  65.3 14.2 %gate_up.5 = (f32[384,1664]{1,0:T(8,128)}, f32[384,1664]{1,0:T(8,128)}) custom-call(s32[4]{0:T(128)} %pad_add_fusion.3.idx_ref, bf16[400,512]{1,0:T(8,128)(2,1)} %copy-done.7, bf16[400,512]{1,0:T(8,128)(2,1)} %copy-done.9, bf16[400,512]{1,0:T(8,128)(2,1)} %copy-done.13, bf16[400,512]{1,0:T(8,128)(2,1)} %copy-done.16, f32[384,128]{1,0:T(8,128)} %broadcast_in_dim.5.refs_4_, ...), custom_call_target="tpu_custom_call" | custom-call | flops 5234491392 | bytes 18743296 | tf_op jit(solution)/shard_map/gate_up/pallas_call | solution.py:78
  80.4 14.3 %gate_up.6 = (f32[384,1664]{1,0:T(8,128)}, f32[384,1664]{1,0:T(8,128)}) custom-call(s32[4]{0:T(128)} %pad_add_fusion.2.idx_ref, bf16[400,512]{1,0:T(8,128)(2,1)} %copy-done.6, bf16[400,512]{1,0:T(8,128)(2,1)} %copy-done.11, bf16[400,512]{1,0:T(8,128)(2,1)} %copy-done.12, bf16[400,512]{1,0:T(8,128)(2,1)} %copy-done.17, f32[384,128]{1,0:T(8,128)} %broadcast_in_dim.5.refs_4_, ...), custom_call_target="tpu_custom_call" | custom-call | flops 5234491392 | bytes 18743296 | tf_op jit(solution)/shard_map/gate_up/pallas_call | solution.py:78
  95.5 13.1 %gate_up.7.hidden_ref = bf16[384,1664]{1,0:T(8,128)(2,1)} custom-call(s32[4]{0:T(128)} %pad_add_fusion.1.idx_ref, bf16[400,512]{1,0:T(8,128)(2,1)} %copy-done.8, bf16[400,512]{1,0:T(8,128)(2,1)} %copy-done.10, bf16[400,512]{1,0:T(8,128)(2,1)} %copy-done.14, bf16[400,512]{1,0:T(8,128)(2,1)} %copy-done.15, f32[384,128]{1,0:T(8,128)} %broadcast_in_dim.5.refs_4_, ...), custom_call_target="tpu_custom_call" | custom-call | flops 5234491392 | bytes 18743296 | tf_op jit(solution)/shard_map/gate_up/pallas_call | solution.py:78
  108.6 5.3 %down.9 = bf16[2,384,512]{2,1,0:T(8,128)(2,1)} custom-call(s32[2]{0:T(128)} %pad_add_fusion.5.idx_ref, bf16[384,1664]{1,0:T(8,128)(2,1)} %gate_up.7.hidden_ref, bf16[1664,8192]{1,0:T(8,128)(2,1)} %weight_ref.15), custom_call_target="tpu_custom_call" | custom-call | flops 1308622848 | bytes 4980736 | tf_op jit(solution)/shard_map/down/pallas_call | solution.py:107
  114.4 5.1 %down.11 = bf16[2,384,512]{2,1,0:T(8,128)(2,1)} custom-call(s32[2]{0:T(128)} %pad_add_fusion.7.idx_ref, bf16[384,1664]{1,0:T(8,128)(2,1)} %gate_up.7.hidden_ref, bf16[1664,8192]{1,0:T(8,128)(2,1)} %weight_ref.15), custom_call_target="tpu_custom_call" | custom-call | flops 1308622848 | bytes 4980736 | tf_op jit(solution)/shard_map/down/pallas_call | solution.py:107
  119.5 5.0 %down.13 = bf16[2,384,512]{2,1,0:T(8,128)(2,1)} custom-call(s32[2]{0:T(128)} %pad_add_fusion.9.idx_ref, bf16[384,1664]{1,0:T(8,128)(2,1)} %gate_up.7.hidden_ref, bf16[1664,8192]{1,0:T(8,128)(2,1)} %weight_ref.15), custom_call_target="tpu_custom_call" | custom-call | flops 1308622848 | bytes 4980736 | tf_op jit(solution)/shard_map/down/pallas_call | solution.py:107
  125.0 5.1 %down.15 = bf16[2,384,512]{2,1,0:T(8,128)(2,1)} custom-call(s32[2]{0:T(128)} %pad_add_fusion.11.idx_ref, bf16[384,1664]{1,0:T(8,128)(2,1)} %gate_up.7.hidden_ref, bf16[1664,8192]{1,0:T(8,128)(2,1)} %weight_ref.15), custom_call_target="tpu_custom_call" | custom-call | flops 1308622848 | bytes 4980736 | tf_op jit(solution)/shard_map/down/pallas_call | solution.py:107
  130.1 5.2 %down.8 = f32[2,384,512]{2,1,0:T(8,128)} custom-call(s32[2]{0:T(128)} %pad_add_fusion.idx_ref, bf16[384,1664]{1,0:T(8,128)(2,1)} %gate_up.7.hidden_ref, bf16[1664,8192]{1,0:T(8,128)(2,1)} %weight_ref.15), custom_call_target="tpu_custom_call" | custom-call | flops 1308622848 | bytes 4980736 | tf_op jit(solution)/shard_map/down/pallas_call | solution.py:107
  135.3 5.2 %down.10 = f32[2,384,512]{2,1,0:T(8,128)} custom-call(s32[2]{0:T(128)} %pad_add_fusion.6.idx_ref, bf16[384,1664]{1,0:T(8,128)(2,1)} %gate_up.7.hidden_ref, bf16[1664,8192]{1,0:T(8,128)(2,1)} %weight_ref.15), custom_call_target="tpu_custom_call" | custom-call | flops 1308622848 | bytes 4980736 | tf_op jit(solution)/shard_map/down/pallas_call | solution.py:107
  140.5 5.2 %down.12 = f32[2,384,512]{2,1,0:T(8,128)} custom-call(s32[2]{0:T(128)} %pad_add_fusion.8.idx_ref, bf16[384,1664]{1,0:T(8,128)(2,1)} %gate_up.7.hidden_ref, bf16[1664,8192]{1,0:T(8,128)(2,1)} %weight_ref.15), custom_call_target="tpu_custom_call" | custom-call | flops 1308622848 | bytes 4980736 | tf_op jit(solution)/shard_map/down/pallas_call | solution.py:107
  145.6 5.2 %down.14 = f32[2,384,512]{2,1,0:T(8,128)} custom-call(s32[2]{0:T(128)} %pad_add_fusion.10.idx_ref, bf16[384,1664]{1,0:T(8,128)(2,1)} %gate_up.7.hidden_ref, bf16[1664,8192]{1,0:T(8,128)(2,1)} %weight_ref.15), custom_call_target="tpu_custom_call" | custom-call | flops 1308622848 | bytes 4980736 | tf_op jit(solution)/shard_map/down/pallas_call | solution.py:107
  158.2 6.2 %collective-permute-done.21 = bf16[384,512]{1,0:T(8,128)(2,1)S(1)} collective-permute-done((bf16[384,512]{1,0:T(8,128)(2,1)S(1)}, bf16[384,512]{1,0:T(8,128)(2,1)S(1)}, u32[]{:S(2)}, u32[]{:S(2)}) %collective-permute-start.21) | collective-permute-done | bytes 393248 | tf_op jit(solution)/shard_map/ppermute | solution.py:17
  164.6 5.0 %collective-permute-start.22 = (bf16[384,512]{1,0:T(8,128)(2,1)S(1)}, bf16[384,512]{1,0:T(8,128)(2,1)S(1)}, u32[]{:S(2)}, u32[]{:S(2)}) collective-permute-start(bf16[384,512]{1,0:T(8,128)(2,1)S(1)} %fusion.17), channel_id=1, source_target_pairs={{0,12},{1,13},{2,14},{3,15},{4,8},{5,9},{6,10},{7,11},{8,4},{9,5},... | collective-permute-start | bytes 1179656 | tf_op jit(solution)/shard_map/ppermute | solution.py:17
  169.6 3.2 %collective-permute-done.24 = bf16[384,512]{1,0:T(8,128)(2,1)S(1)} collective-permute-done((bf16[384,512]{1,0:T(8,128)(2,1)S(1)}, bf16[384,512]{1,0:T(8,128)(2,1)S(1)}, u32[]{:S(2)}, u32[]{:S(2)}) %collective-permute-start.24) | collective-permute-done | bytes 393248 | tf_op jit(solution)/shard_map/ppermute | solution.py:17
  173.1 8.0 %collective-permute-start.25 = (bf16[384,512]{1,0:T(8,128)(2,1)S(1)}, bf16[384,512]{1,0:T(8,128)(2,1)S(1)}, u32[]{:S(2)}, u32[]{:S(2)}) collective-permute-start(bf16[384,512]{1,0:T(8,128)(2,1)S(1)} %fusion.13), channel_id=1, source_target_pairs={{0,8},{1,9},{2,10},{3,11},{4,12},{5,13},{6,14},{7,15},{8,0},{9,1},... | collective-permute-start | bytes 1179656 | tf_op jit(solution)/shard_map/ppermute | solution.py:17
  181.5 7.1 %collective-permute-start.28 = (bf16[384,512]{1,0:T(8,128)(2,1)S(1)}, bf16[384,512]{1,0:T(8,128)(2,1)S(1)}, u32[]{:S(2)}, u32[]{:S(2)}) collective-permute-start(bf16[384,512]{1,0:T(8,128)(2,1)S(1)} %fusion.9), channel_id=1, source_target_pairs={{0,4},{1,5},{2,6},{3,7},{4,0},{5,1},{6,2},{7,3},{8,12},{9,13},{10,... | collective-permute-start | bytes 1179656 | tf_op jit(solution)/shard_map/ppermute | solution.py:17
  189.2 14.3 %collective-permute-done.25 = bf16[384,512]{1,0:T(8,128)(2,1)S(1)} collective-permute-done((bf16[384,512]{1,0:T(8,128)(2,1)S(1)}, bf16[384,512]{1,0:T(8,128)(2,1)S(1)}, u32[]{:S(2)}, u32[]{:S(2)}) %collective-permute-start.25) | collective-permute-done | bytes 393248 | tf_op jit(solution)/shard_map/ppermute | solution.py:17
  (123 shorter events, 33.8 us)
Async XLA Ops:
  8.5 16.1 %collective-permute-start.17 = (bf16[400,512]{1,0:T(8,128)(2,1)S(1)}, bf16[400,512]{1,0:T(8,128)(2,1)S(1)}, u32[]{:S(2)}, u32[]{:S(2)}) collective-permute-start(bf16[400,512]{1,0:T(8,128)(2,1)S(1)} %pad_maximum_fusion.refs_0_), channel_id=1, source_target_pairs={{0,2},{1,3},{2,0},{3,1},{4,6},{5,7},{6,4},{7,5},{8,10},{9,11},{10,... | collective-permute-start | bytes 1228808 | tf_op jit(solution)/shard_map/ppermute | solution.py:17
  10.4 26.9 %collective-permute-start.18 = (bf16[400,512]{1,0:T(8,128)(2,1)S(1)}, bf16[400,512]{1,0:T(8,128)(2,1)S(1)}, u32[]{:S(2)}, u32[]{:S(2)}) collective-permute-start(bf16[400,512]{1,0:T(8,128)(2,1)S(1)} %pad_maximum_fusion.refs_0_), channel_id=1, source_target_pairs={{0,1},{1,0},{2,3},{3,2},{4,5},{5,4},{6,7},{7,6},{8,9},{9,8},{10,11... | collective-permute-start | bytes 1228808 | tf_op jit(solution)/shard_map/ppermute | solution.py:17
  15.4 20.3 %collective-permute-start.13 = (bf16[400,512]{1,0:T(8,128)(2,1)S(1)}, bf16[400,512]{1,0:T(8,128)(2,1)S(1)}, u32[]{:S(2)}, u32[]{:S(2)}) collective-permute-start(bf16[400,512]{1,0:T(8,128)(2,1)S(1)} %pad_maximum_fusion.refs_0_), channel_id=1, source_target_pairs={{0,4},{1,5},{2,6},{3,7},{4,0},{5,1},{6,2},{7,3},{8,12},{9,13},{10,... | collective-permute-start | bytes 1228808 | tf_op jit(solution)/shard_map/ppermute | solution.py:17
  16.1 31.3 %collective-permute-start.9 = (bf16[400,512]{1,0:T(8,128)(2,1)S(1)}, bf16[400,512]{1,0:T(8,128)(2,1)S(1)}, u32[]{:S(2)}, u32[]{:S(2)}) collective-permute-start(bf16[400,512]{1,0:T(8,128)(2,1)S(1)} %pad_maximum_fusion.refs_0_), channel_id=1, source_target_pairs={{0,8},{1,9},{2,10},{3,11},{4,12},{5,13},{6,14},{7,15},{8,0},{9,1},... | collective-permute-start | bytes 1228808 | tf_op jit(solution)/shard_map/ppermute | solution.py:17
  24.4 23.5 %collective-permute-start = (bf16[400,512]{1,0:T(8,128)(2,1)S(1)}, bf16[400,512]{1,0:T(8,128)(2,1)S(1)}, u32[]{:S(2)}, u32[]{:S(2)}) collective-permute-start(bf16[400,512]{1,0:T(8,128)(2,1)S(1)} %pad_maximum_fusion.refs_0_), channel_id=1, source_target_pairs={{0,12},{1,13},{2,14},{3,15},{4,8},{5,9},{6,10},{7,11},{8,4},{9,5},... | collective-permute-start | bytes 1228808 | tf_op jit(solution)/shard_map/ppermute | solution.py:17
  24.6 23.3 %collective-permute-start.19 = (bf16[400,512]{1,0:T(8,128)(2,1)S(1)}, bf16[400,512]{1,0:T(8,128)(2,1)S(1)}, u32[]{:S(2)}, u32[]{:S(2)}) collective-permute-start(bf16[400,512]{1,0:T(8,128)(2,1)S(1)} %collective-permute-done.17.refs_1_), channel_id=1, source_target_pairs={{0,1},{1,0},{2,3},{3,2},{4,5},{5,4},{6,7},{7,6},{8,9},{9,8},{10,11... | collective-permute-start | bytes 1228808 | tf_op jit(solution)/shard_map/ppermute | solution.py:17
  37.3 25.8 %collective-permute-start.15 = (bf16[400,512]{1,0:T(8,128)(2,1)S(1)}, bf16[400,512]{1,0:T(8,128)(2,1)S(1)}, u32[]{:S(2)}, u32[]{:S(2)}) collective-permute-start(bf16[400,512]{1,0:T(8,128)(2,1)S(1)} %collective-permute-done.13.refs_0_), channel_id=1, source_target_pairs={{0,1},{1,0},{2,3},{3,2},{4,5},{5,4},{6,7},{7,6},{8,9},{9,8},{10,11... | collective-permute-start | bytes 1228808 | tf_op jit(solution)/shard_map/ppermute | solution.py:17
  47.4 16.1 %collective-permute-start.10 = (bf16[400,512]{1,0:T(8,128)(2,1)S(1)}, bf16[400,512]{1,0:T(8,128)(2,1)S(1)}, u32[]{:S(2)}, u32[]{:S(2)}) collective-permute-start(bf16[400,512]{1,0:T(8,128)(2,1)S(1)} %collective-permute-done.9.refs_0_), channel_id=1, source_target_pairs={{0,2},{1,3},{2,0},{3,1},{4,6},{5,7},{6,4},{7,5},{8,10},{9,11},{10,... | collective-permute-start | bytes 1228808 | tf_op jit(solution)/shard_map/ppermute | solution.py:17
  48.0 31.5 %collective-permute-start.11 = (bf16[400,512]{1,0:T(8,128)(2,1)S(1)}, bf16[400,512]{1,0:T(8,128)(2,1)S(1)}, u32[]{:S(2)}, u32[]{:S(2)}) collective-permute-start(bf16[400,512]{1,0:T(8,128)(2,1)S(1)} %collective-permute-done.9.refs_0_), channel_id=1, source_target_pairs={{0,1},{1,0},{2,3},{3,2},{4,5},{5,4},{6,7},{7,6},{8,9},{9,8},{10,11... | collective-permute-start | bytes 1228808 | tf_op jit(solution)/shard_map/ppermute | solution.py:17
  48.0 16.4 %collective-permute-start.1 = (bf16[400,512]{1,0:T(8,128)(2,1)S(1)}, bf16[400,512]{1,0:T(8,128)(2,1)S(1)}, u32[]{:S(2)}, u32[]{:S(2)}) collective-permute-start(bf16[400,512]{1,0:T(8,128)(2,1)S(1)} %collective-permute-done.refs_0_), channel_id=1, source_target_pairs={{0,2},{1,3},{2,0},{3,1},{4,6},{5,7},{6,4},{7,5},{8,10},{9,11},{10,... | collective-permute-start | bytes 1228808 | tf_op jit(solution)/shard_map/ppermute | solution.py:17
  49.6 14.9 %collective-permute-start.16 = (bf16[400,512]{1,0:T(8,128)(2,1)S(1)}, bf16[400,512]{1,0:T(8,128)(2,1)S(1)}, u32[]{:S(2)}, u32[]{:S(2)}) collective-permute-start(bf16[400,512]{1,0:T(8,128)(2,1)S(1)} %collective-permute-done.14.refs_1_), channel_id=1, source_target_pairs={{0,1},{1,0},{2,3},{3,2},{4,5},{5,4},{6,7},{7,6},{8,9},{9,8},{10,11... | collective-permute-start | bytes 1228808 | tf_op jit(solution)/shard_map/ppermute | solution.py:17
  63.1 31.6 %collective-permute-start.2 = (bf16[400,512]{1,0:T(8,128)(2,1)S(1)}, bf16[400,512]{1,0:T(8,128)(2,1)S(1)}, u32[]{:S(2)}, u32[]{:S(2)}) collective-permute-start(bf16[400,512]{1,0:T(8,128)(2,1)S(1)} %collective-permute-done.refs_0_), channel_id=1, source_target_pairs={{0,1},{1,0},{2,3},{3,2},{4,5},{5,4},{6,7},{7,6},{8,9},{9,8},{10,11... | collective-permute-start | bytes 1228808 | tf_op jit(solution)/shard_map/ppermute | solution.py:17
  63.5 15.9 %collective-permute-start.12 = (bf16[400,512]{1,0:T(8,128)(2,1)S(1)}, bf16[400,512]{1,0:T(8,128)(2,1)S(1)}, u32[]{:S(2)}, u32[]{:S(2)}) collective-permute-start(bf16[400,512]{1,0:T(8,128)(2,1)S(1)} %collective-permute-done.10.refs_1_), channel_id=1, source_target_pairs={{0,1},{1,0},{2,3},{3,2},{4,5},{5,4},{6,7},{7,6},{8,9},{9,8},{10,11... | collective-permute-start | bytes 1228808 | tf_op jit(solution)/shard_map/ppermute | solution.py:17
  64.4 30.2 %collective-permute-start.3 = (bf16[400,512]{1,0:T(8,128)(2,1)S(1)}, bf16[400,512]{1,0:T(8,128)(2,1)S(1)}, u32[]{:S(2)}, u32[]{:S(2)}) collective-permute-start(bf16[400,512]{1,0:T(8,128)(2,1)S(1)} %collective-permute-done.1.refs_1_), channel_id=1, source_target_pairs={{0,1},{1,0},{2,3},{3,2},{4,5},{5,4},{6,7},{7,6},{8,9},{9,8},{10,11... | collective-permute-start | bytes 1228808 | tf_op jit(solution)/shard_map/ppermute | solution.py:17
  113.9 36.9 %collective-permute-start.20 = (bf16[2,384,512]{2,1,0:T(8,128)(2,1)}, bf16[2,384,512]{2,1,0:T(8,128)(2,1)S(1)}, u32[]{:S(2)}, u32[]{:S(2)}) collective-permute-start(bf16[2,384,512]{2,1,0:T(8,128)(2,1)} %down.9), channel_id=1, source_target_pairs={{0,1},{1,0},{2,3},{3,2},{4,5},{5,4},{6,7},{7,6},{8,9},{9,8},{10,11... | collective-permute-start | bytes 2359304 | tf_op jit(solution)/shard_map/ppermute | solution.py:17
  119.4 33.3 %collective-permute-start.23 = (bf16[2,384,512]{2,1,0:T(8,128)(2,1)}, bf16[2,384,512]{2,1,0:T(8,128)(2,1)S(1)}, u32[]{:S(2)}, u32[]{:S(2)}) collective-permute-start(bf16[2,384,512]{2,1,0:T(8,128)(2,1)} %down.11), channel_id=1, source_target_pairs={{0,1},{1,0},{2,3},{3,2},{4,5},{5,4},{6,7},{7,6},{8,9},{9,8},{10,11... | collective-permute-start | bytes 2359304 | tf_op jit(solution)/shard_map/ppermute | solution.py:17
  124.5 30.5 %collective-permute-start.26 = (bf16[2,384,512]{2,1,0:T(8,128)(2,1)}, bf16[2,384,512]{2,1,0:T(8,128)(2,1)S(1)}, u32[]{:S(2)}, u32[]{:S(2)}) collective-permute-start(bf16[2,384,512]{2,1,0:T(8,128)(2,1)} %down.13), channel_id=1, source_target_pairs={{0,1},{1,0},{2,3},{3,2},{4,5},{5,4},{6,7},{7,6},{8,9},{9,8},{10,11... | collective-permute-start | bytes 2359304 | tf_op jit(solution)/shard_map/ppermute | solution.py:17
  130.1 26.5 %collective-permute-start.29 = (bf16[2,384,512]{2,1,0:T(8,128)(2,1)}, bf16[2,384,512]{2,1,0:T(8,128)(2,1)S(1)}, u32[]{:S(2)}, u32[]{:S(2)}) collective-permute-start(bf16[2,384,512]{2,1,0:T(8,128)(2,1)} %down.15), channel_id=1, source_target_pairs={{0,1},{1,0},{2,3},{3,2},{4,5},{5,4},{6,7},{7,6},{8,9},{9,8},{10,11... | collective-permute-start | bytes 2359304 | tf_op jit(solution)/shard_map/ppermute | solution.py:17
  154.0 18.8 %collective-permute-start.24 = (bf16[384,512]{1,0:T(8,128)(2,1)S(1)}, bf16[384,512]{1,0:T(8,128)(2,1)S(1)}, u32[]{:S(2)}, u32[]{:S(2)}) collective-permute-start(bf16[384,512]{1,0:T(8,128)(2,1)S(1)} %fusion.19), channel_id=1, source_target_pairs={{0,2},{1,3},{2,0},{3,1},{4,6},{5,7},{6,4},{7,5},{8,10},{9,11},{10,... | collective-permute-start | bytes 1179656 | tf_op jit(solution)/shard_map/ppermute | solution.py:17
  155.6 25.6 %collective-permute-start.27 = (bf16[384,512]{1,0:T(8,128)(2,1)S(1)}, bf16[384,512]{1,0:T(8,128)(2,1)S(1)}, u32[]{:S(2)}, u32[]{:S(2)}) collective-permute-start(bf16[384,512]{1,0:T(8,128)(2,1)S(1)} %fusion.20), channel_id=1, source_target_pairs={{0,2},{1,3},{2,0},{3,1},{4,6},{5,7},{6,4},{7,5},{8,10},{9,11},{10,... | collective-permute-start | bytes 1179656 | tf_op jit(solution)/shard_map/ppermute | solution.py:17
  157.2 32.1 %collective-permute-start.30 = (bf16[384,512]{1,0:T(8,128)(2,1)S(1)}, bf16[384,512]{1,0:T(8,128)(2,1)S(1)}, u32[]{:S(2)}, u32[]{:S(2)}) collective-permute-start(bf16[384,512]{1,0:T(8,128)(2,1)S(1)} %fusion.21), channel_id=1, source_target_pairs={{0,2},{1,3},{2,0},{3,1},{4,6},{5,7},{6,4},{7,5},{8,10},{9,11},{10,... | collective-permute-start | bytes 1179656 | tf_op jit(solution)/shard_map/ppermute | solution.py:17
  164.6 24.6 %collective-permute-start.22 = (bf16[384,512]{1,0:T(8,128)(2,1)S(1)}, bf16[384,512]{1,0:T(8,128)(2,1)S(1)}, u32[]{:S(2)}, u32[]{:S(2)}) collective-permute-start(bf16[384,512]{1,0:T(8,128)(2,1)S(1)} %fusion.17), channel_id=1, source_target_pairs={{0,12},{1,13},{2,14},{3,15},{4,8},{5,9},{6,10},{7,11},{8,4},{9,5},... | collective-permute-start | bytes 1179656 | tf_op jit(solution)/shard_map/ppermute | solution.py:17
  173.1 30.5 %collective-permute-start.25 = (bf16[384,512]{1,0:T(8,128)(2,1)S(1)}, bf16[384,512]{1,0:T(8,128)(2,1)S(1)}, u32[]{:S(2)}, u32[]{:S(2)}) collective-permute-start(bf16[384,512]{1,0:T(8,128)(2,1)S(1)} %fusion.13), channel_id=1, source_target_pairs={{0,8},{1,9},{2,10},{3,11},{4,12},{5,13},{6,14},{7,15},{8,0},{9,1},... | collective-permute-start | bytes 1179656 | tf_op jit(solution)/shard_map/ppermute | solution.py:17
  181.5 23.3 %collective-permute-start.28 = (bf16[384,512]{1,0:T(8,128)(2,1)S(1)}, bf16[384,512]{1,0:T(8,128)(2,1)S(1)}, u32[]{:S(2)}, u32[]{:S(2)}) collective-permute-start(bf16[384,512]{1,0:T(8,128)(2,1)S(1)} %fusion.9), channel_id=1, source_target_pairs={{0,4},{1,5},{2,6},{3,7},{4,0},{5,1},{6,2},{7,3},{8,12},{9,13},{10,... | collective-permute-start | bytes 1179656 | tf_op jit(solution)/shard_map/ppermute | solution.py:17
  (28 other events, 298.4 us)

commit v2 on v0

v2 whole, which is shorter than its diff:
```python
import functools

import jax
import jax.numpy as jnp
from jax import lax
from jax.experimental import pallas as pl
from jax.experimental.pallas import tpu as pltpu
from jax.sharding import PartitionSpec as P

epsilon = 1e-05
INNER = 4
LINE = 4
VMEM_LIMIT = 30 * 1024 * 1024

PAIRS = ((0, 1), (1, 0), (2, 3), (3, 2))
MIDDLE = ((1, 2), (2, 1))
OUTWARD = ((1, 0), (2, 3))
INWARD = ((0, 1), (3, 2))


def swap(x, mask):
    return lax.ppermute(x, "gx", [(i, i ^ mask) for i in range(INNER * LINE)])


def along(x, pairs):
    moves = [(a * INNER + q, b * INNER + q) for a, b in pairs for q in range(INNER)]
    return lax.ppermute(x, "gx", moves)


def pick(table, s):
    value = jnp.int32(table[0])
    for i, entry in enumerate(table[1:], 1):
        value = jnp.where(s == i, jnp.int32(entry), value)
    return value


def gate_up_body(codes, first, last, rows, main, features, me_ref, *refs):
    count = len(codes)
    blocks = refs[:count]
    stats_ref, gate_ref, up_ref = refs[count : count + 3]
    rest = refs[count + 3 :]
    if not first:
        before = rest[:3]
        rest = rest[3:]
    if last:
        hidden_ref, *rest = rest
    gate_acc, up_acc, mixed_acc, factor_ref = rest[-4:]
    step = pl.program_id(0)

    @pl.when(step == 0)
    def _():
        total = jnp.sum(stats_ref[:, :rows], axis=0, keepdims=True)
        factor = lax.rsqrt(total / features + epsilon)
        factor_ref[...] = jnp.broadcast_to(factor, (128, rows)).T

    for s in range(count):

        @pl.when(step == s)
        def _(s=s):
            gain = stats_ref[pl.ds(me_ref[0] ^ codes[s], 1), rows:]
            x = blocks[s][...].astype(jnp.float32)
            normed = (x * factor_ref[:, :1] * gain).astype(jnp.bfloat16)
            gate = gate_ref[...]
            up = up_ref[...]
            mixed = jnp.concatenate([gate[:, main:], up[:, main:]], axis=1)
            sums = []
            for acc, old, weight in zip(
                (gate_acc, up_acc, mixed_acc),
                (None,) * 3 if first else before,
                (gate[:, :main], up[:, :main], mixed),
            ):
                value = jnp.dot(normed, weight, preferred_element_type=jnp.float32)
                if s:
                    value = acc[...] + value
                elif old is not None:
                    value = old[...] + value
                if s == count - 1 and last:
                    sums.append(value)
                else:
                    acc[...] = value
            if sums:
                g, u, m = sums
                rem = m.shape[1] // 2
                hidden_ref[:, :main] = (g / (1.0 + jnp.exp(-g)) * u).astype(jnp.bfloat16)
                g, u = m[:, :rem], m[:, rem:]
                hidden_ref[:, main:] = (g / (1.0 + jnp.exp(-g)) * u).astype(jnp.bfloat16)


def gate_up(me, blocks, codes, stats, gate_weight, up_weight, acc, last):
    rows, depth = blocks[0].shape
    features, ff = gate_weight.shape
    main = ff // 256 * 256 if ff % 256 else ff - 256
    rem = ff - main
    first = acc is None
    count = len(blocks)
    whole = lambda shape: pl.BlockSpec(shape, lambda s, me: (0, 0))
    weight = pl.BlockSpec((depth, ff), lambda s, me: (me[0] ^ pick(codes, s), 0))
    in_specs = [whole(b.shape) for b in blocks] + [whole(stats.shape), weight, weight]
    args = list(blocks) + [stats, gate_weight, up_weight]
    shapes = [(rows, main), (rows, main), (rows, 2 * rem)]
    if not first:
        in_specs += [whole(s) for s in shapes]
        args += list(acc)
    scratch = [pltpu.VMEM((rows, 128), jnp.float32)]
    if last:
        out_shape = [jax.ShapeDtypeStruct((rows, ff), jnp.bfloat16)]
        out_specs = [whole((rows, ff))]
        scratch = [pltpu.VMEM(s, jnp.float32) for s in shapes] + scratch
    else:
        out_shape = [jax.ShapeDtypeStruct(s, jnp.float32) for s in shapes]
        out_specs = [whole(s) for s in shapes]
    return pl.pallas_call(
        functools.partial(gate_up_body, codes, first, last, rows, main, features),
        grid_spec=pltpu.PrefetchScalarGridSpec(
            num_scalar_prefetch=1,
            grid=(count,),
            in_specs=in_specs,
            out_specs=out_specs,
            scratch_shapes=scratch,
        ),
        out_shape=out_shape,
        compiler_params=pltpu.CompilerParams(vmem_limit_bytes=VMEM_LIMIT),
        cost_estimate=pl.CostEstimate(
            flops=4 * rows * depth * count * ff,
            bytes_accessed=4 * depth * count * ff,
            transcendentals=0,
        ),
        name="gate_up",
    )(me, *args)


def down_block(hidden_ref, weight_ref):
    ff = hidden_ref.shape[1]
    main = ff // 256 * 256
    value = jnp.dot(
        hidden_ref[:, :main], weight_ref[:main, :], preferred_element_type=jnp.float32
    )
    if main < ff:
        value = value + jnp.dot(
            hidden_ref[:, main:], weight_ref[main:, :], preferred_element_type=jnp.float32
        )
    return value


def away_body(me_ref, hidden_ref, weight_ref, after_ref, out_ref):
    out_ref[0] = down_block(hidden_ref, weight_ref).astype(out_ref.dtype)


def stay_body(me_ref, hidden_ref, weight_ref, got_ref, far_ref, near_ref):
    value = down_block(hidden_ref, weight_ref) + got_ref[0].astype(jnp.float32)

    @pl.when(pl.program_id(0) == 0)
    def _():
        far_ref[...] = value.astype(far_ref.dtype)

    @pl.when(pl.program_id(0) == 1)
    def _():
        near_ref[...] = value


def down(body, me, codes, hidden, down_weight, width, extra, extra_spec, out_shape, out_specs):
    rows, ff = hidden.shape
    count = len(codes)
    return pl.pallas_call(
        body,
        grid_spec=pltpu.PrefetchScalarGridSpec(
            num_scalar_prefetch=1,
            grid=(count,),
            in_specs=[
                pl.BlockSpec((rows, ff), lambda s, me: (0, 0)),
                pl.BlockSpec((ff, width), lambda s, me: (0, me[0] ^ pick(codes, s))),
                extra_spec,
            ],
            out_specs=out_specs,
        ),
        out_shape=out_shape,
        compiler_params=pltpu.CompilerParams(vmem_limit_bytes=VMEM_LIMIT),
        cost_estimate=pl.CostEstimate(
            flops=2 * rows * ff * width * count,
            bytes_accessed=2 * ff * width * count,
            transcendentals=0,
        ),
        name=body.__name__,
    )(me, hidden, down_weight, extra)


def overlapped(activations, norm_gain, gate_weight, up_weight, down_weight):
    rows, width = activations.shape
    index = lax.axis_index("gx").astype(jnp.int32)
    z = index // INNER
    edge = (z == 0) | (z == LINE - 1)
    me = index[None]
    resident = activations.astype(jnp.float32)

    stats = jnp.concatenate(
        [jnp.sum(resident * resident, axis=1), norm_gain.astype(jnp.float32)]
    )
    stats = lax.all_gather(stats, "gx")

    neighbour = along(activations, PAIRS)
    inner = along(activations, MIDDLE)
    second_edge = along(inner, OUTWARD)
    second_middle = along(neighbour, MIDDLE)
    third_edge = along(second_middle, OUTWARD)
    slots = [
        activations,
        neighbour,
        jnp.where(edge, second_edge, second_middle),
        jnp.where(edge, third_edge, inner),
    ]
    groups = []
    for slot in slots:
        across = swap(slot, 2)
        groups.append([slot, swap(slot, 1), across, swap(across, 1)])

    order = (0, 1, 2, 3)
    parts = [
        [(k, q) for k in (0,) for q in order],
        [(k, q) for k in (1,) for q in order],
        [(k, q) for k in (2,) for q in order] + [(3, 0), (3, 1)],
        [(3, 2), (3, 3)],
    ]
    acc = None
    for i, part in enumerate(parts):
        codes = tuple(INNER * k + (0, 1, 2, 3)[q] for k, q in part)
        blocks = [groups[k][q] for k, q in part]
        acc = gate_up(
            me, blocks, codes, stats, gate_weight, up_weight, acc, i == len(parts) - 1
        )
    hidden = acc[0]

    def away(k, after):
        return down(
            away_body, me, (INNER * k + 3, INNER * k + 1), hidden, down_weight, width,
            after, pl.BlockSpec(memory_space=pl.ANY),
            jax.ShapeDtypeStruct((2, rows, width), jnp.bfloat16),
            pl.BlockSpec((1, rows, width), lambda s, me: (s, 0, 0)),
        )

    def stay(k, got):
        constant = pl.BlockSpec((rows, width), lambda s, me: (0, 0))
        return down(
            stay_body, me, (INNER * k + 2, INNER * k), hidden, down_weight, width,
            got, pl.BlockSpec((1, rows, width), lambda s, me: (s, 0, 0)),
            [
                jax.ShapeDtypeStruct((rows, width), jnp.bfloat16),
                jax.ShapeDtypeStruct((rows, width), jnp.float32),
            ],
            [constant, constant],
        )

    narrow = lambda x: x.astype(jnp.bfloat16)
    wide = lambda x: x.astype(jnp.float32)

    sums = [None] * LINE
    fars = [None] * LINE
    sent = {LINE - 1: away(LINE - 1, hidden)}
    for k in reversed(range(LINE)):
        if k:
            sent[k - 1] = away(k - 1, fars[k + 1] if k + 1 < LINE else sent[k])
        fars[k], near = stay(k, swap(sent[k], 1))
        sums[k] = near + wide(swap(fars[k], 2))

    middle_two = sums[2] + wide(along(narrow(sums[3]), INWARD))
    middle_three = sums[3] + wide(along(narrow(sums[2]), INWARD))
    one = sums[1] + wide(along(narrow(middle_two), MIDDLE))
    branch = (
        sums[0]
        + wide(along(narrow(one), PAIRS))
        + wide(along(narrow(middle_three), MIDDLE))
    )
    return (resident + branch).astype(jnp.bfloat16)


def plain(activations, norm_gain, gate_weight, up_weight, down_weight):
    resident = activations.astype(jnp.float32)
    totals = lax.psum(jnp.sum(resident * resident, axis=1), "gx")
    factor = lax.rsqrt(totals / (resident.shape[1] * lax.axis_size("gx")) + epsilon)
    normed = (resident * factor[:, None] * norm_gain.astype(jnp.float32)[None, :]).astype(
        jnp.bfloat16
    )
    pieces = lax.all_gather(normed, "gx", axis=1, tiled=True)
    gate_sum = jnp.dot(pieces, gate_weight, preferred_element_type=jnp.float32)
    up_sum = jnp.dot(pieces, up_weight, preferred_element_type=jnp.float32)
    hidden = (jax.nn.silu(gate_sum) * up_sum).astype(jnp.bfloat16)
    summed = lax.psum_scatter(
        lax.dot_general(
            down_weight, hidden, (((0,), (1,)), ((), ())), preferred_element_type=jnp.float32
        ),
        "gx",
        scatter_dimension=0,
        tiled=True,
    )
    return (resident + summed.T).astype(jnp.bfloat16)


def per_device(n, activations, norm_gain, gate_weight, up_weight, down_weight):
    args = (activations, norm_gain, gate_weight, up_weight, down_weight)
    rows, width = activations.shape
    tiled = rows % 128 == 0 and width % 128 == 0 and gate_weight.shape[1] % 128 == 0
    if n == INNER * LINE and tiled:
        return overlapped(*args)
    return plain(*args)


def solution(mesh):
    in_specs = (P("groups", "gx"), P("gx"), P(None, "gx"), P(None, "gx"), P("gx", None))
    out_specs = P("groups", "gx")
    return jax.shard_map(
        functools.partial(per_device, mesh.shape["gx"]),
        mesh=mesh,
        in_specs=in_specs,
        out_specs=out_specs,
        check_vma=False,
    )
```

time: 303 us -> 148 us (0.49)
  the two profiles are of different devices: /device:TPU:0 before, /device:TPU:16 now
where the time goes in v2:
time: 148 us; the launch traced here: 147 us
  Pallas kernels  63 us (43%)
  starting transfers between devices  33.9 us (23%)
  waiting for transfers between devices  25.3 us (17%)
  blocking collectives  20.1 us (14%)
  other arithmetic  3.58 us (2%)
    pallas_call x4, Pallas kernels, gate_up(): pl.pallas_call(functools.partial(gate_up_body, codes, first, last, rows,...  36.8 us
    pallas_call x8, Pallas kernels, down(): pl.pallas_call(body, grid_spec=pltpu.PrefetchScalarGridSpec(num_scalar_pr...  26.2 us
    ppermute x10, waiting for transfers between devices, along(): return lax.ppermute(x, 'gx', moves)  22.4 us
    all_gather x1, blocking collectives, overlapped(): stats = lax.all_gather(stats, 'gx')  20.1 us
    ppermute x10, starting transfers between devices, along(): return lax.ppermute(x, 'gx', moves)  19.9 us
    ppermute x20, starting transfers between devices, swap(): return lax.ppermute(x, 'gx', [(i, i ^ mask) for i in range(INNER * LINE)])  14.1 us
  transfers between devices with their start and end apart: 30, of which 9 were waited for; matrix products, arithmetic and copies ran while one was open for 2% of the time, Pallas kernels for 37%

profile of v2, /device:TPU:16, one launch (start us, length us, event | category | flops | bytes accessed | tf_op | source)
XLA Modules:
  0.0 147.3 jit_solution(15550437562064944125)
XLA Ops:
  1.6 1.9 %collective-permute-start.3 = (bf16[384,512]{1,0:T(8,128)(2,1)}, bf16[384,512]{1,0:T(8,128)(2,1)S(1)}, u32[]{:S(2)}, u32[]{:S(2)}) collective-permute-start(bf16[384,512]{1,0:T(8,128)(2,1)} %refs_0_.1), channel_id=1, source_target_pairs={{4,8},{5,9},{6,10},{7,11},{8,4},{9,5},{10,6},{11,7},{20,24},{21,25... | collective-permute-start | bytes 1179656 | tf_op jit(solution)/shard_map/ppermute | solution.py:27
  5.1 6.0 %collective-permute-done.refs_0_ = bf16[384,512]{1,0:T(8,128)(2,1)S(1)} collective-permute-done((bf16[384,512]{1,0:T(8,128)(2,1)}, bf16[384,512]{1,0:T(8,128)(2,1)S(1)}, u32[]{:S(2)}, u32[]{:S(2)}) %collective-permute-start) | collective-permute-done | bytes 393248 | tf_op jit(solution)/shard_map/ppermute | solution.py:27
  11.1 2.3 %collective-permute-start.1 = (bf16[384,512]{1,0:T(8,128)(2,1)S(1)}, bf16[384,512]{1,0:T(8,128)(2,1)S(1)}, u32[]{:S(2)}, u32[]{:S(2)}) collective-permute-start(bf16[384,512]{1,0:T(8,128)(2,1)S(1)} %collective-permute-done.refs_0_), channel_id=1, source_target_pairs={{4,8},{5,9},{6,10},{7,11},{8,4},{9,5},{10,6},{11,7},{20,24},{21,25... | collective-permute-start | bytes 1179656 | tf_op jit(solution)/shard_map/ppermute | solution.py:27
  19.3 20.1 %all-gather.1 = f32[16,1,896]{2,1,0:T(1,128)S(1)} all-gather(f32[1,1,896]{2,1,0:T(1,128)S(1)} %reshape.1), channel_id=2, replica_groups=mesh['groups'=2,'gx'=16] {'gx'}, dimensions={0}, use_global_device_ids=true | all-gather | bytes 60928 | tf_op jit(solution)/shard_map/all_gather | solution.py:198
  40.3 3.2 %collective-permute-start.2 = (bf16[384,512]{1,0:T(8,128)(2,1)S(1)}, bf16[384,512]{1,0:T(8,128)(2,1)S(1)}, u32[]{:S(2)}, u32[]{:S(2)}) collective-permute-start(bf16[384,512]{1,0:T(8,128)(2,1)S(1)} %collective-permute-done.1), channel_id=1, source_target_pairs={{4,0},{5,1},{6,2},{7,3},{8,12},{9,13},{10,14},{11,15},{20,16},{21,... | collective-permute-start | bytes 1179656 | tf_op jit(solution)/shard_map/ppermute | solution.py:27
  44.6 9.1 %gate_up.4 = (f32[384,1536]{1,0:T(8,128)S(1)}, f32[384,1536]{1,0:T(8,128)S(1)}, f32[384,256]{1,0:T(8,128)S(1)}) custom-call(s32[1]{0:T(128)} %bitcast.me_ref, bf16[384,512]{1,0:T(8,128)(2,1)S(1)} %copy-done, bf16[384,512]{1,0:T(8,128)(2,1)S(1)} %collective-permute-done.14.refs_1_, bf16[384,512]{1,0:T(8,128)(2,1)S(1)} %collective-permute-done.15.refs_2_, ...), custom_call_target="tpu_custom_call" | custom-call | flops 5234491392 | bytes 13631488 | tf_op jit(solution)/shard_map/gate_up/pallas_call | solution.py:112
  56.0 9.1 %gate_up.5 = (f32[384,1536]{1,0:T(8,128)S(1)}, f32[384,1536]{1,0:T(8,128)S(1)}, f32[384,256]{1,0:T(8,128)S(1)}) custom-call(s32[1]{0:T(128)} %bitcast.me_ref, bf16[384,512]{1,0:T(8,128)(2,1)S(1)} %collective-permute-done.refs_0_, bf16[384,512]{1,0:T(8,128)(2,1)S(1)} %collective-permute-done.11.refs_1_, bf16[384,512]{1,0:T(8,128)(2,1)S(1)} %collective-permute-done.12.refs_2_, ...), custom_call_target="tpu_custom_call" | custom-call | flops 5234491392 | bytes 13631488 | tf_op jit(solution)/shard_map/gate_up/pallas_call | solution.py:112
  65.7 13.0 %gate_up.6 = (f32[384,1536]{1,0:T(8,128)S(1)}, f32[384,1536]{1,0:T(8,128)S(1)}, f32[384,256]{1,0:T(8,128)S(1)}) custom-call(s32[1]{0:T(128)} %bitcast.me_ref, bf16[384,512]{1,0:T(8,128)(2,1)S(1)} %broadcast_select_fusion.refs_0_, bf16[384,512]{1,0:T(8,128)(2,1)S(1)} %collective-permute-done.7.refs_1_, bf16[384,512]{1,0:T(8,128)(2,1)S(1)} %collective-permute-done.8.refs_2_, ...), custom_call_target="tpu_custom_call" | custom-call | flops 7851737088 | bytes 20447232 | tf_op jit(solution)/shard_map/gate_up/pallas_call | solution.py:112
  78.8 5.6 %gate_up.7.hidden_ref.after_ref = bf16[384,1664]{1,0:T(8,128)(2,1)S(1)} custom-call(s32[1]{0:T(128)} %bitcast.me_ref, bf16[384,512]{1,0:T(8,128)(2,1)S(1)} %collective-permute-done.4.refs_0_, bf16[384,512]{1,0:T(8,128)(2,1)S(1)} %collective-permute-done.5.refs_1_, f32[16,896]{1,0:T(8,128)S(1)} %bitcast.7, bf16[8192,1664]{1,0:T(8,128)(2,1)} %refs_3_.1, ...), custom_call_target="tpu_custom_call" | custom-call | flops 2617245696 | bytes 6815744 | tf_op jit(solution)/shard_map/gate_up/pallas_call | solution.py:112
  84.4 3.2 %away_body.4.after_ref = bf16[2,384,512]{2,1,0:T(8,128)(2,1)S(1)} custom-call(s32[1]{0:T(128)} %bitcast.me_ref, bf16[384,1664]{1,0:T(8,128)(2,1)S(1)} %gate_up.7.hidden_ref.after_ref, bf16[1664,8192]{1,0:T(8,128)(2,1)} %weight_ref.15, bf16[384,1664]{1,0:T(8,128)(2,1)S(1)} %gate_up.7.hidden_ref.after_ref), custom_call_target="tpu_custom_call" | custom-call | flops 1308622848 | bytes 3407872 | tf_op jit(solution)/shard_map/away_body/pallas_call | solution.py:164
  88.0 3.2 %away_body.5 = bf16[2,384,512]{2,1,0:T(8,128)(2,1)S(1)} custom-call(s32[1]{0:T(128)} %bitcast.me_ref, bf16[384,1664]{1,0:T(8,128)(2,1)S(1)} %gate_up.7.hidden_ref.after_ref, bf16[1664,8192]{1,0:T(8,128)(2,1)} %weight_ref.15, bf16[2,384,512]{2,1,0:T(8,128)(2,1)S(1)} %away_body.4.after_ref), custom_call_target="tpu_custom_call" | custom-call | flops 1308622848 | bytes 3407872 | tf_op jit(solution)/shard_map/away_body/pallas_call | solution.py:164
  91.5 3.3 %stay_body.6 = (bf16[384,512]{1,0:T(8,128)(2,1)S(1)}, f32[384,512]{1,0:T(8,128)S(1)}) custom-call(s32[1]{0:T(128)} %bitcast.me_ref, bf16[384,1664]{1,0:T(8,128)(2,1)S(1)} %gate_up.7.hidden_ref.after_ref, bf16[1664,8192]{1,0:T(8,128)(2,1)} %weight_ref.15, bf16[2,384,512]{2,1,0:T(8,128)(2,1)S(1)} %collective-permute-done.20.got_ref), custom_call_target="tpu_custom_call" | custom-call | flops 1308622848 | bytes 3407872 | tf_op jit(solution)/shard_map/stay_body/pallas_call | solution.py:164
  96.6 3.2 %away_body.7 = bf16[2,384,512]{2,1,0:T(8,128)(2,1)S(1)} custom-call(s32[1]{0:T(128)} %bitcast.me_ref, bf16[384,1664]{1,0:T(8,128)(2,1)S(1)} %gate_up.7.hidden_ref.after_ref, bf16[1664,8192]{1,0:T(8,128)(2,1)} %weight_ref.15, bf16[384,512]{1,0:T(8,128)(2,1)S(1)} %get-tuple-element.34.after_ref), custom_call_target="tpu_custom_call" | custom-call | flops 1308622848 | bytes 3407872 | tf_op jit(solution)/shard_map/away_body/pallas_call | solution.py:164
  100.0 3.3 %stay_body.4 = (bf16[384,512]{1,0:T(8,128)(2,1)S(1)}, f32[384,512]{1,0:T(8,128)S(1)}) custom-call(s32[1]{0:T(128)} %bitcast.me_ref, bf16[384,1664]{1,0:T(8,128)(2,1)S(1)} %gate_up.7.hidden_ref.after_ref, bf16[1664,8192]{1,0:T(8,128)(2,1)} %weight_ref.15, bf16[2,384,512]{2,1,0:T(8,128)(2,1)S(1)} %collective-permute-done.17.got_ref), custom_call_target="tpu_custom_call" | custom-call | flops 1308622848 | bytes 3407872 | tf_op jit(solution)/shard_map/stay_body/pallas_call | solution.py:164
  103.7 2.5 %collective-permute-done.24 = bf16[384,512]{1,0:T(8,128)(2,1)S(1)} collective-permute-done((bf16[384,512]{1,0:T(8,128)(2,1)S(1)}, bf16[384,512]{1,0:T(8,128)(2,1)S(1)}, u32[]{:S(2)}, u32[]{:S(2)}) %collective-permute-start.24) | collective-permute-done | bytes 393248 | tf_op jit(solution)/shard_map/ppermute | solution.py:22
  107.6 3.2 %away_body.6 = bf16[2,384,512]{2,1,0:T(8,128)(2,1)S(1)} custom-call(s32[1]{0:T(128)} %bitcast.me_ref, bf16[384,1664]{1,0:T(8,128)(2,1)S(1)} %gate_up.7.hidden_ref.after_ref, bf16[1664,8192]{1,0:T(8,128)(2,1)} %weight_ref.15, bf16[384,512]{1,0:T(8,128)(2,1)S(1)} %get-tuple-element.31.after_ref), custom_call_target="tpu_custom_call" | custom-call | flops 1308622848 | bytes 3407872 | tf_op jit(solution)/shard_map/away_body/pallas_call | solution.py:164
  110.9 3.3 %stay_body.7 = (bf16[384,512]{1,0:T(8,128)(2,1)S(1)}, f32[384,512]{1,0:T(8,128)S(1)}) custom-call(s32[1]{0:T(128)} %bitcast.me_ref, bf16[384,1664]{1,0:T(8,128)(2,1)S(1)} %gate_up.7.hidden_ref.after_ref, bf16[1664,8192]{1,0:T(8,128)(2,1)} %weight_ref.15, bf16[2,384,512]{2,1,0:T(8,128)(2,1)S(1)} %collective-permute-done.21.got_ref), custom_call_target="tpu_custom_call" | custom-call | flops 1308622848 | bytes 3407872 | tf_op jit(solution)/shard_map/stay_body/pallas_call | solution.py:164
  114.3 2.5 %collective-permute-start.22 = (bf16[384,512]{1,0:T(8,128)(2,1)S(1)}, bf16[384,512]{1,0:T(8,128)(2,1)S(1)}, u32[]{:S(2)}, u32[]{:S(2)}) collective-permute-start(bf16[384,512]{1,0:T(8,128)(2,1)S(1)} %get-tuple-element.36), channel_id=1, source_target_pairs={{0,2},{1,3},{2,0},{3,1},{4,6},{5,7},{6,4},{7,5},{8,10},{9,11},{10,... | collective-permute-start | bytes 1179656 | tf_op jit(solution)/shard_map/ppermute | solution.py:22
  118.9 3.7 %collective-permute-start.26 = (bf16[384,512]{1,0:T(8,128)(2,1)S(1)}, bf16[384,512]{1,0:T(8,128)(2,1)S(1)}, u32[]{:S(2)}, u32[]{:S(2)}) collective-permute-start(bf16[384,512]{1,0:T(8,128)(2,1)S(1)} %get-tuple-element.39), channel_id=1, source_target_pairs={{4,8},{5,9},{6,10},{7,11},{8,4},{9,5},{10,6},{11,7},{20,24},{21,25... | collective-permute-start | bytes 1179656 | tf_op jit(solution)/shard_map/ppermute | solution.py:27
  123.8 3.3 %stay_body.5 = (bf16[384,512]{1,0:T(8,128)(2,1)S(1)}, f32[384,512]{1,0:T(8,128)S(1)}) custom-call(s32[1]{0:T(128)} %bitcast.me_ref, bf16[384,1664]{1,0:T(8,128)(2,1)S(1)} %gate_up.7.hidden_ref.after_ref, bf16[1664,8192]{1,0:T(8,128)(2,1)} %weight_ref.15, bf16[2,384,512]{2,1,0:T(8,128)(2,1)S(1)} %collective-permute-done.18.got_ref), custom_call_target="tpu_custom_call" | custom-call | flops 1308622848 | bytes 3407872 | tf_op jit(solution)/shard_map/stay_body/pallas_call | solution.py:164
  131.9 4.6 %collective-permute-done.28 = bf16[384,512]{1,0:T(8,128)(2,1)S(1)} collective-permute-done((bf16[384,512]{1,0:T(8,128)(2,1)S(1)}, bf16[384,512]{1,0:T(8,128)(2,1)S(1)}, u32[]{:S(2)}, u32[]{:S(2)}) %collective-permute-start.28) | collective-permute-done | bytes 393248 | tf_op jit(solution)/shard_map/ppermute | solution.py:27
  136.6 1.9 %collective-permute-start.29 = (bf16[384,512]{1,0:T(8,128)(2,1)S(1)}, bf16[384,512]{1,0:T(8,128)(2,1)S(1)}, u32[]{:S(2)}, u32[]{:S(2)}) collective-permute-start(bf16[384,512]{1,0:T(8,128)(2,1)S(1)} %add_convert_fusion), channel_id=1, source_target_pairs={{4,8},{5,9},{6,10},{7,11},{8,4},{9,5},{10,6},{11,7},{20,24},{21,25... | collective-permute-start | bytes 1179656 | tf_op jit(solution)/shard_map/ppermute | solution.py:27
  138.6 3.5 %collective-permute-done.27 = bf16[384,512]{1,0:T(8,128)(2,1)S(1)} collective-permute-done((bf16[384,512]{1,0:T(8,128)(2,1)S(1)}, bf16[384,512]{1,0:T(8,128)(2,1)S(1)}, u32[]{:S(2)}, u32[]{:S(2)}) %collective-permute-start.27) | collective-permute-done | bytes 393248 | tf_op jit(solution)/shard_map/ppermute | solution.py:27
  142.1 4.2 %collective-permute-done.29 = bf16[384,512]{1,0:T(8,128)(2,1)S(1)} collective-permute-done((bf16[384,512]{1,0:T(8,128)(2,1)S(1)}, bf16[384,512]{1,0:T(8,128)(2,1)S(1)}, u32[]{:S(2)}, u32[]{:S(2)}) %collective-permute-start.29) | collective-permute-done | bytes 393248 | tf_op jit(solution)/shard_map/ppermute | solution.py:27
  (65 shorter events, 27.5 us)
Async XLA Ops:
  1.6 12.7 %collective-permute-start.3 = (bf16[384,512]{1,0:T(8,128)(2,1)}, bf16[384,512]{1,0:T(8,128)(2,1)S(1)}, u32[]{:S(2)}, u32[]{:S(2)}) collective-permute-start(bf16[384,512]{1,0:T(8,128)(2,1)} %refs_0_.1), channel_id=1, source_target_pairs={{4,8},{5,9},{6,10},{7,11},{8,4},{9,5},{10,6},{11,7},{20,24},{21,25... | collective-permute-start | bytes 1179656 | tf_op jit(solution)/shard_map/ppermute | solution.py:27
  3.5 15.6 %collective-permute-start.15 = (bf16[384,512]{1,0:T(8,128)(2,1)}, bf16[384,512]{1,0:T(8,128)(2,1)S(1)}, u32[]{:S(2)}, u32[]{:S(2)}) collective-permute-start(bf16[384,512]{1,0:T(8,128)(2,1)} %refs_0_.1), channel_id=1, source_target_pairs={{0,2},{1,3},{2,0},{3,1},{4,6},{5,7},{6,4},{7,5},{8,10},{9,11},{10,... | collective-permute-start | bytes 1179656 | tf_op jit(solution)/shard_map/ppermute | solution.py:22
  11.1 28.4 %collective-permute-start.1 = (bf16[384,512]{1,0:T(8,128)(2,1)S(1)}, bf16[384,512]{1,0:T(8,128)(2,1)S(1)}, u32[]{:S(2)}, u32[]{:S(2)}) collective-permute-start(bf16[384,512]{1,0:T(8,128)(2,1)S(1)} %collective-permute-done.refs_0_), channel_id=1, source_target_pairs={{4,8},{5,9},{6,10},{7,11},{8,4},{9,5},{10,6},{11,7},{20,24},{21,25... | collective-permute-start | bytes 1179656 | tf_op jit(solution)/shard_map/ppermute | solution.py:27
  14.2 25.6 %collective-permute-start.6 = (bf16[384,512]{1,0:T(8,128)(2,1)S(1)}, bf16[384,512]{1,0:T(8,128)(2,1)S(1)}, u32[]{:S(2)}, u32[]{:S(2)}) collective-permute-start(bf16[384,512]{1,0:T(8,128)(2,1)S(1)} %collective-permute-done.3), channel_id=1, source_target_pairs={{4,0},{5,1},{6,2},{7,3},{8,12},{9,13},{10,14},{11,15},{20,16},{21,... | collective-permute-start | bytes 1179656 | tf_op jit(solution)/shard_map/ppermute | solution.py:27
  15.6 24.7 %collective-permute-start.14 = (bf16[384,512]{1,0:T(8,128)(2,1)}, bf16[384,512]{1,0:T(8,128)(2,1)S(1)}, u32[]{:S(2)}, u32[]{:S(2)}) collective-permute-start(bf16[384,512]{1,0:T(8,128)(2,1)} %refs_0_.1), channel_id=1, source_target_pairs={{0,1},{1,0},{2,3},{3,2},{4,5},{5,4},{6,7},{7,6},{8,9},{9,8},{10,11... | collective-permute-start | bytes 1179656 | tf_op jit(solution)/shard_map/ppermute | solution.py:22
  17.5 25.9 %collective-permute-start.12 = (bf16[384,512]{1,0:T(8,128)(2,1)S(1)}, bf16[384,512]{1,0:T(8,128)(2,1)S(1)}, u32[]{:S(2)}, u32[]{:S(2)}) collective-permute-start(bf16[384,512]{1,0:T(8,128)(2,1)S(1)} %collective-permute-done.refs_0_), channel_id=1, source_target_pairs={{0,2},{1,3},{2,0},{3,1},{4,6},{5,7},{6,4},{7,5},{8,10},{9,11},{10,... | collective-permute-start | bytes 1179656 | tf_op jit(solution)/shard_map/ppermute | solution.py:22
  19.1 21.2 %collective-permute-start.16 = (bf16[384,512]{1,0:T(8,128)(2,1)S(1)}, bf16[384,512]{1,0:T(8,128)(2,1)S(1)}, u32[]{:S(2)}, u32[]{:S(2)}) collective-permute-start(bf16[384,512]{1,0:T(8,128)(2,1)S(1)} %collective-permute-done.15.refs_2_), channel_id=1, source_target_pairs={{0,1},{1,0},{2,3},{3,2},{4,5},{5,4},{6,7},{7,6},{8,9},{9,8},{10,11... | collective-permute-start | bytes 1179656 | tf_op jit(solution)/shard_map/ppermute | solution.py:22
  39.4 14.8 %collective-permute-start.11 = (bf16[384,512]{1,0:T(8,128)(2,1)S(1)}, bf16[384,512]{1,0:T(8,128)(2,1)S(1)}, u32[]{:S(2)}, u32[]{:S(2)}) collective-permute-start(bf16[384,512]{1,0:T(8,128)(2,1)S(1)} %collective-permute-done.refs_0_), channel_id=1, source_target_pairs={{0,1},{1,0},{2,3},{3,2},{4,5},{5,4},{6,7},{7,6},{8,9},{9,8},{10,11... | collective-permute-start | bytes 1179656 | tf_op jit(solution)/shard_map/ppermute | solution.py:22
  39.9 16.1 %collective-permute-start.8 = (bf16[384,512]{1,0:T(8,128)(2,1)S(1)}, bf16[384,512]{1,0:T(8,128)(2,1)S(1)}, u32[]{:S(2)}, u32[]{:S(2)}) collective-permute-start(bf16[384,512]{1,0:T(8,128)(2,1)S(1)} %broadcast_select_fusion.refs_0_), channel_id=1, source_target_pairs={{0,2},{1,3},{2,0},{3,1},{4,6},{5,7},{6,4},{7,5},{8,10},{9,11},{10,... | collective-permute-start | bytes 1179656 | tf_op jit(solution)/shard_map/ppermute | solution.py:22
  40.2 25.5 %collective-permute-start.7 = (bf16[384,512]{1,0:T(8,128)(2,1)S(1)}, bf16[384,512]{1,0:T(8,128)(2,1)S(1)}, u32[]{:S(2)}, u32[]{:S(2)}) collective-permute-start(bf16[384,512]{1,0:T(8,128)(2,1)S(1)} %broadcast_select_fusion.refs_0_), channel_id=1, source_target_pairs={{0,1},{1,0},{2,3},{3,2},{4,5},{5,4},{6,7},{7,6},{8,9},{9,8},{10,11... | collective-permute-start | bytes 1179656 | tf_op jit(solution)/shard_map/ppermute | solution.py:22
  40.3 13.4 %collective-permute-start.2 = (bf16[384,512]{1,0:T(8,128)(2,1)S(1)}, bf16[384,512]{1,0:T(8,128)(2,1)S(1)}, u32[]{:S(2)}, u32[]{:S(2)}) collective-permute-start(bf16[384,512]{1,0:T(8,128)(2,1)S(1)} %collective-permute-done.1), channel_id=1, source_target_pairs={{4,0},{5,1},{6,2},{7,3},{8,12},{9,13},{10,14},{11,15},{20,16},{21,... | collective-permute-start | bytes 1179656 | tf_op jit(solution)/shard_map/ppermute | solution.py:27
  43.4 12.6 %collective-permute-start.13 = (bf16[384,512]{1,0:T(8,128)(2,1)S(1)}, bf16[384,512]{1,0:T(8,128)(2,1)S(1)}, u32[]{:S(2)}, u32[]{:S(2)}) collective-permute-start(bf16[384,512]{1,0:T(8,128)(2,1)S(1)} %collective-permute-done.12.refs_2_), channel_id=1, source_target_pairs={{0,1},{1,0},{2,3},{3,2},{4,5},{5,4},{6,7},{7,6},{8,9},{9,8},{10,11... | collective-permute-start | bytes 1179656 | tf_op jit(solution)/shard_map/ppermute | solution.py:22
  53.7 12.0 %collective-permute-start.10 = (bf16[384,512]{1,0:T(8,128)(2,1)S(1)}, bf16[384,512]{1,0:T(8,128)(2,1)S(1)}, u32[]{:S(2)}, u32[]{:S(2)}) collective-permute-start(bf16[384,512]{1,0:T(8,128)(2,1)S(1)} %broadcast_select_fusion.1.refs_4_), channel_id=1, source_target_pairs={{0,1},{1,0},{2,3},{3,2},{4,5},{5,4},{6,7},{7,6},{8,9},{9,8},{10,11... | collective-permute-start | bytes 1179656 | tf_op jit(solution)/shard_map/ppermute | solution.py:22
  54.2 11.3 %collective-permute-start.4 = (bf16[384,512]{1,0:T(8,128)(2,1)S(1)}, bf16[384,512]{1,0:T(8,128)(2,1)S(1)}, u32[]{:S(2)}, u32[]{:S(2)}) collective-permute-start(bf16[384,512]{1,0:T(8,128)(2,1)S(1)} %broadcast_select_fusion.1.refs_4_), channel_id=1, source_target_pairs={{0,2},{1,3},{2,0},{3,1},{4,6},{5,7},{6,4},{7,5},{8,10},{9,11},{10,... | collective-permute-start | bytes 1179656 | tf_op jit(solution)/shard_map/ppermute | solution.py:22
  65.5 13.3 %collective-permute-start.5 = (bf16[384,512]{1,0:T(8,128)(2,1)S(1)}, bf16[384,512]{1,0:T(8,128)(2,1)S(1)}, u32[]{:S(2)}, u32[]{:S(2)}) collective-permute-start(bf16[384,512]{1,0:T(8,128)(2,1)S(1)} %collective-permute-done.4.refs_0_), channel_id=1, source_target_pairs={{0,1},{1,0},{2,3},{3,2},{4,5},{5,4},{6,7},{7,6},{8,9},{9,8},{10,11... | collective-permute-start | bytes 1179656 | tf_op jit(solution)/shard_map/ppermute | solution.py:22
  94.8 11.3 %collective-permute-start.24 = (bf16[384,512]{1,0:T(8,128)(2,1)S(1)}, bf16[384,512]{1,0:T(8,128)(2,1)S(1)}, u32[]{:S(2)}, u32[]{:S(2)}) collective-permute-start(bf16[384,512]{1,0:T(8,128)(2,1)S(1)} %get-tuple-element.34.after_ref), channel_id=1, source_target_pairs={{0,2},{1,3},{2,0},{3,1},{4,6},{5,7},{6,4},{7,5},{8,10},{9,11},{10,... | collective-permute-start | bytes 1179656 | tf_op jit(solution)/shard_map/ppermute | solution.py:22
  103.3 13.5 %collective-permute-start.23 = (bf16[384,512]{1,0:T(8,128)(2,1)S(1)}, bf16[384,512]{1,0:T(8,128)(2,1)S(1)}, u32[]{:S(2)}, u32[]{:S(2)}) collective-permute-start(bf16[384,512]{1,0:T(8,128)(2,1)S(1)} %get-tuple-element.31.after_ref), channel_id=1, source_target_pairs={{0,2},{1,3},{2,0},{3,1},{4,6},{5,7},{6,4},{7,5},{8,10},{9,11},{10,... | collective-permute-start | bytes 1179656 | tf_op jit(solution)/shard_map/ppermute | solution.py:22
  106.3 12.4 %collective-permute-start.25 = (bf16[384,512]{1,0:T(8,128)(2,1)S(1)}, bf16[384,512]{1,0:T(8,128)(2,1)S(1)}, u32[]{:S(2)}, u32[]{:S(2)}) collective-permute-start(bf16[384,512]{1,0:T(8,128)(2,1)S(1)} %fusion.3), channel_id=1, source_target_pairs={{0,4},{1,5},{2,6},{3,7},{12,8},{13,9},{14,10},{15,11},{16,20},{17,... | collective-permute-start | bytes 1179656 | tf_op jit(solution)/shard_map/ppermute | solution.py:27
  110.9 13.0 %collective-permute-start.18 = (bf16[2,384,512]{2,1,0:T(8,128)(2,1)S(1)}, bf16[2,384,512]{2,1,0:T(8,128)(2,1)S(1)}, u32[]{:S(2)}, u32[]{:S(2)}) collective-permute-start(bf16[2,384,512]{2,1,0:T(8,128)(2,1)S(1)} %away_body.6), channel_id=1, source_target_pairs={{0,1},{1,0},{2,3},{3,2},{4,5},{5,4},{6,7},{7,6},{8,9},{9,8},{10,11... | collective-permute-start | bytes 2359304 | tf_op jit(solution)/shard_map/ppermute | solution.py:22
  114.3 14.7 %collective-permute-start.22 = (bf16[384,512]{1,0:T(8,128)(2,1)S(1)}, bf16[384,512]{1,0:T(8,128)(2,1)S(1)}, u32[]{:S(2)}, u32[]{:S(2)}) collective-permute-start(bf16[384,512]{1,0:T(8,128)(2,1)S(1)} %get-tuple-element.36), channel_id=1, source_target_pairs={{0,2},{1,3},{2,0},{3,1},{4,6},{5,7},{6,4},{7,5},{8,10},{9,11},{10,... | collective-permute-start | bytes 1179656 | tf_op jit(solution)/shard_map/ppermute | solution.py:22
  118.9 11.4 %collective-permute-start.26 = (bf16[384,512]{1,0:T(8,128)(2,1)S(1)}, bf16[384,512]{1,0:T(8,128)(2,1)S(1)}, u32[]{:S(2)}, u32[]{:S(2)}) collective-permute-start(bf16[384,512]{1,0:T(8,128)(2,1)S(1)} %get-tuple-element.39), channel_id=1, source_target_pairs={{4,8},{5,9},{6,10},{7,11},{8,4},{9,5},{10,6},{11,7},{20,24},{21,25... | collective-permute-start | bytes 1179656 | tf_op jit(solution)/shard_map/ppermute | solution.py:27
  122.5 13.9 %collective-permute-start.28 = (bf16[384,512]{1,0:T(8,128)(2,1)S(1)}, bf16[384,512]{1,0:T(8,128)(2,1)S(1)}, u32[]{:S(2)}, u32[]{:S(2)}) collective-permute-start(bf16[384,512]{1,0:T(8,128)(2,1)S(1)} %get-tuple-element.40), channel_id=1, source_target_pairs={{0,4},{1,5},{2,6},{3,7},{12,8},{13,9},{14,10},{15,11},{16,20},{17,... | collective-permute-start | bytes 1179656 | tf_op jit(solution)/shard_map/ppermute | solution.py:27
  127.2 11.4 %collective-permute-start.19 = (bf16[384,512]{1,0:T(8,128)(2,1)S(1)}, bf16[384,512]{1,0:T(8,128)(2,1)S(1)}, u32[]{:S(2)}, u32[]{:S(2)}) collective-permute-start(bf16[384,512]{1,0:T(8,128)(2,1)S(1)} %get-tuple-element.33), channel_id=1, source_target_pairs={{0,2},{1,3},{2,0},{3,1},{4,6},{5,7},{6,4},{7,5},{8,10},{9,11},{10,... | collective-permute-start | bytes 1179656 | tf_op jit(solution)/shard_map/ppermute | solution.py:22
  130.5 11.6 %collective-permute-start.27 = (bf16[384,512]{1,0:T(8,128)(2,1)S(1)}, bf16[384,512]{1,0:T(8,128)(2,1)S(1)}, u32[]{:S(2)}, u32[]{:S(2)}) collective-permute-start(bf16[384,512]{1,0:T(8,128)(2,1)S(1)} %add_convert_fusion.1), channel_id=1, source_target_pairs={{0,4},{1,5},{2,6},{3,7},{4,0},{5,1},{6,2},{7,3},{8,12},{9,13},{10,... | collective-permute-start | bytes 1179656 | tf_op jit(solution)/shard_map/ppermute | solution.py:27
  (8 other events, 74.3 us)

commit v3 on v2

--- a/solution.py
+++ b/solution.py
@@ -10,6 +10,7 @@
 epsilon = 1e-05
 INNER = 4
 LINE = 4
+UNIT = 256
 VMEM_LIMIT = 30 * 1024 * 1024
 
 PAIRS = ((0, 1), (1, 0), (2, 3), (3, 2))
@@ -32,6 +33,23 @@
     for i, entry in enumerate(table[1:], 1):
         value = jnp.where(s == i, jnp.int32(entry), value)
     return value
+
+
+def accumulator(unit, rows):
+    return pltpu.ACC(unit)((rows, UNIT), jnp.float32)
+
+
+def multiply(lhs_ref, tiles, accs):
+    for i in range(max(len(t) for t in tiles)):
+        for unit, tile in enumerate(tiles):
+            if i < len(tile):
+                pltpu.matmul_push_rhs(tile[i][0](), i % 2, unit)
+        for unit, tile in enumerate(tiles):
+            if i < len(tile):
+                at = tile[i][1]
+                pltpu.matmul_acc_lhs(
+                    accs[unit], lhs_ref[:, at : at + UNIT], load_staged_rhs=i % 2
+                )
 
 
 def gate_up_body(codes, first, last, rows, main, features, me_ref, *refs):
@@ -44,52 +62,95 @@
         rest = rest[3:]
     if last:
         hidden_ref, *rest = rest
-    gate_acc, up_acc, mixed_acc, factor_ref = rest[-4:]
+    gate_acc, up_acc, mixed_acc, factor_ref, normed_ref = rest[-5:]
     step = pl.program_id(0)
+    depth, ff = gate_ref.shape
 
     @pl.when(step == 0)
     def _():
-        total = jnp.sum(stats_ref[:, :rows], axis=0, keepdims=True)
-        factor = lax.rsqrt(total / features + epsilon)
+        factor = lax.rsqrt(stats_ref[:1, :rows] / features + epsilon)
         factor_ref[...] = jnp.broadcast_to(factor, (128, rows)).T
 
     for s in range(count):
 
         @pl.when(step == s)
         def _(s=s):
-            gain = stats_ref[pl.ds(me_ref[0] ^ codes[s], 1), rows:]
+            gain = stats_ref[1 + codes[s] : 2 + codes[s], :depth]
             x = blocks[s][...].astype(jnp.float32)
-            normed = (x * factor_ref[:, :1] * gain).astype(jnp.bfloat16)
-            gate = gate_ref[...]
-            up = up_ref[...]
-            mixed = jnp.concatenate([gate[:, main:], up[:, main:]], axis=1)
-            sums = []
-            for acc, old, weight in zip(
-                (gate_acc, up_acc, mixed_acc),
-                (None,) * 3 if first else before,
-                (gate[:, :main], up[:, :main], mixed),
-            ):
-                value = jnp.dot(normed, weight, preferred_element_type=jnp.float32)
-                if s:
-                    value = acc[...] + value
-                elif old is not None:
-                    value = old[...] + value
-                if s == count - 1 and last:
-                    sums.append(value)
-                else:
-                    acc[...] = value
-            if sums:
-                g, u, m = sums
-                rem = m.shape[1] // 2
-                hidden_ref[:, :main] = (g / (1.0 + jnp.exp(-g)) * u).astype(jnp.bfloat16)
-                g, u = m[:, :rem], m[:, rem:]
-                hidden_ref[:, main:] = (g / (1.0 + jnp.exp(-g)) * u).astype(jnp.bfloat16)
+            normed_ref[...] = (x * factor_ref[:, :1] * gain).astype(jnp.bfloat16)
+
+    def tile(ref, n):
+        return [
+            (lambda k=k: ref[k : k + UNIT, n : n + UNIT], k) for k in range(0, depth, UNIT)
+        ]
+
+    def mixed(k):
+        return lambda: jnp.concatenate(
+            [gate_ref[k : k + UNIT, main:], up_ref[k : k + UNIT, main:]], axis=1
+        )
+
+    def keep(ref, old, n, value):
+        at = (slice(None), slice(n, n + UNIT))
+
+        if first:
+
+            @pl.when(step == 0)
+            def _():
+                ref[at] = value
+
+            @pl.when(step > 0)
+            def _():
+                ref[at] += value
+
+        else:
+
+            @pl.when(step == 0)
+            def _():
+                ref[at] = old[at] + value
+
+            @pl.when(step > 0)
+            def _():
+                ref[at] += value
+
+    before = (None,) * 3 if first else before
+
+    def run(a0, a1, b0, b1):
+        units = ((a0, a1), (b0, b1))
+        for j, n in enumerate(range(0, main, UNIT)):
+            accs = units[j % 2]
+            multiply(normed_ref, [tile(gate_ref, n), tile(up_ref, n)], accs)
+            keep(gate_acc, before[0], n, pltpu.matmul_pop(accs[0]))
+            keep(up_acc, before[1], n, pltpu.matmul_pop(accs[1]))
+        ks = list(range(0, depth, UNIT))
+        accs = units[(main // UNIT) % 2]
+        multiply(
+            normed_ref,
+            [[(mixed(k), k) for k in ks[0::2]], [(mixed(k), k) for k in ks[1::2]]],
+            accs,
+        )
+        keep(mixed_acc, before[2], 0, pltpu.matmul_pop(accs[0]) + pltpu.matmul_pop(accs[1]))
+
+    pl.run_scoped(run, *(accumulator(unit, rows) for unit in (0, 1, 0, 1)))
+
+    if last:
+
+        @pl.when(step == count - 1)
+        def _():
+            rem = ff - main
+            for n in range(0, main, UNIT):
+                g, u = gate_acc[:, n : n + UNIT], up_acc[:, n : n + UNIT]
+                hidden_ref[:, n : n + UNIT] = (g / (1.0 + jnp.exp(-g)) * u).astype(
+                    jnp.bfloat16
+                )
+            g, u = mixed_acc[:, :rem], mixed_acc[:, rem:]
+            hidden_ref[:, main:ff] = (g / (1.0 + jnp.exp(-g)) * u).astype(jnp.bfloat16)
+            hidden_ref[:, ff:] = jnp.zeros((rows, rem), jnp.bfloat16)
 
 
 def gate_up(me, blocks, codes, stats, gate_weight, up_weight, acc, last):
     rows, depth = blocks[0].shape
     features, ff = gate_weight.shape
-    main = ff // 256 * 256 if ff % 256 else ff - 256
+    main = ff // UNIT * UNIT
     rem = ff - main
     first = acc is None
     count = len(blocks)
@@ -101,10 +162,10 @@
     if not first:
         in_specs += [whole(s) for s in shapes]
         args += list(acc)
-    scratch = [pltpu.VMEM((rows, 128), jnp.float32)]
+    scratch = [pltpu.VMEM((rows, 128), jnp.float32), pltpu.VMEM((rows, depth), jnp.bfloat16)]
     if last:
-        out_shape = [jax.ShapeDtypeStruct((rows, ff), jnp.bfloat16)]
-        out_specs = [whole((rows, ff))]
+        out_shape = [jax.ShapeDtypeStruct((rows, ff + rem), jnp.bfloat16)]
+        out_specs = [whole((rows, ff + rem))]
         scratch = [pltpu.VMEM(s, jnp.float32) for s in shapes] + scratch
     else:
         out_shape = [jax.ShapeDtypeStruct(s, jnp.float32) for s in shapes]
@@ -129,37 +190,51 @@
     )(me, *args)
 
 
-def down_block(hidden_ref, weight_ref):
-    ff = hidden_ref.shape[1]
-    main = ff // 256 * 256
-    value = jnp.dot(
-        hidden_ref[:, :main], weight_ref[:main, :], preferred_element_type=jnp.float32
-    )
-    if main < ff:
-        value = value + jnp.dot(
-            hidden_ref[:, main:], weight_ref[main:, :], preferred_element_type=jnp.float32
-        )
-    return value
+def down_block(hidden_ref, weight_ref, use):
+    ff, width = weight_ref.shape
+    main = ff // UNIT * UNIT
+
+    def tile(n):
+        whole = [
+            (lambda k=k: weight_ref[k : k + UNIT, n : n + UNIT], k) for k in range(0, main, UNIT)
+        ]
+        zeros = jnp.zeros((main + UNIT - ff, UNIT), weight_ref.dtype)
+        part = lambda: jnp.concatenate([weight_ref[main:, n : n + UNIT], zeros], axis=0)
+        return whole + [(part, main)]
+
+    def run(*accs):
+        multiply(hidden_ref, [tile(0), tile(UNIT)], accs)
+        for i, acc in enumerate(accs):
+            use((slice(None), slice(i * UNIT, (i + 1) * UNIT)), pltpu.matmul_pop(acc))
+
+    pl.run_scoped(run, *(accumulator(unit, hidden_ref.shape[0]) for unit in (0, 1)))
 
 
 def away_body(me_ref, hidden_ref, weight_ref, after_ref, out_ref):
-    out_ref[0] = down_block(hidden_ref, weight_ref).astype(out_ref.dtype)
+    def use(at, value):
+        out_ref[(0,) + at] = value.astype(out_ref.dtype)
+
+    down_block(hidden_ref, weight_ref, use)
 
 
 def stay_body(me_ref, hidden_ref, weight_ref, got_ref, far_ref, near_ref):
-    value = down_block(hidden_ref, weight_ref) + got_ref[0].astype(jnp.float32)
-
-    @pl.when(pl.program_id(0) == 0)
-    def _():
-        far_ref[...] = value.astype(far_ref.dtype)
-
-    @pl.when(pl.program_id(0) == 1)
-    def _():
-        near_ref[...] = value
+    def use(at, value):
+        value = value + got_ref[(0,) + at].astype(jnp.float32)
+
+        @pl.when(pl.program_id(0) == 0)
+        def _():
+            far_ref[at] = value.astype(far_ref.dtype)
+
+        @pl.when(pl.program_id(0) == 1)
+        def _():
+            near_ref[at] = value
+
+    down_block(hidden_ref, weight_ref, use)
 
 
 def down(body, me, codes, hidden, down_weight, width, extra, extra_spec, out_shape, out_specs):
-    rows, ff = hidden.shape
+    rows = hidden.shape[0]
+    ff = down_weight.shape[0]
     count = len(codes)
     return pl.pallas_call(
         body,
@@ -167,7 +242,7 @@
             num_scalar_prefetch=1,
             grid=(count,),
             in_specs=[
-                pl.BlockSpec((rows, ff), lambda s, me: (0, 0)),
+                pl.BlockSpec(hidden.shape, lambda s, me: (0, 0)),
                 pl.BlockSpec((ff, width), lambda s, me: (0, me[0] ^ pick(codes, s))),
                 extra_spec,
             ],
@@ -192,10 +267,11 @@
     me = index[None]
     resident = activations.astype(jnp.float32)
 
-    stats = jnp.concatenate(
-        [jnp.sum(resident * resident, axis=1), norm_gain.astype(jnp.float32)]
-    )
-    stats = lax.all_gather(stats, "gx")
+    total = jnp.sum(resident * resident, axis=1)
+    stats = jnp.stack([jnp.pad(total, (0, width - rows)), norm_gain.astype(jnp.float32)])
+    for bit in range(4):
+        other = swap(stats, 1 << bit)
+        stats = jnp.concatenate([stats[:1] + other[:1], stats[1:], other[1:]])
 
     neighbour = along(activations, PAIRS)
     inner = along(activations, MIDDLE)
@@ -297,7 +373,7 @@
 def per_device(n, activations, norm_gain, gate_weight, up_weight, down_weight):
     args = (activations, norm_gain, gate_weight, up_weight, down_weight)
     rows, width = activations.shape
-    tiled = rows % 128 == 0 and width % 128 == 0 and gate_weight.shape[1] % 128 == 0
+    tiled = rows % 128 == 0 and rows <= width == 2 * UNIT and gate_weight.shape[1] % UNIT == 128
     if n == INNER * LINE and tiled:
         return overlapped(*args)
     return plain(*args)

time: 148 us -> 169 us (1.14)
  the two profiles are of different devices: /device:TPU:16 before, /device:TPU:8 now
where the time goes in v3:
time: 169 us; the launch traced here: 168 us
  Pallas kernels  90.2 us (53%)
  waiting for transfers between devices  39 us (23%)
  starting transfers between devices  33.7 us (20%)
  other arithmetic  3.63 us (2%)
    pallas_call x4, Pallas kernels, gate_up(): pl.pallas_call(functools.partial(gate_up_body, codes, first, last, rows,...  63.3 us
    pallas_call x8, Pallas kernels, down(): pl.pallas_call(body, grid_spec=pltpu.PrefetchScalarGridSpec(num_scalar_pr...  26.9 us
    ppermute x10, starting transfers between devices, along(): return lax.ppermute(x, 'gx', moves)  22.5 us
    ppermute x24, waiting for transfers between devices, swap(): return lax.ppermute(x, 'gx', [(i, i ^ mask) for i in range(INNER * LINE)])  20.6 us
    ppermute x10, waiting for transfers between devices, along(): return lax.ppermute(x, 'gx', moves)  18.4 us
    ppermute x24, starting transfers between devices, swap(): return lax.ppermute(x, 'gx', [(i, i ^ mask) for i in range(INNER * LINE)])  11.3 us
  transfers between devices with their start and end apart: 34, of which 11 were waited for; matrix products, arithmetic and copies ran while one was open for 1% of the time, Pallas kernels for 46%

profile of v3, /device:TPU:8, one launch (start us, length us, event | category | flops | bytes accessed | tf_op | source)
XLA Modules:
  0.0 168.5 jit_solution(11419680846540731978)
XLA Ops:
  2.0 5.0 %collective-permute-start.3 = (bf16[384,512]{1,0:T(8,128)(2,1)}, bf16[384,512]{1,0:T(8,128)(2,1)S(1)}, u32[]{:S(2)}, u32[]{:S(2)}) collective-permute-start(bf16[384,512]{1,0:T(8,128)(2,1)} %refs_0_.1), channel_id=1, source_target_pairs={{4,8},{5,9},{6,10},{7,11},{8,4},{9,5},{10,6},{11,7},{20,24},{21,25... | collective-permute-start | bytes 1179656 | tf_op jit(solution)/shard_map/ppermute | solution.py:28
  10.9 3.7 %collective-permute-done.8 = f32[5,512]{1,0:T(8,128)S(1)} collective-permute-done((f32[5,512]{1,0:T(8,128)S(1)}, f32[5,512]{1,0:T(8,128)S(1)}, u32[]{:S(2)}, u32[]{:S(2)}) %collective-permute-start.8) | collective-permute-done | bytes 10272 | tf_op jit(solution)/shard_map/ppermute | solution.py:23
  14.7 2.9 %collective-permute-start.1 = (bf16[384,512]{1,0:T(8,128)(2,1)S(1)}, bf16[384,512]{1,0:T(8,128)(2,1)S(1)}, u32[]{:S(2)}, u32[]{:S(2)}) collective-permute-start(bf16[384,512]{1,0:T(8,128)(2,1)S(1)} %collective-permute-done.refs_0_), channel_id=1, source_target_pairs={{4,8},{5,9},{6,10},{7,11},{8,4},{9,5},{10,6},{11,7},{20,24},{21,25... | collective-permute-start | bytes 1179656 | tf_op jit(solution)/shard_map/ppermute | solution.py:28
  19.2 7.9 %collective-permute-done.9 = f32[9,512]{1,0:T(8,128)S(1)} collective-permute-done((f32[9,512]{1,0:T(8,128)S(1)}, f32[9,512]{1,0:T(8,128)S(1)}, u32[]{:S(2)}, u32[]{:S(2)}) %collective-permute-start.9) | collective-permute-done | bytes 18464 | tf_op jit(solution)/shard_map/ppermute | solution.py:23
  30.4 4.4 %collective-permute-start.2 = (bf16[384,512]{1,0:T(8,128)(2,1)S(1)}, bf16[384,512]{1,0:T(8,128)(2,1)S(1)}, u32[]{:S(2)}, u32[]{:S(2)}) collective-permute-start(bf16[384,512]{1,0:T(8,128)(2,1)S(1)} %collective-permute-done.1), channel_id=1, source_target_pairs={{4,0},{5,1},{6,2},{7,3},{8,12},{9,13},{10,14},{11,15},{20,16},{21,... | collective-permute-start | bytes 1179656 | tf_op jit(solution)/shard_map/ppermute | solution.py:28
  34.8 4.4 %collective-permute-done.16.refs_2_ = bf16[384,512]{1,0:T(8,128)(2,1)S(1)} collective-permute-done((bf16[384,512]{1,0:T(8,128)(2,1)S(1)}, bf16[384,512]{1,0:T(8,128)(2,1)S(1)}, u32[]{:S(2)}, u32[]{:S(2)}) %collective-permute-start.16) | collective-permute-done | bytes 393248 | tf_op jit(solution)/shard_map/ppermute | solution.py:23
  40.2 15.4 %gate_up.4 = (f32[384,1536]{1,0:T(8,128)S(1)}, f32[384,1536]{1,0:T(8,128)S(1)}, f32[384,256]{1,0:T(8,128)S(1)}) custom-call(s32[1]{0:T(128)} %bitcast.me_ref, bf16[384,512]{1,0:T(8,128)(2,1)S(1)} %copy-done, bf16[384,512]{1,0:T(8,128)(2,1)S(1)} %collective-permute-done.18.refs_1_, bf16[384,512]{1,0:T(8,128)(2,1)S(1)} %collective-permute-done.19.refs_2_, ...), custom_call_target="tpu_custom_call" | custom-call | flops 5234491392 | bytes 13631488 | tf_op jit(solution)/shard_map/gate_up/pallas_call | solution.py:173
  57.7 15.7 %gate_up.5 = (f32[384,1536]{1,0:T(8,128)S(1)}, f32[384,1536]{1,0:T(8,128)S(1)}, f32[384,256]{1,0:T(8,128)S(1)}) custom-call(s32[1]{0:T(128)} %bitcast.me_ref, bf16[384,512]{1,0:T(8,128)(2,1)S(1)} %collective-permute-done.refs_0_, bf16[384,512]{1,0:T(8,128)(2,1)S(1)} %collective-permute-done.15.refs_1_, bf16[384,512]{1,0:T(8,128)(2,1)S(1)} %collective-permute-done.16.refs_2_, ...), custom_call_target="tpu_custom_call" | custom-call | flops 5234491392 | bytes 13631488 | tf_op jit(solution)/shard_map/gate_up/pallas_call | solution.py:173
  74.0 22.6 %gate_up.6 = (f32[384,1536]{1,0:T(8,128)S(1)}, f32[384,1536]{1,0:T(8,128)S(1)}, f32[384,256]{1,0:T(8,128)S(1)}) custom-call(s32[1]{0:T(128)} %bitcast.me_ref, bf16[384,512]{1,0:T(8,128)(2,1)S(1)} %broadcast_select_fusion.refs_0_, bf16[384,512]{1,0:T(8,128)(2,1)S(1)} %collective-permute-done.11.refs_1_, bf16[384,512]{1,0:T(8,128)(2,1)S(1)} %collective-permute-done.12.refs_2_, ...), custom_call_target="tpu_custom_call" | custom-call | flops 7851737088 | bytes 20447232 | tf_op jit(solution)/shard_map/gate_up/pallas_call | solution.py:173
  96.7 9.6 %gate_up.7.hidden_ref.after_ref = bf16[384,1792]{1,0:T(8,128)(2,1)S(1)} custom-call(s32[1]{0:T(128)} %bitcast.me_ref, bf16[384,512]{1,0:T(8,128)(2,1)S(1)} %collective-permute-done.4.refs_0_, bf16[384,512]{1,0:T(8,128)(2,1)S(1)} %collective-permute-done.5.refs_1_, f32[17,512]{1,0:T(8,128)S(1)} %concatenate.23.refs_4_.refs_6_.refs_2_, ...), custom_call_target="tpu_custom_call" | custom-call | flops 2617245696 | bytes 6815744 | tf_op jit(solution)/shard_map/gate_up/pallas_call | solution.py:173
  106.3 3.3 %away_body.4.after_ref = bf16[2,384,512]{2,1,0:T(8,128)(2,1)S(1)} custom-call(s32[1]{0:T(128)} %bitcast.me_ref, bf16[384,1792]{1,0:T(8,128)(2,1)S(1)} %gate_up.7.hidden_ref.after_ref, bf16[1664,8192]{1,0:T(8,128)(2,1)} %weight_ref.15, bf16[384,1792]{1,0:T(8,128)(2,1)S(1)} %gate_up.7.hidden_ref.after_ref), custom_call_target="tpu_custom_call" | custom-call | flops 1308622848 | bytes 3407872 | tf_op jit(solution)/shard_map/away_body/pallas_call | solution.py:239
  109.7 3.2 %away_body.5 = bf16[2,384,512]{2,1,0:T(8,128)(2,1)S(1)} custom-call(s32[1]{0:T(128)} %bitcast.me_ref, bf16[384,1792]{1,0:T(8,128)(2,1)S(1)} %gate_up.7.hidden_ref.after_ref, bf16[1664,8192]{1,0:T(8,128)(2,1)} %weight_ref.15, bf16[2,384,512]{2,1,0:T(8,128)(2,1)S(1)} %away_body.4.after_ref), custom_call_target="tpu_custom_call" | custom-call | flops 1308622848 | bytes 3407872 | tf_op jit(solution)/shard_map/away_body/pallas_call | solution.py:239
  113.5 3.5 %stay_body.6 = (bf16[384,512]{1,0:T(8,128)(2,1)S(1)}, f32[384,512]{1,0:T(8,128)S(1)}) custom-call(s32[1]{0:T(128)} %bitcast.me_ref, bf16[384,1792]{1,0:T(8,128)(2,1)S(1)} %gate_up.7.hidden_ref.after_ref, bf16[1664,8192]{1,0:T(8,128)(2,1)} %weight_ref.15, bf16[2,384,512]{2,1,0:T(8,128)(2,1)S(1)} %collective-permute-done.24.got_ref), custom_call_target="tpu_custom_call" | custom-call | flops 1308622848 | bytes 3407872 | tf_op jit(solution)/shard_map/stay_body/pallas_call | solution.py:239
  117.5 3.2 %away_body.7 = bf16[2,384,512]{2,1,0:T(8,128)(2,1)S(1)} custom-call(s32[1]{0:T(128)} %bitcast.me_ref, bf16[384,1792]{1,0:T(8,128)(2,1)S(1)} %gate_up.7.hidden_ref.after_ref, bf16[1664,8192]{1,0:T(8,128)(2,1)} %weight_ref.15, bf16[384,512]{1,0:T(8,128)(2,1)S(1)} %get-tuple-element.34.after_ref), custom_call_target="tpu_custom_call" | custom-call | flops 1308622848 | bytes 3407872 | tf_op jit(solution)/shard_map/away_body/pallas_call | solution.py:239
  120.8 3.5 %stay_body.4 = (bf16[384,512]{1,0:T(8,128)(2,1)S(1)}, f32[384,512]{1,0:T(8,128)S(1)}) custom-call(s32[1]{0:T(128)} %bitcast.me_ref, bf16[384,1792]{1,0:T(8,128)(2,1)S(1)} %gate_up.7.hidden_ref.after_ref, bf16[1664,8192]{1,0:T(8,128)(2,1)} %weight_ref.15, bf16[2,384,512]{2,1,0:T(8,128)(2,1)S(1)} %collective-permute-done.21.got_ref), custom_call_target="tpu_custom_call" | custom-call | flops 1308622848 | bytes 3407872 | tf_op jit(solution)/shard_map/stay_body/pallas_call | solution.py:239
  125.9 2.7 %collective-permute-done.28 = bf16[384,512]{1,0:T(8,128)(2,1)S(1)} collective-permute-done((bf16[384,512]{1,0:T(8,128)(2,1)S(1)}, bf16[384,512]{1,0:T(8,128)(2,1)S(1)}, u32[]{:S(2)}, u32[]{:S(2)}) %collective-permute-start.28) | collective-permute-done | bytes 393248 | tf_op jit(solution)/shard_map/ppermute | solution.py:23
  130.0 3.3 %away_body.6 = bf16[2,384,512]{2,1,0:T(8,128)(2,1)S(1)} custom-call(s32[1]{0:T(128)} %bitcast.me_ref, bf16[384,1792]{1,0:T(8,128)(2,1)S(1)} %gate_up.7.hidden_ref.after_ref, bf16[1664,8192]{1,0:T(8,128)(2,1)} %weight_ref.15, bf16[384,512]{1,0:T(8,128)(2,1)S(1)} %get-tuple-element.31.after_ref), custom_call_target="tpu_custom_call" | custom-call | flops 1308622848 | bytes 3407872 | tf_op jit(solution)/shard_map/away_body/pallas_call | solution.py:239
  133.4 3.5 %stay_body.7 = (bf16[384,512]{1,0:T(8,128)(2,1)S(1)}, f32[384,512]{1,0:T(8,128)S(1)}) custom-call(s32[1]{0:T(128)} %bitcast.me_ref, bf16[384,1792]{1,0:T(8,128)(2,1)S(1)} %gate_up.7.hidden_ref.after_ref, bf16[1664,8192]{1,0:T(8,128)(2,1)} %weight_ref.15, bf16[2,384,512]{2,1,0:T(8,128)(2,1)S(1)} %collective-permute-done.25.got_ref), custom_call_target="tpu_custom_call" | custom-call | flops 1308622848 | bytes 3407872 | tf_op jit(solution)/shard_map/stay_body/pallas_call | solution.py:239
  136.9 3.5 %collective-permute-done.29 = bf16[384,512]{1,0:T(8,128)(2,1)S(1)} collective-permute-done((bf16[384,512]{1,0:T(8,128)(2,1)S(1)}, bf16[384,512]{1,0:T(8,128)(2,1)S(1)}, u32[]{:S(2)}, u32[]{:S(2)}) %collective-permute-start.29) | collective-permute-done | bytes 393248 | tf_op jit(solution)/shard_map/ppermute | solution.py:28
  140.6 3.5 %collective-permute-start.30 = (bf16[384,512]{1,0:T(8,128)(2,1)S(1)}, bf16[384,512]{1,0:T(8,128)(2,1)S(1)}, u32[]{:S(2)}, u32[]{:S(2)}) collective-permute-start(bf16[384,512]{1,0:T(8,128)(2,1)S(1)} %get-tuple-element.39), channel_id=1, source_target_pairs={{4,8},{5,9},{6,10},{7,11},{8,4},{9,5},{10,6},{11,7},{20,24},{21,25... | collective-permute-start | bytes 1179656 | tf_op jit(solution)/shard_map/ppermute | solution.py:28
  145.4 3.5 %stay_body.5 = (bf16[384,512]{1,0:T(8,128)(2,1)S(1)}, f32[384,512]{1,0:T(8,128)S(1)}) custom-call(s32[1]{0:T(128)} %bitcast.me_ref, bf16[384,1792]{1,0:T(8,128)(2,1)S(1)} %gate_up.7.hidden_ref.after_ref, bf16[1664,8192]{1,0:T(8,128)(2,1)} %weight_ref.15, bf16[2,384,512]{2,1,0:T(8,128)(2,1)S(1)} %collective-permute-done.22.got_ref), custom_call_target="tpu_custom_call" | custom-call | flops 1308622848 | bytes 3407872 | tf_op jit(solution)/shard_map/stay_body/pallas_call | solution.py:239
  152.4 5.2 %collective-permute-done.32 = bf16[384,512]{1,0:T(8,128)(2,1)S(1)} collective-permute-done((bf16[384,512]{1,0:T(8,128)(2,1)S(1)}, bf16[384,512]{1,0:T(8,128)(2,1)S(1)}, u32[]{:S(2)}, u32[]{:S(2)}) %collective-permute-start.32) | collective-permute-done | bytes 393248 | tf_op jit(solution)/shard_map/ppermute | solution.py:28
  159.7 3.5 %collective-permute-done.31 = bf16[384,512]{1,0:T(8,128)(2,1)S(1)} collective-permute-done((bf16[384,512]{1,0:T(8,128)(2,1)S(1)}, bf16[384,512]{1,0:T(8,128)(2,1)S(1)}, u32[]{:S(2)}, u32[]{:S(2)}) %collective-permute-start.31) | collective-permute-done | bytes 393248 | tf_op jit(solution)/shard_map/ppermute | solution.py:28
  163.2 4.3 %collective-permute-done.33 = bf16[384,512]{1,0:T(8,128)(2,1)S(1)} collective-permute-done((bf16[384,512]{1,0:T(8,128)(2,1)S(1)}, bf16[384,512]{1,0:T(8,128)(2,1)S(1)}, u32[]{:S(2)}, u32[]{:S(2)}) %collective-permute-start.33) | collective-permute-done | bytes 393248 | tf_op jit(solution)/shard_map/ppermute | solution.py:28
  (82 shorter events, 26.9 us)
Async XLA Ops:
  1.9 12.7 %collective-permute-start = (bf16[384,512]{1,0:T(8,128)(2,1)}, bf16[384,512]{1,0:T(8,128)(2,1)S(1)}, u32[]{:S(2)}, u32[]{:S(2)}) collective-permute-start(bf16[384,512]{1,0:T(8,128)(2,1)} %refs_0_.1), channel_id=1, source_target_pairs={{0,4},{1,5},{2,6},{3,7},{4,0},{5,1},{6,2},{7,3},{8,12},{9,13},{10,... | collective-permute-start | bytes 1179656 | tf_op jit(solution)/shard_map/ppermute | solution.py:28
  2.0 15.5 %collective-permute-start.3 = (bf16[384,512]{1,0:T(8,128)(2,1)}, bf16[384,512]{1,0:T(8,128)(2,1)S(1)}, u32[]{:S(2)}, u32[]{:S(2)}) collective-permute-start(bf16[384,512]{1,0:T(8,128)(2,1)} %refs_0_.1), channel_id=1, source_target_pairs={{4,8},{5,9},{6,10},{7,11},{8,4},{9,5},{10,6},{11,7},{20,24},{21,25... | collective-permute-start | bytes 1179656 | tf_op jit(solution)/shard_map/ppermute | solution.py:28
  8.7 20.0 %collective-permute-start.19 = (bf16[384,512]{1,0:T(8,128)(2,1)}, bf16[384,512]{1,0:T(8,128)(2,1)S(1)}, u32[]{:S(2)}, u32[]{:S(2)}) collective-permute-start(bf16[384,512]{1,0:T(8,128)(2,1)} %refs_0_.1), channel_id=1, source_target_pairs={{0,2},{1,3},{2,0},{3,1},{4,6},{5,7},{6,4},{7,5},{8,10},{9,11},{10,... | collective-permute-start | bytes 1179656 | tf_op jit(solution)/shard_map/ppermute | solution.py:23
  14.7 14.2 %collective-permute-start.1 = (bf16[384,512]{1,0:T(8,128)(2,1)S(1)}, bf16[384,512]{1,0:T(8,128)(2,1)S(1)}, u32[]{:S(2)}, u32[]{:S(2)}) collective-permute-start(bf16[384,512]{1,0:T(8,128)(2,1)S(1)} %collective-permute-done.refs_0_), channel_id=1, source_target_pairs={{4,8},{5,9},{6,10},{7,11},{8,4},{9,5},{10,6},{11,7},{20,24},{21,25... | collective-permute-start | bytes 1179656 | tf_op jit(solution)/shard_map/ppermute | solution.py:28
  17.5 11.9 %collective-permute-start.10 = (bf16[384,512]{1,0:T(8,128)(2,1)S(1)}, bf16[384,512]{1,0:T(8,128)(2,1)S(1)}, u32[]{:S(2)}, u32[]{:S(2)}) collective-permute-start(bf16[384,512]{1,0:T(8,128)(2,1)S(1)} %collective-permute-done.3), channel_id=1, source_target_pairs={{4,0},{5,1},{6,2},{7,3},{8,12},{9,13},{10,14},{11,15},{20,16},{21,... | collective-permute-start | bytes 1179656 | tf_op jit(solution)/shard_map/ppermute | solution.py:28
  19.1 11.0 %collective-permute-start.18 = (bf16[384,512]{1,0:T(8,128)(2,1)}, bf16[384,512]{1,0:T(8,128)(2,1)S(1)}, u32[]{:S(2)}, u32[]{:S(2)}) collective-permute-start(bf16[384,512]{1,0:T(8,128)(2,1)} %refs_0_.1), channel_id=1, source_target_pairs={{0,1},{1,0},{2,3},{3,2},{4,5},{5,4},{6,7},{7,6},{8,9},{9,8},{10,11... | collective-permute-start | bytes 1179656 | tf_op jit(solution)/shard_map/ppermute | solution.py:23
  27.1 12.1 %collective-permute-start.16 = (bf16[384,512]{1,0:T(8,128)(2,1)S(1)}, bf16[384,512]{1,0:T(8,128)(2,1)S(1)}, u32[]{:S(2)}, u32[]{:S(2)}) collective-permute-start(bf16[384,512]{1,0:T(8,128)(2,1)S(1)} %collective-permute-done.refs_0_), channel_id=1, source_target_pairs={{0,2},{1,3},{2,0},{3,1},{4,6},{5,7},{6,4},{7,5},{8,10},{9,11},{10,... | collective-permute-start | bytes 1179656 | tf_op jit(solution)/shard_map/ppermute | solution.py:23
  28.9 27.3 %collective-permute-start.15 = (bf16[384,512]{1,0:T(8,128)(2,1)S(1)}, bf16[384,512]{1,0:T(8,128)(2,1)S(1)}, u32[]{:S(2)}, u32[]{:S(2)}) collective-permute-start(bf16[384,512]{1,0:T(8,128)(2,1)S(1)} %collective-permute-done.refs_0_), channel_id=1, source_target_pairs={{0,1},{1,0},{2,3},{3,2},{4,5},{5,4},{6,7},{7,6},{8,9},{9,8},{10,11... | collective-permute-start | bytes 1179656 | tf_op jit(solution)/shard_map/ppermute | solution.py:23
  29.5 28.2 %collective-permute-start.12 = (bf16[384,512]{1,0:T(8,128)(2,1)S(1)}, bf16[384,512]{1,0:T(8,128)(2,1)S(1)}, u32[]{:S(2)}, u32[]{:S(2)}) collective-permute-start(bf16[384,512]{1,0:T(8,128)(2,1)S(1)} %broadcast_select_fusion.refs_0_), channel_id=1, source_target_pairs={{0,2},{1,3},{2,0},{3,1},{4,6},{5,7},{6,4},{7,5},{8,10},{9,11},{10,... | collective-permute-start | bytes 1179656 | tf_op jit(solution)/shard_map/ppermute | solution.py:23
  30.1 43.9 %collective-permute-start.11 = (bf16[384,512]{1,0:T(8,128)(2,1)S(1)}, bf16[384,512]{1,0:T(8,128)(2,1)S(1)}, u32[]{:S(2)}, u32[]{:S(2)}) collective-permute-start(bf16[384,512]{1,0:T(8,128)(2,1)S(1)} %broadcast_select_fusion.refs_0_), channel_id=1, source_target_pairs={{0,1},{1,0},{2,3},{3,2},{4,5},{5,4},{6,7},{7,6},{8,9},{9,8},{10,11... | collective-permute-start | bytes 1179656 | tf_op jit(solution)/shard_map/ppermute | solution.py:23
  30.4 25.2 %collective-permute-start.2 = (bf16[384,512]{1,0:T(8,128)(2,1)S(1)}, bf16[384,512]{1,0:T(8,128)(2,1)S(1)}, u32[]{:S(2)}, u32[]{:S(2)}) collective-permute-start(bf16[384,512]{1,0:T(8,128)(2,1)S(1)} %collective-permute-done.1), channel_id=1, source_target_pairs={{4,0},{5,1},{6,2},{7,3},{8,12},{9,13},{10,14},{11,15},{20,16},{21,... | collective-permute-start | bytes 1179656 | tf_op jit(solution)/shard_map/ppermute | solution.py:28
  39.2 18.5 %collective-permute-start.17 = (bf16[384,512]{1,0:T(8,128)(2,1)S(1)}, bf16[384,512]{1,0:T(8,128)(2,1)S(1)}, u32[]{:S(2)}, u32[]{:S(2)}) collective-permute-start(bf16[384,512]{1,0:T(8,128)(2,1)S(1)} %collective-permute-done.16.refs_2_), channel_id=1, source_target_pairs={{0,1},{1,0},{2,3},{3,2},{4,5},{5,4},{6,7},{7,6},{8,9},{9,8},{10,11... | collective-permute-start | bytes 1179656 | tf_op jit(solution)/shard_map/ppermute | solution.py:23
  55.6 18.4 %collective-permute-start.14 = (bf16[384,512]{1,0:T(8,128)(2,1)S(1)}, bf16[384,512]{1,0:T(8,128)(2,1)S(1)}, u32[]{:S(2)}, u32[]{:S(2)}) collective-permute-start(bf16[384,512]{1,0:T(8,128)(2,1)S(1)} %broadcast_select_fusion.1.refs_4_), channel_id=1, source_target_pairs={{0,1},{1,0},{2,3},{3,2},{4,5},{5,4},{6,7},{7,6},{8,9},{9,8},{10,11... | collective-permute-start | bytes 1179656 | tf_op jit(solution)/shard_map/ppermute | solution.py:23
  56.2 17.3 %collective-permute-start.4 = (bf16[384,512]{1,0:T(8,128)(2,1)S(1)}, bf16[384,512]{1,0:T(8,128)(2,1)S(1)}, u32[]{:S(2)}, u32[]{:S(2)}) collective-permute-start(bf16[384,512]{1,0:T(8,128)(2,1)S(1)} %broadcast_select_fusion.1.refs_4_), channel_id=1, source_target_pairs={{0,2},{1,3},{2,0},{3,1},{4,6},{5,7},{6,4},{7,5},{8,10},{9,11},{10,... | collective-permute-start | bytes 1179656 | tf_op jit(solution)/shard_map/ppermute | solution.py:23
  57.7 16.3 %collective-permute-start.13 = (bf16[384,512]{1,0:T(8,128)(2,1)S(1)}, bf16[384,512]{1,0:T(8,128)(2,1)S(1)}, u32[]{:S(2)}, u32[]{:S(2)}) collective-permute-start(bf16[384,512]{1,0:T(8,128)(2,1)S(1)} %collective-permute-done.12.refs_2_), channel_id=1, source_target_pairs={{0,1},{1,0},{2,3},{3,2},{4,5},{5,4},{6,7},{7,6},{8,9},{9,8},{10,11... | collective-permute-start | bytes 1179656 | tf_op jit(solution)/shard_map/ppermute | solution.py:23
  73.4 23.2 %collective-permute-start.5 = (bf16[384,512]{1,0:T(8,128)(2,1)S(1)}, bf16[384,512]{1,0:T(8,128)(2,1)S(1)}, u32[]{:S(2)}, u32[]{:S(2)}) collective-permute-start(bf16[384,512]{1,0:T(8,128)(2,1)S(1)} %collective-permute-done.4.refs_0_), channel_id=1, source_target_pairs={{0,1},{1,0},{2,3},{3,2},{4,5},{5,4},{6,7},{7,6},{8,9},{9,8},{10,11... | collective-permute-start | bytes 1179656 | tf_op jit(solution)/shard_map/ppermute | solution.py:23
  116.9 11.6 %collective-permute-start.28 = (bf16[384,512]{1,0:T(8,128)(2,1)S(1)}, bf16[384,512]{1,0:T(8,128)(2,1)S(1)}, u32[]{:S(2)}, u32[]{:S(2)}) collective-permute-start(bf16[384,512]{1,0:T(8,128)(2,1)S(1)} %get-tuple-element.34.after_ref), channel_id=1, source_target_pairs={{0,2},{1,3},{2,0},{3,1},{4,6},{5,7},{6,4},{7,5},{8,10},{9,11},{10,... | collective-permute-start | bytes 1179656 | tf_op jit(solution)/shard_map/ppermute | solution.py:23
  120.8 12.6 %collective-permute-start.25 = (bf16[2,384,512]{2,1,0:T(8,128)(2,1)S(1)}, bf16[2,384,512]{2,1,0:T(8,128)(2,1)S(1)}, u32[]{:S(2)}, u32[]{:S(2)}) collective-permute-start(bf16[2,384,512]{2,1,0:T(8,128)(2,1)S(1)} %away_body.7), channel_id=1, source_target_pairs={{0,1},{1,0},{2,3},{3,2},{4,5},{5,4},{6,7},{7,6},{8,9},{9,8},{10,11... | collective-permute-start | bytes 2359304 | tf_op jit(solution)/shard_map/ppermute | solution.py:23
  124.3 12.6 %collective-permute-start.27 = (bf16[384,512]{1,0:T(8,128)(2,1)S(1)}, bf16[384,512]{1,0:T(8,128)(2,1)S(1)}, u32[]{:S(2)}, u32[]{:S(2)}) collective-permute-start(bf16[384,512]{1,0:T(8,128)(2,1)S(1)} %get-tuple-element.31.after_ref), channel_id=1, source_target_pairs={{0,2},{1,3},{2,0},{3,1},{4,6},{5,7},{6,4},{7,5},{8,10},{9,11},{10,... | collective-permute-start | bytes 1179656 | tf_op jit(solution)/shard_map/ppermute | solution.py:23
  128.7 11.7 %collective-permute-start.29 = (bf16[384,512]{1,0:T(8,128)(2,1)S(1)}, bf16[384,512]{1,0:T(8,128)(2,1)S(1)}, u32[]{:S(2)}, u32[]{:S(2)}) collective-permute-start(bf16[384,512]{1,0:T(8,128)(2,1)S(1)} %fusion.3), channel_id=1, source_target_pairs={{0,4},{1,5},{2,6},{3,7},{12,8},{13,9},{14,10},{15,11},{16,20},{17,... | collective-permute-start | bytes 1179656 | tf_op jit(solution)/shard_map/ppermute | solution.py:28
  133.3 12.1 %collective-permute-start.22 = (bf16[2,384,512]{2,1,0:T(8,128)(2,1)S(1)}, bf16[2,384,512]{2,1,0:T(8,128)(2,1)S(1)}, u32[]{:S(2)}, u32[]{:S(2)}) collective-permute-start(bf16[2,384,512]{2,1,0:T(8,128)(2,1)S(1)} %away_body.6), channel_id=1, source_target_pairs={{0,1},{1,0},{2,3},{3,2},{4,5},{5,4},{6,7},{7,6},{8,9},{9,8},{10,11... | collective-permute-start | bytes 2359304 | tf_op jit(solution)/shard_map/ppermute | solution.py:23
  136.8 12.6 %collective-permute-start.26 = (bf16[384,512]{1,0:T(8,128)(2,1)S(1)}, bf16[384,512]{1,0:T(8,128)(2,1)S(1)}, u32[]{:S(2)}, u32[]{:S(2)}) collective-permute-start(bf16[384,512]{1,0:T(8,128)(2,1)S(1)} %get-tuple-element.36), channel_id=1, source_target_pairs={{0,2},{1,3},{2,0},{3,1},{4,6},{5,7},{6,4},{7,5},{8,10},{9,11},{10,... | collective-permute-start | bytes 1179656 | tf_op jit(solution)/shard_map/ppermute | solution.py:23
  144.1 13.5 %collective-permute-start.32 = (bf16[384,512]{1,0:T(8,128)(2,1)S(1)}, bf16[384,512]{1,0:T(8,128)(2,1)S(1)}, u32[]{:S(2)}, u32[]{:S(2)}) collective-permute-start(bf16[384,512]{1,0:T(8,128)(2,1)S(1)} %get-tuple-element.40), channel_id=1, source_target_pairs={{0,4},{1,5},{2,6},{3,7},{12,8},{13,9},{14,10},{15,11},{16,20},{17,... | collective-permute-start | bytes 1179656 | tf_op jit(solution)/shard_map/ppermute | solution.py:28
  151.5 11.6 %collective-permute-start.31 = (bf16[384,512]{1,0:T(8,128)(2,1)S(1)}, bf16[384,512]{1,0:T(8,128)(2,1)S(1)}, u32[]{:S(2)}, u32[]{:S(2)}) collective-permute-start(bf16[384,512]{1,0:T(8,128)(2,1)S(1)} %add_convert_fusion.1), channel_id=1, source_target_pairs={{0,4},{1,5},{2,6},{3,7},{4,0},{5,1},{6,2},{7,3},{8,12},{9,13},{10,... | collective-permute-start | bytes 1179656 | tf_op jit(solution)/shard_map/ppermute | solution.py:28
  (12 other events, 85.2 us)

commit v4 on v0

v4 whole, which is shorter than its diff:
```python
import functools

import jax
import jax.numpy as jnp
from jax import lax
from jax.experimental import pallas as pl
from jax.experimental.pallas import tpu as pltpu
from jax.sharding import PartitionSpec as P

epsilon = 1e-05
INNER = 4
LINE = 4
EXTRA = 16
VMEM_LIMIT = 30 * 1024 * 1024

PAIRS = ((0, 1), (1, 0), (2, 3), (3, 2))
MIDDLE = ((1, 2), (2, 1))
OUTWARD = ((1, 0), (2, 3))
INWARD = ((0, 1), (3, 2))


def along(x, pairs):
    moves = [(a * INNER + q, b * INNER + q) for a, b in pairs for q in range(INNER)]
    return lax.ppermute(x, "gx", moves)


def prepare_body(x_ref, gain_ref, out_ref):
    rows, width = x_ref.shape
    x = x_ref[...].astype(jnp.float32)
    out_ref[:rows, :] = (x * gain_ref[...].astype(jnp.float32)).astype(jnp.bfloat16)
    squares = jnp.broadcast_to(jnp.sum(x * x, axis=1, keepdims=True), (rows, 128)).T[:EXTRA]
    row = lax.broadcasted_iota(jnp.int32, (EXTRA, rows), 0)
    parts = jnp.zeros((EXTRA, rows), jnp.float32)
    for i in range(3):
        part = squares.astype(jnp.bfloat16).astype(jnp.float32)
        parts = jnp.where(row == i, part, parts)
        squares = squares - part
    out_ref[rows:, :rows] = parts.astype(jnp.bfloat16)
    if rows < width:
        out_ref[rows:, rows:] = jnp.zeros((EXTRA, width - rows), jnp.bfloat16)


def prepare(activations, norm_gain):
    rows, width = activations.shape
    return pl.pallas_call(
        prepare_body,
        out_shape=jax.ShapeDtypeStruct((rows + EXTRA, width), jnp.bfloat16),
        compiler_params=pltpu.CompilerParams(vmem_limit_bytes=VMEM_LIMIT),
        name="prepare",
    )(activations, norm_gain[None, :])


def gate_up_body(first, last, rows, main, features, me_ref, x_ref, gate_ref, up_ref, *rest):
    if not first:
        before = rest[:4]
        rest = rest[4:]
    if last:
        hidden_ref, *rest = rest
    accs = rest
    step = pl.program_id(0)
    x = x_ref[0, :rows, :]
    mixed = jnp.concatenate([gate_ref[:, main:], up_ref[:, main:]], axis=1)
    weights = (gate_ref[:, :main], up_ref[:, :main], mixed)

    def values():
        for weight in weights:
            yield jnp.dot(x, weight, preferred_element_type=jnp.float32)
        squares = x_ref[0, rows:, :].astype(jnp.float32)
        yield jnp.broadcast_to(jnp.sum(squares, axis=0, keepdims=True), accs[3].shape)

    @pl.when(step == 0)
    def _():
        for i, value in enumerate(values()):
            accs[i][...] = value if first else before[i][...] + value

    @pl.when(step > 0)
    def _():
        for i, value in enumerate(values()):
            accs[i][...] += value

    if last:

        @pl.when(step == pl.num_programs(0) - 1)
        def _():
            factor = lax.rsqrt(accs[3][:1, :rows] / features + epsilon)
            factor = jnp.broadcast_to(factor, (128, rows)).T[:, :1]

            def act(g, u):
                g, u = g * factor, u * factor
                return (g / (1.0 + jnp.exp(-g)) * u).astype(jnp.bfloat16)

            rem = mixed.shape[1] // 2
            hidden_ref[:, :main] = act(accs[0][...], accs[1][...])
            hidden_ref[:, main:] = act(accs[2][:, :rem], accs[2][:, rem:])


def gate_up(start, x, gate_weight, up_weight, acc, last):
    count, height, depth = x.shape
    rows = height - EXTRA
    features, ff = gate_weight.shape
    main = ff // 256 * 256 if ff % 256 else ff - 256
    rem = ff - main
    first = acc is None
    whole = lambda shape: pl.BlockSpec(shape, lambda s, me: (0, 0))
    weight = pl.BlockSpec((depth, ff), lambda s, me: (me[0] + s, 0))
    in_specs = [pl.BlockSpec((1, height, depth), lambda s, me: (s, 0, 0)), weight, weight]
    args = [x, gate_weight, up_weight]
    shapes = [(rows, main), (rows, main), (rows, 2 * rem), (8, depth)]
    if not first:
        in_specs += [whole(s) for s in shapes]
        args += list(acc)
    if last:
        out_shape = [jax.ShapeDtypeStruct((rows, ff), jnp.bfloat16)]
        out_specs = [whole((rows, ff))]
        scratch = [pltpu.VMEM(s, jnp.float32) for s in shapes]
    else:
        out_shape = [jax.ShapeDtypeStruct(s, jnp.float32) for s in shapes]
        out_specs = [whole(s) for s in shapes]
        scratch = []
    return pl.pallas_call(
        functools.partial(gate_up_body, first, last, rows, main, features),
        grid_spec=pltpu.PrefetchScalarGridSpec(
            num_scalar_prefetch=1,
            grid=(count,),
            in_specs=in_specs,
            out_specs=out_specs,
            scratch_shapes=scratch,
        ),
        out_shape=out_shape,
        compiler_params=pltpu.CompilerParams(vmem_limit_bytes=VMEM_LIMIT),
        cost_estimate=pl.CostEstimate(
            flops=4 * rows * depth * count * ff,
            bytes_accessed=4 * depth * count * ff,
            transcendentals=0,
        ),
        name="gate_up",
    )(start, *args)


def down_block(hidden_ref, weight_ref):
    ff = hidden_ref.shape[1]
    main = ff // 256 * 256
    value = jnp.dot(
        hidden_ref[:, :main], weight_ref[:main, :], preferred_element_type=jnp.float32
    )
    if main < ff:
        value = value + jnp.dot(
            hidden_ref[:, main:], weight_ref[main:, :], preferred_element_type=jnp.float32
        )
    return value


def down_body(start_ref, hidden_ref, weight_ref, out_ref):
    out_ref[0] = down_block(hidden_ref, weight_ref).astype(out_ref.dtype)


def down(start, hidden, down_weight, width):
    rows, ff = hidden.shape
    return pl.pallas_call(
        down_body,
        grid_spec=pltpu.PrefetchScalarGridSpec(
            num_scalar_prefetch=1,
            grid=(INNER,),
            in_specs=[
                pl.BlockSpec((rows, ff), lambda s, me: (0, 0)),
                pl.BlockSpec((ff, width), lambda s, me: (0, me[0] + s)),
            ],
            out_specs=pl.BlockSpec((1, rows, width), lambda s, me: (s, 0, 0)),
        ),
        out_shape=jax.ShapeDtypeStruct((INNER, rows, width), jnp.bfloat16),
        compiler_params=pltpu.CompilerParams(vmem_limit_bytes=VMEM_LIMIT),
        cost_estimate=pl.CostEstimate(
            flops=2 * rows * ff * width * INNER,
            bytes_accessed=2 * ff * width * INNER,
            transcendentals=0,
        ),
        name="down",
    )(start, hidden, down_weight)


def overlapped(activations, norm_gain, gate_weight, up_weight, down_weight):
    width = activations.shape[1]
    z = lax.axis_index("gx").astype(jnp.int32) // INNER
    edge = (z == 0) | (z == LINE - 1)
    starts = [((z ^ k) * INNER)[None] for k in range(LINE)]
    teams = [[i * INNER + q for q in range(INNER)] for i in range(LINE)]
    resident = activations.astype(jnp.float32)

    shard = prepare(activations, norm_gain)
    neighbour = along(shard, PAIRS)
    inner = along(shard, MIDDLE)
    second_edge = along(inner, OUTWARD)
    second_middle = along(neighbour, MIDDLE)
    third_edge = along(second_middle, OUTWARD)
    slots = [
        shard,
        neighbour,
        jnp.where(edge, second_edge, second_middle),
        jnp.where(edge, third_edge, inner),
    ]
    acc = None
    for k in range(LINE):
        x = lax.all_gather(slots[k], "gx", axis_index_groups=teams)
        acc = gate_up(starts[k], x, gate_weight, up_weight, acc, k == LINE - 1)
    hidden = acc[0]

    narrow = lambda x: x.astype(jnp.bfloat16)
    wide = lambda x: x.astype(jnp.float32)

    sums = [None] * LINE
    for k in reversed(range(LINE)):
        partial = down(starts[k], hidden, down_weight, width)
        sums[k] = lax.psum_scatter(partial, "gx", axis_index_groups=teams)

    middle_two = wide(sums[2]) + wide(along(sums[3], INWARD))
    middle_three = wide(sums[3]) + wide(along(sums[2], INWARD))
    one = wide(sums[1]) + wide(along(narrow(middle_two), MIDDLE))
    branch = (
        wide(sums[0])
        + wide(along(narrow(one), PAIRS))
        + wide(along(narrow(middle_three), MIDDLE))
    )
    return (resident + branch).astype(jnp.bfloat16)


def plain(activations, norm_gain, gate_weight, up_weight, down_weight):
    resident = activations.astype(jnp.float32)
    totals = lax.psum(jnp.sum(resident * resident, axis=1), "gx")
    factor = lax.rsqrt(totals / (resident.shape[1] * lax.axis_size("gx")) + epsilon)
    normed = (resident * factor[:, None] * norm_gain.astype(jnp.float32)[None, :]).astype(
        jnp.bfloat16
    )
    pieces = lax.all_gather(normed, "gx", axis=1, tiled=True)
    gate_sum = jnp.dot(pieces, gate_weight, preferred_element_type=jnp.float32)
    up_sum = jnp.dot(pieces, up_weight, preferred_element_type=jnp.float32)
    hidden = (jax.nn.silu(gate_sum) * up_sum).astype(jnp.bfloat16)
    summed = lax.psum_scatter(
        lax.dot_general(
            down_weight, hidden, (((0,), (1,)), ((), ())), preferred_element_type=jnp.float32
        ),
        "gx",
        scatter_dimension=0,
        tiled=True,
    )
    return (resident + summed.T).astype(jnp.bfloat16)


def per_device(n, activations, norm_gain, gate_weight, up_weight, down_weight):
    args = (activations, norm_gain, gate_weight, up_weight, down_weight)
    rows, width = activations.shape
    tiled = rows % 128 == 0 and width % 128 == 0 and gate_weight.shape[1] % 128 == 0
    tiled = tiled and rows <= width
    if n == INNER * LINE and tiled:
        return overlapped(*args)
    return plain(*args)


def solution(mesh):
    in_specs = (P("groups", "gx"), P("gx"), P(None, "gx"), P(None, "gx"), P("gx", None))
    out_specs = P("groups", "gx")
    return jax.shard_map(
        functools.partial(per_device, mesh.shape["gx"]),
        mesh=mesh,
        in_specs=in_specs,
        out_specs=out_specs,
        check_vma=False,
    )
```

time: 303 us -> 255 us (0.84)
  waiting for transfers between devices: 196 us -> 127 us
  Pallas kernels: 0 us -> 66 us
  matrix products: 52.6 us -> 0 us
  blocking collectives: 34.9 us -> 0 us
  local copies, waits for them, and re-layouts: 0.01 us -> 23.6 us
  starting transfers between devices: 0.04 us -> 17.2 us
    pallas_call x0 -> x9, Pallas kernels: none -> 66 us  [the longest x4 38.4 us: gate_up(): pl.pallas_call(functools.partial(gate_up_body, first, last, rows, main, f...]
    all_gather x1 -> x4, waiting for transfers between devices: 63 us -> 0.02 us  [overlapped(): x = lax.all_gather(slots[k], 'gx', axis_index_groups=teams)]
    dot_general x3 -> x0, matrix products: 52.6 us -> none  [the longest x1 19.2 us: per_device(): lax.dot_general(down_weight, hidden, (((0,), (1,)), ((), ())), preferred_...]
    reduce_scatter x1 -> x4, waiting for transfers between devices: 133 us -> 80.6 us  [overlapped(): sums[k] = lax.psum_scatter(partial, 'gx', axis_index_groups=teams)]
    ppermute x0 -> x10, waiting for transfers between devices: none -> 45.8 us  [along(): return lax.ppermute(x, 'gx', moves)]
    psum x1 -> x0, blocking collectives: 34.9 us -> none  [per_device(): totals = lax.psum(jnp.sum(resident * resident, axis=1), 'gx')]
    unnamed x4 -> x34, local copies, waits for them, and re-layouts: 0.01 us -> 23 us
    ppermute x0 -> x10, starting transfers between devices: none -> 16.8 us  [along(): return lax.ppermute(x, 'gx', moves)]
  transfers between devices with their start and end apart: 2 -> 18, of which waited for: 2 -> 8; matrix products, arithmetic and copies ran while one was open for 0% -> 2% of each run, Pallas kernels for 0% -> 19%
where the time goes in v4:
time: 255 us; the launch traced here: 254 us
  waiting for transfers between devices  127 us (50%)
  Pallas kernels  66 us (26%)
  local copies, waits for them, and re-layouts  23.6 us (9%)
  starting transfers between devices  17.2 us (7%)
  between operations  13.7 us (5%)
  other arithmetic  6.87 us (3%)
    reduce_scatter x4, waiting for transfers between devices, overlapped(): sums[k] = lax.psum_scatter(partial, 'gx', axis_index_groups=teams)  80.6 us
    ppermute x10, waiting for transfers between devices, along(): return lax.ppermute(x, 'gx', moves)  45.8 us
    pallas_call x4, Pallas kernels, gate_up(): pl.pallas_call(functools.partial(gate_up_body, first, last, rows, main, f...  38.4 us
    pallas_call x4, Pallas kernels, down(): pl.pallas_call(down_body, grid_spec=pltpu.PrefetchScalarGridSpec(num_scal...  26.6 us
    unnamed x34, local copies, waits for them, and re-layouts  23 us
    ppermute x10, starting transfers between devices, along(): return lax.ppermute(x, 'gx', moves)  16.8 us
  transfers between devices with their start and end apart: 18, of which 8 were waited for; matrix products, arithmetic and copies ran while one was open for 2% of the time, Pallas kernels for 19%

profile of v4, /device:TPU:0, one launch (start us, length us, event | category | flops | bytes accessed | tf_op | source)
XLA Modules:
  0.0 254.0 jit_solution(15580647804600619447)
XLA Ops:
  9.3 3.1 %collective-permute-start = (bf16[400,512]{1,0:T(8,128)(2,1)}, bf16[400,512]{1,0:T(8,128)(2,1)S(1)}, u32[]{:S(2)}, u32[]{:S(2)}) collective-permute-start(bf16[400,512]{1,0:T(8,128)(2,1)} %prepare.1), channel_id=1, source_target_pairs={{0,4},{1,5},{2,6},{3,7},{4,0},{5,1},{6,2},{7,3},{8,12},{9,13},{10,... | collective-permute-start | bytes 1228808 | tf_op jit(solution)/shard_map/ppermute | solution.py:24
  12.4 9.7 %collective-permute-done = bf16[400,512]{1,0:T(8,128)(2,1)S(1)} collective-permute-done((bf16[400,512]{1,0:T(8,128)(2,1)}, bf16[400,512]{1,0:T(8,128)(2,1)S(1)}, u32[]{:S(2)}, u32[]{:S(2)}) %collective-permute-start) | collective-permute-done | bytes 409632 | tf_op jit(solution)/shard_map/ppermute | solution.py:24
  25.6 20.7 %collective-permute-done.4 = bf16[400,512]{1,0:T(8,128)(2,1)S(1)} collective-permute-done((bf16[400,512]{1,0:T(8,128)(2,1)S(1)}, bf16[400,512]{1,0:T(8,128)(2,1)S(1)}, u32[]{:S(2)}, u32[]{:S(2)}) %collective-permute-start.4) | collective-permute-done | bytes 409632 | tf_op jit(solution)/shard_map/ppermute | solution.py:24
  48.5 8.5 %collective-permute-done.2 = bf16[400,512]{1,0:T(8,128)(2,1)S(1)} collective-permute-done((bf16[400,512]{1,0:T(8,128)(2,1)S(1)}, bf16[400,512]{1,0:T(8,128)(2,1)S(1)}, u32[]{:S(2)}, u32[]{:S(2)}) %collective-permute-start.2) | collective-permute-done | bytes 409632 | tf_op jit(solution)/shard_map/ppermute | solution.py:24
  59.4 9.4 %gate_up.4 = (f32[384,1536]{1,0:T(8,128)S(1)}, f32[384,1536]{1,0:T(8,128)S(1)}, f32[384,256]{1,0:T(8,128)S(1)}, f32[8,512]{1,0:T(8,128)S(1)}) custom-call(s32[1]{0:T(128)} %bitcast.me_ref.start_ref, bf16[4,400,512]{2,1,0:T(8,128)(2,1)S(1)} %bitcast.19, bf16[8192,1664]{1,0:T(8,128)(2,1)} %gate_ref.7, bf16[8192,1664]{1,0:T(8,128)(2,1)} %up_ref.7), custom_call_target="tpu_custom_call" | custom-call | flops 5234491392 | bytes 13631488 | tf_op jit(solution)/shard_map/gate_up/pallas_call | solution.py:120
  71.6 1.7 copy-done.3
  73.3 1.7 copy-done.5
  76.4 9.5 %gate_up.5 = (f32[384,1536]{1,0:T(8,128)S(1)}, f32[384,1536]{1,0:T(8,128)S(1)}, f32[384,256]{1,0:T(8,128)S(1)}, f32[8,512]{1,0:T(8,128)S(1)}) custom-call(s32[1]{0:T(128)} %bitcast.5.me_ref.start_ref, bf16[4,400,512]{2,1,0:T(8,128)(2,1)S(1)} %bitcast.20, bf16[8192,1664]{1,0:T(8,128)(2,1)} %gate_ref.7, bf16[8192,1664]{1,0:T(8,128)(2,1)} %up_ref.7, ...), custom_call_target="tpu_custom_call" | custom-call | flops 5234491392 | bytes 13631488 | tf_op jit(solution)/shard_map/gate_up/pallas_call | solution.py:120
  87.4 1.7 copy-done.1
  90.5 9.3 %gate_up.6 = (f32[384,1536]{1,0:T(8,128)S(1)}, f32[384,1536]{1,0:T(8,128)S(1)}, f32[384,256]{1,0:T(8,128)S(1)}, f32[8,512]{1,0:T(8,128)S(1)}) custom-call(s32[1]{0:T(128)} %bitcast.3.me_ref.start_ref, bf16[4,400,512]{2,1,0:T(8,128)(2,1)S(1)} %bitcast.21, bf16[8192,1664]{1,0:T(8,128)(2,1)} %gate_ref.7, bf16[8192,1664]{1,0:T(8,128)(2,1)} %up_ref.7, ...), custom_call_target="tpu_custom_call" | custom-call | flops 5234491392 | bytes 13631488 | tf_op jit(solution)/shard_map/gate_up/pallas_call | solution.py:120
  102.7 1.7 copy-done.7
  107.4 10.2 %gate_up.7.hidden_ref = bf16[384,1664]{1,0:T(8,128)(2,1)S(1)} custom-call(s32[1]{0:T(128)} %bitcast.1.me_ref.start_ref, bf16[4,400,512]{2,1,0:T(8,128)(2,1)S(1)} %bitcast.18, bf16[8192,1664]{1,0:T(8,128)(2,1)} %gate_ref.7, bf16[8192,1664]{1,0:T(8,128)(2,1)} %up_ref.7, f32[384,1536]{1,0:T(8,128)S(1)} %copy-done.7, f32[384,1536]{1,0:T(8,128)S(1)} %copy-done.9, ...), custom_call_target="tpu_custom_call" | custom-call | flops 5234491392 | bytes 13631488 | tf_op jit(solution)/shard_map/gate_up/pallas_call | solution.py:120
  117.7 6.6 %down.7 = bf16[4,384,512]{2,1,0:T(8,128)(2,1)} custom-call(s32[1]{0:T(128)} %bitcast.1.me_ref.start_ref, bf16[384,1664]{1,0:T(8,128)(2,1)S(1)} %gate_up.7.hidden_ref, bf16[1664,8192]{1,0:T(8,128)(2,1)} %weight_ref.7), custom_call_target="tpu_custom_call" | custom-call | flops 2617245696 | bytes 6815744 | tf_op jit(solution)/shard_map/down/pallas_call | solution.py:159
  124.5 6.6 %down.6 = bf16[4,384,512]{2,1,0:T(8,128)(2,1)} custom-call(s32[1]{0:T(128)} %bitcast.3.me_ref.start_ref, bf16[384,1664]{1,0:T(8,128)(2,1)S(1)} %gate_up.7.hidden_ref, bf16[1664,8192]{1,0:T(8,128)(2,1)} %weight_ref.7), custom_call_target="tpu_custom_call" | custom-call | flops 2617245696 | bytes 6815744 | tf_op jit(solution)/shard_map/down/pallas_call | solution.py:159
  131.1 6.8 %down.5 = bf16[4,384,512]{2,1,0:T(8,128)(2,1)} custom-call(s32[1]{0:T(128)} %bitcast.5.me_ref.start_ref, bf16[384,1664]{1,0:T(8,128)(2,1)S(1)} %gate_up.7.hidden_ref, bf16[1664,8192]{1,0:T(8,128)(2,1)} %weight_ref.7), custom_call_target="tpu_custom_call" | custom-call | flops 2617245696 | bytes 6815744 | tf_op jit(solution)/shard_map/down/pallas_call | solution.py:159
  137.9 6.7 %down.4 = bf16[4,384,512]{2,1,0:T(8,128)(2,1)} custom-call(s32[1]{0:T(128)} %bitcast.me_ref.start_ref, bf16[384,1664]{1,0:T(8,128)(2,1)S(1)} %gate_up.7.hidden_ref, bf16[1664,8192]{1,0:T(8,128)(2,1)} %weight_ref.7), custom_call_target="tpu_custom_call" | custom-call | flops 2617245696 | bytes 6815744 | tf_op jit(solution)/shard_map/down/pallas_call | solution.py:159
  144.7 8.2 %reduce-scatter.11.cloned.1.call-done = bf16[1,384,512]{2,1,0:T(8,128)(2,1)} async-done(((bf16[4,384,512]{2,1,0:T(8,128)(2,1)}), bf16[1,384,512]{2,1,0:T(8,128)(2,1)}) %reduce-scatter.11.cloned.1.call-update) | async-done | bytes 393232 | tf_op jit(solution)/shard_map/reduce_scatter | solution.py:213
  152.8 3.4 %collective-permute-start.5 = (bf16[384,512]{1,0:T(8,128)(2,1)}, bf16[384,512]{1,0:T(8,128)(2,1)S(1)}, u32[]{:S(2)}, u32[]{:S(2)}) collective-permute-start(bf16[384,512]{1,0:T(8,128)(2,1)} %bitcast.22), channel_id=1, source_target_pairs={{0,4},{1,5},{2,6},{3,7},{12,8},{13,9},{14,10},{15,11},{16,20},{17,... | collective-permute-start | bytes 1179656 | tf_op jit(solution)/shard_map/ppermute | solution.py:24
  156.2 27.4 %reduce-scatter.9.cloned.1.call-done = bf16[1,384,512]{2,1,0:T(8,128)(2,1)} async-done(((bf16[4,384,512]{2,1,0:T(8,128)(2,1)}), bf16[1,384,512]{2,1,0:T(8,128)(2,1)}) %reduce-scatter.9.cloned.1.call-update) | async-done | bytes 393232 | tf_op jit(solution)/shard_map/reduce_scatter | solution.py:213
  183.6 3.4 %collective-permute-start.8 = (bf16[384,512]{1,0:T(8,128)(2,1)}, bf16[384,512]{1,0:T(8,128)(2,1)S(1)}, u32[]{:S(2)}, u32[]{:S(2)}) collective-permute-start(bf16[384,512]{1,0:T(8,128)(2,1)} %bitcast.23), channel_id=1, source_target_pairs={{0,4},{1,5},{2,6},{3,7},{12,8},{13,9},{14,10},{15,11},{16,20},{17,... | collective-permute-start | bytes 1179656 | tf_op jit(solution)/shard_map/ppermute | solution.py:24
  188.8 6.8 %collective-permute-done.8 = bf16[384,512]{1,0:T(8,128)(2,1)S(1)} collective-permute-done((bf16[384,512]{1,0:T(8,128)(2,1)}, bf16[384,512]{1,0:T(8,128)(2,1)S(1)}, u32[]{:S(2)}, u32[]{:S(2)}) %collective-permute-start.8) | collective-permute-done | bytes 393248 | tf_op jit(solution)/shard_map/ppermute | solution.py:24
  197.4 16.9 %reduce-scatter.7.cloned.1.call-done = bf16[1,384,512]{2,1,0:T(8,128)(2,1)} async-done(((bf16[4,384,512]{2,1,0:T(8,128)(2,1)}), bf16[1,384,512]{2,1,0:T(8,128)(2,1)}) %reduce-scatter.7.cloned.1.call-update) | async-done | bytes 393232 | tf_op jit(solution)/shard_map/reduce_scatter | solution.py:213
  216.9 28.3 %reduce-scatter.5.cloned.1.call-done = bf16[1,384,512]{2,1,0:T(8,128)(2,1)} async-done(((bf16[4,384,512]{2,1,0:T(8,128)(2,1)}), bf16[1,384,512]{2,1,0:T(8,128)(2,1)}) %reduce-scatter.5.cloned.1.call-update) | async-done | bytes 393232 | tf_op jit(solution)/shard_map/reduce_scatter | solution.py:213
  245.2 1.9 fusion.3
  (70 shorter events, 30.4 us)
Async XLA Ops:
  6.5 51.4 %all-gather.15.cloned.1.call-start = ((), (), s32[]{:S(2)}) async-start(), calls=%async_computation.11 | async-start | bytes 2048000 | tf_op jit(solution)/shard_map/all_gather | solution.py:203
  9.2 62.4 %all-gather.13.cloned.1.call-start = ((), (), s32[]{:S(2)}) async-start(), calls=%async_computation.10 | async-start | bytes 2048000 | tf_op jit(solution)/shard_map/all_gather | solution.py:203
  9.3 12.8 %collective-permute-start = (bf16[400,512]{1,0:T(8,128)(2,1)}, bf16[400,512]{1,0:T(8,128)(2,1)S(1)}, u32[]{:S(2)}, u32[]{:S(2)}) collective-permute-start(bf16[400,512]{1,0:T(8,128)(2,1)} %prepare.1), channel_id=1, source_target_pairs={{0,4},{1,5},{2,6},{3,7},{4,0},{5,1},{6,2},{7,3},{8,12},{9,13},{10,... | collective-permute-start | bytes 1228808 | tf_op jit(solution)/shard_map/ppermute | solution.py:24
  22.8 64.5 %all-gather.11.cloned.1.call-start = ((), (), s32[]{:S(2)}) async-start(), calls=%async_computation.9 | async-start | bytes 2048000 | tf_op jit(solution)/shard_map/all_gather | solution.py:203
  22.9 1.4 collective-permute-start.3
  23.6 2.0 collective-permute-start.1
  24.3 22.0 %collective-permute-start.4 = (bf16[400,512]{1,0:T(8,128)(2,1)S(1)}, bf16[400,512]{1,0:T(8,128)(2,1)S(1)}, u32[]{:S(2)}, u32[]{:S(2)}) collective-permute-start(bf16[400,512]{1,0:T(8,128)(2,1)S(1)} %collective-permute-done.3), channel_id=1, source_target_pairs={{4,0},{5,1},{6,2},{7,3},{8,12},{9,13},{10,14},{11,15},{20,16},{21,... | collective-permute-start | bytes 1228808 | tf_op jit(solution)/shard_map/ppermute | solution.py:24
  47.2 55.5 %all-gather.9.cloned.1.call-start = ((), (), s32[]{:S(2)}) async-start(), calls=%async_computation.8 | async-start | bytes 2048000 | tf_op jit(solution)/shard_map/all_gather | solution.py:203
  47.2 9.8 %collective-permute-start.2 = (bf16[400,512]{1,0:T(8,128)(2,1)S(1)}, bf16[400,512]{1,0:T(8,128)(2,1)S(1)}, u32[]{:S(2)}, u32[]{:S(2)}) collective-permute-start(bf16[400,512]{1,0:T(8,128)(2,1)S(1)} %collective-permute-done.1), channel_id=1, source_target_pairs={{4,0},{5,1},{6,2},{7,3},{8,12},{9,13},{10,14},{11,15},{20,16},{21,... | collective-permute-start | bytes 1228808 | tf_op jit(solution)/shard_map/ppermute | solution.py:24
  57.9 94.9 %reduce-scatter.11.cloned.1.call-start = ((), (), s32[]{:S(2)}) async-start(), calls=%async_computation.7 | async-start | bytes 1966080 | tf_op jit(solution)/shard_map/reduce_scatter | solution.py:213
  71.6 1.7 copy-start.3
  73.3 1.7 copy-start.5
  87.4 1.7 copy-start.1
  102.7 1.7 copy-start.7
  104.3 1.7 copy-start.9
  124.2 59.3 %reduce-scatter.9.cloned.1.call-start = ((), (), s32[]{:S(2)}) async-start(), calls=%async_computation.6 | async-start | bytes 1966080 | tf_op jit(solution)/shard_map/reduce_scatter | solution.py:213
  131.0 83.2 %reduce-scatter.7.cloned.1.call-start = ((), (), s32[]{:S(2)}) async-start(), calls=%async_computation.5 | async-start | bytes 1966080 | tf_op jit(solution)/shard_map/reduce_scatter | solution.py:213
  137.9 107.3 %reduce-scatter.5.cloned.1.call-start = ((), (), s32[]{:S(2)}) async-start(), calls=%async_computation.4 | async-start | bytes 1966080 | tf_op jit(solution)/shard_map/reduce_scatter | solution.py:213
  144.6 100.6 %copy-start.15 = (bf16[384,512]{1,0:T(8,128)(2,1)S(1)}, bf16[384,512]{1,0:T(8,128)(2,1)}, u32[]{:S(2)}) copy-start(bf16[384,512]{1,0:T(8,128)(2,1)} %x_ref.1) | copy-start | bytes 1179652
  152.8 34.2 %collective-permute-start.5 = (bf16[384,512]{1,0:T(8,128)(2,1)}, bf16[384,512]{1,0:T(8,128)(2,1)S(1)}, u32[]{:S(2)}, u32[]{:S(2)}) collective-permute-start(bf16[384,512]{1,0:T(8,128)(2,1)} %bitcast.22), channel_id=1, source_target_pairs={{0,4},{1,5},{2,6},{3,7},{12,8},{13,9},{14,10},{15,11},{16,20},{17,... | collective-permute-start | bytes 1179656 | tf_op jit(solution)/shard_map/ppermute | solution.py:24
  183.6 12.0 %collective-permute-start.8 = (bf16[384,512]{1,0:T(8,128)(2,1)}, bf16[384,512]{1,0:T(8,128)(2,1)S(1)}, u32[]{:S(2)}, u32[]{:S(2)}) collective-permute-start(bf16[384,512]{1,0:T(8,128)(2,1)} %bitcast.23), channel_id=1, source_target_pairs={{0,4},{1,5},{2,6},{3,7},{12,8},{13,9},{14,10},{15,11},{16,20},{17,... | collective-permute-start | bytes 1179656 | tf_op jit(solution)/shard_map/ppermute | solution.py:24
  188.1 26.2 %collective-permute-start.6 = (bf16[384,512]{1,0:T(8,128)(2,1)S(1)}, bf16[384,512]{1,0:T(8,128)(2,1)S(1)}, u32[]{:S(2)}, u32[]{:S(2)}) collective-permute-start(bf16[384,512]{1,0:T(8,128)(2,1)S(1)} %add_convert_fusion.1), channel_id=1, source_target_pairs={{4,8},{5,9},{6,10},{7,11},{8,4},{9,5},{10,6},{11,7},{20,24},{21,25... | collective-permute-start | bytes 1179656 | tf_op jit(solution)/shard_map/ppermute | solution.py:24
  196.7 48.5 %collective-permute-start.9 = (bf16[384,512]{1,0:T(8,128)(2,1)S(1)}, bf16[384,512]{1,0:T(8,128)(2,1)S(1)}, u32[]{:S(2)}, u32[]{:S(2)}) collective-permute-start(bf16[384,512]{1,0:T(8,128)(2,1)S(1)} %add_convert_fusion), channel_id=1, source_target_pairs={{4,8},{5,9},{6,10},{7,11},{8,4},{9,5},{10,6},{11,7},{20,24},{21,25... | collective-permute-start | bytes 1179656 | tf_op jit(solution)/shard_map/ppermute | solution.py:24
  215.4 29.8 %collective-permute-start.7 = (bf16[384,512]{1,0:T(8,128)(2,1)S(1)}, bf16[384,512]{1,0:T(8,128)(2,1)S(1)}, u32[]{:S(2)}, u32[]{:S(2)}) collective-permute-start(bf16[384,512]{1,0:T(8,128)(2,1)S(1)} %fusion), channel_id=1, source_target_pairs={{0,4},{1,5},{2,6},{3,7},{4,0},{5,1},{6,2},{7,3},{8,12},{9,13},{10,... | collective-permute-start | bytes 1179656 | tf_op jit(solution)/shard_map/ppermute | solution.py:24
  (11 other events, 14.6 us)
Sparse Core Ops, SparseCore 0:
  9.3 22.7 all-gather.14
  33.7 20.0 all-gather.12
  55.3 20.0 all-gather.10
  76.8 20.0 all-gather.8
  124.4 28.3 reduce-scatter.10
  155.4 28.1 reduce-scatter.8
  186.1 28.1 reduce-scatter.6
  216.9 28.1 reduce-scatter.4

commit v5 on v4

v5 whole, which is shorter than its diff:
```python
import functools

import jax
import jax.numpy as jnp
from jax import lax
from jax.experimental import pallas as pl
from jax.experimental.pallas import tpu as pltpu
from jax.sharding import PartitionSpec as P

epsilon = 1e-05
INNER = 4
LINE = 4
EXTRA = 16
VMEM_LIMIT = 30 * 1024 * 1024

PAIRS = ((0, 1), (1, 0), (2, 3), (3, 2))
MIDDLE = ((1, 2), (2, 1))
OUTWARD = ((1, 0), (2, 3))
INWARD = ((0, 1), (3, 2))


def swap(x, mask):
    return lax.ppermute(x, "gx", [(i, i ^ mask) for i in range(INNER * LINE)])


def along(x, pairs):
    moves = [(a * INNER + q, b * INNER + q) for a, b in pairs for q in range(INNER)]
    return lax.ppermute(x, "gx", moves)


def pick(table, s):
    value = jnp.int32(table[0])
    for i, entry in enumerate(table[1:], 1):
        value = jnp.where(s == i, jnp.int32(entry), value)
    return value


def prepare_body(x_ref, gain_ref, out_ref):
    rows, width = x_ref.shape
    x = x_ref[...].astype(jnp.float32)
    gain = gain_ref[...].astype(jnp.float32).reshape(1, width)
    out_ref[:rows, :] = (x * gain).astype(jnp.bfloat16)
    squares = jnp.broadcast_to(jnp.sum(x * x, axis=1, keepdims=True), (rows, 128)).T[:EXTRA]
    row = lax.broadcasted_iota(jnp.int32, (EXTRA, rows), 0)
    parts = jnp.zeros((EXTRA, rows), jnp.float32)
    for i in range(3):
        part = squares.astype(jnp.bfloat16).astype(jnp.float32)
        parts = jnp.where(row == i, part, parts)
        squares = squares - part
    out_ref[rows:, :rows] = parts.astype(jnp.bfloat16)
    if rows < width:
        out_ref[rows:, rows:] = jnp.zeros((EXTRA, width - rows), jnp.bfloat16)


def prepare(activations, norm_gain):
    rows, width = activations.shape
    return pl.pallas_call(
        prepare_body,
        out_shape=jax.ShapeDtypeStruct((rows + EXTRA, width), jnp.bfloat16),
        compiler_params=pltpu.CompilerParams(vmem_limit_bytes=VMEM_LIMIT),
        name="prepare",
    )(activations, norm_gain)


def gate_up_body(codes, first, last, rows, main, features, me_ref, *refs):
    count = len(codes)
    blocks = refs[:count]
    gate_ref, up_ref, *rest = refs[count:]
    if not first:
        before = rest[:4]
        rest = rest[4:]
    if last:
        hidden_ref, *rest = rest
    accs = rest
    step = pl.program_id(0)

    for s in range(count):

        @pl.when(step == s)
        def _(s=s):
            x = blocks[s][:rows, :]
            gate, up = gate_ref[...], up_ref[...]
            mixed = jnp.concatenate([gate[:, main:], up[:, main:]], axis=1)
            values = [
                jnp.dot(x, weight, preferred_element_type=jnp.float32)
                for weight in (gate[:, :main], up[:, :main], mixed)
            ]
            squares = blocks[s][rows:, :].astype(jnp.float32)
            squares = jnp.sum(squares, axis=0, keepdims=True)
            values.append(jnp.broadcast_to(squares, accs[3].shape))
            if s:
                values = [acc[...] + value for acc, value in zip(accs, values)]
            elif not first:
                values = [old[...] + value for old, value in zip(before, values)]
            if not last or s < count - 1:
                for acc, value in zip(accs, values):
                    acc[...] = value
                return
            factor = lax.rsqrt(values[3][:1, :rows] / features + epsilon)
            factor = jnp.broadcast_to(factor, (128, rows)).T[:, :1]

            def act(g, u):
                g, u = g * factor, u * factor
                return (g / (1.0 + jnp.exp(-g)) * u).astype(jnp.bfloat16)

            gate, up, both, _ = values
            rem = both.shape[1] // 2
            hidden_ref[:, :main] = act(gate, up)
            hidden_ref[:, main:] = act(both[:, :rem], both[:, rem:])


def gate_up(me, blocks, codes, gate_weight, up_weight, acc, last):
    height, depth = blocks[0].shape
    count = len(blocks)
    rows = height - EXTRA
    features, ff = gate_weight.shape
    main = ff // 256 * 256 if ff % 256 else ff - 256
    rem = ff - main
    first = acc is None
    whole = lambda shape: pl.BlockSpec(shape, lambda s, me: (0, 0))
    weight = pl.BlockSpec((depth, ff), lambda s, me: (me[0] ^ pick(codes, s), 0))
    in_specs = [whole(b.shape) for b in blocks] + [weight, weight]
    args = [*blocks, gate_weight, up_weight]
    shapes = [(rows, main), (rows, main), (rows, 2 * rem), (8, depth)]
    if not first:
        in_specs += [whole(s) for s in shapes]
        args += list(acc)
    if last:
        out_shape = [jax.ShapeDtypeStruct((rows, ff), jnp.bfloat16)]
        out_specs = [whole((rows, ff))]
        scratch = [pltpu.VMEM(s, jnp.float32) for s in shapes]
    else:
        out_shape = [jax.ShapeDtypeStruct(s, jnp.float32) for s in shapes]
        out_specs = [whole(s) for s in shapes]
        scratch = []
    return pl.pallas_call(
        functools.partial(gate_up_body, codes, first, last, rows, main, features),
        grid_spec=pltpu.PrefetchScalarGridSpec(
            num_scalar_prefetch=1,
            grid=(count,),
            in_specs=in_specs,
            out_specs=out_specs,
            scratch_shapes=scratch,
        ),
        out_shape=out_shape,
        compiler_params=pltpu.CompilerParams(vmem_limit_bytes=VMEM_LIMIT),
        cost_estimate=pl.CostEstimate(
            flops=4 * rows * depth * count * ff // 8,
            bytes_accessed=4 * depth * count * ff // 8,
            transcendentals=0,
        ),
        name="gate_up",
    )(me, *args)


def down_block(hidden_ref, weight_ref):
    ff = hidden_ref.shape[1]
    main = ff // 256 * 256
    value = jnp.dot(
        hidden_ref[:, :main], weight_ref[:main, :], preferred_element_type=jnp.float32
    )
    if main < ff:
        value = value + jnp.dot(
            hidden_ref[:, main:], weight_ref[main:, :], preferred_element_type=jnp.float32
        )
    return value


def down_body(jobs, me_ref, hidden_ref, weight_ref, *refs):
    outs = dict(zip(dict.fromkeys(kind for _, kind in jobs), refs[-len({kind for _, kind in jobs}) :]))
    step = pl.program_id(0)
    value = down_block(hidden_ref, weight_ref)
    place = 0
    for s, (_, kind) in enumerate(jobs):

        @pl.when(step == s)
        def _(s=s, kind=kind, place=place):
            if kind == "sent":
                outs[kind][place] = value.astype(jnp.bfloat16)
            elif kind == "far":
                outs[kind][...] = (value + refs[0][0].astype(jnp.float32)).astype(jnp.bfloat16)
            else:
                outs[kind][...] = value + refs[0][1].astype(jnp.float32)

        place += kind == "sent"


def down(me, jobs, hidden, down_weight, width, got):
    rows, ff = hidden.shape
    codes = [code for code, _ in jobs]
    whole = lambda shape: pl.BlockSpec(shape, lambda s, me: (0,) * len(shape))
    kinds = [kind for _, kind in jobs]
    shapes = {
        "far": ((rows, width), jnp.bfloat16),
        "near": ((rows, width), jnp.float32),
        "sent": ((kinds.count("sent"), rows, width), jnp.bfloat16),
    }
    shapes = [shapes[kind] for kind in dict.fromkeys(kinds)]
    extra = [] if got is None else [got]
    return pl.pallas_call(
        functools.partial(down_body, jobs),
        grid_spec=pltpu.PrefetchScalarGridSpec(
            num_scalar_prefetch=1,
            grid=(len(jobs),),
            in_specs=[
                whole(hidden.shape),
                pl.BlockSpec((ff, width), lambda s, me: (0, me[0] ^ pick(codes, s))),
            ]
            + [whole(x.shape) for x in extra],
            out_specs=[whole(shape) for shape, _ in shapes],
        ),
        out_shape=[jax.ShapeDtypeStruct(*shape) for shape in shapes],
        compiler_params=pltpu.CompilerParams(vmem_limit_bytes=VMEM_LIMIT),
        cost_estimate=pl.CostEstimate(
            flops=2 * rows * ff * width * len(jobs) // 8,
            bytes_accessed=2 * ff * width * len(jobs) // 8,
            transcendentals=0,
        ),
        name="down",
    )(me, hidden, down_weight, *extra)


def after(x, *others):
    return lax.optimization_barrier((x, *others))[0]


def overlapped(activations, norm_gain, gate_weight, up_weight, down_weight):
    width = activations.shape[1]
    index = lax.axis_index("gx").astype(jnp.int32)
    me = index[None]
    z = index // INNER
    edge = (z == 0) | (z == LINE - 1)
    resident = activations.astype(jnp.float32)

    def multiply(acc, *blocks):
        x, codes = zip(*blocks)
        return gate_up(me, x, codes, gate_weight, up_weight, acc, len(blocks) == 2 and codes[0] == 14)

    own = prepare(activations, norm_gain)
    one = along(own, PAIRS)
    inner = along(own, MIDDLE)
    own_y = swap(own, 2)
    own_c = swap(own, 1)
    acc = multiply(None, (own, 0), (own_c, 1))
    one, inner = after((one, inner), acc[0])
    two_edge = along(inner, OUTWARD)
    two_middle = along(one, MIDDLE)
    one_y = swap(one, 2)
    one_c = swap(one, 1)
    own_yc = swap(own_y, 1)
    acc = multiply(acc, (own_y, 2), (own_yc, 3), (one, 4), (one_c, 5))
    two_edge, two_middle = after((two_edge, two_middle), acc[0])
    two = jnp.where(edge, two_edge, two_middle)
    three_edge = along(two_middle, OUTWARD)
    two_y = swap(two, 2)
    two_c = swap(two, 1)
    one_yc = swap(one_y, 1)
    acc = multiply(acc, (one_y, 6), (one_yc, 7), (two, 8), (two_c, 9))
    three_edge = after(three_edge, acc[0])
    three = jnp.where(edge, three_edge, inner)
    three_y = swap(three, 2)
    three_c = swap(three, 1)
    two_yc = swap(two_y, 1)
    acc = multiply(acc, (two_y, 10), (two_yc, 11), (three, 12), (three_c, 13))
    three_y = after(three_y, acc[0])
    hidden = multiply(acc, (three_y, 14), (swap(three_y, 1), 15))[0]

    narrow = lambda x: x.astype(jnp.bfloat16)
    wide = lambda x: x.astype(jnp.float32)

    def blocks(hidden, stay, away, got=None):
        jobs = []
        if stay is not None:
            jobs += [(INNER * stay + 2, "far"), (INNER * stay, "near")]
        for k in away:
            jobs += [(INNER * k + 3, "sent"), (INNER * k + 1, "sent")]
        return down(me, jobs, hidden, down_weight, width, got)

    sent = blocks(hidden, None, (3, 2))[0]
    got_three, got_two = swap(sent[:2], 1), swap(sent[2:], 1)
    far, near_three = blocks(hidden, 3, (), got_three)
    far_three = swap(far, 2)
    far, near_two, sent = blocks(after(hidden, far), 2, (1,), got_two)
    got_one = swap(sent, 1)
    far_two = swap(far, 2)
    three = near_three + wide(far_three)
    three_sent = along(narrow(three), INWARD)
    far, near_one, sent = blocks(after(hidden, far), 1, (0,), got_one)
    got_own = swap(sent, 1)
    far_one = swap(far, 2)
    two = near_two + wide(far_two)
    two_sent = along(narrow(two), INWARD)
    two = two + wide(three_sent)
    two_passed = along(narrow(two), MIDDLE)
    far, near_own = blocks(after(hidden, far), 0, (), got_own)
    far_own = swap(far, 2)
    one = near_one + wide(after(far_one, far)) + wide(two_passed)
    three = three + wide(after(two_sent, far))
    branch = (
        near_own
        + wide(far_own)
        + wide(along(narrow(one), PAIRS))
        + wide(along(narrow(three), MIDDLE))
    )
    return (resident + branch).astype(jnp.bfloat16)


def plain(activations, norm_gain, gate_weight, up_weight, down_weight):
    resident = activations.astype(jnp.float32)
    totals = lax.psum(jnp.sum(resident * resident, axis=1), "gx")
    factor = lax.rsqrt(totals / (resident.shape[1] * lax.axis_size("gx")) + epsilon)
    normed = (resident * factor[:, None] * norm_gain.astype(jnp.float32)[None, :]).astype(
        jnp.bfloat16
    )
    pieces = lax.all_gather(normed, "gx", axis=1, tiled=True)
    gate_sum = jnp.dot(pieces, gate_weight, preferred_element_type=jnp.float32)
    up_sum = jnp.dot(pieces, up_weight, preferred_element_type=jnp.float32)
    hidden = (jax.nn.silu(gate_sum) * up_sum).astype(jnp.bfloat16)
    summed = lax.psum_scatter(
        lax.dot_general(
            down_weight, hidden, (((0,), (1,)), ((), ())), preferred_element_type=jnp.float32
        ),
        "gx",
        scatter_dimension=0,
        tiled=True,
    )
    return (resident + summed.T).astype(jnp.bfloat16)


def per_device(n, activations, norm_gain, gate_weight, up_weight, down_weight):
    args = (activations, norm_gain, gate_weight, up_weight, down_weight)
    rows, width = activations.shape
    tiled = rows % 128 == 0 and width % 128 == 0 and gate_weight.shape[1] % 128 == 0
    tiled = tiled and rows <= width
    if n == INNER * LINE and tiled:
        return overlapped(*args)
    return plain(*args)


def solution(mesh):
    in_specs = (P("groups", "gx"), P("gx"), P(None, "gx"), P(None, "gx"), P("gx", None))
    out_specs = P("groups", "gx")
    return jax.shard_map(
        functools.partial(per_device, mesh.shape["gx"]),
        mesh=mesh,
        in_specs=in_specs,
        out_specs=out_specs,
        check_vma=False,
    )
```

time: 255 us -> 134 us (0.53)
  waiting for transfers between devices: 127 us -> 25.3 us
  starting transfers between devices: 17.2 us -> 33.5 us
  local copies, waits for them, and re-layouts: 23.6 us -> 8.35 us
  between operations: 13.7 us -> 0.31 us
  other arithmetic: 6.87 us -> 2.75 us
  Pallas kernels: 66 us -> 62 us
    reduce_scatter x4 -> x0, waiting for transfers between devices: 80.6 us -> none  [overlapped(): sums[k] = lax.psum_scatter(partial, 'gx', axis_index_groups=teams)]
    ppermute x10, waiting for transfers between devices: 45.8 us -> 11.6 us  [along(): return lax.ppermute(x, 'gx', moves)]
    unnamed x34 -> x18, local copies, waits for them, and re-layouts: 23 us -> 8.24 us
    ppermute x0 -> x20, waiting for transfers between devices: none -> 13.7 us  [swap(): return lax.ppermute(x, 'gx', [(i, i ^ mask) for i in range(INNER * LINE)])]
    ppermute x0 -> x20, starting transfers between devices: none -> 11.5 us  [swap(): return lax.ppermute(x, 'gx', [(i, i ^ mask) for i in range(INNER * LINE)])]
    ppermute x10, starting transfers between devices: 16.8 us -> 22.1 us  [along(): return lax.ppermute(x, 'gx', moves)]
    pallas_call x8 -> x10, Pallas kernels: 65 us -> 61.8 us  [the longest x5 37.4 us: gate_up(): pl.pallas_call(functools.partial(gate_up_body, codes, first, last, rows,...]
    convert_element_type x3 -> x4, other arithmetic: 3.29 us -> 0.64 us  [overlapped(): narrow = lambda x: x.astype(jnp.bfloat16)]
  transfers between devices with their start and end apart: 18 -> 30, of which waited for: 8 -> 13; matrix products, arithmetic and copies ran while one was open for 2% -> 1% of each run, Pallas kernels for 19% -> 38%
where the time goes in v5:
time: 134 us; the launch traced here: 132 us
  Pallas kernels  62 us (46%)
  starting transfers between devices  33.5 us (25%)
  waiting for transfers between devices  25.3 us (19%)
  local copies, waits for them, and re-layouts  8.35 us (6%)
  other arithmetic  2.75 us (2%)
    pallas_call x5, Pallas kernels, gate_up(): pl.pallas_call(functools.partial(gate_up_body, codes, first, last, rows,...  37.4 us
    pallas_call x5, Pallas kernels, down(): pl.pallas_call(functools.partial(down_body, jobs), grid_spec=pltpu.Prefet...  24.4 us
    ppermute x10, starting transfers between devices, along(): return lax.ppermute(x, 'gx', moves)  22.1 us
    ppermute x20, waiting for transfers between devices, swap(): return lax.ppermute(x, 'gx', [(i, i ^ mask) for i in range(INNER * LINE)])  13.7 us
    ppermute x10, waiting for transfers between devices, along(): return lax.ppermute(x, 'gx', moves)  11.6 us
    ppermute x20, starting transfers between devices, swap(): return lax.ppermute(x, 'gx', [(i, i ^ mask) for i in range(INNER * LINE)])  11.5 us
    unnamed x18, local copies, waits for them, and re-layouts  8.24 us
  transfers between devices with their start and end apart: 30, of which 13 were waited for; matrix products, arithmetic and copies ran while one was open for 1% of the time, Pallas kernels for 38%

profile of v5, /device:TPU:0, one launch (start us, length us, event | category | flops | bytes accessed | tf_op | source)
XLA Modules:
  0.0 132.3 jit_solution(884399242979427782)
XLA Ops:
  2.4 2.6 %collective-permute-start = (bf16[400,512]{1,0:T(8,128)(2,1)S(1)}, bf16[400,512]{1,0:T(8,128)(2,1)S(1)}, u32[]{:S(2)}, u32[]{:S(2)}) collective-permute-start(bf16[400,512]{1,0:T(8,128)(2,1)S(1)} %prepare.1.refs_0_), channel_id=1, source_target_pairs={{0,4},{1,5},{2,6},{3,7},{4,0},{5,1},{6,2},{7,3},{8,12},{9,13},{10,... | collective-permute-start | bytes 1228808 | tf_op jit(solution)/shard_map/ppermute | solution.py:28
  9.8 5.1 %gate_up.5 = (f32[384,1536]{1,0:T(8,128)S(1)}, f32[384,1536]{1,0:T(8,128)S(1)}, f32[384,256]{1,0:T(8,128)S(1)}, f32[8,512]{1,0:T(8,128)S(1)}) custom-call(s32[1]{0:T(128)} %bitcast.me_ref, bf16[400,512]{1,0:T(8,128)(2,1)S(1)} %prepare.1.refs_0_, bf16[400,512]{1,0:T(8,128)(2,1)S(1)} %copy-done.5, bf16[8192,1664]{1,0:T(8,128)(2,1)} %refs_2_.3, ...), custom_call_target="tpu_custom_call" | custom-call | flops 327155712 | bytes 851968 | tf_op jit(solution)/shard_map/gate_up/pallas_call | solution.py:136
  20.8 1.6 %collective-permute-start.9 = (bf16[400,512]{1,0:T(8,128)(2,1)S(1)}, bf16[400,512]{1,0:T(8,128)(2,1)S(1)}, u32[]{:S(2)}, u32[]{:S(2)}) collective-permute-start(bf16[400,512]{1,0:T(8,128)(2,1)S(1)} %collective-permute-done.refs_2_), channel_id=1, source_target_pairs={{0,2},{1,3},{2,0},{3,1},{4,6},{5,7},{6,4},{7,5},{8,10},{9,11},{10,... | collective-permute-start | bytes 1228808 | tf_op jit(solution)/shard_map/ppermute | solution.py:23
  22.4 1.7 %copy-done.1 = f32[384,1536]{1,0:T(8,128)S(1)} copy-done((f32[384,1536]{1,0:T(8,128)S(1)}, f32[384,1536]{1,0:T(8,128)}, u32[]{:S(2)}) %copy-start.1) | copy-done | bytes 2359320
  25.1 9.2 %gate_up.6 = (f32[384,1536]{1,0:T(8,128)S(1)}, f32[384,1536]{1,0:T(8,128)S(1)}, f32[384,256]{1,0:T(8,128)S(1)}, f32[8,512]{1,0:T(8,128)S(1)}) custom-call(s32[1]{0:T(128)} %bitcast.me_ref, bf16[400,512]{1,0:T(8,128)(2,1)} %collective-permute-done.5.refs_0_, bf16[400,512]{1,0:T(8,128)(2,1)} %collective-permute-done.6.refs_1_, ...), custom_call_target="tpu_custom_call" | custom-call | flops 654311424 | bytes 1703936 | tf_op jit(solution)/shard_map/gate_up/pallas_call | solution.py:136
  38.3 1.6 %collective-permute-start.13 = (bf16[400,512]{1,0:T(8,128)(2,1)S(1)}, bf16[400,512]{1,0:T(8,128)(2,1)S(1)}, u32[]{:S(2)}, u32[]{:S(2)}) collective-permute-start(bf16[400,512]{1,0:T(8,128)(2,1)S(1)} %broadcast_select_fusion.1.refs_2_), channel_id=1, source_target_pairs={{0,2},{1,3},{2,0},{3,1},{4,6},{5,7},{6,4},{7,5},{8,10},{9,11},{10,... | collective-permute-start | bytes 1228808 | tf_op jit(solution)/shard_map/ppermute | solution.py:23
  39.9 8.9 %gate_up.7 = (f32[384,1536]{1,0:T(8,128)S(1)}, f32[384,1536]{1,0:T(8,128)S(1)}, f32[384,256]{1,0:T(8,128)S(1)}, f32[8,512]{1,0:T(8,128)S(1)}) custom-call(s32[1]{0:T(128)} %bitcast.me_ref, bf16[400,512]{1,0:T(8,128)(2,1)S(1)} %collective-permute-done.9.refs_0_, bf16[400,512]{1,0:T(8,128)(2,1)S(1)} %collective-permute-done.10.refs_1_, ...), custom_call_target="tpu_custom_call" | custom-call | flops 654311424 | bytes 1703936 | tf_op jit(solution)/shard_map/gate_up/pallas_call | solution.py:136
  48.8 3.7 %collective-permute-done.8 = bf16[400,512]{1,0:T(8,128)(2,1)S(1)} collective-permute-done((bf16[400,512]{1,0:T(8,128)(2,1)}, bf16[400,512]{1,0:T(8,128)(2,1)S(1)}, u32[]{:S(2)}, u32[]{:S(2)}) %collective-permute-start.8) | collective-permute-done | bytes 409632 | tf_op jit(solution)/shard_map/ppermute | solution.py:28
  54.9 8.8 %gate_up.8 = (f32[384,1536]{1,0:T(8,128)S(1)}, f32[384,1536]{1,0:T(8,128)S(1)}, f32[384,256]{1,0:T(8,128)S(1)}, f32[8,512]{1,0:T(8,128)S(1)}) custom-call(s32[1]{0:T(128)} %bitcast.me_ref, bf16[400,512]{1,0:T(8,128)(2,1)S(1)} %collective-permute-done.13.refs_0_, bf16[400,512]{1,0:T(8,128)(2,1)S(1)} %collective-permute-done.14.refs_1_, ...), custom_call_target="tpu_custom_call" | custom-call | flops 654311424 | bytes 1703936 | tf_op jit(solution)/shard_map/gate_up/pallas_call | solution.py:136
  64.6 1.7 %collective-permute-done.16.refs_1_ = bf16[400,512]{1,0:T(8,128)(2,1)S(1)} collective-permute-done((bf16[400,512]{1,0:T(8,128)(2,1)S(1)}, bf16[400,512]{1,0:T(8,128)(2,1)S(1)}, u32[]{:S(2)}, u32[]{:S(2)}) %collective-permute-start.16) | collective-permute-done | bytes 409632 | tf_op jit(solution)/shard_map/ppermute | solution.py:23
  66.3 5.5 %gate_up.9.hidden_ref = bf16[384,1664]{1,0:T(8,128)(2,1)S(1)} custom-call(s32[1]{0:T(128)} %bitcast.me_ref, bf16[400,512]{1,0:T(8,128)(2,1)S(1)} %collective-permute-done.12.refs_0_, bf16[400,512]{1,0:T(8,128)(2,1)S(1)} %collective-permute-done.16.refs_1_, bf16[8192,1664]{1,0:T(8,128)(2,1)} %refs_2_.3, bf16[8192,1664]{1,0:T(8,128)(2,1)} %refs_3_.3, ...), custom_call_target="tpu_custom_call" | custom-call | flops 327155712 | bytes 851968 | tf_op jit(solution)/shard_map/gate_up/pallas_call | solution.py:136
  71.8 5.8 %down.5 = bf16[4,384,512]{2,1,0:T(8,128)(2,1)S(1)} custom-call(s32[1]{0:T(128)} %bitcast.me_ref, bf16[384,1664]{1,0:T(8,128)(2,1)S(1)} %gate_up.9.hidden_ref, bf16[1664,8192]{1,0:T(8,128)(2,1)} %weight_ref.9), custom_call_target="tpu_custom_call" | custom-call | flops 327155712 | bytes 851968 | tf_op jit(solution)/shard_map/down/pallas_call | solution.py:200
  78.3 1.8 %collective-permute-done.17.refs_0_ = bf16[2,384,512]{2,1,0:T(8,128)(2,1)S(1)} collective-permute-done((bf16[2,384,512]{2,1,0:T(8,128)(2,1)S(1)}, bf16[2,384,512]{2,1,0:T(8,128)(2,1)S(1)}, u32[]{:S(2)}, u32[]{:S(2)}) %collective-permute-start.17) | collective-permute-done | bytes 786464 | tf_op jit(solution)/shard_map/ppermute | solution.py:23
  80.1 3.4 %down.6 = (bf16[384,512]{1,0:T(8,128)(2,1)S(1)}, f32[384,512]{1,0:T(8,128)S(1)}) custom-call(s32[1]{0:T(128)} %bitcast.me_ref, bf16[384,1664]{1,0:T(8,128)(2,1)S(1)} %gate_up.9.hidden_ref, bf16[1664,8192]{1,0:T(8,128)(2,1)} %weight_ref.9, bf16[2,384,512]{2,1,0:T(8,128)(2,1)S(1)} %collective-permute-done.17.refs_0_), custom_call_target="tpu_custom_call" | custom-call | flops 163577856 | bytes 425984 | tf_op jit(solution)/shard_map/down/pallas_call | solution.py:200
  84.0 5.9 %down.7 = (bf16[384,512]{1,0:T(8,128)(2,1)S(1)}, f32[384,512]{1,0:T(8,128)S(1)}, bf16[2,384,512]{2,1,0:T(8,128)(2,1)S(1)}) custom-call(s32[1]{0:T(128)} %bitcast.me_ref, bf16[384,1664]{1,0:T(8,128)(2,1)S(1)} %gate_up.9.hidden_ref, bf16[1664,8192]{1,0:T(8,128)(2,1)} %weight_ref.9, bf16[2,384,512]{2,1,0:T(8,128)(2,1)S(1)} %collective-permute-done.18.refs_0_), custom_call_target="tpu_custom_call" | custom-call | flops 327155712 | bytes 851968 | tf_op jit(solution)/shard_map/down/pallas_call | solution.py:200
  91.6 3.9 %collective-permute-done.24 = bf16[384,512]{1,0:T(8,128)(2,1)S(1)} collective-permute-done((bf16[384,512]{1,0:T(8,128)(2,1)S(1)}, bf16[384,512]{1,0:T(8,128)(2,1)S(1)}, u32[]{:S(2)}, u32[]{:S(2)}) %collective-permute-start.24) | collective-permute-done | bytes 393248 | tf_op jit(solution)/shard_map/ppermute | solution.py:23
  95.6 3.5 %collective-permute-start.25 = (bf16[384,512]{1,0:T(8,128)(2,1)S(1)}, bf16[384,512]{1,0:T(8,128)(2,1)S(1)}, u32[]{:S(2)}, u32[]{:S(2)}) collective-permute-start(bf16[384,512]{1,0:T(8,128)(2,1)S(1)} %fusion.1), channel_id=1, source_target_pairs={{0,4},{1,5},{2,6},{3,7},{12,8},{13,9},{14,10},{15,11},{16,20},{17,... | collective-permute-start | bytes 1179656 | tf_op jit(solution)/shard_map/ppermute | solution.py:28
  99.2 5.9 %down.8 = (bf16[384,512]{1,0:T(8,128)(2,1)S(1)}, f32[384,512]{1,0:T(8,128)S(1)}, bf16[2,384,512]{2,1,0:T(8,128)(2,1)S(1)}) custom-call(s32[1]{0:T(128)} %bitcast.me_ref, bf16[384,1664]{1,0:T(8,128)(2,1)S(1)} %gate_up.9.hidden_ref, bf16[1664,8192]{1,0:T(8,128)(2,1)} %weight_ref.9, bf16[2,384,512]{2,1,0:T(8,128)(2,1)S(1)} %collective-permute-done.19.refs_0_), custom_call_target="tpu_custom_call" | custom-call | flops 327155712 | bytes 851968 | tf_op jit(solution)/shard_map/down/pallas_call | solution.py:200
  107.1 7.0 %collective-permute-start.28 = (bf16[384,512]{1,0:T(8,128)(2,1)S(1)}, bf16[384,512]{1,0:T(8,128)(2,1)S(1)}, u32[]{:S(2)}, u32[]{:S(2)}) collective-permute-start(bf16[384,512]{1,0:T(8,128)(2,1)S(1)} %get-tuple-element.82), channel_id=1, source_target_pairs={{0,4},{1,5},{2,6},{3,7},{12,8},{13,9},{14,10},{15,11},{16,20},{17,... | collective-permute-start | bytes 1179656 | tf_op jit(solution)/shard_map/ppermute | solution.py:28
  114.0 3.4 %down.9 = (bf16[384,512]{1,0:T(8,128)(2,1)S(1)}, f32[384,512]{1,0:T(8,128)S(1)}) custom-call(s32[1]{0:T(128)} %bitcast.me_ref, bf16[384,1664]{1,0:T(8,128)(2,1)S(1)} %gate_up.9.hidden_ref, bf16[1664,8192]{1,0:T(8,128)(2,1)} %weight_ref.9, bf16[2,384,512]{2,1,0:T(8,128)(2,1)S(1)} %collective-permute-done.20.refs_0_), custom_call_target="tpu_custom_call" | custom-call | flops 163577856 | bytes 425984 | tf_op jit(solution)/shard_map/down/pallas_call | solution.py:200
  117.6 2.0 %collective-permute-start.27 = (bf16[384,512]{1,0:T(8,128)(2,1)S(1)}, bf16[384,512]{1,0:T(8,128)(2,1)S(1)}, u32[]{:S(2)}, u32[]{:S(2)}) collective-permute-start(bf16[384,512]{1,0:T(8,128)(2,1)S(1)} %add_convert_fusion.2), channel_id=1, source_target_pairs={{0,4},{1,5},{2,6},{3,7},{4,0},{5,1},{6,2},{7,3},{8,12},{9,13},{10,... | collective-permute-start | bytes 1179656 | tf_op jit(solution)/shard_map/ppermute | solution.py:28
  119.6 3.0 %collective-permute-done.28 = bf16[384,512]{1,0:T(8,128)(2,1)S(1)} collective-permute-done((bf16[384,512]{1,0:T(8,128)(2,1)S(1)}, bf16[384,512]{1,0:T(8,128)(2,1)S(1)}, u32[]{:S(2)}, u32[]{:S(2)}) %collective-permute-start.28) | collective-permute-done | bytes 393248 | tf_op jit(solution)/shard_map/ppermute | solution.py:28
  124.6 3.6 %collective-permute-done.27 = bf16[384,512]{1,0:T(8,128)(2,1)S(1)} collective-permute-done((bf16[384,512]{1,0:T(8,128)(2,1)S(1)}, bf16[384,512]{1,0:T(8,128)(2,1)S(1)}, u32[]{:S(2)}, u32[]{:S(2)}) %collective-permute-start.27) | collective-permute-done | bytes 393248 | tf_op jit(solution)/shard_map/ppermute | solution.py:28
  128.3 3.0 %collective-permute-done.21 = bf16[384,512]{1,0:T(8,128)(2,1)S(1)} collective-permute-done((bf16[384,512]{1,0:T(8,128)(2,1)S(1)}, bf16[384,512]{1,0:T(8,128)(2,1)S(1)}, u32[]{:S(2)}, u32[]{:S(2)}) %collective-permute-start.21) | collective-permute-done | bytes 393248 | tf_op jit(solution)/shard_map/ppermute | solution.py:23
  (73 shorter events, 29.5 us)
Async XLA Ops:
  1.9 6.1 %collective-permute-start.2 = (bf16[400,512]{1,0:T(8,128)(2,1)S(1)}, bf16[400,512]{1,0:T(8,128)(2,1)S(1)}, u32[]{:S(2)}, u32[]{:S(2)}) collective-permute-start(bf16[400,512]{1,0:T(8,128)(2,1)S(1)} %prepare.1.refs_0_), channel_id=1, source_target_pairs={{0,1},{1,0},{2,3},{3,2},{4,5},{5,4},{6,7},{7,6},{8,9},{9,8},{10,11... | collective-permute-start | bytes 1228808 | tf_op jit(solution)/shard_map/ppermute | solution.py:23
  2.4 14.6 %collective-permute-start = (bf16[400,512]{1,0:T(8,128)(2,1)S(1)}, bf16[400,512]{1,0:T(8,128)(2,1)S(1)}, u32[]{:S(2)}, u32[]{:S(2)}) collective-permute-start(bf16[400,512]{1,0:T(8,128)(2,1)S(1)} %prepare.1.refs_0_), channel_id=1, source_target_pairs={{0,4},{1,5},{2,6},{3,7},{4,0},{5,1},{6,2},{7,3},{8,12},{9,13},{10,... | collective-permute-start | bytes 1228808 | tf_op jit(solution)/shard_map/ppermute | solution.py:28
  5.1 11.9 %collective-permute-start.1 = (bf16[400,512]{1,0:T(8,128)(2,1)S(1)}, bf16[400,512]{1,0:T(8,128)(2,1)}, u32[]{:S(2)}, u32[]{:S(2)}) collective-permute-start(bf16[400,512]{1,0:T(8,128)(2,1)S(1)} %prepare.1.refs_0_), channel_id=1, source_target_pairs={{4,8},{5,9},{6,10},{7,11},{8,4},{9,5},{10,6},{11,7},{20,24},{21,25... | collective-permute-start | bytes 1228808 | tf_op jit(solution)/shard_map/ppermute | solution.py:28
  6.5 11.6 %collective-permute-start.5 = (bf16[400,512]{1,0:T(8,128)(2,1)S(1)}, bf16[400,512]{1,0:T(8,128)(2,1)}, u32[]{:S(2)}, u32[]{:S(2)}) collective-permute-start(bf16[400,512]{1,0:T(8,128)(2,1)S(1)} %prepare.1.refs_0_), channel_id=1, source_target_pairs={{0,2},{1,3},{2,0},{3,1},{4,6},{5,7},{6,4},{7,5},{8,10},{9,11},{10,... | collective-permute-start | bytes 1228808 | tf_op jit(solution)/shard_map/ppermute | solution.py:23
  17.0 5.4 %collective-permute-start.7 = (bf16[400,512]{1,0:T(8,128)(2,1)S(1)}, bf16[400,512]{1,0:T(8,128)(2,1)}, u32[]{:S(2)}, u32[]{:S(2)}) collective-permute-start(bf16[400,512]{1,0:T(8,128)(2,1)S(1)} %collective-permute-done.refs_2_), channel_id=1, source_target_pairs={{0,1},{1,0},{2,3},{3,2},{4,5},{5,4},{6,7},{7,6},{8,9},{9,8},{10,11... | collective-permute-start | bytes 1228808 | tf_op jit(solution)/shard_map/ppermute | solution.py:23
  18.1 4.3 %collective-permute-start.6 = (bf16[400,512]{1,0:T(8,128)(2,1)}, bf16[400,512]{1,0:T(8,128)(2,1)}, u32[]{:S(2)}, u32[]{:S(2)}) collective-permute-start(bf16[400,512]{1,0:T(8,128)(2,1)} %collective-permute-done.5.refs_0_), channel_id=1, source_target_pairs={{0,1},{1,0},{2,3},{3,2},{4,5},{5,4},{6,7},{7,6},{8,9},{9,8},{10,11... | collective-permute-start | bytes 1228808 | tf_op jit(solution)/shard_map/ppermute | solution.py:23
  18.1 16.2 %collective-permute-start.4 = (bf16[400,512]{1,0:T(8,128)(2,1)S(1)}, bf16[400,512]{1,0:T(8,128)(2,1)}, u32[]{:S(2)}, u32[]{:S(2)}) collective-permute-start(bf16[400,512]{1,0:T(8,128)(2,1)S(1)} %collective-permute-done.refs_2_), channel_id=1, source_target_pairs={{4,8},{5,9},{6,10},{7,11},{8,4},{9,5},{10,6},{11,7},{20,24},{21,25... | collective-permute-start | bytes 1228808 | tf_op jit(solution)/shard_map/ppermute | solution.py:28
  19.6 15.7 %collective-permute-start.3 = (bf16[400,512]{1,0:T(8,128)(2,1)}, bf16[400,512]{1,0:T(8,128)(2,1)}, u32[]{:S(2)}, u32[]{:S(2)}) collective-permute-start(bf16[400,512]{1,0:T(8,128)(2,1)} %collective-permute-done.1), channel_id=1, source_target_pairs={{4,0},{5,1},{6,2},{7,3},{8,12},{9,13},{10,14},{11,15},{20,16},{21,... | collective-permute-start | bytes 1228808 | tf_op jit(solution)/shard_map/ppermute | solution.py:28
  20.8 15.5 %collective-permute-start.9 = (bf16[400,512]{1,0:T(8,128)(2,1)S(1)}, bf16[400,512]{1,0:T(8,128)(2,1)S(1)}, u32[]{:S(2)}, u32[]{:S(2)}) collective-permute-start(bf16[400,512]{1,0:T(8,128)(2,1)S(1)} %collective-permute-done.refs_2_), channel_id=1, source_target_pairs={{0,2},{1,3},{2,0},{3,1},{4,6},{5,7},{6,4},{7,5},{8,10},{9,11},{10,... | collective-permute-start | bytes 1228808 | tf_op jit(solution)/shard_map/ppermute | solution.py:23
  36.8 15.6 %collective-permute-start.8 = (bf16[400,512]{1,0:T(8,128)(2,1)}, bf16[400,512]{1,0:T(8,128)(2,1)S(1)}, u32[]{:S(2)}, u32[]{:S(2)}) collective-permute-start(bf16[400,512]{1,0:T(8,128)(2,1)} %collective-permute-done.4), channel_id=1, source_target_pairs={{4,0},{5,1},{6,2},{7,3},{8,12},{9,13},{10,14},{11,15},{20,16},{21,... | collective-permute-start | bytes 1228808 | tf_op jit(solution)/shard_map/ppermute | solution.py:28
  38.3 14.3 %collective-permute-start.13 = (bf16[400,512]{1,0:T(8,128)(2,1)S(1)}, bf16[400,512]{1,0:T(8,128)(2,1)S(1)}, u32[]{:S(2)}, u32[]{:S(2)}) collective-permute-start(bf16[400,512]{1,0:T(8,128)(2,1)S(1)} %broadcast_select_fusion.1.refs_2_), channel_id=1, source_target_pairs={{0,2},{1,3},{2,0},{3,1},{4,6},{5,7},{6,4},{7,5},{8,10},{9,11},{10,... | collective-permute-start | bytes 1228808 | tf_op jit(solution)/shard_map/ppermute | solution.py:23
  53.1 11.5 %collective-permute-start.12 = (bf16[400,512]{1,0:T(8,128)(2,1)S(1)}, bf16[400,512]{1,0:T(8,128)(2,1)S(1)}, u32[]{:S(2)}, u32[]{:S(2)}) collective-permute-start(bf16[400,512]{1,0:T(8,128)(2,1)S(1)} %broadcast_select_fusion.refs_2_), channel_id=1, source_target_pairs={{0,2},{1,3},{2,0},{3,1},{4,6},{5,7},{6,4},{7,5},{8,10},{9,11},{10,... | collective-permute-start | bytes 1228808 | tf_op jit(solution)/shard_map/ppermute | solution.py:23
  77.9 6.1 %collective-permute-start.18 = (bf16[2,384,512]{2,1,0:T(8,128)(2,1)S(1)}, bf16[2,384,512]{2,1,0:T(8,128)(2,1)S(1)}, u32[]{:S(2)}, u32[]{:S(2)}) collective-permute-start(bf16[2,384,512]{2,1,0:T(8,128)(2,1)S(1)} %get-tuple-element.79), channel_id=1, source_target_pairs={{0,1},{1,0},{2,3},{3,2},{4,5},{5,4},{6,7},{7,6},{8,9},{9,8},{10,11... | collective-permute-start | bytes 2359304 | tf_op jit(solution)/shard_map/ppermute | solution.py:23
  83.5 12.0 %collective-permute-start.24 = (bf16[384,512]{1,0:T(8,128)(2,1)S(1)}, bf16[384,512]{1,0:T(8,128)(2,1)S(1)}, u32[]{:S(2)}, u32[]{:S(2)}) collective-permute-start(bf16[384,512]{1,0:T(8,128)(2,1)S(1)} %get-tuple-element.64), channel_id=1, source_target_pairs={{0,2},{1,3},{2,0},{3,1},{4,6},{5,7},{6,4},{7,5},{8,10},{9,11},{10,... | collective-permute-start | bytes 1179656 | tf_op jit(solution)/shard_map/ppermute | solution.py:23
  89.9 9.2 %collective-permute-start.19 = (bf16[2,384,512]{2,1,0:T(8,128)(2,1)S(1)}, bf16[2,384,512]{2,1,0:T(8,128)(2,1)S(1)}, u32[]{:S(2)}, u32[]{:S(2)}) collective-permute-start(bf16[2,384,512]{2,1,0:T(8,128)(2,1)S(1)} %get-tuple-element.68), channel_id=1, source_target_pairs={{0,1},{1,0},{2,3},{3,2},{4,5},{5,4},{6,7},{7,6},{8,9},{9,8},{10,11... | collective-permute-start | bytes 2359304 | tf_op jit(solution)/shard_map/ppermute | solution.py:23
  90.0 15.8 %collective-permute-start.23 = (bf16[384,512]{1,0:T(8,128)(2,1)S(1)}, bf16[384,512]{1,0:T(8,128)(2,1)S(1)}, u32[]{:S(2)}, u32[]{:S(2)}) collective-permute-start(bf16[384,512]{1,0:T(8,128)(2,1)S(1)} %get-tuple-element.66), channel_id=1, source_target_pairs={{0,2},{1,3},{2,0},{3,1},{4,6},{5,7},{6,4},{7,5},{8,10},{9,11},{10,... | collective-permute-start | bytes 1179656 | tf_op jit(solution)/shard_map/ppermute | solution.py:23
  95.6 10.6 %collective-permute-start.25 = (bf16[384,512]{1,0:T(8,128)(2,1)S(1)}, bf16[384,512]{1,0:T(8,128)(2,1)S(1)}, u32[]{:S(2)}, u32[]{:S(2)}) collective-permute-start(bf16[384,512]{1,0:T(8,128)(2,1)S(1)} %fusion.1), channel_id=1, source_target_pairs={{0,4},{1,5},{2,6},{3,7},{12,8},{13,9},{14,10},{15,11},{16,20},{17,... | collective-permute-start | bytes 1179656 | tf_op jit(solution)/shard_map/ppermute | solution.py:28
  105.1 8.9 %collective-permute-start.20 = (bf16[2,384,512]{2,1,0:T(8,128)(2,1)S(1)}, bf16[2,384,512]{2,1,0:T(8,128)(2,1)S(1)}, u32[]{:S(2)}, u32[]{:S(2)}) collective-permute-start(bf16[2,384,512]{2,1,0:T(8,128)(2,1)S(1)} %get-tuple-element.71), channel_id=1, source_target_pairs={{0,1},{1,0},{2,3},{3,2},{4,5},{5,4},{6,7},{7,6},{8,9},{9,8},{10,11... | collective-permute-start | bytes 2359304 | tf_op jit(solution)/shard_map/ppermute | solution.py:23
  105.2 12.3 %collective-permute-start.22 = (bf16[384,512]{1,0:T(8,128)(2,1)S(1)}, bf16[384,512]{1,0:T(8,128)(2,1)S(1)}, u32[]{:S(2)}, u32[]{:S(2)}) collective-permute-start(bf16[384,512]{1,0:T(8,128)(2,1)S(1)} %get-tuple-element.69), channel_id=1, source_target_pairs={{0,2},{1,3},{2,0},{3,1},{4,6},{5,7},{6,4},{7,5},{8,10},{9,11},{10,... | collective-permute-start | bytes 1179656 | tf_op jit(solution)/shard_map/ppermute | solution.py:23
  106.4 11.1 %collective-permute-start.26 = (bf16[384,512]{1,0:T(8,128)(2,1)S(1)}, bf16[384,512]{1,0:T(8,128)(2,1)S(1)}, u32[]{:S(2)}, u32[]{:S(2)}) collective-permute-start(bf16[384,512]{1,0:T(8,128)(2,1)S(1)} %get-tuple-element.81), channel_id=1, source_target_pairs={{4,8},{5,9},{6,10},{7,11},{8,4},{9,5},{10,6},{11,7},{20,24},{21,25... | collective-permute-start | bytes 1179656 | tf_op jit(solution)/shard_map/ppermute | solution.py:28
  107.1 15.5 %collective-permute-start.28 = (bf16[384,512]{1,0:T(8,128)(2,1)S(1)}, bf16[384,512]{1,0:T(8,128)(2,1)S(1)}, u32[]{:S(2)}, u32[]{:S(2)}) collective-permute-start(bf16[384,512]{1,0:T(8,128)(2,1)S(1)} %get-tuple-element.82), channel_id=1, source_target_pairs={{0,4},{1,5},{2,6},{3,7},{12,8},{13,9},{14,10},{15,11},{16,20},{17,... | collective-permute-start | bytes 1179656 | tf_op jit(solution)/shard_map/ppermute | solution.py:28
  117.6 10.6 %collective-permute-start.27 = (bf16[384,512]{1,0:T(8,128)(2,1)S(1)}, bf16[384,512]{1,0:T(8,128)(2,1)S(1)}, u32[]{:S(2)}, u32[]{:S(2)}) collective-permute-start(bf16[384,512]{1,0:T(8,128)(2,1)S(1)} %add_convert_fusion.2), channel_id=1, source_target_pairs={{0,4},{1,5},{2,6},{3,7},{4,0},{5,1},{6,2},{7,3},{8,12},{9,13},{10,... | collective-permute-start | bytes 1179656 | tf_op jit(solution)/shard_map/ppermute | solution.py:28
  122.7 5.5 %collective-permute-start.29 = (bf16[384,512]{1,0:T(8,128)(2,1)S(1)}, bf16[384,512]{1,0:T(8,128)(2,1)S(1)}, u32[]{:S(2)}, u32[]{:S(2)}) collective-permute-start(bf16[384,512]{1,0:T(8,128)(2,1)S(1)} %add_convert_fusion.1), channel_id=1, source_target_pairs={{4,8},{5,9},{6,10},{7,11},{8,4},{9,5},{10,6},{11,7},{20,24},{21,25... | collective-permute-start | bytes 1179656 | tf_op jit(solution)/shard_map/ppermute | solution.py:28
  123.4 7.8 %collective-permute-start.21 = (bf16[384,512]{1,0:T(8,128)(2,1)S(1)}, bf16[384,512]{1,0:T(8,128)(2,1)S(1)}, u32[]{:S(2)}, u32[]{:S(2)}) collective-permute-start(bf16[384,512]{1,0:T(8,128)(2,1)S(1)} %get-tuple-element.73), channel_id=1, source_target_pairs={{0,2},{1,3},{2,0},{3,1},{4,6},{5,7},{6,4},{7,5},{8,10},{9,11},{10,... | collective-permute-start | bytes 1179656 | tf_op jit(solution)/shard_map/ppermute | solution.py:23
  (15 other events, 37.5 us)

commit v6 on v4

v6 whole, which is shorter than its diff:
```python
import functools

import jax
import jax.numpy as jnp
import numpy as np
from jax import lax
from jax.experimental import pallas as pl
from jax.experimental.pallas import tpu as pltpu
from jax.sharding import PartitionSpec as P

epsilon = 1e-05
LINE = 4
EXTRA = 16
VMEM_LIMIT = 24 * 1024 * 1024

TAKEN = {
    (True, 0): (0, 2, 3, 6, 7),
    (True, 1): (0, 1, 4, 5, 7),
    (False, 0): (0, 2, 4, 1, 5),
    (False, 1): (0, 6, 3, 7, 5),
}


def device(z, y, core):
    return z * 4 + y * 2 + core


def step(number):
    moves = []
    for z in range(LINE):
        for y in range(2):
            along = (z ^ 1, y)
            across = (z, y ^ 1)
            inside = (z ^ 3, y) if 0 < z < LINE - 1 else across
            goals = {
                1: (along, inside),
                2: (inside, along),
                3: (along, across),
                4: (across,),
            }[number]
            moves += [(device(z, y, c), device(*goal, c)) for c, goal in enumerate(goals)]
    return moves


def send(x, number):
    return lax.ppermute(x, "gx", step(number))


def swap(x):
    return lax.ppermute(x, "gx", [(i, i ^ 1) for i in range(4 * LINE)])


def after(x, *others):
    return lax.optimization_barrier((x, *others))[0]


def prepare_body(x_ref, gain_ref, out_ref):
    rows, width = x_ref.shape
    x = x_ref[...].astype(jnp.float32)
    gain = gain_ref[...].astype(jnp.float32).reshape(1, width)
    out_ref[:rows, :] = (x * gain).astype(jnp.bfloat16)
    squares = jnp.broadcast_to(jnp.sum(x * x, axis=1, keepdims=True), (rows, 128)).T[:EXTRA]
    row = lax.broadcasted_iota(jnp.int32, (EXTRA, rows), 0)
    parts = jnp.zeros((EXTRA, rows), jnp.float32)
    for i in range(3):
        part = squares.astype(jnp.bfloat16).astype(jnp.float32)
        parts = jnp.where(row == i, part, parts)
        squares = squares - part
    out_ref[rows:, :rows] = parts.astype(jnp.bfloat16)
    if rows < width:
        out_ref[rows:, rows:] = jnp.zeros((EXTRA, width - rows), jnp.bfloat16)


def prepare(activations, norm_gain):
    rows, width = activations.shape
    return pl.pallas_call(
        prepare_body,
        out_shape=jax.ShapeDtypeStruct((rows + EXTRA, width), jnp.bfloat16),
        compiler_params=pltpu.CompilerParams(vmem_limit_bytes=VMEM_LIMIT),
        name="prepare",
    )(activations, norm_gain)


def gate_up_body(count, first, last, rows, main, features, order_ref, *refs):
    pairs = refs[:count]
    gate_ref, up_ref, *rest = refs[count:]
    if not first:
        before = rest[:4]
        rest = rest[4:]
    if last:
        hidden_ref, *rest = rest
    accs = rest
    now = pl.program_id(0)

    def products(x_ref):
        x = x_ref[0, :rows, :]
        gate, up = gate_ref[...], up_ref[...]
        mixed = jnp.concatenate([gate[:, main:], up[:, main:]], axis=1)
        values = [
            jnp.dot(x, weight, preferred_element_type=jnp.float32)
            for weight in (gate[:, :main], up[:, :main], mixed)
        ]
        squares = jnp.sum(x_ref[0, rows:, :].astype(jnp.float32), axis=0, keepdims=True)
        return values + [jnp.broadcast_to(squares, accs[3].shape)]

    for p, x_ref in enumerate(pairs):
        if not p:

            @pl.when(now == 0)
            def _():
                for i, value in enumerate(products(pairs[0])):
                    accs[i][...] = value if first else before[i][...] + value

        @pl.when((now >= max(2 * p, 1)) & (now < 2 * p + 2))
        def _(x_ref=x_ref):
            for acc, value in zip(accs, products(x_ref)):
                acc[...] += value

    if last:

        @pl.when(now == 2 * count - 1)
        def _():
            factor = lax.rsqrt(accs[3][:1, :rows] / features + epsilon)
            factor = jnp.broadcast_to(factor, (128, rows)).T[:, :1]

            def act(g, u):
                g, u = g * factor, u * factor
                return (g / (1.0 + jnp.exp(-g)) * u).astype(jnp.bfloat16)

            rem = accs[2].shape[1] // 2
            hidden_ref[:, :main] = act(accs[0][...], accs[1][...])
            hidden_ref[:, main:] = act(accs[2][:, :rem], accs[2][:, rem:])


def gate_up(order, places, pairs, gate_weight, up_weight, acc, last=False):
    height, depth = pairs[0].shape[1:]
    count = len(pairs)
    rows = height - EXTRA
    features, ff = gate_weight.shape
    main = ff // 256 * 256 if ff % 256 else ff - 256
    rem = ff - main
    first = acc is None
    whole = lambda shape: pl.BlockSpec(shape, lambda s, order: (0, 0))

    def shard(p):
        return pl.BlockSpec(
            (1, height, depth), lambda s, order: (jnp.clip(s - 2 * p, 0, 1), 0, 0)
        )

    def rows_of(s, order):
        place = jnp.int32(places[0])
        for p in range(1, count):
            place = jnp.where(s >= 2 * p, jnp.int32(places[p]), place)
        return (order[place] * 2 + s % 2, 0)

    weight = pl.BlockSpec((depth, ff), rows_of)
    in_specs = [shard(p) for p in range(count)] + [weight, weight]
    args = [*pairs, gate_weight, up_weight]
    shapes = [(rows, main), (rows, main), (rows, 2 * rem), (8, depth)]
    aliases = {}
    if not first:
        if not last:
            aliases = {1 + len(args) + i: i for i in range(4)}
        in_specs += [whole(s) for s in shapes]
        args += list(acc)
    if last:
        out_shape = [jax.ShapeDtypeStruct((rows, ff), jnp.bfloat16)]
        out_specs = [whole((rows, ff))]
        scratch = [pltpu.VMEM(s, jnp.float32) for s in shapes]
    else:
        out_shape = [jax.ShapeDtypeStruct(s, jnp.float32) for s in shapes]
        out_specs = [whole(s) for s in shapes]
        scratch = []
    return pl.pallas_call(
        functools.partial(gate_up_body, count, first, last, rows, main, features),
        grid_spec=pltpu.PrefetchScalarGridSpec(
            num_scalar_prefetch=1,
            grid=(2 * count,),
            in_specs=in_specs,
            out_specs=out_specs,
            scratch_shapes=scratch,
        ),
        out_shape=out_shape,
        input_output_aliases=aliases,
        compiler_params=pltpu.CompilerParams(vmem_limit_bytes=VMEM_LIMIT),
        cost_estimate=pl.CostEstimate(
            flops=rows * depth * count * ff,
            bytes_accessed=depth * count * ff,
            transcendentals=0,
        ),
        name="gate_up",
    )(order, *args)


def down_block(hidden_ref, weight_ref):
    ff = hidden_ref.shape[1]
    main = ff // 256 * 256
    value = jnp.dot(
        hidden_ref[:, :main], weight_ref[:main, :], preferred_element_type=jnp.float32
    )
    if main < ff:
        value = value + jnp.dot(
            hidden_ref[:, main:], weight_ref[main:, :], preferred_element_type=jnp.float32
        )
    return value


def down_body(kinds, order_ref, hidden_ref, weight_ref, *outs):
    now = pl.program_id(0)
    value = down_block(hidden_ref, weight_ref)
    for p, kind in enumerate(kinds):

        if kind == "kept":

            @pl.when(now // 2 == p)
            def _(kept=outs[p]):
                kept[now % 2] = value

        else:
            for half in range(2):

                @pl.when(now == 2 * p + half)
                def _(sent=outs[p + half]):
                    sent[...] = value.astype(sent.dtype)


def down(order, places, hidden, down_weight, width):
    rows, ff = hidden.shape
    count = len(places)
    specs = {
        "kept": [pl.BlockSpec((2, rows, width), lambda s, order: (0, 0, 0))],
        "sent": [pl.BlockSpec((rows, width), lambda s, order: (0, 0))] * 2,
    }
    specs = [(spec, kind) for kind in places for spec in specs[kind]]
    dtypes = {"sent": jnp.bfloat16, "kept": jnp.float32}

    def columns_of(s, order):
        place = jnp.int32(list(places.values())[0])
        for p, other in enumerate(places.values()):
            place = jnp.where(s >= 2 * p, jnp.int32(other), place)
        return (0, order[place] * 2 + s % 2)

    return pl.pallas_call(
        functools.partial(down_body, tuple(places)),
        grid_spec=pltpu.PrefetchScalarGridSpec(
            num_scalar_prefetch=1,
            grid=(2 * count,),
            in_specs=[
                pl.BlockSpec((rows, ff), lambda s, order: (0, 0)),
                pl.BlockSpec((ff, width), columns_of),
            ],
            out_specs=[spec for spec, _ in specs],
        ),
        out_shape=[
            jax.ShapeDtypeStruct(spec.block_shape, dtypes[kind]) for spec, kind in specs
        ],
        compiler_params=pltpu.CompilerParams(vmem_limit_bytes=VMEM_LIMIT),
        cost_estimate=pl.CostEstimate(
            flops=rows * ff * width * count // 4,
            bytes_accessed=ff * width * count // 4,
            transcendentals=0,
        ),
        name="down",
    )(order, hidden, down_weight)


def overlapped(activations, norm_gain, gate_weight, up_weight, down_weight):
    width = activations.shape[1]
    index = lax.axis_index("gx").astype(jnp.int32)
    core = index & 1
    z = index >> 2
    end = (z == 0) | (z == LINE - 1)
    middle_one = ~end & (core == 1)
    resident = activations.astype(jnp.float32)
    narrow = lambda x: x.astype(jnp.bfloat16)
    wide = lambda x: x.astype(jnp.float32)

    mine = [TAKEN[e, c] for e in (True, False) for c in (0, 1)]
    others = [TAKEN[e, 1 - c] for e in (True, False) for c in (0, 1)]
    codes = np.array(
        [(0, m[1], o[1], m[2], o[2], m[3], o[3], m[4]) for m, o in zip(mine, others)], np.int32
    )
    OWN, MINE, OTHER, LAST = 0, (None, 1, 3, 5), (None, 2, 4, 6), 7
    variant = jnp.where(end, 0, 2) + core
    order = (index >> 1) ^ lax.dynamic_slice(jnp.asarray(codes), (variant, 0), (1, 8))[0]

    multiply = functools.partial(gate_up, order)
    shard = prepare(activations, norm_gain)
    partner = swap(shard)
    own = jnp.stack([jnp.where(core == 0, shard, partner), jnp.where(core == 0, partner, shard)])
    one = send(own, 1)
    acc = multiply((OWN,), (own,), gate_weight, up_weight, None)
    one = after(one, acc[0])
    two = send(one, 2)
    one_other = swap(one)
    acc = multiply((MINE[1],), (one,), gate_weight, up_weight, acc)
    two = after(two, acc[0])
    three = send(jnp.where(middle_one, one, two), 3)
    two_other = swap(two)
    acc = multiply((OTHER[1], MINE[2]), (one_other, two), gate_weight, up_weight, acc)
    three = after(three, acc[0])
    four = send(jnp.where(end, three, two), 4)
    three_other = swap(three)
    acc = multiply((OTHER[2], MINE[3]), (two_other, three), gate_weight, up_weight, acc)
    four = after(four, acc[0])
    four_other = swap(four)
    acc = multiply((OTHER[3],), (three_other,), gate_weight, up_weight, acc)
    four = jnp.where(core == 0, four, after(four_other, acc[0]))
    hidden = multiply((LAST,), (four,), gate_weight, up_weight, acc, last=True)[0]

    def partial(hidden, place):
        places = {"kept": MINE[place], "sent": OTHER[place]}
        kept, *sent = down(order, places, hidden, down_weight, width)
        return kept, sent

    def add(kept, sent, *more):
        halves = [kept[i] + wide(swap(sent[i])) for i in range(2)]
        for x in more:
            halves = [half + x[i] for i, half in enumerate(halves)]
        return jnp.stack([narrow(half) for half in halves])

    zero = jnp.zeros((), jnp.float32)
    (kept,) = down(order, {"kept": LAST}, hidden, down_weight, width)
    total = add(kept, [narrow(kept[0]), narrow(kept[1])])
    four = wide(send(total, 4))
    kept, sent = partial(after(hidden, total), 3)
    total = add(kept, sent, jnp.where(end, four, zero))
    three = wide(send(total, 3))
    kept, sent = partial(after(hidden, total), 2)
    total = add(
        kept, sent, jnp.where(end, zero, four), jnp.where(middle_one, zero, three)
    )
    two = wide(send(total, 2))
    kept, sent = partial(after(hidden, total), 1)
    total = add(kept, sent, two, jnp.where(middle_one, three, zero))
    one = wide(send(total, 1))
    (kept,) = down(order, {"kept": OWN}, after(hidden, total), down_weight, width)
    total = kept + one
    first, second = total[0], total[1]
    got = swap(narrow(jnp.where(core == 0, second, first)))
    branch = jnp.where(core == 0, first, second) + wide(got)
    return (resident + branch).astype(jnp.bfloat16)


def plain(activations, norm_gain, gate_weight, up_weight, down_weight):
    resident = activations.astype(jnp.float32)
    totals = lax.psum(jnp.sum(resident * resident, axis=1), "gx")
    factor = lax.rsqrt(totals / (resident.shape[1] * lax.axis_size("gx")) + epsilon)
    normed = (resident * factor[:, None] * norm_gain.astype(jnp.float32)[None, :]).astype(
        jnp.bfloat16
    )
    pieces = lax.all_gather(normed, "gx", axis=1, tiled=True)
    gate_sum = jnp.dot(pieces, gate_weight, preferred_element_type=jnp.float32)
    up_sum = jnp.dot(pieces, up_weight, preferred_element_type=jnp.float32)
    hidden = (jax.nn.silu(gate_sum) * up_sum).astype(jnp.bfloat16)
    summed = lax.psum_scatter(
        lax.dot_general(
            down_weight, hidden, (((0,), (1,)), ((), ())), preferred_element_type=jnp.float32
        ),
        "gx",
        scatter_dimension=0,
        tiled=True,
    )
    return (resident + summed.T).astype(jnp.bfloat16)


def per_device(n, activations, norm_gain, gate_weight, up_weight, down_weight):
    args = (activations, norm_gain, gate_weight, up_weight, down_weight)
    rows, width = activations.shape
    tiled = rows % 128 == 0 and width % 128 == 0 and gate_weight.shape[1] % 128 == 0
    tiled = tiled and rows <= width
    if n == 4 * LINE and tiled:
        return overlapped(*args)
    return plain(*args)


def solution(mesh):
    in_specs = (P("groups", "gx"), P("gx"), P(None, "gx"), P(None, "gx"), P("gx", None))
    out_specs = P("groups", "gx")
    return jax.shard_map(
        functools.partial(per_device, mesh.shape["gx"]),
        mesh=mesh,
        in_specs=in_specs,
        out_specs=out_specs,
        check_vma=False,
    )
```

time: 255 us -> 145 us (0.57)
  waiting for transfers between devices: 127 us -> 33.1 us
  between operations: 13.7 us -> 0.37 us
  local copies, waits for them, and re-layouts: 23.6 us -> 13.6 us
  starting transfers between devices: 17.2 us -> 25.3 us
    reduce_scatter x4 -> x0, waiting for transfers between devices: 80.6 us -> none  [overlapped(): sums[k] = lax.psum_scatter(partial, 'gx', axis_index_groups=teams)]
    ppermute x10 -> x22, waiting for transfers between devices: 45.8 us -> 33.1 us  [the longest x8 28.2 us: send(): return lax.ppermute(x, 'gx', step(number))]
    unnamed x34 -> x12, local copies, waits for them, and re-layouts: 23 us -> 13.5 us
    ppermute x10 -> x22, starting transfers between devices: 16.8 us -> 25.3 us  [the longest x8 22.2 us: send(): return lax.ppermute(x, 'gx', step(number))]
    another operation x0 -> x10, other arithmetic: none -> 3.48 us  [the longest x8 2.46 us: add(): return jnp.stack([narrow(half) for half in halves])]
    convert_element_type x3 -> x1, other arithmetic: 3.29 us -> 0.07 us  [overlapped(): narrow = lambda x: x.astype(jnp.bfloat16)]
    pallas_call x8 -> x11, Pallas kernels: 65 us -> 64 us  [the longest x6 44 us: gate_up(): pl.pallas_call(functools.partial(gate_up_body, count, first, last, rows,...]
  transfers between devices with their start and end apart: 18 -> 22, of which waited for: 8 -> 12; matrix products, arithmetic and copies ran while one was open for 2% -> 2% of each run, Pallas kernels for 19% -> 38%
where the time goes in v6:
time: 145 us; the launch traced here: 144 us
  Pallas kernels  64.2 us (44%)
  waiting for transfers between devices  33.1 us (23%)
  starting transfers between devices  25.3 us (17%)
  local copies, waits for them, and re-layouts  13.6 us (9%)
  other arithmetic  7.74 us (5%)
    pallas_call x6, Pallas kernels, gate_up(): pl.pallas_call(functools.partial(gate_up_body, count, first, last, rows,...  44 us
    ppermute x8, waiting for transfers between devices, send(): return lax.ppermute(x, 'gx', step(number))  28.2 us
    ppermute x8, starting transfers between devices, send(): return lax.ppermute(x, 'gx', step(number))  22.2 us
    pallas_call x5, Pallas kernels, down(): pl.pallas_call(functools.partial(down_body, tuple(places)), grid_spec=plt...  20 us
    unnamed x12, local copies, waits for them, and re-layouts  13.5 us
    ppermute x14, waiting for transfers between devices, swap(): return lax.ppermute(x, 'gx', [(i, i ^ 1) for i in range(4 * LINE)])  4.89 us
    ppermute x14, starting transfers between devices, swap(): return lax.ppermute(x, 'gx', [(i, i ^ 1) for i in range(4 * LINE)])  3.08 us
  transfers between devices with their start and end apart: 22, of which 12 were waited for; matrix products, arithmetic and copies ran while one was open for 2% of the time, Pallas kernels for 38%

profile of v6, /device:TPU:0, one launch (start us, length us, event | category | flops | bytes accessed | tf_op | source)
XLA Modules:
  0.0 144.3 jit_solution(6658900683980742000)
XLA Ops:
  4.8 2.9 %collective-permute-start.1 = (bf16[2,400,512]{2,1,0:T(8,128)(2,1)}, bf16[2,400,512]{2,1,0:T(8,128)(2,1)}, u32[]{:S(2)}, u32[]{:S(2)}) collective-permute-start(bf16[2,400,512]{2,1,0:T(8,128)(2,1)} %pad_maximum_fusion.refs_0_), channel_id=1, source_target_pairs={{0,4},{1,3},{2,6},{3,1},{4,0},{5,9},{6,2},{7,11},{8,12},{9,5},{10,... | collective-permute-start | bytes 2457608 | tf_op jit(solution)/shard_map/ppermute | solution.py:46
  8.5 5.8 %gate_up.6 = (f32[384,1536]{1,0:T(8,128)S(1)}, f32[384,1536]{1,0:T(8,128)S(1)}, f32[384,256]{1,0:T(8,128)S(1)}, f32[8,512]{1,0:T(8,128)S(1)}) custom-call(s32[8]{0:T(128)S(1)} %xor_bitcast_fusion.order_ref, bf16[2,400,512]{2,1,0:T(8,128)(2,1)} %pad_maximum_fusion.refs_0_, bf16[8192,1664]{1,0:T(8,128)(2,1)} %refs_1_.7, bf16[8192,1664]{1,0:T(8,128)(2,1)} %refs_2_.11), custom_call_target="tpu_custom_call" | custom-call | flops 327155712 | bytes 851968 | tf_op jit(solution)/shard_map/gate_up/pallas_call | solution.py:174
  15.7 2.7 %collective-permute-done.1.refs_0_ = bf16[2,400,512]{2,1,0:T(8,128)(2,1)} collective-permute-done((bf16[2,400,512]{2,1,0:T(8,128)(2,1)}, bf16[2,400,512]{2,1,0:T(8,128)(2,1)}, u32[]{:S(2)}, u32[]{:S(2)}) %collective-permute-start.1) | collective-permute-done | bytes 819232 | tf_op jit(solution)/shard_map/ppermute | solution.py:46
  22.0 6.0 %gate_up.7 = (f32[384,1536]{1,0:T(8,128)S(1)}, f32[384,1536]{1,0:T(8,128)S(1)}, f32[384,256]{1,0:T(8,128)S(1)}, f32[8,512]{1,0:T(8,128)S(1)}) custom-call(s32[8]{0:T(128)S(1)} %xor_bitcast_fusion.order_ref, bf16[2,400,512]{2,1,0:T(8,128)(2,1)} %collective-permute-done.1.refs_0_, ...), custom_call_target="tpu_custom_call", output_to_operand_aliasing={{0}: (4, {}), {1}: (5, {}), {2}: (6, {}), {3}: (7, {})} | custom-call | flops 327155712 | bytes 851968 | tf_op jit(solution)/shard_map/gate_up/pallas_call | solution.py:174
  28.0 3.0 %collective-permute-done.2.refs_1_ = bf16[2,400,512]{2,1,0:T(8,128)(2,1)} collective-permute-done((bf16[2,400,512]{2,1,0:T(8,128)(2,1)}, bf16[2,400,512]{2,1,0:T(8,128)(2,1)}, u32[]{:S(2)}, u32[]{:S(2)}) %collective-permute-start.2) | collective-permute-done | bytes 819232 | tf_op jit(solution)/shard_map/ppermute | solution.py:46
  32.3 2.1 %collective-permute-start.3 = (bf16[2,400,512]{2,1,0:T(8,128)(2,1)S(1)}, bf16[2,400,512]{2,1,0:T(8,128)(2,1)S(1)}, u32[]{:S(2)}, u32[]{:S(2)}) collective-permute-start(bf16[2,400,512]{2,1,0:T(8,128)(2,1)S(1)} %broadcast_select_fusion), channel_id=1, source_target_pairs={{0,4},{1,3},{2,6},{3,1},{4,0},{5,7},{6,2},{7,5},{8,12},{9,11},{10,... | collective-permute-start | bytes 2457608 | tf_op jit(solution)/shard_map/ppermute | solution.py:46
  34.4 9.9 %gate_up.8 = (f32[384,1536]{1,0:T(8,128)S(1)}, f32[384,1536]{1,0:T(8,128)S(1)}, f32[384,256]{1,0:T(8,128)S(1)}, f32[8,512]{1,0:T(8,128)S(1)}) custom-call(s32[8]{0:T(128)S(1)} %xor_bitcast_fusion.order_ref, bf16[2,400,512]{2,1,0:T(8,128)(2,1)S(1)} %collective-permute-done.4.refs_0_, ...), custom_call_target="tpu_custom_call", output_to_operand_aliasing={{0}: (5, {}), {1}: (6, {}), {2}: (7, {}), {3}: (8, {})} | custom-call | flops 654311424 | bytes 1703936 | tf_op jit(solution)/shard_map/gate_up/pallas_call | solution.py:174
  44.8 4.1 %collective-permute-start.5 = (bf16[2,400,512]{2,1,0:T(8,128)(2,1)S(1)}, bf16[2,400,512]{2,1,0:T(8,128)(2,1)S(1)}, u32[]{:S(2)}, u32[]{:S(2)}) collective-permute-start(bf16[2,400,512]{2,1,0:T(8,128)(2,1)S(1)} %broadcast_select_fusion.1), channel_id=1, source_target_pairs={{0,2},{2,0},{4,6},{6,4},{8,10},{10,8},{12,14},{14,12},{16,18},{18,... | collective-permute-start | bytes 2457608 | tf_op jit(solution)/shard_map/ppermute | solution.py:46
  48.9 9.7 %gate_up.9 = (f32[384,1536]{1,0:T(8,128)S(1)}, f32[384,1536]{1,0:T(8,128)S(1)}, f32[384,256]{1,0:T(8,128)S(1)}, f32[8,512]{1,0:T(8,128)S(1)}) custom-call(s32[8]{0:T(128)S(1)} %xor_bitcast_fusion.order_ref, bf16[2,400,512]{2,1,0:T(8,128)(2,1)S(1)} %collective-permute-done.6.refs_0_, ...), custom_call_target="tpu_custom_call", output_to_operand_aliasing={{0}: (5, {}), {1}: (6, {}), {2}: (7, {}), {3}: (8, {})} | custom-call | flops 654311424 | bytes 1703936 | tf_op jit(solution)/shard_map/gate_up/pallas_call | solution.py:174
  59.2 5.9 %gate_up.10 = (f32[384,1536]{1,0:T(8,128)S(1)}, f32[384,1536]{1,0:T(8,128)S(1)}, f32[384,256]{1,0:T(8,128)S(1)}, f32[8,512]{1,0:T(8,128)S(1)}) custom-call(s32[8]{0:T(128)S(1)} %xor_bitcast_fusion.order_ref, bf16[2,400,512]{2,1,0:T(8,128)(2,1)S(1)} %collective-permute-done.8.refs_0_, ...), custom_call_target="tpu_custom_call", output_to_operand_aliasing={{0}: (4, {}), {1}: (5, {}), {2}: (6, {}), {3}: (7, {})} | custom-call | flops 327155712 | bytes 851968 | tf_op jit(solution)/shard_map/gate_up/pallas_call | solution.py:174
  65.2 6.8 %gate_up.11.hidden_ref = bf16[384,1664]{1,0:T(8,128)(2,1)S(1)} custom-call(s32[8]{0:T(128)S(1)} %xor_bitcast_fusion.order_ref, bf16[2,400,512]{2,1,0:T(8,128)(2,1)S(1)} %broadcast_select_fusion.2.refs_0_, bf16[8192,1664]{1,0:T(8,128)(2,1)} %refs_1_.7, bf16[8192,1664]{1,0:T(8,128)(2,1)} %refs_2_.11, f32[384,1536]{1,0:T(8,128)S(1)} %get-tuple-element.63.refs_3_, ...), custom_call_target="tpu_custom_call" | custom-call | flops 327155712 | bytes 851968 | tf_op jit(solution)/shard_map/gate_up/pallas_call | solution.py:174
  72.0 8.7 %copy-done = bf16[1664,8192]{1,0:T(8,128)(2,1)S(1)} copy-done((bf16[1664,8192]{1,0:T(8,128)(2,1)S(1)}, bf16[1664,8192]{1,0:T(8,128)(2,1)}, u32[]{:S(2)}) %copy-start) | copy-done | bytes 27263000
  80.8 2.7 %down.5 = f32[2,384,512]{2,1,0:T(8,128)S(1)} custom-call(s32[8]{0:T(128)S(1)} %xor_bitcast_fusion.order_ref, bf16[384,1664]{1,0:T(8,128)(2,1)S(1)} %gate_up.11.hidden_ref, bf16[1664,8192]{1,0:T(8,128)(2,1)S(1)} %copy-done), custom_call_target="tpu_custom_call" | custom-call | flops 81788928 | bytes 212992 | tf_op jit(solution)/shard_map/down/pallas_call | solution.py:243
  86.3 4.1 %collective-permute-start.12 = (bf16[2,384,512]{2,1,0:T(8,128)(2,1)S(1)}, bf16[2,384,512]{2,1,0:T(8,128)(2,1)S(1)}, u32[]{:S(2)}, u32[]{:S(2)}) collective-permute-start(bf16[2,384,512]{2,1,0:T(8,128)(2,1)S(1)} %pad_maximum_fusion.1), channel_id=1, source_target_pairs={{0,2},{2,0},{4,6},{6,4},{8,10},{10,8},{12,14},{14,12},{16,18},{18,... | collective-permute-start | bytes 2359304 | tf_op jit(solution)/shard_map/ppermute | solution.py:46
  90.4 4.9 %down.6 = (f32[2,384,512]{2,1,0:T(8,128)S(1)}, bf16[384,512]{1,0:T(8,128)(2,1)S(1)}, bf16[384,512]{1,0:T(8,128)(2,1)S(1)}) custom-call(s32[8]{0:T(128)S(1)} %xor_bitcast_fusion.order_ref, bf16[384,1664]{1,0:T(8,128)(2,1)S(1)} %gate_up.11.hidden_ref, bf16[1664,8192]{1,0:T(8,128)(2,1)S(1)} %copy-done), custom_call_target="tpu_custom_call" | custom-call | flops 163577856 | bytes 425984 | tf_op jit(solution)/shard_map/down/pallas_call | solution.py:243
  95.8 4.6 %collective-permute-done.12 = bf16[2,384,512]{2,1,0:T(8,128)(2,1)S(1)} collective-permute-done((bf16[2,384,512]{2,1,0:T(8,128)(2,1)S(1)}, bf16[2,384,512]{2,1,0:T(8,128)(2,1)S(1)}, u32[]{:S(2)}, u32[]{:S(2)}) %collective-permute-start.12) | collective-permute-done | bytes 786464 | tf_op jit(solution)/shard_map/ppermute | solution.py:46
  101.3 2.9 %collective-permute-start.15 = (bf16[2,384,512]{2,1,0:T(8,128)(2,1)S(1)}, bf16[2,384,512]{2,1,0:T(8,128)(2,1)S(1)}, u32[]{:S(2)}, u32[]{:S(2)}) collective-permute-start(bf16[2,384,512]{2,1,0:T(8,128)(2,1)S(1)} %pad_maximum_fusion.2), channel_id=1, source_target_pairs={{0,4},{1,3},{2,6},{3,1},{4,0},{5,7},{6,2},{7,5},{8,12},{9,11},{10,... | collective-permute-start | bytes 2359304 | tf_op jit(solution)/shard_map/ppermute | solution.py:46
  104.3 4.8 %down.7 = (f32[2,384,512]{2,1,0:T(8,128)S(1)}, bf16[384,512]{1,0:T(8,128)(2,1)S(1)}, bf16[384,512]{1,0:T(8,128)(2,1)S(1)}) custom-call(s32[8]{0:T(128)S(1)} %xor_bitcast_fusion.order_ref, bf16[384,1664]{1,0:T(8,128)(2,1)S(1)} %gate_up.11.hidden_ref, bf16[1664,8192]{1,0:T(8,128)(2,1)S(1)} %copy-done), custom_call_target="tpu_custom_call" | custom-call | flops 163577856 | bytes 425984 | tf_op jit(solution)/shard_map/down/pallas_call | solution.py:243
  109.7 4.5 %collective-permute-done.15 = bf16[2,384,512]{2,1,0:T(8,128)(2,1)S(1)} collective-permute-done((bf16[2,384,512]{2,1,0:T(8,128)(2,1)S(1)}, bf16[2,384,512]{2,1,0:T(8,128)(2,1)S(1)}, u32[]{:S(2)}, u32[]{:S(2)}) %collective-permute-start.15) | collective-permute-done | bytes 786464 | tf_op jit(solution)/shard_map/ppermute | solution.py:46
  115.4 2.6 %collective-permute-start.18 = (bf16[2,384,512]{2,1,0:T(8,128)(2,1)S(1)}, bf16[2,384,512]{2,1,0:T(8,128)(2,1)S(1)}, u32[]{:S(2)}, u32[]{:S(2)}) collective-permute-start(bf16[2,384,512]{2,1,0:T(8,128)(2,1)S(1)} %pad_maximum_fusion.3), channel_id=1, source_target_pairs={{0,2},{1,5},{2,0},{3,7},{4,8},{5,1},{6,10},{7,3},{8,4},{9,13},{10,... | collective-permute-start | bytes 2359304 | tf_op jit(solution)/shard_map/ppermute | solution.py:46
  118.0 4.8 %down.8 = (f32[2,384,512]{2,1,0:T(8,128)S(1)}, bf16[384,512]{1,0:T(8,128)(2,1)S(1)}, bf16[384,512]{1,0:T(8,128)(2,1)S(1)}) custom-call(s32[8]{0:T(128)S(1)} %xor_bitcast_fusion.order_ref, bf16[384,1664]{1,0:T(8,128)(2,1)S(1)} %gate_up.11.hidden_ref, bf16[1664,8192]{1,0:T(8,128)(2,1)S(1)} %copy-done), custom_call_target="tpu_custom_call" | custom-call | flops 163577856 | bytes 425984 | tf_op jit(solution)/shard_map/down/pallas_call | solution.py:243
  123.4 4.7 %collective-permute-done.18 = bf16[2,384,512]{2,1,0:T(8,128)(2,1)S(1)} collective-permute-done((bf16[2,384,512]{2,1,0:T(8,128)(2,1)S(1)}, bf16[2,384,512]{2,1,0:T(8,128)(2,1)S(1)}, u32[]{:S(2)}, u32[]{:S(2)}) %collective-permute-start.18) | collective-permute-done | bytes 786464 | tf_op jit(solution)/shard_map/ppermute | solution.py:46
  130.6 2.7 %down.9 = f32[2,384,512]{2,1,0:T(8,128)S(1)} custom-call(s32[8]{0:T(128)S(1)} %xor_bitcast_fusion.order_ref, bf16[384,1664]{1,0:T(8,128)(2,1)S(1)} %gate_up.11.hidden_ref, bf16[1664,8192]{1,0:T(8,128)(2,1)S(1)} %copy-done), custom_call_target="tpu_custom_call" | custom-call | flops 81788928 | bytes 212992 | tf_op jit(solution)/shard_map/down/pallas_call | solution.py:243
  133.4 7.8 %collective-permute-done.20 = bf16[2,384,512]{2,1,0:T(8,128)(2,1)S(1)} collective-permute-done((bf16[2,384,512]{2,1,0:T(8,128)(2,1)S(1)}, bf16[2,384,512]{2,1,0:T(8,128)(2,1)S(1)}, u32[]{:S(2)}, u32[]{:S(2)}) %collective-permute-start.20) | collective-permute-done | bytes 786464 | tf_op jit(solution)/shard_map/ppermute | solution.py:46
  (65 shorter events, 25.2 us)
Async XLA Ops:
  1.9 1.9 %collective-permute-start = (bf16[400,512]{1,0:T(8,128)(2,1)S(1)}, bf16[400,512]{1,0:T(8,128)(2,1)S(1)}, u32[]{:S(2)}, u32[]{:S(2)}) collective-permute-start(bf16[400,512]{1,0:T(8,128)(2,1)S(1)} %prepare.1), channel_id=1, source_target_pairs={{0,1},{1,0},{2,3},{3,2},{4,5},{5,4},{6,7},{7,6},{8,9},{9,8},{10,11... | collective-permute-start | bytes 1228808 | tf_op jit(solution)/shard_map/ppermute | solution.py:50
  4.8 13.6 %collective-permute-start.1 = (bf16[2,400,512]{2,1,0:T(8,128)(2,1)}, bf16[2,400,512]{2,1,0:T(8,128)(2,1)}, u32[]{:S(2)}, u32[]{:S(2)}) collective-permute-start(bf16[2,400,512]{2,1,0:T(8,128)(2,1)} %pad_maximum_fusion.refs_0_), channel_id=1, source_target_pairs={{0,4},{1,3},{2,6},{3,1},{4,0},{5,9},{6,2},{7,11},{8,12},{9,5},{10,... | collective-permute-start | bytes 2457608 | tf_op jit(solution)/shard_map/ppermute | solution.py:46
  18.4 12.7 %collective-permute-start.2 = (bf16[2,400,512]{2,1,0:T(8,128)(2,1)}, bf16[2,400,512]{2,1,0:T(8,128)(2,1)}, u32[]{:S(2)}, u32[]{:S(2)}) collective-permute-start(bf16[2,400,512]{2,1,0:T(8,128)(2,1)} %collective-permute-done.1.refs_0_), channel_id=1, source_target_pairs={{0,2},{1,5},{2,0},{3,7},{4,8},{5,1},{6,10},{7,3},{8,4},{9,13},{10,... | collective-permute-start | bytes 2457608 | tf_op jit(solution)/shard_map/ppermute | solution.py:46
  20.4 14.0 %collective-permute-start.4 = (bf16[2,400,512]{2,1,0:T(8,128)(2,1)}, bf16[2,400,512]{2,1,0:T(8,128)(2,1)S(1)}, u32[]{:S(2)}, u32[]{:S(2)}) collective-permute-start(bf16[2,400,512]{2,1,0:T(8,128)(2,1)} %collective-permute-done.1.refs_0_), channel_id=1, source_target_pairs={{0,1},{1,0},{2,3},{3,2},{4,5},{5,4},{6,7},{7,6},{8,9},{9,8},{10,11... | collective-permute-start | bytes 2457608 | tf_op jit(solution)/shard_map/ppermute | solution.py:50
  32.3 12.4 %collective-permute-start.3 = (bf16[2,400,512]{2,1,0:T(8,128)(2,1)S(1)}, bf16[2,400,512]{2,1,0:T(8,128)(2,1)S(1)}, u32[]{:S(2)}, u32[]{:S(2)}) collective-permute-start(bf16[2,400,512]{2,1,0:T(8,128)(2,1)S(1)} %broadcast_select_fusion), channel_id=1, source_target_pairs={{0,4},{1,3},{2,6},{3,1},{4,0},{5,7},{6,2},{7,5},{8,12},{9,11},{10,... | collective-permute-start | bytes 2457608 | tf_op jit(solution)/shard_map/ppermute | solution.py:46
  34.4 14.6 %collective-permute-start.6 = (bf16[2,400,512]{2,1,0:T(8,128)(2,1)}, bf16[2,400,512]{2,1,0:T(8,128)(2,1)S(1)}, u32[]{:S(2)}, u32[]{:S(2)}) collective-permute-start(bf16[2,400,512]{2,1,0:T(8,128)(2,1)} %collective-permute-done.2.refs_1_), channel_id=1, source_target_pairs={{0,1},{1,0},{2,3},{3,2},{4,5},{5,4},{6,7},{7,6},{8,9},{9,8},{10,11... | collective-permute-start | bytes 2457608 | tf_op jit(solution)/shard_map/ppermute | solution.py:50
  44.8 14.2 %collective-permute-start.5 = (bf16[2,400,512]{2,1,0:T(8,128)(2,1)S(1)}, bf16[2,400,512]{2,1,0:T(8,128)(2,1)S(1)}, u32[]{:S(2)}, u32[]{:S(2)}) collective-permute-start(bf16[2,400,512]{2,1,0:T(8,128)(2,1)S(1)} %broadcast_select_fusion.1), channel_id=1, source_target_pairs={{0,2},{2,0},{4,6},{6,4},{8,10},{10,8},{12,14},{14,12},{16,18},{18,... | collective-permute-start | bytes 2457608 | tf_op jit(solution)/shard_map/ppermute | solution.py:46
  48.9 10.3 %collective-permute-start.8 = (bf16[2,400,512]{2,1,0:T(8,128)(2,1)S(1)}, bf16[2,400,512]{2,1,0:T(8,128)(2,1)S(1)}, u32[]{:S(2)}, u32[]{:S(2)}) collective-permute-start(bf16[2,400,512]{2,1,0:T(8,128)(2,1)S(1)} %collective-permute-done.3.refs_1_), channel_id=1, source_target_pairs={{0,1},{1,0},{2,3},{3,2},{4,5},{5,4},{6,7},{7,6},{8,9},{9,8},{10,11... | collective-permute-start | bytes 2457608 | tf_op jit(solution)/shard_map/ppermute | solution.py:50
  59.0 6.1 %collective-permute-start.7 = (bf16[2,400,512]{2,1,0:T(8,128)(2,1)S(1)}, bf16[2,400,512]{2,1,0:T(8,128)(2,1)S(1)}, u32[]{:S(2)}, u32[]{:S(2)}) collective-permute-start(bf16[2,400,512]{2,1,0:T(8,128)(2,1)S(1)} %collective-permute-done.5), channel_id=1, source_target_pairs={{0,1},{1,0},{2,3},{3,2},{4,5},{5,4},{6,7},{7,6},{8,9},{9,8},{10,11... | collective-permute-start | bytes 2457608 | tf_op jit(solution)/shard_map/ppermute | solution.py:50
  72.0 8.8 %copy-start = (bf16[1664,8192]{1,0:T(8,128)(2,1)S(1)}, bf16[1664,8192]{1,0:T(8,128)(2,1)}, u32[]{:S(2)}) copy-start(bf16[1664,8192]{1,0:T(8,128)(2,1)} %weight_ref.9) | copy-start | bytes 81788928
  83.6 1.8 %collective-permute-start.10 = (bf16[384,512]{1,0:T(8,128)(2,1)S(1)}, bf16[384,512]{1,0:T(8,128)(2,1)S(1)}, u32[]{:S(2)}, u32[]{:S(2)}) collective-permute-start(bf16[384,512]{1,0:T(8,128)(2,1)S(1)} %get-tuple-element.90), channel_id=1, source_target_pairs={{0,1},{1,0},{2,3},{3,2},{4,5},{5,4},{6,7},{7,6},{8,9},{9,8},{10,11... | collective-permute-start | bytes 1179656 | tf_op jit(solution)/shard_map/ppermute | solution.py:50
  84.0 1.9 %collective-permute-start.9 = (bf16[384,512]{1,0:T(8,128)(2,1)S(1)}, bf16[384,512]{1,0:T(8,128)(2,1)S(1)}, u32[]{:S(2)}, u32[]{:S(2)}) collective-permute-start(bf16[384,512]{1,0:T(8,128)(2,1)S(1)} %get-tuple-element.89), channel_id=1, source_target_pairs={{0,1},{1,0},{2,3},{3,2},{4,5},{5,4},{6,7},{7,6},{8,9},{9,8},{10,11... | collective-permute-start | bytes 1179656 | tf_op jit(solution)/shard_map/ppermute | solution.py:50
  86.3 14.2 %collective-permute-start.12 = (bf16[2,384,512]{2,1,0:T(8,128)(2,1)S(1)}, bf16[2,384,512]{2,1,0:T(8,128)(2,1)S(1)}, u32[]{:S(2)}, u32[]{:S(2)}) collective-permute-start(bf16[2,384,512]{2,1,0:T(8,128)(2,1)S(1)} %pad_maximum_fusion.1), channel_id=1, source_target_pairs={{0,2},{2,0},{4,6},{6,4},{8,10},{10,8},{12,14},{14,12},{16,18},{18,... | collective-permute-start | bytes 2359304 | tf_op jit(solution)/shard_map/ppermute | solution.py:46
  95.3 5.5 %collective-permute-start.11 = (bf16[384,512]{1,0:T(8,128)(2,1)S(1)}, bf16[384,512]{1,0:T(8,128)(2,1)S(1)}, u32[]{:S(2)}, u32[]{:S(2)}) collective-permute-start(bf16[384,512]{1,0:T(8,128)(2,1)S(1)} %get-tuple-element.70), channel_id=1, source_target_pairs={{0,1},{1,0},{2,3},{3,2},{4,5},{5,4},{6,7},{7,6},{8,9},{9,8},{10,11... | collective-permute-start | bytes 1179656 | tf_op jit(solution)/shard_map/ppermute | solution.py:50
  95.3 5.4 %collective-permute-start.13 = (bf16[384,512]{1,0:T(8,128)(2,1)S(1)}, bf16[384,512]{1,0:T(8,128)(2,1)S(1)}, u32[]{:S(2)}, u32[]{:S(2)}) collective-permute-start(bf16[384,512]{1,0:T(8,128)(2,1)S(1)} %get-tuple-element.71), channel_id=1, source_target_pairs={{0,1},{1,0},{2,3},{3,2},{4,5},{5,4},{6,7},{7,6},{8,9},{9,8},{10,11... | collective-permute-start | bytes 1179656 | tf_op jit(solution)/shard_map/ppermute | solution.py:50
  101.3 12.9 %collective-permute-start.15 = (bf16[2,384,512]{2,1,0:T(8,128)(2,1)S(1)}, bf16[2,384,512]{2,1,0:T(8,128)(2,1)S(1)}, u32[]{:S(2)}, u32[]{:S(2)}) collective-permute-start(bf16[2,384,512]{2,1,0:T(8,128)(2,1)S(1)} %pad_maximum_fusion.2), channel_id=1, source_target_pairs={{0,4},{1,3},{2,6},{3,1},{4,0},{5,7},{6,2},{7,5},{8,12},{9,11},{10,... | collective-permute-start | bytes 2359304 | tf_op jit(solution)/shard_map/ppermute | solution.py:46
  109.1 5.5 %collective-permute-start.14 = (bf16[384,512]{1,0:T(8,128)(2,1)S(1)}, bf16[384,512]{1,0:T(8,128)(2,1)S(1)}, u32[]{:S(2)}, u32[]{:S(2)}) collective-permute-start(bf16[384,512]{1,0:T(8,128)(2,1)S(1)} %get-tuple-element.74), channel_id=1, source_target_pairs={{0,1},{1,0},{2,3},{3,2},{4,5},{5,4},{6,7},{7,6},{8,9},{9,8},{10,11... | collective-permute-start | bytes 1179656 | tf_op jit(solution)/shard_map/ppermute | solution.py:50
  109.2 5.5 %collective-permute-start.16 = (bf16[384,512]{1,0:T(8,128)(2,1)S(1)}, bf16[384,512]{1,0:T(8,128)(2,1)S(1)}, u32[]{:S(2)}, u32[]{:S(2)}) collective-permute-start(bf16[384,512]{1,0:T(8,128)(2,1)S(1)} %get-tuple-element.75), channel_id=1, source_target_pairs={{0,1},{1,0},{2,3},{3,2},{4,5},{5,4},{6,7},{7,6},{8,9},{9,8},{10,11... | collective-permute-start | bytes 1179656 | tf_op jit(solution)/shard_map/ppermute | solution.py:50
  115.4 12.7 %collective-permute-start.18 = (bf16[2,384,512]{2,1,0:T(8,128)(2,1)S(1)}, bf16[2,384,512]{2,1,0:T(8,128)(2,1)S(1)}, u32[]{:S(2)}, u32[]{:S(2)}) collective-permute-start(bf16[2,384,512]{2,1,0:T(8,128)(2,1)S(1)} %pad_maximum_fusion.3), channel_id=1, source_target_pairs={{0,2},{1,5},{2,0},{3,7},{4,8},{5,1},{6,10},{7,3},{8,4},{9,13},{10,... | collective-permute-start | bytes 2359304 | tf_op jit(solution)/shard_map/ppermute | solution.py:46
  122.9 5.4 %collective-permute-start.17 = (bf16[384,512]{1,0:T(8,128)(2,1)S(1)}, bf16[384,512]{1,0:T(8,128)(2,1)S(1)}, u32[]{:S(2)}, u32[]{:S(2)}) collective-permute-start(bf16[384,512]{1,0:T(8,128)(2,1)S(1)} %get-tuple-element.78), channel_id=1, source_target_pairs={{0,1},{1,0},{2,3},{3,2},{4,5},{5,4},{6,7},{7,6},{8,9},{9,8},{10,11... | collective-permute-start | bytes 1179656 | tf_op jit(solution)/shard_map/ppermute | solution.py:50
  123.0 5.4 %collective-permute-start.19 = (bf16[384,512]{1,0:T(8,128)(2,1)S(1)}, bf16[384,512]{1,0:T(8,128)(2,1)S(1)}, u32[]{:S(2)}, u32[]{:S(2)}) collective-permute-start(bf16[384,512]{1,0:T(8,128)(2,1)S(1)} %get-tuple-element.79), channel_id=1, source_target_pairs={{0,1},{1,0},{2,3},{3,2},{4,5},{5,4},{6,7},{7,6},{8,9},{9,8},{10,11... | collective-permute-start | bytes 1179656 | tf_op jit(solution)/shard_map/ppermute | solution.py:50
  129.1 12.1 %collective-permute-start.20 = (bf16[2,384,512]{2,1,0:T(8,128)(2,1)S(1)}, bf16[2,384,512]{2,1,0:T(8,128)(2,1)S(1)}, u32[]{:S(2)}, u32[]{:S(2)}) collective-permute-start(bf16[2,384,512]{2,1,0:T(8,128)(2,1)S(1)} %pad_maximum_fusion.4), channel_id=1, source_target_pairs={{0,4},{1,3},{2,6},{3,1},{4,0},{5,9},{6,2},{7,11},{8,12},{9,5},{10,... | collective-permute-start | bytes 2359304 | tf_op jit(solution)/shard_map/ppermute | solution.py:46
  133.4 9.9 %copy-start.4 = (bf16[384,512]{1,0:T(8,128)(2,1)S(1)}, bf16[384,512]{1,0:T(8,128)(2,1)}, u32[]{:S(2)}) copy-start(bf16[384,512]{1,0:T(8,128)(2,1)} %x_ref.1) | copy-start | bytes 1179652
  141.5 1.8 %collective-permute-start.21 = (bf16[384,512]{1,0:T(8,128)(2,1)S(1)}, bf16[384,512]{1,0:T(8,128)(2,1)S(1)}, u32[]{:S(2)}, u32[]{:S(2)}) collective-permute-start(bf16[384,512]{1,0:T(8,128)(2,1)S(1)} %fusion.22), channel_id=1, source_target_pairs={{0,1},{1,0},{2,3},{3,2},{4,5},{5,4},{6,7},{7,6},{8,9},{9,8},{10,11... | collective-permute-start | bytes 1179656 | tf_op jit(solution)/shard_map/ppermute | solution.py:50
  (4 other events, 4.8 us)

commit v7 on v5

v7 whole, which is shorter than its diff:
```python
import functools

import jax
import jax.numpy as jnp
import numpy as np
from jax import lax
from jax.experimental import pallas as pl
from jax.experimental.pallas import tpu as pltpu
from jax.sharding import PartitionSpec as P

epsilon = 1e-05
LINE = 4
EXTRA = 16
VMEM_LIMIT = 36 * 1024 * 1024

ALONG = (lambda z, y: (z ^ 1, y),) * 2
INSIDE = (lambda z, y: (z, y ^ 1), lambda z, y: (z ^ 3, y))
ACROSS = (lambda z, y: (z, y ^ 1),) * 2

TAKEN = np.array([(0, 2, 1, 4, 3, 6, 5, 7), (0, 2, 6, 3, 4, 1, 7, 5)], np.int32)


def send(x, move):
    pairs = []
    for z in range(LINE):
        for y in range(2):
            to_z, to_y = move[0 < z < LINE - 1](z, y)
            pairs += [(z * 4 + y * 2 + c, to_z * 4 + to_y * 2 + c) for c in range(2)]
    return lax.ppermute(x, "gx", pairs)


def swap(x):
    return lax.ppermute(x, "gx", [(i, i ^ 1) for i in range(4 * LINE)])


def after(x, *others):
    return lax.optimization_barrier((x, *others))[0]


def pick(table, s):
    value = jnp.int32(table[0])
    for i, entry in enumerate(table[1:], 1):
        value = jnp.where(s == i, jnp.int32(entry), value)
    return value


def prepare_body(x_ref, gain_ref, out_ref):
    rows, width = x_ref.shape
    x = x_ref[...].astype(jnp.float32)
    gain = gain_ref[...].astype(jnp.float32).reshape(1, width)
    out_ref[:rows, :] = (x * gain).astype(jnp.bfloat16)
    squares = jnp.broadcast_to(jnp.sum(x * x, axis=1, keepdims=True), (rows, 128)).T[:EXTRA]
    row = lax.broadcasted_iota(jnp.int32, (EXTRA, rows), 0)
    parts = jnp.zeros((EXTRA, rows), jnp.float32)
    for i in range(3):
        part = squares.astype(jnp.bfloat16).astype(jnp.float32)
        parts = jnp.where(row == i, part, parts)
        squares = squares - part
    out_ref[rows:, :rows] = parts.astype(jnp.bfloat16)
    if rows < width:
        out_ref[rows:, rows:] = jnp.zeros((EXTRA, width - rows), jnp.bfloat16)


def prepare(activations, norm_gain):
    rows, width = activations.shape
    return pl.pallas_call(
        prepare_body,
        out_shape=jax.ShapeDtypeStruct((rows + EXTRA, width), jnp.bfloat16),
        compiler_params=pltpu.CompilerParams(vmem_limit_bytes=VMEM_LIMIT),
        name="prepare",
    )(activations, norm_gain)


def gate_up_body(count, first, last, rows, main, features, order_ref, *refs):
    blocks = refs[:count]
    gate_ref, up_ref, *rest = refs[count:]
    if not first:
        before = rest[:4]
        rest = rest[4:]
    if last:
        hidden_ref, *rest = rest
    accs = rest
    step = pl.program_id(0)

    for s in range(count):

        @pl.when(step == s)
        def _(s=s):
            x = blocks[s][:rows, :]
            gate, up = gate_ref[...], up_ref[...]
            mixed = jnp.concatenate([gate[:, main:], up[:, main:]], axis=1)
            values = [
                jnp.dot(x, weight, preferred_element_type=jnp.float32)
                for weight in (gate[:, :main], up[:, :main], mixed)
            ]
            squares = blocks[s][rows:, :].astype(jnp.float32)
            squares = jnp.sum(squares, axis=0, keepdims=True)
            values.append(jnp.broadcast_to(squares, accs[3].shape))
            if s:
                values = [acc[...] + value for acc, value in zip(accs, values)]
            elif not first:
                values = [old[...] + value for old, value in zip(before, values)]
            if not last or s < count - 1:
                for acc, value in zip(accs, values):
                    acc[...] = value
                return
            factor = lax.rsqrt(values[3][:1, :rows] / features + epsilon)
            factor = jnp.broadcast_to(factor, (128, rows)).T[:, :1]

            def act(g, u):
                g, u = g * factor, u * factor
                return (g / (1.0 + jnp.exp(-g)) * u).astype(jnp.bfloat16)

            gate, up, both, _ = values
            rem = both.shape[1] // 2
            hidden_ref[:, :main] = act(gate, up)
            hidden_ref[:, main:] = act(both[:, :rem], both[:, rem:])


def gate_up(order, places, blocks, gate_weight, up_weight, acc, last=False):
    height, depth = blocks[0].shape
    count = len(blocks)
    rows = height - EXTRA
    features, ff = gate_weight.shape
    main = ff // 256 * 256 if ff % 256 else ff - 256
    rem = ff - main
    first = acc is None
    whole = lambda shape: pl.BlockSpec(shape, lambda s, order: (0, 0))
    weight = pl.BlockSpec((depth, ff), lambda s, order: (order[pick(places, s)], 0))
    in_specs = [whole(b.shape) for b in blocks] + [weight, weight]
    args = [*blocks, gate_weight, up_weight]
    shapes = [(rows, main), (rows, main), (rows, 2 * rem), (8, depth)]
    if not first:
        in_specs += [whole(s) for s in shapes]
        args += list(acc)
    if last:
        out_shape = [jax.ShapeDtypeStruct((rows, ff), jnp.bfloat16)]
        out_specs = [whole((rows, ff))]
        scratch = [pltpu.VMEM(s, jnp.float32) for s in shapes]
    else:
        out_shape = [jax.ShapeDtypeStruct(s, jnp.float32) for s in shapes]
        out_specs = [whole(s) for s in shapes]
        scratch = []
    return pl.pallas_call(
        functools.partial(gate_up_body, count, first, last, rows, main, features),
        grid_spec=pltpu.PrefetchScalarGridSpec(
            num_scalar_prefetch=1,
            grid=(count,),
            in_specs=in_specs,
            out_specs=out_specs,
            scratch_shapes=scratch,
        ),
        out_shape=out_shape,
        compiler_params=pltpu.CompilerParams(vmem_limit_bytes=VMEM_LIMIT),
        cost_estimate=pl.CostEstimate(
            flops=4 * rows * depth * count * ff // 8,
            bytes_accessed=4 * depth * count * ff // 8,
            transcendentals=0,
        ),
        name="gate_up",
    )(order, *args)


def down_block(hidden_ref, weight_ref):
    ff = hidden_ref.shape[1]
    main = ff // 256 * 256
    value = jnp.dot(
        hidden_ref[:, :main], weight_ref[:main, :], preferred_element_type=jnp.float32
    )
    if main < ff:
        value = value + jnp.dot(
            hidden_ref[:, main:], weight_ref[main:, :], preferred_element_type=jnp.float32
        )
    return value


def down_body(kinds, order_ref, hidden_ref, weight_ref, *outs):
    now = pl.program_id(0)
    value = down_block(hidden_ref, weight_ref)
    for s, kind in enumerate(kinds):

        @pl.when(now == s)
        def _(out=outs[s], kind=kind):
            out[...] = value.astype(out.dtype)


def down(order, jobs, hidden, down_weight, width):
    rows, ff = hidden.shape
    count = len(jobs)
    places, kinds = zip(*jobs)
    return pl.pallas_call(
        functools.partial(down_body, kinds),
        grid_spec=pltpu.PrefetchScalarGridSpec(
            num_scalar_prefetch=1,
            grid=(count,),
            in_specs=[
                pl.BlockSpec((rows, ff), lambda s, order: (0, 0)),
                pl.BlockSpec((ff, width), lambda s, order: (0, order[pick(places, s)])),
            ],
            out_specs=[pl.BlockSpec((rows, width), lambda s, order: (0, 0))] * count,
        ),
        out_shape=[jax.ShapeDtypeStruct((rows, width), kind) for kind in kinds],
        compiler_params=pltpu.CompilerParams(vmem_limit_bytes=VMEM_LIMIT),
        cost_estimate=pl.CostEstimate(
            flops=rows * ff * width * count // 4,
            bytes_accessed=ff * width * count // 4,
            transcendentals=0,
        ),
        name="down",
    )(order, hidden, down_weight)


def overlapped(activations, norm_gain, gate_weight, up_weight, down_weight):
    width = activations.shape[1]
    index = lax.axis_index("gx").astype(jnp.int32)
    z = index >> 2
    end = (z == 0) | (z == LINE - 1)
    resident = activations.astype(jnp.float32)

    taken = jnp.where(end, jnp.asarray(TAKEN[0]), jnp.asarray(TAKEN[1]))
    order = ((index >> 1) ^ taken) * 2 + (index & 1)
    order = jnp.concatenate([order, order ^ 1])
    OWN, ONE, ONE_IN, TWO, TWO_IN, THREE, THREE_ACROSS, FOUR = range(8)

    def multiply(acc, *shards, last=False):
        places = [place + 8 * other for place, other, _ in shards]
        blocks = [x for _, _, x in shards]
        return gate_up(order, places, blocks, gate_weight, up_weight, acc, last)

    own = prepare(activations, norm_gain)
    one, one_in = send(own, ALONG), send(own, INSIDE)
    acc = multiply(None, (OWN, 0, own), (OWN, 1, swap(own)))
    one, one_in = after((one, one_in), acc[3])
    two, two_in = send(one_in, ALONG), send(one, INSIDE)
    acc = multiply(
        acc,
        (ONE, 0, one), (ONE_IN, 0, one_in), (ONE, 1, swap(one)), (ONE_IN, 1, swap(one_in)),
    )
    two, two_in = after((two, two_in), acc[3])
    three, three_across = send(two_in, ALONG), send(jnp.where(end, two, one_in), ACROSS)
    acc = multiply(
        acc,
        (TWO, 0, two), (TWO_IN, 0, two_in), (TWO, 1, swap(two)), (TWO_IN, 1, swap(two_in)),
    )
    three, three_across = after((three, three_across), acc[3])
    four = send(jnp.where(end, three, two_in), ACROSS)
    acc = multiply(
        acc,
        (THREE, 0, three), (THREE_ACROSS, 0, three_across),
        (THREE, 1, swap(three)), (THREE_ACROSS, 1, swap(three_across)),
    )
    four = after(four, acc[3])
    hidden = multiply(acc, (FOUR, 0, four), (FOUR, 1, swap(four)), last=True)[0]

    narrow = lambda x: x.astype(jnp.bfloat16)
    wide = lambda x: x.astype(jnp.float32)
    zero = jnp.zeros((), jnp.float32)

    def partials(hidden, kept, sent):
        jobs = [(place, jnp.float32) for place in kept]
        jobs += [(place + 8, jnp.bfloat16) for place in sent]
        outs = down(order, jobs, hidden, down_weight, width)
        return *outs[: len(kept)], *(swap(x) for x in outs[len(kept) :])

    (other_four,) = partials(hidden, (), (FOUR,))
    four, other_three, other_across = partials(hidden, (FOUR,), (THREE, THREE_ACROSS))
    four = narrow(four + wide(other_four))
    got = wide(send(four, ACROSS))
    three, across, other_two, other_in = partials(
        after(hidden, four), (THREE, THREE_ACROSS), (TWO, TWO_IN)
    )
    across = narrow(across + wide(other_across))
    got_across = wide(send(across, ACROSS))
    three = narrow(three + wide(other_three) + jnp.where(end, got, zero))
    got_three = wide(send(three, ALONG))
    two, two_in, other_one, other_one_in = partials(
        after(hidden, three, across), (TWO, TWO_IN), (ONE, ONE_IN)
    )
    two = narrow(two + wide(other_two) + jnp.where(end, got_across, zero))
    got_two = wide(send(two, ALONG))
    two_in = narrow(two_in + wide(other_in) + jnp.where(end, zero, got) + got_three)
    got_in = wide(send(two_in, INSIDE))
    one, one_in, other_own = partials(after(hidden, two, two_in), (ONE, ONE_IN), (OWN,))
    one_in = narrow(one_in + wide(other_one_in) + jnp.where(end, zero, got_across) + got_two)
    got_one_in = wide(send(one_in, INSIDE))
    one = narrow(one + wide(other_one) + got_in)
    got_one = wide(send(one, ALONG))
    (kept,) = partials(after(hidden, one, one_in), (OWN,), ())
    branch = kept + wide(other_own)
    return (resident + branch + got_one + got_one_in).astype(jnp.bfloat16)


def plain(activations, norm_gain, gate_weight, up_weight, down_weight):
    resident = activations.astype(jnp.float32)
    totals = lax.psum(jnp.sum(resident * resident, axis=1), "gx")
    factor = lax.rsqrt(totals / (resident.shape[1] * lax.axis_size("gx")) + epsilon)
    normed = (resident * factor[:, None] * norm_gain.astype(jnp.float32)[None, :]).astype(
        jnp.bfloat16
    )
    pieces = lax.all_gather(normed, "gx", axis=1, tiled=True)
    gate_sum = jnp.dot(pieces, gate_weight, preferred_element_type=jnp.float32)
    up_sum = jnp.dot(pieces, up_weight, preferred_element_type=jnp.float32)
    hidden = (jax.nn.silu(gate_sum) * up_sum).astype(jnp.bfloat16)
    summed = lax.psum_scatter(
        lax.dot_general(
            down_weight, hidden, (((0,), (1,)), ((), ())), preferred_element_type=jnp.float32
        ),
        "gx",
        scatter_dimension=0,
        tiled=True,
    )
    return (resident + summed.T).astype(jnp.bfloat16)


def per_device(n, activations, norm_gain, gate_weight, up_weight, down_weight):
    args = (activations, norm_gain, gate_weight, up_weight, down_weight)
    rows, width = activations.shape
    tiled = rows % 128 == 0 and width % 128 == 0 and gate_weight.shape[1] % 128 == 0
    tiled = tiled and rows <= width
    if n == 4 * LINE and tiled:
        return overlapped(*args)
    return plain(*args)


def solution(mesh):
    in_specs = (P("groups", "gx"), P("gx"), P(None, "gx"), P(None, "gx"), P("gx", None))
    out_specs = P("groups", "gx")
    return jax.shard_map(
        functools.partial(per_device, mesh.shape["gx"]),
        mesh=mesh,
        in_specs=in_specs,
        out_specs=out_specs,
        check_vma=False,
    )
```

time: 134 us -> 117 us (0.87)
  starting transfers between devices: 33.5 us -> 24 us
  Pallas kernels: 62 us -> 69.7 us
  waiting for transfers between devices: 25.3 us -> 17.8 us
  local copies, waits for them, and re-layouts: 8.35 us -> 1.68 us
    ppermute x30, starting transfers between devices: 33.5 us -> 24 us  [the longest x14 20.1 us: send(): return lax.ppermute(x, 'gx', pairs)]
    pallas_call x10 -> x11, Pallas kernels: 61.8 us -> 69.5 us  [the longest x5 40.4 us: gate_up(): pl.pallas_call(functools.partial(gate_up_body, count, first, last, rows,...]
    ppermute x30, waiting for transfers between devices: 25.3 us -> 17.8 us  [the longest x14 15.7 us: send(): return lax.ppermute(x, 'gx', pairs)]
    unnamed x18 -> x6, local copies, waits for them, and re-layouts: 8.24 us -> 1.68 us
  transfers between devices with their start and end apart: 30 -> 30, of which waited for: 13 -> 11; matrix products, arithmetic and copies ran while one was open for 1% -> 2% of each run, Pallas kernels for 38% -> 52%
where the time goes in v7:
time: 117 us; the launch traced here: 116 us
  Pallas kernels  69.7 us (60%)
  starting transfers between devices  24 us (21%)
  waiting for transfers between devices  17.8 us (15%)
  other arithmetic  3.05 us (3%)
  local copies, waits for them, and re-layouts  1.68 us (1%)
    pallas_call x5, Pallas kernels, gate_up(): pl.pallas_call(functools.partial(gate_up_body, count, first, last, rows,...  40.4 us
    pallas_call x6, Pallas kernels, down(): pl.pallas_call(functools.partial(down_body, kinds), grid_spec=pltpu.Prefe...  29.1 us
    ppermute x14, starting transfers between devices, send(): return lax.ppermute(x, 'gx', pairs)  20.1 us
    ppermute x14, waiting for transfers between devices, send(): return lax.ppermute(x, 'gx', pairs)  15.7 us
    ppermute x16, starting transfers between devices, swap(): return lax.ppermute(x, 'gx', [(i, i ^ 1) for i in range(4 * LINE)])  3.92 us
  transfers between devices with their start and end apart: 30, of which 11 were waited for; matrix products, arithmetic and copies ran while one was open for 2% of the time, Pallas kernels for 52%

profile of v7, /device:TPU:0, one launch (start us, length us, event | category | flops | bytes accessed | tf_op | source)
XLA Modules:
  0.0 116.5 jit_solution(11510003206046102050)
XLA Ops:
  2.4 2.6 %collective-permute-start.1 = (bf16[400,512]{1,0:T(8,128)(2,1)S(1)}, bf16[400,512]{1,0:T(8,128)(2,1)S(1)}, u32[]{:S(2)}, u32[]{:S(2)}) collective-permute-start(bf16[400,512]{1,0:T(8,128)(2,1)S(1)} %prepare.1.refs_0_), channel_id=1, source_target_pairs={{0,2},{1,3},{2,0},{3,1},{4,8},{5,9},{6,10},{7,11},{8,4},{9,5},{10,... | collective-permute-start | bytes 1228808 | tf_op jit(solution)/shard_map/ppermute | solution.py:29
  5.0 1.6 %collective-permute-start = (bf16[400,512]{1,0:T(8,128)(2,1)S(1)}, bf16[400,512]{1,0:T(8,128)(2,1)S(1)}, u32[]{:S(2)}, u32[]{:S(2)}) collective-permute-start(bf16[400,512]{1,0:T(8,128)(2,1)S(1)} %prepare.1.refs_0_), channel_id=1, source_target_pairs={{0,4},{1,5},{2,6},{3,7},{4,0},{5,1},{6,2},{7,3},{8,12},{9,13},{10,... | collective-permute-start | bytes 1228808 | tf_op jit(solution)/shard_map/ppermute | solution.py:29
  7.4 5.7 %gate_up.5 = (f32[384,1536]{1,0:T(8,128)S(1)}, f32[384,1536]{1,0:T(8,128)S(1)}, f32[384,256]{1,0:T(8,128)S(1)}, f32[8,512]{1,0:T(8,128)S(1)}) custom-call(s32[16]{0:T(128)S(1)} %pad_add_fusion.order_ref, bf16[400,512]{1,0:T(8,128)(2,1)S(1)} %prepare.1.refs_0_, bf16[400,512]{1,0:T(8,128)(2,1)S(1)} %collective-permute-done.2.refs_1_, ...), custom_call_target="tpu_custom_call" | custom-call | flops 327155712 | bytes 851968 | tf_op jit(solution)/shard_map/gate_up/pallas_call | solution.py:144
  13.1 2.0 %collective-permute-done.1.refs_1_ = bf16[400,512]{1,0:T(8,128)(2,1)S(1)} collective-permute-done((bf16[400,512]{1,0:T(8,128)(2,1)S(1)}, bf16[400,512]{1,0:T(8,128)(2,1)S(1)}, u32[]{:S(2)}, u32[]{:S(2)}) %collective-permute-start.1) | collective-permute-done | bytes 409632 | tf_op jit(solution)/shard_map/ppermute | solution.py:29
  15.1 1.5 %collective-permute-done.refs_0_ = bf16[400,512]{1,0:T(8,128)(2,1)S(1)} collective-permute-done((bf16[400,512]{1,0:T(8,128)(2,1)S(1)}, bf16[400,512]{1,0:T(8,128)(2,1)S(1)}, u32[]{:S(2)}, u32[]{:S(2)}) %collective-permute-start) | collective-permute-done | bytes 409632 | tf_op jit(solution)/shard_map/ppermute | solution.py:29
  18.5 1.6 %collective-permute-start.3 = (bf16[400,512]{1,0:T(8,128)(2,1)S(1)}, bf16[400,512]{1,0:T(8,128)(2,1)S(1)}, u32[]{:S(2)}, u32[]{:S(2)}) collective-permute-start(bf16[400,512]{1,0:T(8,128)(2,1)S(1)} %collective-permute-done.1.refs_1_), channel_id=1, source_target_pairs={{0,4},{1,5},{2,6},{3,7},{4,0},{5,1},{6,2},{7,3},{8,12},{9,13},{10,... | collective-permute-start | bytes 1228808 | tf_op jit(solution)/shard_map/ppermute | solution.py:29
  20.1 9.5 %gate_up.6 = (f32[384,1536]{1,0:T(8,128)S(1)}, f32[384,1536]{1,0:T(8,128)S(1)}, f32[384,256]{1,0:T(8,128)S(1)}, f32[8,512]{1,0:T(8,128)S(1)}) custom-call(s32[16]{0:T(128)S(1)} %pad_add_fusion.order_ref, bf16[400,512]{1,0:T(8,128)(2,1)S(1)} %collective-permute-done.refs_0_, bf16[400,512]{1,0:T(8,128)(2,1)S(1)} %collective-permute-done.1.refs_1_, ...), custom_call_target="tpu_custom_call" | custom-call | flops 654311424 | bytes 1703936 | tf_op jit(solution)/shard_map/gate_up/pallas_call | solution.py:144
  30.9 1.5 %collective-permute-start.7 = (bf16[400,512]{1,0:T(8,128)(2,1)S(1)}, bf16[400,512]{1,0:T(8,128)(2,1)S(1)}, u32[]{:S(2)}, u32[]{:S(2)}) collective-permute-start(bf16[400,512]{1,0:T(8,128)(2,1)S(1)} %collective-permute-done.4.refs_1_), channel_id=1, source_target_pairs={{0,4},{1,5},{2,6},{3,7},{4,0},{5,1},{6,2},{7,3},{8,12},{9,13},{10,... | collective-permute-start | bytes 1228808 | tf_op jit(solution)/shard_map/ppermute | solution.py:29
  32.4 9.6 %gate_up.7 = (f32[384,1536]{1,0:T(8,128)S(1)}, f32[384,1536]{1,0:T(8,128)S(1)}, f32[384,256]{1,0:T(8,128)S(1)}, f32[8,512]{1,0:T(8,128)S(1)}) custom-call(s32[16]{0:T(128)S(1)} %pad_add_fusion.order_ref, bf16[400,512]{1,0:T(8,128)(2,1)S(1)} %collective-permute-done.3.refs_0_, bf16[400,512]{1,0:T(8,128)(2,1)S(1)} %collective-permute-done.4.refs_1_, ...), custom_call_target="tpu_custom_call" | custom-call | flops 654311424 | bytes 1703936 | tf_op jit(solution)/shard_map/gate_up/pallas_call | solution.py:144
  42.6 1.5 %collective-permute-start.11 = (bf16[400,512]{1,0:T(8,128)(2,1)S(1)}, bf16[400,512]{1,0:T(8,128)(2,1)S(1)}, u32[]{:S(2)}, u32[]{:S(2)}) collective-permute-start(bf16[400,512]{1,0:T(8,128)(2,1)S(1)} %broadcast_select_fusion), channel_id=1, source_target_pairs={{0,2},{1,3},{2,0},{3,1},{4,6},{5,7},{6,4},{7,5},{8,10},{9,11},{10,... | collective-permute-start | bytes 1228808 | tf_op jit(solution)/shard_map/ppermute | solution.py:29
  44.4 9.4 %gate_up.8 = (f32[384,1536]{1,0:T(8,128)S(1)}, f32[384,1536]{1,0:T(8,128)S(1)}, f32[384,256]{1,0:T(8,128)S(1)}, f32[8,512]{1,0:T(8,128)S(1)}) custom-call(s32[16]{0:T(128)S(1)} %pad_add_fusion.order_ref, bf16[400,512]{1,0:T(8,128)(2,1)S(1)} %collective-permute-done.7.refs_0_, bf16[400,512]{1,0:T(8,128)(2,1)S(1)} %collective-permute-done.8.refs_1_, ...), custom_call_target="tpu_custom_call" | custom-call | flops 654311424 | bytes 1703936 | tf_op jit(solution)/shard_map/gate_up/pallas_call | solution.py:144
  54.1 1.7 %collective-permute-done.14.refs_1_ = bf16[400,512]{1,0:T(8,128)(2,1)S(1)} collective-permute-done((bf16[400,512]{1,0:T(8,128)(2,1)S(1)}, bf16[400,512]{1,0:T(8,128)(2,1)S(1)}, u32[]{:S(2)}, u32[]{:S(2)}) %collective-permute-start.14) | collective-permute-done | bytes 409632 | tf_op jit(solution)/shard_map/ppermute | solution.py:33
  55.9 6.3 %gate_up.9.hidden_ref = bf16[384,1664]{1,0:T(8,128)(2,1)S(1)} custom-call(s32[16]{0:T(128)S(1)} %pad_add_fusion.order_ref, bf16[400,512]{1,0:T(8,128)(2,1)S(1)} %collective-permute-done.11.refs_0_, bf16[400,512]{1,0:T(8,128)(2,1)S(1)} %collective-permute-done.14.refs_1_, bf16[8192,1664]{1,0:T(8,128)(2,1)} %refs_2_.3, bf16[8192,1664]{1,0:T(8,128)(2,1)} %refs_3_.3, ...), custom_call_target="tpu_custom_call" | custom-call | flops 327155712 | bytes 851968 | tf_op jit(solution)/shard_map/gate_up/pallas_call | solution.py:144
  62.2 2.9 %down.7 = bf16[384,512]{1,0:T(8,128)(2,1)S(1)} custom-call(s32[16]{0:T(128)S(1)} %pad_add_fusion.order_ref, bf16[384,1664]{1,0:T(8,128)(2,1)S(1)} %gate_up.9.hidden_ref, bf16[1664,8192]{1,0:T(8,128)(2,1)} %weight_ref.11), custom_call_target="tpu_custom_call" | custom-call | flops 81788928 | bytes 212992 | tf_op jit(solution)/shard_map/down/pallas_call | solution.py:191
  65.2 5.3 %down.6 = (f32[384,512]{1,0:T(8,128)S(1)}, bf16[384,512]{1,0:T(8,128)(2,1)S(1)}, bf16[384,512]{1,0:T(8,128)(2,1)S(1)}) custom-call(s32[16]{0:T(128)S(1)} %pad_add_fusion.order_ref, bf16[384,1664]{1,0:T(8,128)(2,1)S(1)} %gate_up.9.hidden_ref, bf16[1664,8192]{1,0:T(8,128)(2,1)} %weight_ref.11), custom_call_target="tpu_custom_call" | custom-call | flops 245366784 | bytes 638976 | tf_op jit(solution)/shard_map/down/pallas_call | solution.py:191
  71.2 1.5 %collective-permute-start.17 = (bf16[384,512]{1,0:T(8,128)(2,1)S(1)}, bf16[384,512]{1,0:T(8,128)(2,1)S(1)}, u32[]{:S(2)}, u32[]{:S(2)}) collective-permute-start(bf16[384,512]{1,0:T(8,128)(2,1)S(1)} %add_convert_fusion.3), channel_id=1, source_target_pairs={{0,2},{1,3},{2,0},{3,1},{4,6},{5,7},{6,4},{7,5},{8,10},{9,11},{10,... | collective-permute-start | bytes 1179656 | tf_op jit(solution)/shard_map/ppermute | solution.py:29
  72.7 6.4 %down.8 = (f32[384,512]{1,0:T(8,128)S(1)}, f32[384,512]{1,0:T(8,128)S(1)}, bf16[384,512]{1,0:T(8,128)(2,1)S(1)}, bf16[384,512]{1,0:T(8,128)(2,1)S(1)}) custom-call(s32[16]{0:T(128)S(1)} %pad_add_fusion.order_ref, bf16[384,1664]{1,0:T(8,128)(2,1)S(1)} %gate_up.9.hidden_ref, bf16[1664,8192]{1,0:T(8,128)(2,1)} %weight_ref.11), custom_call_target="tpu_custom_call" | custom-call | flops 327155712 | bytes 851968 | tf_op jit(solution)/shard_map/down/pallas_call | solution.py:191
  80.5 2.8 %collective-permute-done.17 = bf16[384,512]{1,0:T(8,128)(2,1)S(1)} collective-permute-done((bf16[384,512]{1,0:T(8,128)(2,1)S(1)}, bf16[384,512]{1,0:T(8,128)(2,1)S(1)}, u32[]{:S(2)}, u32[]{:S(2)}) %collective-permute-start.17) | collective-permute-done | bytes 393248 | tf_op jit(solution)/shard_map/ppermute | solution.py:29
  84.8 6.4 %down.9 = (f32[384,512]{1,0:T(8,128)S(1)}, f32[384,512]{1,0:T(8,128)S(1)}, bf16[384,512]{1,0:T(8,128)(2,1)S(1)}, bf16[384,512]{1,0:T(8,128)(2,1)S(1)}) custom-call(s32[16]{0:T(128)S(1)} %pad_add_fusion.order_ref, bf16[384,1664]{1,0:T(8,128)(2,1)S(1)} %gate_up.9.hidden_ref, bf16[1664,8192]{1,0:T(8,128)(2,1)} %weight_ref.11), custom_call_target="tpu_custom_call" | custom-call | flops 327155712 | bytes 851968 | tf_op jit(solution)/shard_map/down/pallas_call | solution.py:191
  95.2 5.3 %down.10 = (f32[384,512]{1,0:T(8,128)S(1)}, f32[384,512]{1,0:T(8,128)S(1)}, bf16[384,512]{1,0:T(8,128)(2,1)S(1)}) custom-call(s32[16]{0:T(128)S(1)} %pad_add_fusion.order_ref, bf16[384,1664]{1,0:T(8,128)(2,1)S(1)} %gate_up.9.hidden_ref, bf16[1664,8192]{1,0:T(8,128)(2,1)} %weight_ref.11), custom_call_target="tpu_custom_call" | custom-call | flops 245366784 | bytes 638976 | tf_op jit(solution)/shard_map/down/pallas_call | solution.py:191
  103.6 2.0 %collective-permute-done.24 = bf16[384,512]{1,0:T(8,128)(2,1)S(1)} collective-permute-done((bf16[384,512]{1,0:T(8,128)(2,1)S(1)}, bf16[384,512]{1,0:T(8,128)(2,1)S(1)}, u32[]{:S(2)}, u32[]{:S(2)}) %collective-permute-start.24) | collective-permute-done | bytes 393248 | tf_op jit(solution)/shard_map/ppermute | solution.py:29
  107.3 2.9 %down.11 = f32[384,512]{1,0:T(8,128)S(1)} custom-call(s32[16]{0:T(128)S(1)} %pad_add_fusion.order_ref, bf16[384,1664]{1,0:T(8,128)(2,1)S(1)} %gate_up.9.hidden_ref, bf16[1664,8192]{1,0:T(8,128)(2,1)} %weight_ref.11), custom_call_target="tpu_custom_call" | custom-call | flops 81788928 | bytes 212992 | tf_op jit(solution)/shard_map/down/pallas_call | solution.py:191
  110.1 2.8 %collective-permute-done.29 = bf16[384,512]{1,0:T(8,128)(2,1)S(1)} collective-permute-done((bf16[384,512]{1,0:T(8,128)(2,1)S(1)}, bf16[384,512]{1,0:T(8,128)(2,1)S(1)}, u32[]{:S(2)}, u32[]{:S(2)}) %collective-permute-start.29) | collective-permute-done | bytes 393248 | tf_op jit(solution)/shard_map/ppermute | solution.py:29
  113.0 2.5 %collective-permute-done.28 = bf16[384,512]{1,0:T(8,128)(2,1)S(1)} collective-permute-done((bf16[384,512]{1,0:T(8,128)(2,1)S(1)}, bf16[384,512]{1,0:T(8,128)(2,1)S(1)}, u32[]{:S(2)}, u32[]{:S(2)}) %collective-permute-start.28) | collective-permute-done | bytes 393248 | tf_op jit(solution)/shard_map/ppermute | solution.py:29
  (66 shorter events, 21.1 us)
Async XLA Ops:
  1.9 5.5 %collective-permute-start.2 = (bf16[400,512]{1,0:T(8,128)(2,1)S(1)}, bf16[400,512]{1,0:T(8,128)(2,1)S(1)}, u32[]{:S(2)}, u32[]{:S(2)}) collective-permute-start(bf16[400,512]{1,0:T(8,128)(2,1)S(1)} %prepare.1.refs_0_), channel_id=1, source_target_pairs={{0,1},{1,0},{2,3},{3,2},{4,5},{5,4},{6,7},{7,6},{8,9},{9,8},{10,11... | collective-permute-start | bytes 1228808 | tf_op jit(solution)/shard_map/ppermute | solution.py:33
  2.4 12.7 %collective-permute-start.1 = (bf16[400,512]{1,0:T(8,128)(2,1)S(1)}, bf16[400,512]{1,0:T(8,128)(2,1)S(1)}, u32[]{:S(2)}, u32[]{:S(2)}) collective-permute-start(bf16[400,512]{1,0:T(8,128)(2,1)S(1)} %prepare.1.refs_0_), channel_id=1, source_target_pairs={{0,2},{1,3},{2,0},{3,1},{4,8},{5,9},{6,10},{7,11},{8,4},{9,5},{10,... | collective-permute-start | bytes 1228808 | tf_op jit(solution)/shard_map/ppermute | solution.py:29
  5.0 11.5 %collective-permute-start = (bf16[400,512]{1,0:T(8,128)(2,1)S(1)}, bf16[400,512]{1,0:T(8,128)(2,1)S(1)}, u32[]{:S(2)}, u32[]{:S(2)}) collective-permute-start(bf16[400,512]{1,0:T(8,128)(2,1)S(1)} %prepare.1.refs_0_), channel_id=1, source_target_pairs={{0,4},{1,5},{2,6},{3,7},{4,0},{5,1},{6,2},{7,3},{8,12},{9,13},{10,... | collective-permute-start | bytes 1228808 | tf_op jit(solution)/shard_map/ppermute | solution.py:29
  16.6 3.5 %collective-permute-start.5 = (bf16[400,512]{1,0:T(8,128)(2,1)S(1)}, bf16[400,512]{1,0:T(8,128)(2,1)S(1)}, u32[]{:S(2)}, u32[]{:S(2)}) collective-permute-start(bf16[400,512]{1,0:T(8,128)(2,1)S(1)} %collective-permute-done.refs_0_), channel_id=1, source_target_pairs={{0,1},{1,0},{2,3},{3,2},{4,5},{5,4},{6,7},{7,6},{8,9},{9,8},{10,11... | collective-permute-start | bytes 1228808 | tf_op jit(solution)/shard_map/ppermute | solution.py:33
  17.1 12.5 %collective-permute-start.4 = (bf16[400,512]{1,0:T(8,128)(2,1)S(1)}, bf16[400,512]{1,0:T(8,128)(2,1)S(1)}, u32[]{:S(2)}, u32[]{:S(2)}) collective-permute-start(bf16[400,512]{1,0:T(8,128)(2,1)S(1)} %collective-permute-done.refs_0_), channel_id=1, source_target_pairs={{0,2},{1,3},{2,0},{3,1},{4,8},{5,9},{6,10},{7,11},{8,4},{9,5},{10,... | collective-permute-start | bytes 1228808 | tf_op jit(solution)/shard_map/ppermute | solution.py:29
  18.5 11.1 %collective-permute-start.3 = (bf16[400,512]{1,0:T(8,128)(2,1)S(1)}, bf16[400,512]{1,0:T(8,128)(2,1)S(1)}, u32[]{:S(2)}, u32[]{:S(2)}) collective-permute-start(bf16[400,512]{1,0:T(8,128)(2,1)S(1)} %collective-permute-done.1.refs_1_), channel_id=1, source_target_pairs={{0,4},{1,5},{2,6},{3,7},{4,0},{5,1},{6,2},{7,3},{8,12},{9,13},{10,... | collective-permute-start | bytes 1228808 | tf_op jit(solution)/shard_map/ppermute | solution.py:29
  30.2 11.8 %collective-permute-start.8 = (bf16[400,512]{1,0:T(8,128)(2,1)S(1)}, bf16[400,512]{1,0:T(8,128)(2,1)S(1)}, u32[]{:S(2)}, u32[]{:S(2)}) collective-permute-start(bf16[400,512]{1,0:T(8,128)(2,1)S(1)} %broadcast_select_fusion.1), channel_id=1, source_target_pairs={{0,2},{1,3},{2,0},{3,1},{4,6},{5,7},{6,4},{7,5},{8,10},{9,11},{10,... | collective-permute-start | bytes 1228808 | tf_op jit(solution)/shard_map/ppermute | solution.py:29
  30.9 11.2 %collective-permute-start.7 = (bf16[400,512]{1,0:T(8,128)(2,1)S(1)}, bf16[400,512]{1,0:T(8,128)(2,1)S(1)}, u32[]{:S(2)}, u32[]{:S(2)}) collective-permute-start(bf16[400,512]{1,0:T(8,128)(2,1)S(1)} %collective-permute-done.4.refs_1_), channel_id=1, source_target_pairs={{0,4},{1,5},{2,6},{3,7},{4,0},{5,1},{6,2},{7,3},{8,12},{9,13},{10,... | collective-permute-start | bytes 1228808 | tf_op jit(solution)/shard_map/ppermute | solution.py:29
  42.6 11.5 %collective-permute-start.11 = (bf16[400,512]{1,0:T(8,128)(2,1)S(1)}, bf16[400,512]{1,0:T(8,128)(2,1)S(1)}, u32[]{:S(2)}, u32[]{:S(2)}) collective-permute-start(bf16[400,512]{1,0:T(8,128)(2,1)S(1)} %broadcast_select_fusion), channel_id=1, source_target_pairs={{0,2},{1,3},{2,0},{3,1},{4,6},{5,7},{6,4},{7,5},{8,10},{9,11},{10,... | collective-permute-start | bytes 1228808 | tf_op jit(solution)/shard_map/ppermute | solution.py:29
  65.0 6.1 %collective-permute-start.15 = (bf16[384,512]{1,0:T(8,128)(2,1)S(1)}, bf16[384,512]{1,0:T(8,128)(2,1)S(1)}, u32[]{:S(2)}, u32[]{:S(2)}) collective-permute-start(bf16[384,512]{1,0:T(8,128)(2,1)S(1)} %down.7), channel_id=1, source_target_pairs={{0,1},{1,0},{2,3},{3,2},{4,5},{5,4},{6,7},{7,6},{8,9},{9,8},{10,11... | collective-permute-start | bytes 1179656 | tf_op jit(solution)/shard_map/ppermute | solution.py:33
  70.5 8.6 %collective-permute-start.18 = (bf16[384,512]{1,0:T(8,128)(2,1)S(1)}, bf16[384,512]{1,0:T(8,128)(2,1)S(1)}, u32[]{:S(2)}, u32[]{:S(2)}) collective-permute-start(bf16[384,512]{1,0:T(8,128)(2,1)S(1)} %get-tuple-element.74), channel_id=1, source_target_pairs={{0,1},{1,0},{2,3},{3,2},{4,5},{5,4},{6,7},{7,6},{8,9},{9,8},{10,11... | collective-permute-start | bytes 1179656 | tf_op jit(solution)/shard_map/ppermute | solution.py:33
  71.0 9.5 %collective-permute-start.16 = (bf16[384,512]{1,0:T(8,128)(2,1)S(1)}, bf16[384,512]{1,0:T(8,128)(2,1)S(1)}, u32[]{:S(2)}, u32[]{:S(2)}) collective-permute-start(bf16[384,512]{1,0:T(8,128)(2,1)S(1)} %get-tuple-element.72), channel_id=1, source_target_pairs={{0,1},{1,0},{2,3},{3,2},{4,5},{5,4},{6,7},{7,6},{8,9},{9,8},{10,11... | collective-permute-start | bytes 1179656 | tf_op jit(solution)/shard_map/ppermute | solution.py:33
  71.2 12.0 %collective-permute-start.17 = (bf16[384,512]{1,0:T(8,128)(2,1)S(1)}, bf16[384,512]{1,0:T(8,128)(2,1)S(1)}, u32[]{:S(2)}, u32[]{:S(2)}) collective-permute-start(bf16[384,512]{1,0:T(8,128)(2,1)S(1)} %add_convert_fusion.3), channel_id=1, source_target_pairs={{0,2},{1,3},{2,0},{3,1},{4,6},{5,7},{6,4},{7,5},{8,10},{9,11},{10,... | collective-permute-start | bytes 1179656 | tf_op jit(solution)/shard_map/ppermute | solution.py:29
  79.3 11.9 %collective-permute-start.20 = (bf16[384,512]{1,0:T(8,128)(2,1)S(1)}, bf16[384,512]{1,0:T(8,128)(2,1)S(1)}, u32[]{:S(2)}, u32[]{:S(2)}) collective-permute-start(bf16[384,512]{1,0:T(8,128)(2,1)S(1)} %add_convert_fusion.2), channel_id=1, source_target_pairs={{0,2},{1,3},{2,0},{3,1},{4,6},{5,7},{6,4},{7,5},{8,10},{9,11},{10,... | collective-permute-start | bytes 1179656 | tf_op jit(solution)/shard_map/ppermute | solution.py:29
  79.9 11.3 %collective-permute-start.19 = (bf16[384,512]{1,0:T(8,128)(2,1)S(1)}, bf16[384,512]{1,0:T(8,128)(2,1)S(1)}, u32[]{:S(2)}, u32[]{:S(2)}) collective-permute-start(bf16[384,512]{1,0:T(8,128)(2,1)S(1)} %get-tuple-element.77), channel_id=1, source_target_pairs={{0,1},{1,0},{2,3},{3,2},{4,5},{5,4},{6,7},{7,6},{8,9},{9,8},{10,11... | collective-permute-start | bytes 1179656 | tf_op jit(solution)/shard_map/ppermute | solution.py:33
  79.9 13.3 %collective-permute-start.21 = (bf16[384,512]{1,0:T(8,128)(2,1)S(1)}, bf16[384,512]{1,0:T(8,128)(2,1)S(1)}, u32[]{:S(2)}, u32[]{:S(2)}) collective-permute-start(bf16[384,512]{1,0:T(8,128)(2,1)S(1)} %get-tuple-element.79), channel_id=1, source_target_pairs={{0,1},{1,0},{2,3},{3,2},{4,5},{5,4},{6,7},{7,6},{8,9},{9,8},{10,11... | collective-permute-start | bytes 1179656 | tf_op jit(solution)/shard_map/ppermute | solution.py:33
  83.4 10.1 %collective-permute-start.22 = (bf16[384,512]{1,0:T(8,128)(2,1)S(1)}, bf16[384,512]{1,0:T(8,128)(2,1)S(1)}, u32[]{:S(2)}, u32[]{:S(2)}) collective-permute-start(bf16[384,512]{1,0:T(8,128)(2,1)S(1)} %fusion.1), channel_id=1, source_target_pairs={{0,4},{1,5},{2,6},{3,7},{4,0},{5,1},{6,2},{7,3},{8,12},{9,13},{10,... | collective-permute-start | bytes 1179656 | tf_op jit(solution)/shard_map/ppermute | solution.py:29
  91.4 10.5 %collective-permute-start.26 = (bf16[384,512]{1,0:T(8,128)(2,1)S(1)}, bf16[384,512]{1,0:T(8,128)(2,1)S(1)}, u32[]{:S(2)}, u32[]{:S(2)}) collective-permute-start(bf16[384,512]{1,0:T(8,128)(2,1)S(1)} %fusion.6), channel_id=1, source_target_pairs={{0,4},{1,5},{2,6},{3,7},{4,0},{5,1},{6,2},{7,3},{8,12},{9,13},{10,... | collective-permute-start | bytes 1179656 | tf_op jit(solution)/shard_map/ppermute | solution.py:29
  92.7 9.3 %collective-permute-start.25 = (bf16[384,512]{1,0:T(8,128)(2,1)S(1)}, bf16[384,512]{1,0:T(8,128)(2,1)S(1)}, u32[]{:S(2)}, u32[]{:S(2)}) collective-permute-start(bf16[384,512]{1,0:T(8,128)(2,1)S(1)} %get-tuple-element.84), channel_id=1, source_target_pairs={{0,1},{1,0},{2,3},{3,2},{4,5},{5,4},{6,7},{7,6},{8,9},{9,8},{10,11... | collective-permute-start | bytes 1179656 | tf_op jit(solution)/shard_map/ppermute | solution.py:33
  92.7 10.9 %collective-permute-start.23 = (bf16[384,512]{1,0:T(8,128)(2,1)S(1)}, bf16[384,512]{1,0:T(8,128)(2,1)S(1)}, u32[]{:S(2)}, u32[]{:S(2)}) collective-permute-start(bf16[384,512]{1,0:T(8,128)(2,1)S(1)} %get-tuple-element.82), channel_id=1, source_target_pairs={{0,1},{1,0},{2,3},{3,2},{4,5},{5,4},{6,7},{7,6},{8,9},{9,8},{10,11... | collective-permute-start | bytes 1179656 | tf_op jit(solution)/shard_map/ppermute | solution.py:33
  93.8 11.9 %collective-permute-start.24 = (bf16[384,512]{1,0:T(8,128)(2,1)S(1)}, bf16[384,512]{1,0:T(8,128)(2,1)S(1)}, u32[]{:S(2)}, u32[]{:S(2)}) collective-permute-start(bf16[384,512]{1,0:T(8,128)(2,1)S(1)} %fusion.4), channel_id=1, source_target_pairs={{0,2},{1,3},{2,0},{3,1},{4,8},{5,9},{6,10},{7,11},{8,4},{9,5},{10,... | collective-permute-start | bytes 1179656 | tf_op jit(solution)/shard_map/ppermute | solution.py:29
  102.2 10.8 %collective-permute-start.29 = (bf16[384,512]{1,0:T(8,128)(2,1)S(1)}, bf16[384,512]{1,0:T(8,128)(2,1)S(1)}, u32[]{:S(2)}, u32[]{:S(2)}) collective-permute-start(bf16[384,512]{1,0:T(8,128)(2,1)S(1)} %fusion.9), channel_id=1, source_target_pairs={{0,2},{1,3},{2,0},{3,1},{4,8},{5,9},{6,10},{7,11},{8,4},{9,5},{10,... | collective-permute-start | bytes 1179656 | tf_op jit(solution)/shard_map/ppermute | solution.py:29
  103.6 9.3 %collective-permute-start.27 = (bf16[384,512]{1,0:T(8,128)(2,1)S(1)}, bf16[384,512]{1,0:T(8,128)(2,1)S(1)}, u32[]{:S(2)}, u32[]{:S(2)}) collective-permute-start(bf16[384,512]{1,0:T(8,128)(2,1)S(1)} %get-tuple-element.86), channel_id=1, source_target_pairs={{0,1},{1,0},{2,3},{3,2},{4,5},{5,4},{6,7},{7,6},{8,9},{9,8},{10,11... | collective-permute-start | bytes 1179656 | tf_op jit(solution)/shard_map/ppermute | solution.py:33
  105.8 9.6 %collective-permute-start.28 = (bf16[384,512]{1,0:T(8,128)(2,1)S(1)}, bf16[384,512]{1,0:T(8,128)(2,1)S(1)}, u32[]{:S(2)}, u32[]{:S(2)}) collective-permute-start(bf16[384,512]{1,0:T(8,128)(2,1)S(1)} %add_convert_fusion.1), channel_id=1, source_target_pairs={{0,4},{1,5},{2,6},{3,7},{4,0},{5,1},{6,2},{7,3},{8,12},{9,13},{10,... | collective-permute-start | bytes 1179656 | tf_op jit(solution)/shard_map/ppermute | solution.py:29
  (9 other events, 26.6 us)

commit v8 on v7

--- a/solution.py
+++ b/solution.py
@@ -12,6 +12,7 @@
 LINE = 4
 EXTRA = 16
 VMEM_LIMIT = 36 * 1024 * 1024
+PREPARE_LIMIT = 60 * 1024 * 1024
 
 ALONG = (lambda z, y: (z ^ 1, y),) * 2
 INSIDE = (lambda z, y: (z, y ^ 1), lambda z, y: (z ^ 3, y))
@@ -37,18 +38,24 @@
     return lax.optimization_barrier((x, *others))[0]
 
 
-def pick(table, s):
-    value = jnp.int32(table[0])
-    for i, entry in enumerate(table[1:], 1):
-        value = jnp.where(s == i, jnp.int32(entry), value)
-    return value
+def block(me, jobs, s):
+    def pick(table):
+        value = jnp.int32(table[0])
+        for i, entry in enumerate(table[1:], 1):
+            value = jnp.where(s == i, jnp.int32(entry), value)
+        return value
+
+    places, others = zip(*jobs)
+    end = (((me >> 2) ^ (me >> 3)) & 1) == 0
+    code = jnp.where(end, pick(TAKEN[0, places]), pick(TAKEN[1, places]))
+    return ((me >> 1) ^ code) * 2 + ((me & 1) ^ pick(others))
 
 
 def prepare_body(x_ref, gain_ref, out_ref):
     rows, width = x_ref.shape
     x = x_ref[...].astype(jnp.float32)
     gain = gain_ref[...].astype(jnp.float32).reshape(1, width)
-    out_ref[:rows, :] = (x * gain).astype(jnp.bfloat16)
+    out_ref[0, :rows, :] = (x * gain).astype(jnp.bfloat16)
     squares = jnp.broadcast_to(jnp.sum(x * x, axis=1, keepdims=True), (rows, 128)).T[:EXTRA]
     row = lax.broadcasted_iota(jnp.int32, (EXTRA, rows), 0)
     parts = jnp.zeros((EXTRA, rows), jnp.float32)
@@ -56,22 +63,22 @@
         part = squares.astype(jnp.bfloat16).astype(jnp.float32)
         parts = jnp.where(row == i, part, parts)
         squares = squares - part
-    out_ref[rows:, :rows] = parts.astype(jnp.bfloat16)
+    out_ref[0, rows:, :rows] = parts.astype(jnp.bfloat16)
     if rows < width:
-        out_ref[rows:, rows:] = jnp.zeros((EXTRA, width - rows), jnp.bfloat16)
+        out_ref[0, rows:, rows:] = jnp.zeros((EXTRA, width - rows), jnp.bfloat16)
 
 
 def prepare(activations, norm_gain):
     rows, width = activations.shape
     return pl.pallas_call(
         prepare_body,
-        out_shape=jax.ShapeDtypeStruct((rows + EXTRA, width), jnp.bfloat16),
-        compiler_params=pltpu.CompilerParams(vmem_limit_bytes=VMEM_LIMIT),
+        out_shape=jax.ShapeDtypeStruct((1, rows + EXTRA, width), jnp.bfloat16),
+        compiler_params=pltpu.CompilerParams(vmem_limit_bytes=PREPARE_LIMIT),
         name="prepare",
     )(activations, norm_gain)
 
 
-def gate_up_body(count, first, last, rows, main, features, order_ref, *refs):
+def gate_up_body(count, first, last, rows, main, features, me_ref, *refs):
     blocks = refs[:count]
     gate_ref, up_ref, *rest = refs[count:]
     if not first:
@@ -86,14 +93,14 @@
 
         @pl.when(step == s)
         def _(s=s):
-            x = blocks[s][:rows, :]
+            x = blocks[s][0, :rows, :]
             gate, up = gate_ref[...], up_ref[...]
             mixed = jnp.concatenate([gate[:, main:], up[:, main:]], axis=1)
             values = [
                 jnp.dot(x, weight, preferred_element_type=jnp.float32)
                 for weight in (gate[:, :main], up[:, :main], mixed)
             ]
-            squares = blocks[s][rows:, :].astype(jnp.float32)
+            squares = blocks[s][0, rows:, :].astype(jnp.float32)
             squares = jnp.sum(squares, axis=0, keepdims=True)
             values.append(jnp.broadcast_to(squares, accs[3].shape))
             if s:
@@ -117,18 +124,19 @@
             hidden_ref[:, main:] = act(both[:, :rem], both[:, rem:])
 
 
-def gate_up(order, places, blocks, gate_weight, up_weight, acc, last=False):
-    height, depth = blocks[0].shape
-    count = len(blocks)
+def gate_up(me, jobs, shards, gate_weight, up_weight, acc, last=False):
+    height, depth = shards[0][0].shape[1:]
+    count = len(jobs)
     rows = height - EXTRA
     features, ff = gate_weight.shape
     main = ff // 256 * 256 if ff % 256 else ff - 256
     rem = ff - main
     first = acc is None
-    whole = lambda shape: pl.BlockSpec(shape, lambda s, order: (0, 0))
-    weight = pl.BlockSpec((depth, ff), lambda s, order: (order[pick(places, s)], 0))
-    in_specs = [whole(b.shape) for b in blocks] + [weight, weight]
-    args = [*blocks, gate_weight, up_weight]
+    whole = lambda shape: pl.BlockSpec(shape, lambda s, me: (0, 0))
+    weight = pl.BlockSpec((depth, ff), lambda s, me: (block(me[0], jobs, s), 0))
+    shard = lambda i: pl.BlockSpec((1, height, depth), lambda s, me: (i, 0, 0))
+    in_specs = [shard(i) for _, i in shards] + [weight, weight]
+    args = [*(x for x, _ in shards), gate_weight, up_weight]
     shapes = [(rows, main), (rows, main), (rows, 2 * rem), (8, depth)]
     if not first:
         in_specs += [whole(s) for s in shapes]
@@ -158,7 +166,7 @@
             transcendentals=0,
         ),
         name="gate_up",
-    )(order, *args)
+    )(me, *args)
 
 
 def down_block(hidden_ref, weight_ref):
@@ -174,119 +182,112 @@
     return value
 
 
-def down_body(kinds, order_ref, hidden_ref, weight_ref, *outs):
+def down_body(kept, sent, me_ref, hidden_ref, weight_ref, *outs):
     now = pl.program_id(0)
     value = down_block(hidden_ref, weight_ref)
-    for s, kind in enumerate(kinds):
+    for s in range(kept):
 
         @pl.when(now == s)
-        def _(out=outs[s], kind=kind):
-            out[...] = value.astype(out.dtype)
-
-
-def down(order, jobs, hidden, down_weight, width):
+        def _(out=outs[s]):
+            out[...] = value
+
+    for s in range(kept, kept + sent):
+
+        @pl.when(now == s)
+        def _(out=outs[s]):
+            out[...] = value.astype(jnp.bfloat16)
+
+
+def down(me, kept, sent, hidden, down_weight, width):
     rows, ff = hidden.shape
-    count = len(jobs)
-    places, kinds = zip(*jobs)
+    jobs = kept + sent
+    kinds = [jnp.float32] * len(kept) + [jnp.bfloat16] * len(sent)
     return pl.pallas_call(
-        functools.partial(down_body, kinds),
+        functools.partial(down_body, len(kept), len(sent)),
         grid_spec=pltpu.PrefetchScalarGridSpec(
             num_scalar_prefetch=1,
-            grid=(count,),
+            grid=(len(jobs),),
             in_specs=[
-                pl.BlockSpec((rows, ff), lambda s, order: (0, 0)),
-                pl.BlockSpec((ff, width), lambda s, order: (0, order[pick(places, s)])),
+                pl.BlockSpec((rows, ff), lambda s, me: (0, 0)),
+                pl.BlockSpec((ff, width), lambda s, me: (0, block(me[0], jobs, s))),
             ],
-            out_specs=[pl.BlockSpec((rows, width), lambda s, order: (0, 0))] * count,
+            out_specs=[pl.BlockSpec((rows, width), lambda s, me: (0, 0))] * len(jobs),
         ),
         out_shape=[jax.ShapeDtypeStruct((rows, width), kind) for kind in kinds],
         compiler_params=pltpu.CompilerParams(vmem_limit_bytes=VMEM_LIMIT),
         cost_estimate=pl.CostEstimate(
-            flops=rows * ff * width * count // 4,
-            bytes_accessed=ff * width * count // 4,
+            flops=rows * ff * width * len(jobs) // 4,
+            bytes_accessed=ff * width * len(jobs) // 4,
             transcendentals=0,
         ),
         name="down",
-    )(order, hidden, down_weight)
+    )(me, hidden, down_weight)
 
 
 def overlapped(activations, norm_gain, gate_weight, up_weight, down_weight):
     width = activations.shape[1]
     index = lax.axis_index("gx").astype(jnp.int32)
+    me = index[None]
     z = index >> 2
     end = (z == 0) | (z == LINE - 1)
     resident = activations.astype(jnp.float32)
-
-    taken = jnp.where(end, jnp.asarray(TAKEN[0]), jnp.asarray(TAKEN[1]))
-    order = ((index >> 1) ^ taken) * 2 + (index & 1)
-    order = jnp.concatenate([order, order ^ 1])
     OWN, ONE, ONE_IN, TWO, TWO_IN, THREE, THREE_ACROSS, FOUR = range(8)
 
-    def multiply(acc, *shards, last=False):
-        places = [place + 8 * other for place, other, _ in shards]
-        blocks = [x for _, _, x in shards]
-        return gate_up(order, places, blocks, gate_weight, up_weight, acc, last)
+    def multiply(acc, places, shards, last=False):
+        theirs = swap(shards[0] if len(shards) == 1 else jnp.concatenate(shards))
+        jobs = [(place, 0) for place in places] + [(place, 1) for place in places]
+        arrays = [(x, 0) for x in shards] + [(theirs, i) for i in range(len(places))]
+        return gate_up(me, jobs, arrays, gate_weight, up_weight, acc, last)
 
     own = prepare(activations, norm_gain)
     one, one_in = send(own, ALONG), send(own, INSIDE)
-    acc = multiply(None, (OWN, 0, own), (OWN, 1, swap(own)))
+    acc = multiply(None, (OWN,), (own,))
     one, one_in = after((one, one_in), acc[3])
     two, two_in = send(one_in, ALONG), send(one, INSIDE)
-    acc = multiply(
-        acc,
-        (ONE, 0, one), (ONE_IN, 0, one_in), (ONE, 1, swap(one)), (ONE_IN, 1, swap(one_in)),
-    )
+    acc = multiply(acc, (ONE, ONE_IN), (one, one_in))
     two, two_in = after((two, two_in), acc[3])
-    three, three_across = send(two_in, ALONG), send(jnp.where(end, two, one_in), ACROSS)
-    acc = multiply(
-        acc,
-        (TWO, 0, two), (TWO_IN, 0, two_in), (TWO, 1, swap(two)), (TWO_IN, 1, swap(two_in)),
-    )
-    three, three_across = after((three, three_across), acc[3])
+    three, across = send(two_in, ALONG), send(jnp.where(end, two, one_in), ACROSS)
+    acc = multiply(acc, (TWO, TWO_IN), (two, two_in))
+    three, across = after((three, across), acc[3])
     four = send(jnp.where(end, three, two_in), ACROSS)
-    acc = multiply(
-        acc,
-        (THREE, 0, three), (THREE_ACROSS, 0, three_across),
-        (THREE, 1, swap(three)), (THREE_ACROSS, 1, swap(three_across)),
-    )
+    acc = multiply(acc, (THREE, THREE_ACROSS), (three, across))
     four = after(four, acc[3])
-    hidden = multiply(acc, (FOUR, 0, four), (FOUR, 1, swap(four)), last=True)[0]
+    hidden = multiply(acc, (FOUR,), (four,), last=True)[0]
 
     narrow = lambda x: x.astype(jnp.bfloat16)
     wide = lambda x: x.astype(jnp.float32)
     zero = jnp.zeros((), jnp.float32)
 
     def partials(hidden, kept, sent):
-        jobs = [(place, jnp.float32) for place in kept]
-        jobs += [(place + 8, jnp.bfloat16) for place in sent]
-        outs = down(order, jobs, hidden, down_weight, width)
-        return *outs[: len(kept)], *(swap(x) for x in outs[len(kept) :])
-
-    (other_four,) = partials(hidden, (), (FOUR,))
-    four, other_three, other_across = partials(hidden, (FOUR,), (THREE, THREE_ACROSS))
-    four = narrow(four + wide(other_four))
+        kept_jobs, sent_jobs = [(place, 0) for place in kept], [(place, 1) for place in sent]
+        outs = down(me, kept_jobs, sent_jobs, hidden, down_weight, width)
+        return [*outs[: len(kept)], *(wide(swap(x)) for x in outs[len(kept) :])]
+
+    their_four, their_three, their_across = partials(hidden, (), (FOUR, THREE, THREE_ACROSS))
+    (four,) = partials(hidden, (FOUR,), ())
+    four = narrow(four + their_four)
     got = wide(send(four, ACROSS))
-    three, across, other_two, other_in = partials(
+    three, across, their_two, their_in = partials(
         after(hidden, four), (THREE, THREE_ACROSS), (TWO, TWO_IN)
     )
-    across = narrow(across + wide(other_across))
+    across = narrow(across + their_across)
     got_across = wide(send(across, ACROSS))
-    three = narrow(three + wide(other_three) + jnp.where(end, got, zero))
+    three = narrow(three + their_three + jnp.where(end, got, zero))
     got_three = wide(send(three, ALONG))
-    two, two_in, other_one, other_one_in = partials(
+    two, two_in, their_one, their_one_in = partials(
         after(hidden, three, across), (TWO, TWO_IN), (ONE, ONE_IN)
     )
-    two = narrow(two + wide(other_two) + jnp.where(end, got_across, zero))
+    two = narrow(two + their_two + jnp.where(end, got_across, zero))
     got_two = wide(send(two, ALONG))
-    two_in = narrow(two_in + wide(other_in) + jnp.where(end, zero, got) + got_three)
+    two_in = narrow(two_in + their_in + jnp.where(end, zero, got) + got_three)
     got_in = wide(send(two_in, INSIDE))
-    one, one_in, other_own = partials(after(hidden, two, two_in), (ONE, ONE_IN), (OWN,))
-    one_in = narrow(one_in + wide(other_one_in) + jnp.where(end, zero, got_across) + got_two)
+    one, one_in, their_own = partials(after(hidden, two, two_in), (ONE, ONE_IN), (OWN,))
+    one_in = narrow(one_in + their_one_in + jnp.where(end, zero, got_across) + got_two)
     got_one_in = wide(send(one_in, INSIDE))
-    one = narrow(one + wide(other_one) + got_in)
+    one = narrow(one + their_one + got_in)
     got_one = wide(send(one, ALONG))
     (kept,) = partials(after(hidden, one, one_in), (OWN,), ())
-    branch = kept + wide(other_own)
+    branch = kept + their_own
     return (resident + branch + got_one + got_one_in).astype(jnp.bfloat16)
 
 

time: 117 us -> 118 us (level)
  waiting for transfers between devices: 17.8 us -> 23.6 us
  Pallas kernels: 69.7 us -> 64 us
  local copies, waits for them, and re-layouts: 1.68 us -> 7.22 us
  starting transfers between devices: 24 us -> 20.1 us
    unnamed x6 -> x12, local copies, waits for them, and re-layouts: 1.68 us -> 7.22 us
    ppermute x14, waiting for transfers between devices: 15.7 us -> 20.4 us  [send(): return lax.ppermute(x, 'gx', pairs)]
    pallas_call x5, Pallas kernels: 40.4 us -> 36.3 us  [gate_up(): pl.pallas_call(functools.partial(gate_up_body, count, first, last, rows,...]
    ppermute x14, starting transfers between devices: 20.1 us -> 17.6 us  [send(): return lax.ppermute(x, 'gx', pairs)]
    pallas_call x7, Pallas kernels: 29.3 us -> 27.7 us  [the longest x6 25.7 us: down(): pl.pallas_call(functools.partial(down_body, len(kept), len(sent)), grid_s...]
    ppermute x16 -> x13, starting transfers between devices: 3.92 us -> 2.47 us  [swap(): return lax.ppermute(x, 'gx', [(i, i ^ 1) for i in range(4 * LINE)])]
    ppermute x16 -> x13, waiting for transfers between devices: 2.07 us -> 3.22 us  [swap(): return lax.ppermute(x, 'gx', [(i, i ^ 1) for i in range(4 * LINE)])]
  transfers between devices with their start and end apart: 30 -> 27, of which waited for: 11 -> 12; matrix products, arithmetic and copies ran while one was open for 2% -> 1% of each run, Pallas kernels for 52% -> 44%
where the time goes in v8:
time: 118 us
  Pallas kernels  64 us (54%)
  waiting for transfers between devices  23.6 us (20%)
  starting transfers between devices  20.1 us (17%)
  local copies, waits for them, and re-layouts  7.22 us (6%)
  other arithmetic  2.77 us (2%)
    pallas_call x5, Pallas kernels, gate_up(): pl.pallas_call(functools.partial(gate_up_body, count, first, last, rows,...  36.3 us
    pallas_call x6, Pallas kernels, down(): pl.pallas_call(functools.partial(down_body, len(kept), len(sent)), grid_s...  25.7 us
    ppermute x14, waiting for transfers between devices, send(): return lax.ppermute(x, 'gx', pairs)  20.4 us
    ppermute x14, starting transfers between devices, send(): return lax.ppermute(x, 'gx', pairs)  17.6 us
    unnamed x12, local copies, waits for them, and re-layouts  7.22 us
    ppermute x13, waiting for transfers between devices, swap(): return lax.ppermute(x, 'gx', [(i, i ^ 1) for i in range(4 * LINE)])  3.22 us
    ppermute x13, starting transfers between devices, swap(): return lax.ppermute(x, 'gx', [(i, i ^ 1) for i in range(4 * LINE)])  2.47 us
  transfers between devices with their start and end apart: 27, of which 12 were waited for; matrix products, arithmetic and copies ran while one was open for 1% of the time, Pallas kernels for 44%

profile of v8, /device:TPU:0, one launch (start us, length us, event | category | flops | bytes accessed | tf_op | source)
XLA Modules:
  0.0 117.9 jit_solution(4748186370353069882)
XLA Ops:
  0.0 2.0 %prepare.1.refs_0_ = bf16[1,400,512]{2,1,0:T(8,128)(2,1)} custom-call(bf16[384,512]{1,0:T(8,128)(2,1)} %x_ref.1, bf16[512]{0:T(512)(128)(2,1)} %gain_ref.1), custom_call_target="tpu_custom_call" | custom-call | tf_op jit(solution)/shard_map/prepare/pallas_call | solution.py:73
  2.4 2.6 %collective-permute-start = (bf16[1,400,512]{2,1,0:T(8,128)(2,1)}, bf16[1,400,512]{2,1,0:T(8,128)(2,1)S(1)}, u32[]{:S(2)}, u32[]{:S(2)}) collective-permute-start(bf16[1,400,512]{2,1,0:T(8,128)(2,1)} %prepare.1.refs_0_), channel_id=1, source_target_pairs={{0,4},{1,5},{2,6},{3,7},{4,0},{5,1},{6,2},{7,3},{8,12},{9,13},{10,... | collective-permute-start | bytes 1228808 | tf_op jit(solution)/shard_map/ppermute | solution.py:30
  5.0 1.5 %collective-permute-start.1 = (bf16[1,400,512]{2,1,0:T(8,128)(2,1)}, bf16[1,400,512]{2,1,0:T(8,128)(2,1)S(1)}, u32[]{:S(2)}, u32[]{:S(2)}) collective-permute-start(bf16[1,400,512]{2,1,0:T(8,128)(2,1)} %prepare.1.refs_0_), channel_id=1, source_target_pairs={{0,2},{1,3},{2,0},{3,1},{4,8},{5,9},{6,10},{7,11},{8,4},{9,5},{10,... | collective-permute-start | bytes 1228808 | tf_op jit(solution)/shard_map/ppermute | solution.py:30
  7.6 5.0 %gate_up.5 = (f32[384,1536]{1,0:T(8,128)S(1)}, f32[384,1536]{1,0:T(8,128)S(1)}, f32[384,256]{1,0:T(8,128)S(1)}, f32[8,512]{1,0:T(8,128)S(1)}) custom-call(s32[1]{0:T(128)} %bitcast.me_ref, bf16[1,400,512]{2,1,0:T(8,128)(2,1)S(1)} %copy-done.4, bf16[1,400,512]{2,1,0:T(8,128)(2,1)S(1)} %collective-permute-done.2.refs_1_, bf16[8192,1664]{1,0:T(8,128)(2,1)} %refs_2_.3, ...), custom_call_target="tpu_custom_call" | custom-call | flops 327155712 | bytes 851968 | tf_op jit(solution)/shard_map/gate_up/pallas_call | solution.py:152
  12.6 2.8 %collective-permute-done.refs_0_ = bf16[1,400,512]{2,1,0:T(8,128)(2,1)S(1)} collective-permute-done((bf16[1,400,512]{2,1,0:T(8,128)(2,1)}, bf16[1,400,512]{2,1,0:T(8,128)(2,1)S(1)}, u32[]{:S(2)}, u32[]{:S(2)}) %collective-permute-start) | collective-permute-done | bytes 409632 | tf_op jit(solution)/shard_map/ppermute | solution.py:30
  18.5 1.5 %collective-permute-start.4 = (bf16[1,400,512]{2,1,0:T(8,128)(2,1)S(1)}, bf16[1,400,512]{2,1,0:T(8,128)(2,1)S(1)}, u32[]{:S(2)}, u32[]{:S(2)}) collective-permute-start(bf16[1,400,512]{2,1,0:T(8,128)(2,1)S(1)} %collective-permute-done.refs_0_), channel_id=1, source_target_pairs={{0,2},{1,3},{2,0},{3,1},{4,8},{5,9},{6,10},{7,11},{8,4},{9,5},{10,... | collective-permute-start | bytes 1228808 | tf_op jit(solution)/shard_map/ppermute | solution.py:30
  20.0 8.6 %gate_up.6 = (f32[384,1536]{1,0:T(8,128)S(1)}, f32[384,1536]{1,0:T(8,128)S(1)}, f32[384,256]{1,0:T(8,128)S(1)}, f32[8,512]{1,0:T(8,128)S(1)}) custom-call(s32[1]{0:T(128)} %bitcast.me_ref, bf16[1,400,512]{2,1,0:T(8,128)(2,1)S(1)} %collective-permute-done.refs_0_, bf16[1,400,512]{2,1,0:T(8,128)(2,1)S(1)} %collective-permute-done.1.refs_1_, ...), custom_call_target="tpu_custom_call" | custom-call | flops 654311424 | bytes 1703936 | tf_op jit(solution)/shard_map/gate_up/pallas_call | solution.py:152
  34.2 1.7 %copy-done.1 = f32[384,1536]{1,0:T(8,128)S(1)} copy-done((f32[384,1536]{1,0:T(8,128)S(1)}, f32[384,1536]{1,0:T(8,128)}, u32[]{:S(2)}) %copy-start.1) | copy-done | bytes 2359320
  35.9 1.7 %copy-done.3 = f32[384,1536]{1,0:T(8,128)S(1)} copy-done((f32[384,1536]{1,0:T(8,128)S(1)}, f32[384,1536]{1,0:T(8,128)}, u32[]{:S(2)}) %copy-start.3) | copy-done | bytes 2359320
  37.5 8.6 %gate_up.7 = (f32[384,1536]{1,0:T(8,128)S(1)}, f32[384,1536]{1,0:T(8,128)S(1)}, f32[384,256]{1,0:T(8,128)S(1)}, f32[8,512]{1,0:T(8,128)S(1)}) custom-call(s32[1]{0:T(128)} %bitcast.me_ref, bf16[1,400,512]{2,1,0:T(8,128)(2,1)S(1)} %collective-permute-done.3.refs_0_, bf16[1,400,512]{2,1,0:T(8,128)(2,1)S(1)} %collective-permute-done.4.refs_1_, ...), custom_call_target="tpu_custom_call" | custom-call | flops 654311424 | bytes 1703936 | tf_op jit(solution)/shard_map/gate_up/pallas_call | solution.py:152
  48.7 8.7 %gate_up.8 = (f32[384,1536]{1,0:T(8,128)S(1)}, f32[384,1536]{1,0:T(8,128)S(1)}, f32[384,256]{1,0:T(8,128)S(1)}, f32[8,512]{1,0:T(8,128)S(1)}) custom-call(s32[1]{0:T(128)} %bitcast.me_ref, bf16[1,400,512]{2,1,0:T(8,128)(2,1)S(1)} %collective-permute-done.6.refs_0_, bf16[1,400,512]{2,1,0:T(8,128)(2,1)S(1)} %collective-permute-done.7.refs_1_, ...), custom_call_target="tpu_custom_call" | custom-call | flops 654311424 | bytes 1703936 | tf_op jit(solution)/shard_map/gate_up/pallas_call | solution.py:152
  58.3 1.7 %collective-permute-done.11.refs_1_ = bf16[1,400,512]{2,1,0:T(8,128)(2,1)S(1)} collective-permute-done((bf16[1,400,512]{2,1,0:T(8,128)(2,1)S(1)}, bf16[1,400,512]{2,1,0:T(8,128)(2,1)S(1)}, u32[]{:S(2)}, u32[]{:S(2)}) %collective-permute-start.11) | collective-permute-done | bytes 409632 | tf_op jit(solution)/shard_map/ppermute | solution.py:34
  60.1 5.3 %gate_up.9.hidden_ref = bf16[384,1664]{1,0:T(8,128)(2,1)S(1)} custom-call(s32[1]{0:T(128)} %bitcast.me_ref, bf16[1,400,512]{2,1,0:T(8,128)(2,1)S(1)} %collective-permute-done.9.refs_0_, bf16[1,400,512]{2,1,0:T(8,128)(2,1)S(1)} %collective-permute-done.11.refs_1_, bf16[8192,1664]{1,0:T(8,128)(2,1)} %refs_2_.3, bf16[8192,1664]{1,0:T(8,128)(2,1)} %refs_3_.3, ...), custom_call_target="tpu_custom_call" | custom-call | flops 327155712 | bytes 851968 | tf_op jit(solution)/shard_map/gate_up/pallas_call | solution.py:152
  65.4 4.8 %down.7 = (bf16[384,512]{1,0:T(8,128)(2,1)S(1)}, bf16[384,512]{1,0:T(8,128)(2,1)S(1)}, bf16[384,512]{1,0:T(8,128)(2,1)S(1)}) custom-call(s32[1]{0:T(128)} %bitcast.me_ref, bf16[384,1664]{1,0:T(8,128)(2,1)S(1)} %gate_up.9.hidden_ref, bf16[1664,8192]{1,0:T(8,128)(2,1)} %weight_ref.11), custom_call_target="tpu_custom_call" | custom-call | flops 245366784 | bytes 638976 | tf_op jit(solution)/shard_map/down/pallas_call | solution.py:205
  70.7 2.3 %down.6 = f32[384,512]{1,0:T(8,128)S(1)} custom-call(s32[1]{0:T(128)} %bitcast.me_ref, bf16[384,1664]{1,0:T(8,128)(2,1)S(1)} %gate_up.9.hidden_ref, bf16[1664,8192]{1,0:T(8,128)(2,1)} %weight_ref.11), custom_call_target="tpu_custom_call" | custom-call | flops 81788928 | bytes 212992 | tf_op jit(solution)/shard_map/down/pallas_call | solution.py:205
  74.1 5.8 %down.8 = (f32[384,512]{1,0:T(8,128)S(1)}, f32[384,512]{1,0:T(8,128)S(1)}, bf16[384,512]{1,0:T(8,128)(2,1)S(1)}, bf16[384,512]{1,0:T(8,128)(2,1)S(1)}) custom-call(s32[1]{0:T(128)} %bitcast.me_ref, bf16[384,1664]{1,0:T(8,128)(2,1)S(1)} %gate_up.9.hidden_ref, bf16[1664,8192]{1,0:T(8,128)(2,1)} %weight_ref.11), custom_call_target="tpu_custom_call" | custom-call | flops 327155712 | bytes 851968 | tf_op jit(solution)/shard_map/down/pallas_call | solution.py:205
  82.0 3.4 %collective-permute-done.14 = bf16[384,512]{1,0:T(8,128)(2,1)S(1)} collective-permute-done((bf16[384,512]{1,0:T(8,128)(2,1)S(1)}, bf16[384,512]{1,0:T(8,128)(2,1)S(1)}, u32[]{:S(2)}, u32[]{:S(2)}) %collective-permute-start.14) | collective-permute-done | bytes 393248 | tf_op jit(solution)/shard_map/ppermute | solution.py:30
  86.3 5.8 %down.9 = (f32[384,512]{1,0:T(8,128)S(1)}, f32[384,512]{1,0:T(8,128)S(1)}, bf16[384,512]{1,0:T(8,128)(2,1)S(1)}, bf16[384,512]{1,0:T(8,128)(2,1)S(1)}) custom-call(s32[1]{0:T(128)} %bitcast.me_ref, bf16[384,1664]{1,0:T(8,128)(2,1)S(1)} %gate_up.9.hidden_ref, bf16[1664,8192]{1,0:T(8,128)(2,1)} %weight_ref.11), custom_call_target="tpu_custom_call" | custom-call | flops 327155712 | bytes 851968 | tf_op jit(solution)/shard_map/down/pallas_call | solution.py:205
  96.6 4.7 %down.10 = (f32[384,512]{1,0:T(8,128)S(1)}, f32[384,512]{1,0:T(8,128)S(1)}, bf16[384,512]{1,0:T(8,128)(2,1)S(1)}) custom-call(s32[1]{0:T(128)} %bitcast.me_ref, bf16[384,1664]{1,0:T(8,128)(2,1)S(1)} %gate_up.9.hidden_ref, bf16[1664,8192]{1,0:T(8,128)(2,1)} %weight_ref.11), custom_call_target="tpu_custom_call" | custom-call | flops 245366784 | bytes 638976 | tf_op jit(solution)/shard_map/down/pallas_call | solution.py:205
  101.4 2.7 %collective-permute-done.23 = bf16[384,512]{1,0:T(8,128)(2,1)S(1)} collective-permute-done((bf16[384,512]{1,0:T(8,128)(2,1)S(1)}, bf16[384,512]{1,0:T(8,128)(2,1)S(1)}, u32[]{:S(2)}, u32[]{:S(2)}) %collective-permute-start.23) | collective-permute-done | bytes 393248 | tf_op jit(solution)/shard_map/ppermute | solution.py:30
  106.5 2.3 %collective-permute-start.25 = (bf16[384,512]{1,0:T(8,128)(2,1)S(1)}, bf16[384,512]{1,0:T(8,128)(2,1)S(1)}, u32[]{:S(2)}, u32[]{:S(2)}) collective-permute-start(bf16[384,512]{1,0:T(8,128)(2,1)S(1)} %add_convert_fusion.1), channel_id=1, source_target_pairs={{0,4},{1,5},{2,6},{3,7},{4,0},{5,1},{6,2},{7,3},{8,12},{9,13},{10,... | collective-permute-start | bytes 1179656 | tf_op jit(solution)/shard_map/ppermute | solution.py:30
  108.8 2.3 %down.11 = f32[384,512]{1,0:T(8,128)S(1)} custom-call(s32[1]{0:T(128)} %bitcast.me_ref, bf16[384,1664]{1,0:T(8,128)(2,1)S(1)} %gate_up.9.hidden_ref, bf16[1664,8192]{1,0:T(8,128)(2,1)} %weight_ref.11), custom_call_target="tpu_custom_call" | custom-call | flops 81788928 | bytes 212992 | tf_op jit(solution)/shard_map/down/pallas_call | solution.py:205
  111.1 3.3 %collective-permute-done.26 = bf16[384,512]{1,0:T(8,128)(2,1)S(1)} collective-permute-done((bf16[384,512]{1,0:T(8,128)(2,1)S(1)}, bf16[384,512]{1,0:T(8,128)(2,1)S(1)}, u32[]{:S(2)}, u32[]{:S(2)}) %collective-permute-start.26) | collective-permute-done | bytes 393248 | tf_op jit(solution)/shard_map/ppermute | solution.py:30
  114.4 2.5 %collective-permute-done.25 = bf16[384,512]{1,0:T(8,128)(2,1)S(1)} collective-permute-done((bf16[384,512]{1,0:T(8,128)(2,1)S(1)}, bf16[384,512]{1,0:T(8,128)(2,1)S(1)}, u32[]{:S(2)}, u32[]{:S(2)}) %collective-permute-start.25) | collective-permute-done | bytes 393248 | tf_op jit(solution)/shard_map/ppermute | solution.py:30
  (67 shorter events, 26.0 us)
Async XLA Ops:
  2.0 4.5 %collective-permute-start.2 = (bf16[1,400,512]{2,1,0:T(8,128)(2,1)}, bf16[1,400,512]{2,1,0:T(8,128)(2,1)S(1)}, u32[]{:S(2)}, u32[]{:S(2)}) collective-permute-start(bf16[1,400,512]{2,1,0:T(8,128)(2,1)} %prepare.1.refs_0_), channel_id=1, source_target_pairs={{0,1},{1,0},{2,3},{3,2},{4,5},{5,4},{6,7},{7,6},{8,9},{9,8},{10,11... | collective-permute-start | bytes 1228808 | tf_op jit(solution)/shard_map/ppermute | solution.py:34
  2.4 12.9 %collective-permute-start = (bf16[1,400,512]{2,1,0:T(8,128)(2,1)}, bf16[1,400,512]{2,1,0:T(8,128)(2,1)S(1)}, u32[]{:S(2)}, u32[]{:S(2)}) collective-permute-start(bf16[1,400,512]{2,1,0:T(8,128)(2,1)} %prepare.1.refs_0_), channel_id=1, source_target_pairs={{0,4},{1,5},{2,6},{3,7},{4,0},{5,1},{6,2},{7,3},{8,12},{9,13},{10,... | collective-permute-start | bytes 1228808 | tf_op jit(solution)/shard_map/ppermute | solution.py:30
  5.0 11.8 %collective-permute-start.1 = (bf16[1,400,512]{2,1,0:T(8,128)(2,1)}, bf16[1,400,512]{2,1,0:T(8,128)(2,1)S(1)}, u32[]{:S(2)}, u32[]{:S(2)}) collective-permute-start(bf16[1,400,512]{2,1,0:T(8,128)(2,1)} %prepare.1.refs_0_), channel_id=1, source_target_pairs={{0,2},{1,3},{2,0},{3,1},{4,8},{5,9},{6,10},{7,11},{8,4},{9,5},{10,... | collective-permute-start | bytes 1228808 | tf_op jit(solution)/shard_map/ppermute | solution.py:30
  16.9 3.1 %collective-permute-start.5 = (bf16[2,400,512]{2,1,0:T(8,128)(2,1)S(1)}, bf16[2,400,512]{2,1,0:T(8,128)(2,1)S(1)}, u32[]{:S(2)}, u32[]{:S(2)}) collective-permute-start(bf16[2,400,512]{2,1,0:T(8,128)(2,1)S(1)} %pad_maximum_fusion), channel_id=1, source_target_pairs={{0,1},{1,0},{2,3},{3,2},{4,5},{5,4},{6,7},{7,6},{8,9},{9,8},{10,11... | collective-permute-start | bytes 2457608 | tf_op jit(solution)/shard_map/ppermute | solution.py:34
  17.0 14.5 %collective-permute-start.3 = (bf16[1,400,512]{2,1,0:T(8,128)(2,1)S(1)}, bf16[1,400,512]{2,1,0:T(8,128)(2,1)S(1)}, u32[]{:S(2)}, u32[]{:S(2)}) collective-permute-start(bf16[1,400,512]{2,1,0:T(8,128)(2,1)S(1)} %collective-permute-done.1.refs_1_), channel_id=1, source_target_pairs={{0,4},{1,5},{2,6},{3,7},{4,0},{5,1},{6,2},{7,3},{8,12},{9,13},{10,... | collective-permute-start | bytes 1228808 | tf_op jit(solution)/shard_map/ppermute | solution.py:30
  18.5 13.0 %collective-permute-start.4 = (bf16[1,400,512]{2,1,0:T(8,128)(2,1)S(1)}, bf16[1,400,512]{2,1,0:T(8,128)(2,1)S(1)}, u32[]{:S(2)}, u32[]{:S(2)}) collective-permute-start(bf16[1,400,512]{2,1,0:T(8,128)(2,1)S(1)} %collective-permute-done.refs_0_), channel_id=1, source_target_pairs={{0,2},{1,3},{2,0},{3,1},{4,8},{5,9},{6,10},{7,11},{8,4},{9,5},{10,... | collective-permute-start | bytes 1228808 | tf_op jit(solution)/shard_map/ppermute | solution.py:30
  31.8 14.4 %collective-permute-start.7 = (bf16[1,400,512]{2,1,0:T(8,128)(2,1)S(1)}, bf16[1,400,512]{2,1,0:T(8,128)(2,1)S(1)}, u32[]{:S(2)}, u32[]{:S(2)}) collective-permute-start(bf16[1,400,512]{2,1,0:T(8,128)(2,1)S(1)} %broadcast_select_fusion.1), channel_id=1, source_target_pairs={{0,2},{1,3},{2,0},{3,1},{4,6},{5,7},{6,4},{7,5},{8,10},{9,11},{10,... | collective-permute-start | bytes 1228808 | tf_op jit(solution)/shard_map/ppermute | solution.py:30
  32.7 13.4 %collective-permute-start.6 = (bf16[1,400,512]{2,1,0:T(8,128)(2,1)S(1)}, bf16[1,400,512]{2,1,0:T(8,128)(2,1)S(1)}, u32[]{:S(2)}, u32[]{:S(2)}) collective-permute-start(bf16[1,400,512]{2,1,0:T(8,128)(2,1)S(1)} %collective-permute-done.4.refs_1_), channel_id=1, source_target_pairs={{0,4},{1,5},{2,6},{3,7},{4,0},{5,1},{6,2},{7,3},{8,12},{9,13},{10,... | collective-permute-start | bytes 1228808 | tf_op jit(solution)/shard_map/ppermute | solution.py:30
  46.4 11.9 %collective-permute-start.9 = (bf16[1,400,512]{2,1,0:T(8,128)(2,1)S(1)}, bf16[1,400,512]{2,1,0:T(8,128)(2,1)S(1)}, u32[]{:S(2)}, u32[]{:S(2)}) collective-permute-start(bf16[1,400,512]{2,1,0:T(8,128)(2,1)S(1)} %broadcast_select_fusion), channel_id=1, source_target_pairs={{0,2},{1,3},{2,0},{3,1},{4,6},{5,7},{6,4},{7,5},{8,10},{9,11},{10,... | collective-permute-start | bytes 1228808 | tf_op jit(solution)/shard_map/ppermute | solution.py:30
  70.1 3.1 %collective-permute-start.12 = (bf16[384,512]{1,0:T(8,128)(2,1)S(1)}, bf16[384,512]{1,0:T(8,128)(2,1)S(1)}, u32[]{:S(2)}, u32[]{:S(2)}) collective-permute-start(bf16[384,512]{1,0:T(8,128)(2,1)S(1)} %get-tuple-element.69), channel_id=1, source_target_pairs={{0,1},{1,0},{2,3},{3,2},{4,5},{5,4},{6,7},{7,6},{8,9},{9,8},{10,11... | collective-permute-start | bytes 1179656 | tf_op jit(solution)/shard_map/ppermute | solution.py:34
  70.3 9.6 %collective-permute-start.15 = (bf16[384,512]{1,0:T(8,128)(2,1)S(1)}, bf16[384,512]{1,0:T(8,128)(2,1)S(1)}, u32[]{:S(2)}, u32[]{:S(2)}) collective-permute-start(bf16[384,512]{1,0:T(8,128)(2,1)S(1)} %get-tuple-element.74), channel_id=1, source_target_pairs={{0,1},{1,0},{2,3},{3,2},{4,5},{5,4},{6,7},{7,6},{8,9},{9,8},{10,11... | collective-permute-start | bytes 1179656 | tf_op jit(solution)/shard_map/ppermute | solution.py:34
  73.0 9.0 %collective-permute-start.13 = (bf16[384,512]{1,0:T(8,128)(2,1)S(1)}, bf16[384,512]{1,0:T(8,128)(2,1)S(1)}, u32[]{:S(2)}, u32[]{:S(2)}) collective-permute-start(bf16[384,512]{1,0:T(8,128)(2,1)S(1)} %get-tuple-element.72), channel_id=1, source_target_pairs={{0,1},{1,0},{2,3},{3,2},{4,5},{5,4},{6,7},{7,6},{8,9},{9,8},{10,11... | collective-permute-start | bytes 1179656 | tf_op jit(solution)/shard_map/ppermute | solution.py:34
  73.4 12.0 %collective-permute-start.14 = (bf16[384,512]{1,0:T(8,128)(2,1)S(1)}, bf16[384,512]{1,0:T(8,128)(2,1)S(1)}, u32[]{:S(2)}, u32[]{:S(2)}) collective-permute-start(bf16[384,512]{1,0:T(8,128)(2,1)S(1)} %add_convert_fusion.3), channel_id=1, source_target_pairs={{0,2},{1,3},{2,0},{3,1},{4,6},{5,7},{6,4},{7,5},{8,10},{9,11},{10,... | collective-permute-start | bytes 1179656 | tf_op jit(solution)/shard_map/ppermute | solution.py:30
  80.0 13.2 %collective-permute-start.17 = (bf16[384,512]{1,0:T(8,128)(2,1)S(1)}, bf16[384,512]{1,0:T(8,128)(2,1)S(1)}, u32[]{:S(2)}, u32[]{:S(2)}) collective-permute-start(bf16[384,512]{1,0:T(8,128)(2,1)S(1)} %add_convert_fusion.2), channel_id=1, source_target_pairs={{0,2},{1,3},{2,0},{3,1},{4,6},{5,7},{6,4},{7,5},{8,10},{9,11},{10,... | collective-permute-start | bytes 1179656 | tf_op jit(solution)/shard_map/ppermute | solution.py:30
  81.5 11.7 %collective-permute-start.16 = (bf16[384,512]{1,0:T(8,128)(2,1)S(1)}, bf16[384,512]{1,0:T(8,128)(2,1)S(1)}, u32[]{:S(2)}, u32[]{:S(2)}) collective-permute-start(bf16[384,512]{1,0:T(8,128)(2,1)S(1)} %get-tuple-element.77), channel_id=1, source_target_pairs={{0,1},{1,0},{2,3},{3,2},{4,5},{5,4},{6,7},{7,6},{8,9},{9,8},{10,11... | collective-permute-start | bytes 1179656 | tf_op jit(solution)/shard_map/ppermute | solution.py:34
  81.5 13.1 %collective-permute-start.18 = (bf16[384,512]{1,0:T(8,128)(2,1)S(1)}, bf16[384,512]{1,0:T(8,128)(2,1)S(1)}, u32[]{:S(2)}, u32[]{:S(2)}) collective-permute-start(bf16[384,512]{1,0:T(8,128)(2,1)S(1)} %get-tuple-element.79), channel_id=1, source_target_pairs={{0,1},{1,0},{2,3},{3,2},{4,5},{5,4},{6,7},{7,6},{8,9},{9,8},{10,11... | collective-permute-start | bytes 1179656 | tf_op jit(solution)/shard_map/ppermute | solution.py:34
  85.6 10.1 %collective-permute-start.19 = (bf16[384,512]{1,0:T(8,128)(2,1)S(1)}, bf16[384,512]{1,0:T(8,128)(2,1)S(1)}, u32[]{:S(2)}, u32[]{:S(2)}) collective-permute-start(bf16[384,512]{1,0:T(8,128)(2,1)S(1)} %fusion.1), channel_id=1, source_target_pairs={{0,4},{1,5},{2,6},{3,7},{4,0},{5,1},{6,2},{7,3},{8,12},{9,13},{10,... | collective-permute-start | bytes 1179656 | tf_op jit(solution)/shard_map/ppermute | solution.py:30
  93.5 10.6 %collective-permute-start.23 = (bf16[384,512]{1,0:T(8,128)(2,1)S(1)}, bf16[384,512]{1,0:T(8,128)(2,1)S(1)}, u32[]{:S(2)}, u32[]{:S(2)}) collective-permute-start(bf16[384,512]{1,0:T(8,128)(2,1)S(1)} %fusion.6), channel_id=1, source_target_pairs={{0,4},{1,5},{2,6},{3,7},{4,0},{5,1},{6,2},{7,3},{8,12},{9,13},{10,... | collective-permute-start | bytes 1179656 | tf_op jit(solution)/shard_map/ppermute | solution.py:30
  94.1 10.0 %collective-permute-start.22 = (bf16[384,512]{1,0:T(8,128)(2,1)S(1)}, bf16[384,512]{1,0:T(8,128)(2,1)S(1)}, u32[]{:S(2)}, u32[]{:S(2)}) collective-permute-start(bf16[384,512]{1,0:T(8,128)(2,1)S(1)} %get-tuple-element.84), channel_id=1, source_target_pairs={{0,1},{1,0},{2,3},{3,2},{4,5},{5,4},{6,7},{7,6},{8,9},{9,8},{10,11... | collective-permute-start | bytes 1179656 | tf_op jit(solution)/shard_map/ppermute | solution.py:34
  94.1 10.9 %collective-permute-start.20 = (bf16[384,512]{1,0:T(8,128)(2,1)S(1)}, bf16[384,512]{1,0:T(8,128)(2,1)S(1)}, u32[]{:S(2)}, u32[]{:S(2)}) collective-permute-start(bf16[384,512]{1,0:T(8,128)(2,1)S(1)} %get-tuple-element.82), channel_id=1, source_target_pairs={{0,1},{1,0},{2,3},{3,2},{4,5},{5,4},{6,7},{7,6},{8,9},{9,8},{10,11... | collective-permute-start | bytes 1179656 | tf_op jit(solution)/shard_map/ppermute | solution.py:34
  95.9 10.3 %collective-permute-start.21 = (bf16[384,512]{1,0:T(8,128)(2,1)S(1)}, bf16[384,512]{1,0:T(8,128)(2,1)S(1)}, u32[]{:S(2)}, u32[]{:S(2)}) collective-permute-start(bf16[384,512]{1,0:T(8,128)(2,1)S(1)} %fusion.4), channel_id=1, source_target_pairs={{0,2},{1,3},{2,0},{3,1},{4,8},{5,9},{6,10},{7,11},{8,4},{9,5},{10,... | collective-permute-start | bytes 1179656 | tf_op jit(solution)/shard_map/ppermute | solution.py:30
  104.4 10.1 %collective-permute-start.26 = (bf16[384,512]{1,0:T(8,128)(2,1)S(1)}, bf16[384,512]{1,0:T(8,128)(2,1)S(1)}, u32[]{:S(2)}, u32[]{:S(2)}) collective-permute-start(bf16[384,512]{1,0:T(8,128)(2,1)S(1)} %fusion.9), channel_id=1, source_target_pairs={{0,2},{1,3},{2,0},{3,1},{4,8},{5,9},{6,10},{7,11},{8,4},{9,5},{10,... | collective-permute-start | bytes 1179656 | tf_op jit(solution)/shard_map/ppermute | solution.py:30
  105.1 9.4 %collective-permute-start.24 = (bf16[384,512]{1,0:T(8,128)(2,1)S(1)}, bf16[384,512]{1,0:T(8,128)(2,1)S(1)}, u32[]{:S(2)}, u32[]{:S(2)}) collective-permute-start(bf16[384,512]{1,0:T(8,128)(2,1)S(1)} %get-tuple-element.86), channel_id=1, source_target_pairs={{0,1},{1,0},{2,3},{3,2},{4,5},{5,4},{6,7},{7,6},{8,9},{9,8},{10,11... | collective-permute-start | bytes 1179656 | tf_op jit(solution)/shard_map/ppermute | solution.py:34
  106.5 10.4 %collective-permute-start.25 = (bf16[384,512]{1,0:T(8,128)(2,1)S(1)}, bf16[384,512]{1,0:T(8,128)(2,1)S(1)}, u32[]{:S(2)}, u32[]{:S(2)}) collective-permute-start(bf16[384,512]{1,0:T(8,128)(2,1)S(1)} %add_convert_fusion.1), channel_id=1, source_target_pairs={{0,4},{1,5},{2,6},{3,7},{4,0},{5,1},{6,2},{7,3},{8,12},{9,13},{10,... | collective-permute-start | bytes 1179656 | tf_op jit(solution)/shard_map/ppermute | solution.py:30
  (9 other events, 24.4 us)

commit v9 on v8

--- a/solution.py
+++ b/solution.py
@@ -11,6 +11,7 @@
 epsilon = 1e-05
 LINE = 4
 EXTRA = 16
+SPLIT = 2
 VMEM_LIMIT = 36 * 1024 * 1024
 PREPARE_LIMIT = 60 * 1024 * 1024
 
@@ -79,7 +80,7 @@
 
 
 def gate_up_body(count, first, last, rows, main, features, me_ref, *refs):
-    blocks = refs[:count]
+    shards = refs[:count]
     gate_ref, up_ref, *rest = refs[count:]
     if not first:
         before = rest[:4]
@@ -87,41 +88,62 @@
     if last:
         hidden_ref, *rest = rest
     accs = rest
-    step = pl.program_id(0)
-
-    for s in range(count):
-
-        @pl.when(step == s)
-        def _(s=s):
-            x = blocks[s][0, :rows, :]
-            gate, up = gate_ref[...], up_ref[...]
-            mixed = jnp.concatenate([gate[:, main:], up[:, main:]], axis=1)
-            values = [
-                jnp.dot(x, weight, preferred_element_type=jnp.float32)
-                for weight in (gate[:, :main], up[:, :main], mixed)
-            ]
-            squares = blocks[s][0, rows:, :].astype(jnp.float32)
-            squares = jnp.sum(squares, axis=0, keepdims=True)
-            values.append(jnp.broadcast_to(squares, accs[3].shape))
-            if s:
-                values = [acc[...] + value for acc, value in zip(accs, values)]
-            elif not first:
-                values = [old[...] + value for old, value in zip(before, values)]
-            if not last or s < count - 1:
-                for acc, value in zip(accs, values):
-                    acc[...] = value
-                return
-            factor = lax.rsqrt(values[3][:1, :rows] / features + epsilon)
-            factor = jnp.broadcast_to(factor, (128, rows)).T[:, :1]
-
-            def act(g, u):
-                g, u = g * factor, u * factor
-                return (g / (1.0 + jnp.exp(-g)) * u).astype(jnp.bfloat16)
-
-            gate, up, both, _ = values
-            rem = both.shape[1] // 2
-            hidden_ref[:, :main] = act(gate, up)
-            hidden_ref[:, main:] = act(both[:, :rem], both[:, rem:])
+    now = pl.program_id(0)
+    final = SPLIT * count - 1
+
+    def products(x_ref):
+        x = x_ref[0, :rows, :]
+        gate, up = gate_ref[...], up_ref[...]
+        mixed = jnp.concatenate([gate[:, main:], up[:, main:]], axis=1)
+        for weight in (gate[:, :main], up[:, :main], mixed):
+            yield jnp.dot(x, weight, preferred_element_type=jnp.float32)
+
+    def start():
+        for i, value in enumerate(products(shards[0])):
+            accs[i][...] = value if first else before[i][...] + value
+
+    def add(x_ref):
+        for acc, value in zip(accs, products(x_ref)):
+            acc[...] += value
+
+    def finish():
+        gate, up, both = (
+            acc[...] + value for acc, value in zip(accs, products(shards[-1]))
+        )
+        factor = lax.rsqrt(accs[3][:1, :rows] / features + epsilon)
+        factor = jnp.broadcast_to(factor, (128, rows)).T[:, :1]
+
+        def act(g, u):
+            g, u = g * factor, u * factor
+            return (g / (1.0 + jnp.exp(-g)) * u).astype(jnp.bfloat16)
+
+        rem = both.shape[1] // 2
+        hidden_ref[:, :main] = act(gate, up)
+        hidden_ref[:, main:] = act(both[:, :rem], both[:, rem:])
+
+    @pl.when(now == 0)
+    def _():
+        accs[3][...] = jnp.zeros_like(accs[3]) if first else before[3][...]
+
+    for j, x_ref in enumerate(shards):
+        for part in range(SPLIT):
+
+            @pl.when(now == SPLIT * j + part)
+            def _(x_ref=x_ref, part=part):
+                squares = jnp.sum(x_ref[0, rows:, :].astype(jnp.float32), axis=0, keepdims=True)
+                width = squares.shape[1]
+                at = (slice(None), slice(part * width, (part + 1) * width))
+                accs[3][at] += jnp.broadcast_to(squares, (accs[3].shape[0], width))
+
+        low, high = SPLIT * j, SPLIT * (j + 1)
+        if not j:
+            pl.when(now == 0)(start)
+            low = 1
+        if last and j == count - 1:
+            pl.when(now == final)(finish)
+            high -= 1
+        if low < high:
+            pl.when((now >= low) & (now < high))(functools.partial(add, x_ref))
 
 
 def gate_up(me, jobs, shards, gate_weight, up_weight, acc, last=False):
@@ -133,9 +155,12 @@
     rem = ff - main
     first = acc is None
     whole = lambda shape: pl.BlockSpec(shape, lambda s, me: (0, 0))
-    weight = pl.BlockSpec((depth, ff), lambda s, me: (block(me[0], jobs, s), 0))
-    shard = lambda i: pl.BlockSpec((1, height, depth), lambda s, me: (i, 0, 0))
-    in_specs = [shard(i) for _, i in shards] + [weight, weight]
+    weight = pl.BlockSpec((depth // SPLIT, ff), lambda s, me: (block(me[0], jobs, s // SPLIT) * SPLIT + s % SPLIT, 0))
+    shard = lambda j, i: pl.BlockSpec(
+        (1, height, depth // SPLIT),
+        lambda s, me: (i, 0, jnp.clip(s - SPLIT * j, 0, SPLIT - 1)),
+    )
+    in_specs = [shard(j, i) for j, (_, i) in enumerate(shards)] + [weight, weight]
     args = [*(x for x, _ in shards), gate_weight, up_weight]
     shapes = [(rows, main), (rows, main), (rows, 2 * rem), (8, depth)]
     if not first:
@@ -153,7 +178,7 @@
         functools.partial(gate_up_body, count, first, last, rows, main, features),
         grid_spec=pltpu.PrefetchScalarGridSpec(
             num_scalar_prefetch=1,
-            grid=(count,),
+            grid=(SPLIT * count,),
             in_specs=in_specs,
             out_specs=out_specs,
             scratch_shapes=scratch,
@@ -239,7 +264,8 @@
         arrays = [(x, 0) for x in shards] + [(theirs, i) for i in range(len(places))]
         return gate_up(me, jobs, arrays, gate_weight, up_weight, acc, last)
 
-    own = prepare(activations, norm_gain)
+    early, end = lax.optimization_barrier((activations, end))
+    own = prepare(early, norm_gain)
     one, one_in = send(own, ALONG), send(own, INSIDE)
     acc = multiply(None, (OWN,), (own,))
     one, one_in = after((one, one_in), acc[3])

time: 118 us -> 120 us (1.017); the launches traced: 118 us -> 119 us
  Pallas kernels: 64 us -> 72.5 us
  local copies, waits for them, and re-layouts: 7.22 us -> 1.04 us
  waiting for transfers between devices: 23.6 us -> 21.7 us
    pallas_call x5, Pallas kernels: 36.3 us -> 44.8 us  [gate_up(): pl.pallas_call(functools.partial(gate_up_body, count, first, last, rows,...]
    unnamed x12 -> x4, local copies, waits for them, and re-layouts: 7.22 us -> 1.04 us
    ppermute x14, waiting for transfers between devices: 20.4 us -> 18.7 us  [send(): return lax.ppermute(x, 'gx', pairs)]
  transfers between devices with their start and end apart: 27 -> 27, of which waited for: 12 -> 11; matrix products, arithmetic and copies ran while one was open for 1% -> 1% of each run, Pallas kernels for 44% -> 50%
where the time goes in v9:
time: 120 us; the launch traced here: 119 us
  Pallas kernels  72.5 us (60%)
  waiting for transfers between devices  21.7 us (18%)
  starting transfers between devices  20.4 us (17%)
  other arithmetic  2.77 us (2%)
    pallas_call x5, Pallas kernels, gate_up(): pl.pallas_call(functools.partial(gate_up_body, count, first, last, rows,...  44.8 us
    pallas_call x6, Pallas kernels, down(): pl.pallas_call(functools.partial(down_body, len(kept), len(sent)), grid_s...  25.7 us
    ppermute x14, waiting for transfers between devices, send(): return lax.ppermute(x, 'gx', pairs)  18.7 us
    ppermute x14, starting transfers between devices, send(): return lax.ppermute(x, 'gx', pairs)  17.7 us
    ppermute x13, waiting for transfers between devices, swap(): return lax.ppermute(x, 'gx', [(i, i ^ 1) for i in range(4 * LINE)])  3.06 us
    ppermute x13, starting transfers between devices, swap(): return lax.ppermute(x, 'gx', [(i, i ^ 1) for i in range(4 * LINE)])  2.69 us
  transfers between devices with their start and end apart: 27, of which 11 were waited for; matrix products, arithmetic and copies ran while one was open for 1% of the time, Pallas kernels for 50%

profile of v9, /device:TPU:0, one launch (start us, length us, event | category | flops | bytes accessed | tf_op | source)
XLA Modules:
  0.0 118.6 jit_solution(16873358673809127571)
XLA Ops:
  0.0 2.0 %prepare.1.refs_0_ = bf16[1,400,512]{2,1,0:T(8,128)(2,1)} custom-call(bf16[384,512]{1,0:T(8,128)(2,1)} %x_ref, bf16[512]{0:T(512)(128)(2,1)} %gain_ref.1), custom_call_target="tpu_custom_call" | custom-call | tf_op jit(solution)/shard_map/prepare/pallas_call | solution.py:74
  2.4 2.6 %collective-permute-start = (bf16[1,400,512]{2,1,0:T(8,128)(2,1)}, bf16[1,400,512]{2,1,0:T(8,128)(2,1)S(1)}, u32[]{:S(2)}, u32[]{:S(2)}) collective-permute-start(bf16[1,400,512]{2,1,0:T(8,128)(2,1)} %prepare.1.refs_0_), channel_id=1, source_target_pairs={{0,4},{1,5},{2,6},{3,7},{4,0},{5,1},{6,2},{7,3},{8,12},{9,13},{10,... | collective-permute-start | bytes 1228808 | tf_op jit(solution)/shard_map/ppermute | solution.py:31
  5.0 1.5 %collective-permute-start.1 = (bf16[1,400,512]{2,1,0:T(8,128)(2,1)}, bf16[1,400,512]{2,1,0:T(8,128)(2,1)S(1)}, u32[]{:S(2)}, u32[]{:S(2)}) collective-permute-start(bf16[1,400,512]{2,1,0:T(8,128)(2,1)} %prepare.1.refs_0_), channel_id=1, source_target_pairs={{0,2},{1,3},{2,0},{3,1},{4,8},{5,9},{6,10},{7,11},{8,4},{9,5},{10,... | collective-permute-start | bytes 1228808 | tf_op jit(solution)/shard_map/ppermute | solution.py:31
  7.6 5.8 %gate_up.5 = (f32[384,1536]{1,0:T(8,128)S(1)}, f32[384,1536]{1,0:T(8,128)S(1)}, f32[384,256]{1,0:T(8,128)S(1)}, f32[8,512]{1,0:T(8,128)S(1)}) custom-call(s32[1]{0:T(128)} %bitcast.me_ref, bf16[1,400,512]{2,1,0:T(8,128)(2,1)S(1)} %copy-done, bf16[1,400,512]{2,1,0:T(8,128)(2,1)S(1)} %collective-permute-done.2.refs_1_, bf16[8192,1664]{1,0:T(8,128)(2,1)} %refs_2_.3, ...), custom_call_target="tpu_custom_call" | custom-call | flops 327155712 | bytes 851968 | tf_op jit(solution)/shard_map/gate_up/pallas_call | solution.py:177
  13.3 2.0 %collective-permute-done.refs_0_ = bf16[1,400,512]{2,1,0:T(8,128)(2,1)S(1)} collective-permute-done((bf16[1,400,512]{2,1,0:T(8,128)(2,1)}, bf16[1,400,512]{2,1,0:T(8,128)(2,1)S(1)}, u32[]{:S(2)}, u32[]{:S(2)}) %collective-permute-start) | collective-permute-done | bytes 409632 | tf_op jit(solution)/shard_map/ppermute | solution.py:31
  15.4 1.5 %collective-permute-done.1.refs_1_ = bf16[1,400,512]{2,1,0:T(8,128)(2,1)S(1)} collective-permute-done((bf16[1,400,512]{2,1,0:T(8,128)(2,1)}, bf16[1,400,512]{2,1,0:T(8,128)(2,1)S(1)}, u32[]{:S(2)}, u32[]{:S(2)}) %collective-permute-start.1) | collective-permute-done | bytes 409632 | tf_op jit(solution)/shard_map/ppermute | solution.py:31
  17.0 1.5 %collective-permute-start.3 = (bf16[1,400,512]{2,1,0:T(8,128)(2,1)S(1)}, bf16[1,400,512]{2,1,0:T(8,128)(2,1)S(1)}, u32[]{:S(2)}, u32[]{:S(2)}) collective-permute-start(bf16[1,400,512]{2,1,0:T(8,128)(2,1)S(1)} %collective-permute-done.1.refs_1_), channel_id=1, source_target_pairs={{0,4},{1,5},{2,6},{3,7},{4,0},{5,1},{6,2},{7,3},{8,12},{9,13},{10,... | collective-permute-start | bytes 1228808 | tf_op jit(solution)/shard_map/ppermute | solution.py:31
  18.5 1.5 %collective-permute-start.4 = (bf16[1,400,512]{2,1,0:T(8,128)(2,1)S(1)}, bf16[1,400,512]{2,1,0:T(8,128)(2,1)S(1)}, u32[]{:S(2)}, u32[]{:S(2)}) collective-permute-start(bf16[1,400,512]{2,1,0:T(8,128)(2,1)S(1)} %collective-permute-done.refs_0_), channel_id=1, source_target_pairs={{0,2},{1,3},{2,0},{3,1},{4,8},{5,9},{6,10},{7,11},{8,4},{9,5},{10,... | collective-permute-start | bytes 1228808 | tf_op jit(solution)/shard_map/ppermute | solution.py:31
  20.0 10.9 %gate_up.6 = (f32[384,1536]{1,0:T(8,128)S(1)}, f32[384,1536]{1,0:T(8,128)S(1)}, f32[384,256]{1,0:T(8,128)S(1)}, f32[8,512]{1,0:T(8,128)S(1)}) custom-call(s32[1]{0:T(128)} %bitcast.me_ref, bf16[1,400,512]{2,1,0:T(8,128)(2,1)S(1)} %collective-permute-done.refs_0_, bf16[1,400,512]{2,1,0:T(8,128)(2,1)S(1)} %collective-permute-done.1.refs_1_, ...), custom_call_target="tpu_custom_call" | custom-call | flops 654311424 | bytes 1703936 | tf_op jit(solution)/shard_map/gate_up/pallas_call | solution.py:177
  33.6 10.9 %gate_up.7 = (f32[384,1536]{1,0:T(8,128)S(1)}, f32[384,1536]{1,0:T(8,128)S(1)}, f32[384,256]{1,0:T(8,128)S(1)}, f32[8,512]{1,0:T(8,128)S(1)}) custom-call(s32[1]{0:T(128)} %bitcast.me_ref, bf16[1,400,512]{2,1,0:T(8,128)(2,1)S(1)} %collective-permute-done.3.refs_0_, bf16[1,400,512]{2,1,0:T(8,128)(2,1)S(1)} %collective-permute-done.4.refs_1_, ...), custom_call_target="tpu_custom_call" | custom-call | flops 654311424 | bytes 1703936 | tf_op jit(solution)/shard_map/gate_up/pallas_call | solution.py:177
  47.0 10.9 %gate_up.8 = (f32[384,1536]{1,0:T(8,128)S(1)}, f32[384,1536]{1,0:T(8,128)S(1)}, f32[384,256]{1,0:T(8,128)S(1)}, f32[8,512]{1,0:T(8,128)S(1)}) custom-call(s32[1]{0:T(128)} %bitcast.me_ref, bf16[1,400,512]{2,1,0:T(8,128)(2,1)S(1)} %collective-permute-done.6.refs_0_, bf16[1,400,512]{2,1,0:T(8,128)(2,1)S(1)} %collective-permute-done.7.refs_1_, ...), custom_call_target="tpu_custom_call" | custom-call | flops 654311424 | bytes 1703936 | tf_op jit(solution)/shard_map/gate_up/pallas_call | solution.py:177
  58.1 1.6 %collective-permute-done.11.refs_1_ = bf16[1,400,512]{2,1,0:T(8,128)(2,1)S(1)} collective-permute-done((bf16[1,400,512]{2,1,0:T(8,128)(2,1)S(1)}, bf16[1,400,512]{2,1,0:T(8,128)(2,1)S(1)}, u32[]{:S(2)}, u32[]{:S(2)}) %collective-permute-start.11) | collective-permute-done | bytes 409632 | tf_op jit(solution)/shard_map/ppermute | solution.py:35
  59.7 6.3 %gate_up.9.hidden_ref = bf16[384,1664]{1,0:T(8,128)(2,1)S(1)} custom-call(s32[1]{0:T(128)} %bitcast.me_ref, bf16[1,400,512]{2,1,0:T(8,128)(2,1)S(1)} %collective-permute-done.9.refs_0_, bf16[1,400,512]{2,1,0:T(8,128)(2,1)S(1)} %collective-permute-done.11.refs_1_, bf16[8192,1664]{1,0:T(8,128)(2,1)} %refs_2_.3, bf16[8192,1664]{1,0:T(8,128)(2,1)} %refs_3_.3, ...), custom_call_target="tpu_custom_call" | custom-call | flops 327155712 | bytes 851968 | tf_op jit(solution)/shard_map/gate_up/pallas_call | solution.py:177
  66.1 4.8 %down.7 = (bf16[384,512]{1,0:T(8,128)(2,1)S(1)}, bf16[384,512]{1,0:T(8,128)(2,1)S(1)}, bf16[384,512]{1,0:T(8,128)(2,1)S(1)}) custom-call(s32[1]{0:T(128)} %bitcast.me_ref, bf16[384,1664]{1,0:T(8,128)(2,1)S(1)} %gate_up.9.hidden_ref, bf16[1664,8192]{1,0:T(8,128)(2,1)} %weight_ref.11), custom_call_target="tpu_custom_call" | custom-call | flops 245366784 | bytes 638976 | tf_op jit(solution)/shard_map/down/pallas_call | solution.py:230
  71.4 2.3 %down.6 = f32[384,512]{1,0:T(8,128)S(1)} custom-call(s32[1]{0:T(128)} %bitcast.me_ref, bf16[384,1664]{1,0:T(8,128)(2,1)S(1)} %gate_up.9.hidden_ref, bf16[1664,8192]{1,0:T(8,128)(2,1)} %weight_ref.11), custom_call_target="tpu_custom_call" | custom-call | flops 81788928 | bytes 212992 | tf_op jit(solution)/shard_map/down/pallas_call | solution.py:230
  74.8 5.8 %down.8 = (f32[384,512]{1,0:T(8,128)S(1)}, f32[384,512]{1,0:T(8,128)S(1)}, bf16[384,512]{1,0:T(8,128)(2,1)S(1)}, bf16[384,512]{1,0:T(8,128)(2,1)S(1)}) custom-call(s32[1]{0:T(128)} %bitcast.me_ref, bf16[384,1664]{1,0:T(8,128)(2,1)S(1)} %gate_up.9.hidden_ref, bf16[1664,8192]{1,0:T(8,128)(2,1)} %weight_ref.11), custom_call_target="tpu_custom_call" | custom-call | flops 327155712 | bytes 851968 | tf_op jit(solution)/shard_map/down/pallas_call | solution.py:230
  82.7 3.4 %collective-permute-done.14 = bf16[384,512]{1,0:T(8,128)(2,1)S(1)} collective-permute-done((bf16[384,512]{1,0:T(8,128)(2,1)S(1)}, bf16[384,512]{1,0:T(8,128)(2,1)S(1)}, u32[]{:S(2)}, u32[]{:S(2)}) %collective-permute-start.14) | collective-permute-done | bytes 393248 | tf_op jit(solution)/shard_map/ppermute | solution.py:31
  86.9 5.8 %down.9 = (f32[384,512]{1,0:T(8,128)S(1)}, f32[384,512]{1,0:T(8,128)S(1)}, bf16[384,512]{1,0:T(8,128)(2,1)S(1)}, bf16[384,512]{1,0:T(8,128)(2,1)S(1)}) custom-call(s32[1]{0:T(128)} %bitcast.me_ref, bf16[384,1664]{1,0:T(8,128)(2,1)S(1)} %gate_up.9.hidden_ref, bf16[1664,8192]{1,0:T(8,128)(2,1)} %weight_ref.11), custom_call_target="tpu_custom_call" | custom-call | flops 327155712 | bytes 851968 | tf_op jit(solution)/shard_map/down/pallas_call | solution.py:230
  97.3 4.7 %down.10 = (f32[384,512]{1,0:T(8,128)S(1)}, f32[384,512]{1,0:T(8,128)S(1)}, bf16[384,512]{1,0:T(8,128)(2,1)S(1)}) custom-call(s32[1]{0:T(128)} %bitcast.me_ref, bf16[384,1664]{1,0:T(8,128)(2,1)S(1)} %gate_up.9.hidden_ref, bf16[1664,8192]{1,0:T(8,128)(2,1)} %weight_ref.11), custom_call_target="tpu_custom_call" | custom-call | flops 245366784 | bytes 638976 | tf_op jit(solution)/shard_map/down/pallas_call | solution.py:230
  102.1 2.7 %collective-permute-done.23 = bf16[384,512]{1,0:T(8,128)(2,1)S(1)} collective-permute-done((bf16[384,512]{1,0:T(8,128)(2,1)S(1)}, bf16[384,512]{1,0:T(8,128)(2,1)S(1)}, u32[]{:S(2)}, u32[]{:S(2)}) %collective-permute-start.23) | collective-permute-done | bytes 393248 | tf_op jit(solution)/shard_map/ppermute | solution.py:31
  107.2 2.4 %collective-permute-start.25 = (bf16[384,512]{1,0:T(8,128)(2,1)S(1)}, bf16[384,512]{1,0:T(8,128)(2,1)S(1)}, u32[]{:S(2)}, u32[]{:S(2)}) collective-permute-start(bf16[384,512]{1,0:T(8,128)(2,1)S(1)} %add_convert_fusion.1), channel_id=1, source_target_pairs={{0,4},{1,5},{2,6},{3,7},{4,0},{5,1},{6,2},{7,3},{8,12},{9,13},{10,... | collective-permute-start | bytes 1179656 | tf_op jit(solution)/shard_map/ppermute | solution.py:31
  109.6 2.3 %down.11 = f32[384,512]{1,0:T(8,128)S(1)} custom-call(s32[1]{0:T(128)} %bitcast.me_ref, bf16[384,1664]{1,0:T(8,128)(2,1)S(1)} %gate_up.9.hidden_ref, bf16[1664,8192]{1,0:T(8,128)(2,1)} %weight_ref.11), custom_call_target="tpu_custom_call" | custom-call | flops 81788928 | bytes 212992 | tf_op jit(solution)/shard_map/down/pallas_call | solution.py:230
  111.9 3.2 %collective-permute-done.26 = bf16[384,512]{1,0:T(8,128)(2,1)S(1)} collective-permute-done((bf16[384,512]{1,0:T(8,128)(2,1)S(1)}, bf16[384,512]{1,0:T(8,128)(2,1)S(1)}, u32[]{:S(2)}, u32[]{:S(2)}) %collective-permute-start.26) | collective-permute-done | bytes 393248 | tf_op jit(solution)/shard_map/ppermute | solution.py:31
  115.1 2.5 %collective-permute-done.25 = bf16[384,512]{1,0:T(8,128)(2,1)S(1)} collective-permute-done((bf16[384,512]{1,0:T(8,128)(2,1)S(1)}, bf16[384,512]{1,0:T(8,128)(2,1)S(1)}, u32[]{:S(2)}, u32[]{:S(2)}) %collective-permute-start.25) | collective-permute-done | bytes 393248 | tf_op jit(solution)/shard_map/ppermute | solution.py:31
  (59 shorter events, 19.5 us)
Async XLA Ops:
  2.0 4.5 %collective-permute-start.2 = (bf16[1,400,512]{2,1,0:T(8,128)(2,1)}, bf16[1,400,512]{2,1,0:T(8,128)(2,1)S(1)}, u32[]{:S(2)}, u32[]{:S(2)}) collective-permute-start(bf16[1,400,512]{2,1,0:T(8,128)(2,1)} %prepare.1.refs_0_), channel_id=1, source_target_pairs={{0,1},{1,0},{2,3},{3,2},{4,5},{5,4},{6,7},{7,6},{8,9},{9,8},{10,11... | collective-permute-start | bytes 1228808 | tf_op jit(solution)/shard_map/ppermute | solution.py:35
  2.4 12.9 %collective-permute-start = (bf16[1,400,512]{2,1,0:T(8,128)(2,1)}, bf16[1,400,512]{2,1,0:T(8,128)(2,1)S(1)}, u32[]{:S(2)}, u32[]{:S(2)}) collective-permute-start(bf16[1,400,512]{2,1,0:T(8,128)(2,1)} %prepare.1.refs_0_), channel_id=1, source_target_pairs={{0,4},{1,5},{2,6},{3,7},{4,0},{5,1},{6,2},{7,3},{8,12},{9,13},{10,... | collective-permute-start | bytes 1228808 | tf_op jit(solution)/shard_map/ppermute | solution.py:31
  5.0 11.8 %collective-permute-start.1 = (bf16[1,400,512]{2,1,0:T(8,128)(2,1)}, bf16[1,400,512]{2,1,0:T(8,128)(2,1)S(1)}, u32[]{:S(2)}, u32[]{:S(2)}) collective-permute-start(bf16[1,400,512]{2,1,0:T(8,128)(2,1)} %prepare.1.refs_0_), channel_id=1, source_target_pairs={{0,2},{1,3},{2,0},{3,1},{4,8},{5,9},{6,10},{7,11},{8,4},{9,5},{10,... | collective-permute-start | bytes 1228808 | tf_op jit(solution)/shard_map/ppermute | solution.py:31
  16.9 3.1 %collective-permute-start.5 = (bf16[2,400,512]{2,1,0:T(8,128)(2,1)S(1)}, bf16[2,400,512]{2,1,0:T(8,128)(2,1)S(1)}, u32[]{:S(2)}, u32[]{:S(2)}) collective-permute-start(bf16[2,400,512]{2,1,0:T(8,128)(2,1)S(1)} %pad_maximum_fusion), channel_id=1, source_target_pairs={{0,1},{1,0},{2,3},{3,2},{4,5},{5,4},{6,7},{7,6},{8,9},{9,8},{10,11... | collective-permute-start | bytes 2457608 | tf_op jit(solution)/shard_map/ppermute | solution.py:35
  17.0 13.9 %collective-permute-start.3 = (bf16[1,400,512]{2,1,0:T(8,128)(2,1)S(1)}, bf16[1,400,512]{2,1,0:T(8,128)(2,1)S(1)}, u32[]{:S(2)}, u32[]{:S(2)}) collective-permute-start(bf16[1,400,512]{2,1,0:T(8,128)(2,1)S(1)} %collective-permute-done.1.refs_1_), channel_id=1, source_target_pairs={{0,4},{1,5},{2,6},{3,7},{4,0},{5,1},{6,2},{7,3},{8,12},{9,13},{10,... | collective-permute-start | bytes 1228808 | tf_op jit(solution)/shard_map/ppermute | solution.py:31
  18.5 12.4 %collective-permute-start.4 = (bf16[1,400,512]{2,1,0:T(8,128)(2,1)S(1)}, bf16[1,400,512]{2,1,0:T(8,128)(2,1)S(1)}, u32[]{:S(2)}, u32[]{:S(2)}) collective-permute-start(bf16[1,400,512]{2,1,0:T(8,128)(2,1)S(1)} %collective-permute-done.refs_0_), channel_id=1, source_target_pairs={{0,2},{1,3},{2,0},{3,1},{4,8},{5,9},{6,10},{7,11},{8,4},{9,5},{10,... | collective-permute-start | bytes 1228808 | tf_op jit(solution)/shard_map/ppermute | solution.py:31
  31.2 13.4 %collective-permute-start.7 = (bf16[1,400,512]{2,1,0:T(8,128)(2,1)S(1)}, bf16[1,400,512]{2,1,0:T(8,128)(2,1)S(1)}, u32[]{:S(2)}, u32[]{:S(2)}) collective-permute-start(bf16[1,400,512]{2,1,0:T(8,128)(2,1)S(1)} %broadcast_select_fusion.1), channel_id=1, source_target_pairs={{0,2},{1,3},{2,0},{3,1},{4,6},{5,7},{6,4},{7,5},{8,10},{9,11},{10,... | collective-permute-start | bytes 1228808 | tf_op jit(solution)/shard_map/ppermute | solution.py:31
  32.2 12.4 %collective-permute-start.6 = (bf16[1,400,512]{2,1,0:T(8,128)(2,1)S(1)}, bf16[1,400,512]{2,1,0:T(8,128)(2,1)S(1)}, u32[]{:S(2)}, u32[]{:S(2)}) collective-permute-start(bf16[1,400,512]{2,1,0:T(8,128)(2,1)S(1)} %collective-permute-done.4.refs_1_), channel_id=1, source_target_pairs={{0,4},{1,5},{2,6},{3,7},{4,0},{5,1},{6,2},{7,3},{8,12},{9,13},{10,... | collective-permute-start | bytes 1228808 | tf_op jit(solution)/shard_map/ppermute | solution.py:31
  44.8 13.2 %collective-permute-start.9 = (bf16[1,400,512]{2,1,0:T(8,128)(2,1)S(1)}, bf16[1,400,512]{2,1,0:T(8,128)(2,1)S(1)}, u32[]{:S(2)}, u32[]{:S(2)}) collective-permute-start(bf16[1,400,512]{2,1,0:T(8,128)(2,1)S(1)} %broadcast_select_fusion), channel_id=1, source_target_pairs={{0,2},{1,3},{2,0},{3,1},{4,6},{5,7},{6,4},{7,5},{8,10},{9,11},{10,... | collective-permute-start | bytes 1228808 | tf_op jit(solution)/shard_map/ppermute | solution.py:31
  70.8 3.1 %collective-permute-start.12 = (bf16[384,512]{1,0:T(8,128)(2,1)S(1)}, bf16[384,512]{1,0:T(8,128)(2,1)S(1)}, u32[]{:S(2)}, u32[]{:S(2)}) collective-permute-start(bf16[384,512]{1,0:T(8,128)(2,1)S(1)} %get-tuple-element.73), channel_id=1, source_target_pairs={{0,1},{1,0},{2,3},{3,2},{4,5},{5,4},{6,7},{7,6},{8,9},{9,8},{10,11... | collective-permute-start | bytes 1179656 | tf_op jit(solution)/shard_map/ppermute | solution.py:35
  71.0 9.6 %collective-permute-start.15 = (bf16[384,512]{1,0:T(8,128)(2,1)S(1)}, bf16[384,512]{1,0:T(8,128)(2,1)S(1)}, u32[]{:S(2)}, u32[]{:S(2)}) collective-permute-start(bf16[384,512]{1,0:T(8,128)(2,1)S(1)} %get-tuple-element.78), channel_id=1, source_target_pairs={{0,1},{1,0},{2,3},{3,2},{4,5},{5,4},{6,7},{7,6},{8,9},{9,8},{10,11... | collective-permute-start | bytes 1179656 | tf_op jit(solution)/shard_map/ppermute | solution.py:35
  73.7 9.0 %collective-permute-start.13 = (bf16[384,512]{1,0:T(8,128)(2,1)S(1)}, bf16[384,512]{1,0:T(8,128)(2,1)S(1)}, u32[]{:S(2)}, u32[]{:S(2)}) collective-permute-start(bf16[384,512]{1,0:T(8,128)(2,1)S(1)} %get-tuple-element.76), channel_id=1, source_target_pairs={{0,1},{1,0},{2,3},{3,2},{4,5},{5,4},{6,7},{7,6},{8,9},{9,8},{10,11... | collective-permute-start | bytes 1179656 | tf_op jit(solution)/shard_map/ppermute | solution.py:35
  74.1 12.0 %collective-permute-start.14 = (bf16[384,512]{1,0:T(8,128)(2,1)S(1)}, bf16[384,512]{1,0:T(8,128)(2,1)S(1)}, u32[]{:S(2)}, u32[]{:S(2)}) collective-permute-start(bf16[384,512]{1,0:T(8,128)(2,1)S(1)} %add_convert_fusion.3), channel_id=1, source_target_pairs={{0,2},{1,3},{2,0},{3,1},{4,6},{5,7},{6,4},{7,5},{8,10},{9,11},{10,... | collective-permute-start | bytes 1179656 | tf_op jit(solution)/shard_map/ppermute | solution.py:31
  80.8 13.2 %collective-permute-start.17 = (bf16[384,512]{1,0:T(8,128)(2,1)S(1)}, bf16[384,512]{1,0:T(8,128)(2,1)S(1)}, u32[]{:S(2)}, u32[]{:S(2)}) collective-permute-start(bf16[384,512]{1,0:T(8,128)(2,1)S(1)} %add_convert_fusion.2), channel_id=1, source_target_pairs={{0,2},{1,3},{2,0},{3,1},{4,6},{5,7},{6,4},{7,5},{8,10},{9,11},{10,... | collective-permute-start | bytes 1179656 | tf_op jit(solution)/shard_map/ppermute | solution.py:31
  82.2 11.7 %collective-permute-start.16 = (bf16[384,512]{1,0:T(8,128)(2,1)S(1)}, bf16[384,512]{1,0:T(8,128)(2,1)S(1)}, u32[]{:S(2)}, u32[]{:S(2)}) collective-permute-start(bf16[384,512]{1,0:T(8,128)(2,1)S(1)} %get-tuple-element.81), channel_id=1, source_target_pairs={{0,1},{1,0},{2,3},{3,2},{4,5},{5,4},{6,7},{7,6},{8,9},{9,8},{10,11... | collective-permute-start | bytes 1179656 | tf_op jit(solution)/shard_map/ppermute | solution.py:35
  82.2 13.1 %collective-permute-start.18 = (bf16[384,512]{1,0:T(8,128)(2,1)S(1)}, bf16[384,512]{1,0:T(8,128)(2,1)S(1)}, u32[]{:S(2)}, u32[]{:S(2)}) collective-permute-start(bf16[384,512]{1,0:T(8,128)(2,1)S(1)} %get-tuple-element.83), channel_id=1, source_target_pairs={{0,1},{1,0},{2,3},{3,2},{4,5},{5,4},{6,7},{7,6},{8,9},{9,8},{10,11... | collective-permute-start | bytes 1179656 | tf_op jit(solution)/shard_map/ppermute | solution.py:35
  86.3 10.1 %collective-permute-start.19 = (bf16[384,512]{1,0:T(8,128)(2,1)S(1)}, bf16[384,512]{1,0:T(8,128)(2,1)S(1)}, u32[]{:S(2)}, u32[]{:S(2)}) collective-permute-start(bf16[384,512]{1,0:T(8,128)(2,1)S(1)} %fusion.1), channel_id=1, source_target_pairs={{0,4},{1,5},{2,6},{3,7},{4,0},{5,1},{6,2},{7,3},{8,12},{9,13},{10,... | collective-permute-start | bytes 1179656 | tf_op jit(solution)/shard_map/ppermute | solution.py:31
  94.2 10.6 %collective-permute-start.23 = (bf16[384,512]{1,0:T(8,128)(2,1)S(1)}, bf16[384,512]{1,0:T(8,128)(2,1)S(1)}, u32[]{:S(2)}, u32[]{:S(2)}) collective-permute-start(bf16[384,512]{1,0:T(8,128)(2,1)S(1)} %fusion.6), channel_id=1, source_target_pairs={{0,4},{1,5},{2,6},{3,7},{4,0},{5,1},{6,2},{7,3},{8,12},{9,13},{10,... | collective-permute-start | bytes 1179656 | tf_op jit(solution)/shard_map/ppermute | solution.py:31
  94.8 10.0 %collective-permute-start.22 = (bf16[384,512]{1,0:T(8,128)(2,1)S(1)}, bf16[384,512]{1,0:T(8,128)(2,1)S(1)}, u32[]{:S(2)}, u32[]{:S(2)}) collective-permute-start(bf16[384,512]{1,0:T(8,128)(2,1)S(1)} %get-tuple-element.88), channel_id=1, source_target_pairs={{0,1},{1,0},{2,3},{3,2},{4,5},{5,4},{6,7},{7,6},{8,9},{9,8},{10,11... | collective-permute-start | bytes 1179656 | tf_op jit(solution)/shard_map/ppermute | solution.py:35
  94.8 11.0 %collective-permute-start.20 = (bf16[384,512]{1,0:T(8,128)(2,1)S(1)}, bf16[384,512]{1,0:T(8,128)(2,1)S(1)}, u32[]{:S(2)}, u32[]{:S(2)}) collective-permute-start(bf16[384,512]{1,0:T(8,128)(2,1)S(1)} %get-tuple-element.86), channel_id=1, source_target_pairs={{0,1},{1,0},{2,3},{3,2},{4,5},{5,4},{6,7},{7,6},{8,9},{9,8},{10,11... | collective-permute-start | bytes 1179656 | tf_op jit(solution)/shard_map/ppermute | solution.py:35
  96.6 10.3 %collective-permute-start.21 = (bf16[384,512]{1,0:T(8,128)(2,1)S(1)}, bf16[384,512]{1,0:T(8,128)(2,1)S(1)}, u32[]{:S(2)}, u32[]{:S(2)}) collective-permute-start(bf16[384,512]{1,0:T(8,128)(2,1)S(1)} %fusion.4), channel_id=1, source_target_pairs={{0,2},{1,3},{2,0},{3,1},{4,8},{5,9},{6,10},{7,11},{8,4},{9,5},{10,... | collective-permute-start | bytes 1179656 | tf_op jit(solution)/shard_map/ppermute | solution.py:31
  105.1 10.1 %collective-permute-start.26 = (bf16[384,512]{1,0:T(8,128)(2,1)S(1)}, bf16[384,512]{1,0:T(8,128)(2,1)S(1)}, u32[]{:S(2)}, u32[]{:S(2)}) collective-permute-start(bf16[384,512]{1,0:T(8,128)(2,1)S(1)} %fusion.9), channel_id=1, source_target_pairs={{0,2},{1,3},{2,0},{3,1},{4,8},{5,9},{6,10},{7,11},{8,4},{9,5},{10,... | collective-permute-start | bytes 1179656 | tf_op jit(solution)/shard_map/ppermute | solution.py:31
  105.8 9.3 %collective-permute-start.24 = (bf16[384,512]{1,0:T(8,128)(2,1)S(1)}, bf16[384,512]{1,0:T(8,128)(2,1)S(1)}, u32[]{:S(2)}, u32[]{:S(2)}) collective-permute-start(bf16[384,512]{1,0:T(8,128)(2,1)S(1)} %get-tuple-element.90), channel_id=1, source_target_pairs={{0,1},{1,0},{2,3},{3,2},{4,5},{5,4},{6,7},{7,6},{8,9},{9,8},{10,11... | collective-permute-start | bytes 1179656 | tf_op jit(solution)/shard_map/ppermute | solution.py:35
  107.2 10.4 %collective-permute-start.25 = (bf16[384,512]{1,0:T(8,128)(2,1)S(1)}, bf16[384,512]{1,0:T(8,128)(2,1)S(1)}, u32[]{:S(2)}, u32[]{:S(2)}) collective-permute-start(bf16[384,512]{1,0:T(8,128)(2,1)S(1)} %add_convert_fusion.1), channel_id=1, source_target_pairs={{0,4},{1,5},{2,6},{3,7},{4,0},{5,1},{6,2},{7,3},{8,12},{9,13},{10,... | collective-permute-start | bytes 1179656 | tf_op jit(solution)/shard_map/ppermute | solution.py:31
  (5 other events, 18.3 us)

commit v10 on v8

--- a/solution.py
+++ b/solution.py
@@ -80,14 +80,35 @@
 
 def gate_up_body(count, first, last, rows, main, features, me_ref, *refs):
     blocks = refs[:count]
+    if last:
+        *refs, buffer_ref, sems = refs
     gate_ref, up_ref, *rest = refs[count:]
     if not first:
         before = rest[:4]
         rest = rest[4:]
     if last:
-        hidden_ref, *rest = rest
+        down_ref, hidden_ref, *rest = rest
+        *outs, _, _, _, _ = rest
+        rest = rest[len(outs) :]
+        width = outs[0].shape[1]
+        copies = []
+        for i, job in enumerate(last):
+            column = pl.multiple_of(block(me_ref[0], [job], 0) * width, width)
+            at = pl.ds(i * width, width)
+            copies.append(
+                pltpu.make_async_copy(
+                    down_ref.at[:, pl.ds(column, width)], buffer_ref.at[:, at], sems.at[i]
+                )
+            )
     accs = rest
     step = pl.program_id(0)
+
+    if last:
+
+        @pl.when(step == 0)
+        def _():
+            for copy in copies:
+                copy.start()
 
     for s in range(count):
 
@@ -122,9 +143,16 @@
             rem = both.shape[1] // 2
             hidden_ref[:, :main] = act(gate, up)
             hidden_ref[:, main:] = act(both[:, :rem], both[:, rem:])
-
-
-def gate_up(me, jobs, shards, gate_weight, up_weight, acc, last=False):
+            for i in range(0, len(outs), 2):
+                pair = slice(i, i + 2)
+                for copy in copies[pair]:
+                    copy.wait()
+                value = down_block(hidden_ref, buffer_ref.at[:, i * width : (i + 2) * width])
+                for n, out in enumerate(outs[pair]):
+                    out[...] = value[:, n * width : (n + 1) * width].astype(out.dtype)
+
+
+def gate_up(me, jobs, shards, gate_weight, up_weight, acc, last=(), kinds=(), down_weight=None):
     height, depth = shards[0][0].shape[1:]
     count = len(jobs)
     rows = height - EXTRA
@@ -142,9 +170,16 @@
         in_specs += [whole(s) for s in shapes]
         args += list(acc)
     if last:
+        in_specs += [pl.BlockSpec(memory_space=pl.ANY)]
+        args += [down_weight]
         out_shape = [jax.ShapeDtypeStruct((rows, ff), jnp.bfloat16)]
-        out_specs = [whole((rows, ff))]
+        out_shape += [jax.ShapeDtypeStruct((rows, depth), kind) for kind in kinds]
+        out_specs = [whole(x.shape) for x in out_shape]
         scratch = [pltpu.VMEM(s, jnp.float32) for s in shapes]
+        scratch += [
+            pltpu.VMEM((ff, len(last) * depth), jnp.bfloat16),
+            pltpu.SemaphoreType.DMA((len(last),)),
+        ]
     else:
         out_shape = [jax.ShapeDtypeStruct(s, jnp.float32) for s in shapes]
         out_specs = [whole(s) for s in shapes]
@@ -233,13 +268,14 @@
     resident = activations.astype(jnp.float32)
     OWN, ONE, ONE_IN, TWO, TWO_IN, THREE, THREE_ACROSS, FOUR = range(8)
 
-    def multiply(acc, places, shards, last=False):
+    def multiply(acc, places, shards, *more):
         theirs = swap(shards[0] if len(shards) == 1 else jnp.concatenate(shards))
         jobs = [(place, 0) for place in places] + [(place, 1) for place in places]
         arrays = [(x, 0) for x in shards] + [(theirs, i) for i in range(len(places))]
-        return gate_up(me, jobs, arrays, gate_weight, up_weight, acc, last)
-
-    own = prepare(activations, norm_gain)
+        return gate_up(me, jobs, arrays, gate_weight, up_weight, acc, *more)
+
+    early, end = lax.optimization_barrier((activations, end))
+    own = prepare(early, norm_gain)
     one, one_in = send(own, ALONG), send(own, INSIDE)
     acc = multiply(None, (OWN,), (own,))
     one, one_in = after((one, one_in), acc[3])
@@ -252,7 +288,15 @@
     four = send(jnp.where(end, three, two_in), ACROSS)
     acc = multiply(acc, (THREE, THREE_ACROSS), (three, across))
     four = after(four, acc[3])
-    hidden = multiply(acc, (FOUR,), (four,), last=True)[0]
+    narrow_kind = jnp.bfloat16
+    hidden, their_four, four, their_three, their_across = multiply(
+        acc,
+        (FOUR,),
+        (four,),
+        ((FOUR, 1), (FOUR, 0), (THREE, 1), (THREE_ACROSS, 1)),
+        (narrow_kind, jnp.float32, narrow_kind, narrow_kind),
+        down_weight,
+    )
 
     narrow = lambda x: x.astype(jnp.bfloat16)
     wide = lambda x: x.astype(jnp.float32)
@@ -263,8 +307,9 @@
         outs = down(me, kept_jobs, sent_jobs, hidden, down_weight, width)
         return [*outs[: len(kept)], *(wide(swap(x)) for x in outs[len(kept) :])]
 
-    their_four, their_three, their_across = partials(hidden, (), (FOUR, THREE, THREE_ACROSS))
-    (four,) = partials(hidden, (FOUR,), ())
+    their_four, their_three, their_across = (
+        wide(swap(x)) for x in (their_four, their_three, their_across)
+    )
     four = narrow(four + their_four)
     got = wide(send(four, ACROSS))
     three, across, their_two, their_in = partials(

time: 118 us -> 114 us (0.966)
  local copies, waits for them, and re-layouts: 7.22 us -> 1.04 us
  waiting for transfers between devices: 23.6 us -> 28.9 us
  starting transfers between devices: 20.1 us -> 18.6 us
  Pallas kernels: 64 us -> 62.8 us
    pallas_call x6 -> x4, Pallas kernels: 25.7 us -> 18.7 us  [down(): pl.pallas_call(functools.partial(down_body, len(kept), len(sent)), grid_s...]
    unnamed x12 -> x4, local copies, waits for them, and re-layouts: 7.22 us -> 1.04 us
    pallas_call x5, Pallas kernels: 36.3 us -> 42.1 us  [gate_up(): pl.pallas_call(functools.partial(gate_up_body, count, first, last, rows,...]
    ppermute x14, waiting for transfers between devices: 20.4 us -> 24.3 us  [send(): return lax.ppermute(x, 'gx', pairs)]
    ppermute x13, waiting for transfers between devices: 3.22 us -> 4.63 us  [swap(): return lax.ppermute(x, 'gx', [(i, i ^ 1) for i in range(4 * LINE)])]
    ppermute x14, starting transfers between devices: 17.6 us -> 16.2 us  [send(): return lax.ppermute(x, 'gx', pairs)]
  transfers between devices with their start and end apart: 27 -> 27, of which waited for: 12 -> 18; matrix products, arithmetic and copies ran while one was open for 1% -> 1% of each run, Pallas kernels for 44% -> 44%
where the time goes in v10:
time: 114 us
  Pallas kernels  62.8 us (55%)
  waiting for transfers between devices  28.9 us (25%)
  starting transfers between devices  18.6 us (16%)
  other arithmetic  2.65 us (2%)
    pallas_call x5, Pallas kernels, gate_up(): pl.pallas_call(functools.partial(gate_up_body, count, first, last, rows,...  42.1 us
    ppermute x14, waiting for transfers between devices, send(): return lax.ppermute(x, 'gx', pairs)  24.3 us
    pallas_call x4, Pallas kernels, down(): pl.pallas_call(functools.partial(down_body, len(kept), len(sent)), grid_s...  18.7 us
    ppermute x14, starting transfers between devices, send(): return lax.ppermute(x, 'gx', pairs)  16.2 us
    ppermute x13, waiting for transfers between devices, swap(): return lax.ppermute(x, 'gx', [(i, i ^ 1) for i in range(4 * LINE)])  4.63 us
    ppermute x13, starting transfers between devices, swap(): return lax.ppermute(x, 'gx', [(i, i ^ 1) for i in range(4 * LINE)])  2.4 us
  transfers between devices with their start and end apart: 27, of which 18 were waited for; matrix products, arithmetic and copies ran while one was open for 1% of the time, Pallas kernels for 44%

profile of v10, /device:TPU:0, one launch (start us, length us, event | category | flops | bytes accessed | tf_op | source)
XLA Modules:
  0.0 114.2 jit_solution(15719807017302093831)
XLA Ops:
  0.0 2.0 %prepare.1.refs_0_ = bf16[1,400,512]{2,1,0:T(8,128)(2,1)} custom-call(bf16[384,512]{1,0:T(8,128)(2,1)} %x_ref, bf16[512]{0:T(512)(128)(2,1)} %gain_ref.1), custom_call_target="tpu_custom_call" | custom-call | tf_op jit(solution)/shard_map/prepare/pallas_call | solution.py:73
  2.4 2.6 %collective-permute-start = (bf16[1,400,512]{2,1,0:T(8,128)(2,1)}, bf16[1,400,512]{2,1,0:T(8,128)(2,1)S(1)}, u32[]{:S(2)}, u32[]{:S(2)}) collective-permute-start(bf16[1,400,512]{2,1,0:T(8,128)(2,1)} %prepare.1.refs_0_), channel_id=1, source_target_pairs={{0,4},{1,5},{2,6},{3,7},{4,0},{5,1},{6,2},{7,3},{8,12},{9,13},{10,... | collective-permute-start | bytes 1228808 | tf_op jit(solution)/shard_map/ppermute | solution.py:30
  5.0 1.5 %collective-permute-start.1 = (bf16[1,400,512]{2,1,0:T(8,128)(2,1)}, bf16[1,400,512]{2,1,0:T(8,128)(2,1)S(1)}, u32[]{:S(2)}, u32[]{:S(2)}) collective-permute-start(bf16[1,400,512]{2,1,0:T(8,128)(2,1)} %prepare.1.refs_0_), channel_id=1, source_target_pairs={{0,2},{1,3},{2,0},{3,1},{4,8},{5,9},{6,10},{7,11},{8,4},{9,5},{10,... | collective-permute-start | bytes 1228808 | tf_op jit(solution)/shard_map/ppermute | solution.py:30
  7.6 5.0 %gate_up.5 = (f32[384,1536]{1,0:T(8,128)S(1)}, f32[384,1536]{1,0:T(8,128)S(1)}, f32[384,256]{1,0:T(8,128)S(1)}, f32[8,512]{1,0:T(8,128)S(1)}) custom-call(s32[1]{0:T(128)} %bitcast.me_ref, bf16[1,400,512]{2,1,0:T(8,128)(2,1)S(1)} %copy-done, bf16[1,400,512]{2,1,0:T(8,128)(2,1)S(1)} %collective-permute-done.2.refs_1_, bf16[8192,1664]{1,0:T(8,128)(2,1)} %refs_2_.3, ...), custom_call_target="tpu_custom_call" | custom-call | flops 327155712 | bytes 851968 | tf_op jit(solution)/shard_map/gate_up/pallas_call | solution.py:187
  12.6 2.8 %collective-permute-done.refs_0_ = bf16[1,400,512]{2,1,0:T(8,128)(2,1)S(1)} collective-permute-done((bf16[1,400,512]{2,1,0:T(8,128)(2,1)}, bf16[1,400,512]{2,1,0:T(8,128)(2,1)S(1)}, u32[]{:S(2)}, u32[]{:S(2)}) %collective-permute-start) | collective-permute-done | bytes 409632 | tf_op jit(solution)/shard_map/ppermute | solution.py:30
  18.5 1.5 %collective-permute-start.4 = (bf16[1,400,512]{2,1,0:T(8,128)(2,1)S(1)}, bf16[1,400,512]{2,1,0:T(8,128)(2,1)S(1)}, u32[]{:S(2)}, u32[]{:S(2)}) collective-permute-start(bf16[1,400,512]{2,1,0:T(8,128)(2,1)S(1)} %collective-permute-done.refs_0_), channel_id=1, source_target_pairs={{0,2},{1,3},{2,0},{3,1},{4,8},{5,9},{6,10},{7,11},{8,4},{9,5},{10,... | collective-permute-start | bytes 1228808 | tf_op jit(solution)/shard_map/ppermute | solution.py:30
  20.0 8.8 %gate_up.6 = (f32[384,1536]{1,0:T(8,128)S(1)}, f32[384,1536]{1,0:T(8,128)S(1)}, f32[384,256]{1,0:T(8,128)S(1)}, f32[8,512]{1,0:T(8,128)S(1)}) custom-call(s32[1]{0:T(128)} %bitcast.me_ref, bf16[1,400,512]{2,1,0:T(8,128)(2,1)S(1)} %collective-permute-done.refs_0_, bf16[1,400,512]{2,1,0:T(8,128)(2,1)S(1)} %collective-permute-done.1.refs_1_, ...), custom_call_target="tpu_custom_call" | custom-call | flops 654311424 | bytes 1703936 | tf_op jit(solution)/shard_map/gate_up/pallas_call | solution.py:187
  30.2 1.6 %collective-permute-start.7 = (bf16[1,400,512]{2,1,0:T(8,128)(2,1)S(1)}, bf16[1,400,512]{2,1,0:T(8,128)(2,1)S(1)}, u32[]{:S(2)}, u32[]{:S(2)}) collective-permute-start(bf16[1,400,512]{2,1,0:T(8,128)(2,1)S(1)} %broadcast_select_fusion.1), channel_id=1, source_target_pairs={{0,2},{1,3},{2,0},{3,1},{4,6},{5,7},{6,4},{7,5},{8,10},{9,11},{10,... | collective-permute-start | bytes 1228808 | tf_op jit(solution)/shard_map/ppermute | solution.py:30
  32.5 8.6 %gate_up.7 = (f32[384,1536]{1,0:T(8,128)S(1)}, f32[384,1536]{1,0:T(8,128)S(1)}, f32[384,256]{1,0:T(8,128)S(1)}, f32[8,512]{1,0:T(8,128)S(1)}) custom-call(s32[1]{0:T(128)} %bitcast.me_ref, bf16[1,400,512]{2,1,0:T(8,128)(2,1)S(1)} %collective-permute-done.3.refs_0_, bf16[1,400,512]{2,1,0:T(8,128)(2,1)S(1)} %collective-permute-done.4.refs_1_, ...), custom_call_target="tpu_custom_call" | custom-call | flops 654311424 | bytes 1703936 | tf_op jit(solution)/shard_map/gate_up/pallas_call | solution.py:187
  44.2 1.7 %collective-permute-done.10.refs_2_.refs_3_ = bf16[2,400,512]{2,1,0:T(8,128)(2,1)S(1)} collective-permute-done((bf16[2,400,512]{2,1,0:T(8,128)(2,1)S(1)}, bf16[2,400,512]{2,1,0:T(8,128)(2,1)S(1)}, u32[]{:S(2)}, u32[]{:S(2)}) %collective-permute-start.10) | collective-permute-done | bytes 819232 | tf_op jit(solution)/shard_map/ppermute | solution.py:34
  45.9 8.6 %gate_up.8 = (f32[384,1536]{1,0:T(8,128)S(1)}, f32[384,1536]{1,0:T(8,128)S(1)}, f32[384,256]{1,0:T(8,128)S(1)}, f32[8,512]{1,0:T(8,128)S(1)}) custom-call(s32[1]{0:T(128)} %bitcast.me_ref, bf16[1,400,512]{2,1,0:T(8,128)(2,1)S(1)} %collective-permute-done.6.refs_0_, bf16[1,400,512]{2,1,0:T(8,128)(2,1)S(1)} %collective-permute-done.7.refs_1_, ...), custom_call_target="tpu_custom_call" | custom-call | flops 654311424 | bytes 1703936 | tf_op jit(solution)/shard_map/gate_up/pallas_call | solution.py:187
  55.6 1.7 %collective-permute-done.11.refs_1_ = bf16[1,400,512]{2,1,0:T(8,128)(2,1)S(1)} collective-permute-done((bf16[1,400,512]{2,1,0:T(8,128)(2,1)S(1)}, bf16[1,400,512]{2,1,0:T(8,128)(2,1)S(1)}, u32[]{:S(2)}, u32[]{:S(2)}) %collective-permute-start.11) | collective-permute-done | bytes 409632 | tf_op jit(solution)/shard_map/ppermute | solution.py:34
  57.3 11.0 %gate_up.9 = (bf16[384,1664]{1,0:T(8,128)(2,1)S(1)}, bf16[384,512]{1,0:T(8,128)(2,1)S(1)}, f32[384,512]{1,0:T(8,128)S(1)}, bf16[384,512]{1,0:T(8,128)(2,1)S(1)}, bf16[384,512]{1,0:T(8,128)(2,1)S(1)}) custom-call(s32[1]{0:T(128)} %bitcast.me_ref, bf16[1,400,512]{2,1,0:T(8,128)(2,1)S(1)} %collective-permute-done.9.refs_0_, ...), custom_call_target="tpu_custom_call" | custom-call | flops 327155712 | bytes 851968 | tf_op jit(solution)/shard_map/gate_up/pallas_call | solution.py:187
  70.8 5.8 %down.4 = (f32[384,512]{1,0:T(8,128)S(1)}, f32[384,512]{1,0:T(8,128)S(1)}, bf16[384,512]{1,0:T(8,128)(2,1)S(1)}, bf16[384,512]{1,0:T(8,128)(2,1)S(1)}) custom-call(s32[1]{0:T(128)} %bitcast.me_ref, bf16[384,1664]{1,0:T(8,128)(2,1)S(1)} %get-tuple-element.93.hidden_ref, bf16[1664,8192]{1,0:T(8,128)(2,1)} %weight_ref.7), custom_call_target="tpu_custom_call" | custom-call | flops 327155712 | bytes 851968 | tf_op jit(solution)/shard_map/down/pallas_call | solution.py:240
  76.8 1.6 %collective-permute-start.17 = (bf16[384,512]{1,0:T(8,128)(2,1)S(1)}, bf16[384,512]{1,0:T(8,128)(2,1)S(1)}, u32[]{:S(2)}, u32[]{:S(2)}) collective-permute-start(bf16[384,512]{1,0:T(8,128)(2,1)S(1)} %add_convert_fusion.2), channel_id=1, source_target_pairs={{0,2},{1,3},{2,0},{3,1},{4,6},{5,7},{6,4},{7,5},{8,10},{9,11},{10,... | collective-permute-start | bytes 1179656 | tf_op jit(solution)/shard_map/ppermute | solution.py:30
  78.9 3.4 %collective-permute-done.14 = bf16[384,512]{1,0:T(8,128)(2,1)S(1)} collective-permute-done((bf16[384,512]{1,0:T(8,128)(2,1)S(1)}, bf16[384,512]{1,0:T(8,128)(2,1)S(1)}, u32[]{:S(2)}, u32[]{:S(2)}) %collective-permute-start.14) | collective-permute-done | bytes 393248 | tf_op jit(solution)/shard_map/ppermute | solution.py:30
  83.1 5.8 %down.5 = (f32[384,512]{1,0:T(8,128)S(1)}, f32[384,512]{1,0:T(8,128)S(1)}, bf16[384,512]{1,0:T(8,128)(2,1)S(1)}, bf16[384,512]{1,0:T(8,128)(2,1)S(1)}) custom-call(s32[1]{0:T(128)} %bitcast.me_ref, bf16[384,1664]{1,0:T(8,128)(2,1)S(1)} %get-tuple-element.93.hidden_ref, bf16[1664,8192]{1,0:T(8,128)(2,1)} %weight_ref.7), custom_call_target="tpu_custom_call" | custom-call | flops 327155712 | bytes 851968 | tf_op jit(solution)/shard_map/down/pallas_call | solution.py:240
  92.9 4.7 %down.6 = (f32[384,512]{1,0:T(8,128)S(1)}, f32[384,512]{1,0:T(8,128)S(1)}, bf16[384,512]{1,0:T(8,128)(2,1)S(1)}) custom-call(s32[1]{0:T(128)} %bitcast.me_ref, bf16[384,1664]{1,0:T(8,128)(2,1)S(1)} %get-tuple-element.93.hidden_ref, bf16[1664,8192]{1,0:T(8,128)(2,1)} %weight_ref.7), custom_call_target="tpu_custom_call" | custom-call | flops 245366784 | bytes 638976 | tf_op jit(solution)/shard_map/down/pallas_call | solution.py:240
  97.6 2.9 %collective-permute-done.23 = bf16[384,512]{1,0:T(8,128)(2,1)S(1)} collective-permute-done((bf16[384,512]{1,0:T(8,128)(2,1)S(1)}, bf16[384,512]{1,0:T(8,128)(2,1)S(1)}, u32[]{:S(2)}, u32[]{:S(2)}) %collective-permute-start.23) | collective-permute-done | bytes 393248 | tf_op jit(solution)/shard_map/ppermute | solution.py:30
  101.3 2.0 %collective-permute-done.21 = bf16[384,512]{1,0:T(8,128)(2,1)S(1)} collective-permute-done((bf16[384,512]{1,0:T(8,128)(2,1)S(1)}, bf16[384,512]{1,0:T(8,128)(2,1)S(1)}, u32[]{:S(2)}, u32[]{:S(2)}) %collective-permute-start.21) | collective-permute-done | bytes 393248 | tf_op jit(solution)/shard_map/ppermute | solution.py:30
  103.5 1.7 %collective-permute-start.25 = (bf16[384,512]{1,0:T(8,128)(2,1)S(1)}, bf16[384,512]{1,0:T(8,128)(2,1)S(1)}, u32[]{:S(2)}, u32[]{:S(2)}) collective-permute-start(bf16[384,512]{1,0:T(8,128)(2,1)S(1)} %add_convert_fusion.1), channel_id=1, source_target_pairs={{0,4},{1,5},{2,6},{3,7},{4,0},{5,1},{6,2},{7,3},{8,12},{9,13},{10,... | collective-permute-start | bytes 1179656 | tf_op jit(solution)/shard_map/ppermute | solution.py:30
  105.2 2.3 %down.7 = f32[384,512]{1,0:T(8,128)S(1)} custom-call(s32[1]{0:T(128)} %bitcast.me_ref, bf16[384,1664]{1,0:T(8,128)(2,1)S(1)} %get-tuple-element.93.hidden_ref, bf16[1664,8192]{1,0:T(8,128)(2,1)} %weight_ref.7), custom_call_target="tpu_custom_call" | custom-call | flops 81788928 | bytes 212992 | tf_op jit(solution)/shard_map/down/pallas_call | solution.py:240
  107.5 3.5 %collective-permute-done.26 = bf16[384,512]{1,0:T(8,128)(2,1)S(1)} collective-permute-done((bf16[384,512]{1,0:T(8,128)(2,1)S(1)}, bf16[384,512]{1,0:T(8,128)(2,1)S(1)}, u32[]{:S(2)}, u32[]{:S(2)}) %collective-permute-start.26) | collective-permute-done | bytes 393248 | tf_op jit(solution)/shard_map/ppermute | solution.py:30
  111.0 2.1 %collective-permute-done.25 = bf16[384,512]{1,0:T(8,128)(2,1)S(1)} collective-permute-done((bf16[384,512]{1,0:T(8,128)(2,1)S(1)}, bf16[384,512]{1,0:T(8,128)(2,1)S(1)}, u32[]{:S(2)}, u32[]{:S(2)}) %collective-permute-start.25) | collective-permute-done | bytes 393248 | tf_op jit(solution)/shard_map/ppermute | solution.py:30
  (57 shorter events, 20.7 us)
Async XLA Ops:
  2.0 4.5 %collective-permute-start.2 = (bf16[1,400,512]{2,1,0:T(8,128)(2,1)}, bf16[1,400,512]{2,1,0:T(8,128)(2,1)S(1)}, u32[]{:S(2)}, u32[]{:S(2)}) collective-permute-start(bf16[1,400,512]{2,1,0:T(8,128)(2,1)} %prepare.1.refs_0_), channel_id=1, source_target_pairs={{0,1},{1,0},{2,3},{3,2},{4,5},{5,4},{6,7},{7,6},{8,9},{9,8},{10,11... | collective-permute-start | bytes 1228808 | tf_op jit(solution)/shard_map/ppermute | solution.py:34
  2.4 12.9 %collective-permute-start = (bf16[1,400,512]{2,1,0:T(8,128)(2,1)}, bf16[1,400,512]{2,1,0:T(8,128)(2,1)S(1)}, u32[]{:S(2)}, u32[]{:S(2)}) collective-permute-start(bf16[1,400,512]{2,1,0:T(8,128)(2,1)} %prepare.1.refs_0_), channel_id=1, source_target_pairs={{0,4},{1,5},{2,6},{3,7},{4,0},{5,1},{6,2},{7,3},{8,12},{9,13},{10,... | collective-permute-start | bytes 1228808 | tf_op jit(solution)/shard_map/ppermute | solution.py:30
  5.0 11.8 %collective-permute-start.1 = (bf16[1,400,512]{2,1,0:T(8,128)(2,1)}, bf16[1,400,512]{2,1,0:T(8,128)(2,1)S(1)}, u32[]{:S(2)}, u32[]{:S(2)}) collective-permute-start(bf16[1,400,512]{2,1,0:T(8,128)(2,1)} %prepare.1.refs_0_), channel_id=1, source_target_pairs={{0,2},{1,3},{2,0},{3,1},{4,8},{5,9},{6,10},{7,11},{8,4},{9,5},{10,... | collective-permute-start | bytes 1228808 | tf_op jit(solution)/shard_map/ppermute | solution.py:30
  16.9 3.1 %collective-permute-start.5 = (bf16[2,400,512]{2,1,0:T(8,128)(2,1)S(1)}, bf16[2,400,512]{2,1,0:T(8,128)(2,1)S(1)}, u32[]{:S(2)}, u32[]{:S(2)}) collective-permute-start(bf16[2,400,512]{2,1,0:T(8,128)(2,1)S(1)} %pad_maximum_fusion), channel_id=1, source_target_pairs={{0,1},{1,0},{2,3},{3,2},{4,5},{5,4},{6,7},{7,6},{8,9},{9,8},{10,11... | collective-permute-start | bytes 2457608 | tf_op jit(solution)/shard_map/ppermute | solution.py:34
  17.0 11.9 %collective-permute-start.3 = (bf16[1,400,512]{2,1,0:T(8,128)(2,1)S(1)}, bf16[1,400,512]{2,1,0:T(8,128)(2,1)S(1)}, u32[]{:S(2)}, u32[]{:S(2)}) collective-permute-start(bf16[1,400,512]{2,1,0:T(8,128)(2,1)S(1)} %collective-permute-done.1.refs_1_), channel_id=1, source_target_pairs={{0,4},{1,5},{2,6},{3,7},{4,0},{5,1},{6,2},{7,3},{8,12},{9,13},{10,... | collective-permute-start | bytes 1228808 | tf_op jit(solution)/shard_map/ppermute | solution.py:30
  18.5 11.5 %collective-permute-start.4 = (bf16[1,400,512]{2,1,0:T(8,128)(2,1)S(1)}, bf16[1,400,512]{2,1,0:T(8,128)(2,1)S(1)}, u32[]{:S(2)}, u32[]{:S(2)}) collective-permute-start(bf16[1,400,512]{2,1,0:T(8,128)(2,1)S(1)} %collective-permute-done.refs_0_), channel_id=1, source_target_pairs={{0,2},{1,3},{2,0},{3,1},{4,8},{5,9},{6,10},{7,11},{8,4},{9,5},{10,... | collective-permute-start | bytes 1228808 | tf_op jit(solution)/shard_map/ppermute | solution.py:30
  30.1 2.4 %collective-permute-start.8 = (bf16[2,400,512]{2,1,0:T(8,128)(2,1)S(1)}, bf16[2,400,512]{2,1,0:T(8,128)(2,1)S(1)}, u32[]{:S(2)}, u32[]{:S(2)}) collective-permute-start(bf16[2,400,512]{2,1,0:T(8,128)(2,1)S(1)} %pad_maximum_fusion.1), channel_id=1, source_target_pairs={{0,1},{1,0},{2,3},{3,2},{4,5},{5,4},{6,7},{7,6},{8,9},{9,8},{10,11... | collective-permute-start | bytes 2457608 | tf_op jit(solution)/shard_map/ppermute | solution.py:34
  30.2 11.9 %collective-permute-start.7 = (bf16[1,400,512]{2,1,0:T(8,128)(2,1)S(1)}, bf16[1,400,512]{2,1,0:T(8,128)(2,1)S(1)}, u32[]{:S(2)}, u32[]{:S(2)}) collective-permute-start(bf16[1,400,512]{2,1,0:T(8,128)(2,1)S(1)} %broadcast_select_fusion.1), channel_id=1, source_target_pairs={{0,2},{1,3},{2,0},{3,1},{4,6},{5,7},{6,4},{7,5},{8,10},{9,11},{10,... | collective-permute-start | bytes 1228808 | tf_op jit(solution)/shard_map/ppermute | solution.py:30
  31.8 11.6 %collective-permute-start.6 = (bf16[1,400,512]{2,1,0:T(8,128)(2,1)S(1)}, bf16[1,400,512]{2,1,0:T(8,128)(2,1)S(1)}, u32[]{:S(2)}, u32[]{:S(2)}) collective-permute-start(bf16[1,400,512]{2,1,0:T(8,128)(2,1)S(1)} %collective-permute-done.4.refs_1_), channel_id=1, source_target_pairs={{0,4},{1,5},{2,6},{3,7},{4,0},{5,1},{6,2},{7,3},{8,12},{9,13},{10,... | collective-permute-start | bytes 1228808 | tf_op jit(solution)/shard_map/ppermute | solution.py:30
  43.6 11.9 %collective-permute-start.9 = (bf16[1,400,512]{2,1,0:T(8,128)(2,1)S(1)}, bf16[1,400,512]{2,1,0:T(8,128)(2,1)S(1)}, u32[]{:S(2)}, u32[]{:S(2)}) collective-permute-start(bf16[1,400,512]{2,1,0:T(8,128)(2,1)S(1)} %broadcast_select_fusion), channel_id=1, source_target_pairs={{0,2},{1,3},{2,0},{3,1},{4,6},{5,7},{6,4},{7,5},{8,10},{9,11},{10,... | collective-permute-start | bytes 1228808 | tf_op jit(solution)/shard_map/ppermute | solution.py:30
  68.5 8.1 %collective-permute-start.15 = (bf16[384,512]{1,0:T(8,128)(2,1)S(1)}, bf16[384,512]{1,0:T(8,128)(2,1)S(1)}, u32[]{:S(2)}, u32[]{:S(2)}) collective-permute-start(bf16[384,512]{1,0:T(8,128)(2,1)S(1)} %get-tuple-element.82), channel_id=1, source_target_pairs={{0,1},{1,0},{2,3},{3,2},{4,5},{5,4},{6,7},{7,6},{8,9},{9,8},{10,11... | collective-permute-start | bytes 1179656 | tf_op jit(solution)/shard_map/ppermute | solution.py:34
  68.9 10.0 %collective-permute-start.13 = (bf16[384,512]{1,0:T(8,128)(2,1)S(1)}, bf16[384,512]{1,0:T(8,128)(2,1)S(1)}, u32[]{:S(2)}, u32[]{:S(2)}) collective-permute-start(bf16[384,512]{1,0:T(8,128)(2,1)S(1)} %get-tuple-element.80), channel_id=1, source_target_pairs={{0,1},{1,0},{2,3},{3,2},{4,5},{5,4},{6,7},{7,6},{8,9},{9,8},{10,11... | collective-permute-start | bytes 1179656 | tf_op jit(solution)/shard_map/ppermute | solution.py:34
  70.2 12.0 %collective-permute-start.14 = (bf16[384,512]{1,0:T(8,128)(2,1)S(1)}, bf16[384,512]{1,0:T(8,128)(2,1)S(1)}, u32[]{:S(2)}, u32[]{:S(2)}) collective-permute-start(bf16[384,512]{1,0:T(8,128)(2,1)S(1)} %add_convert_fusion.3), channel_id=1, source_target_pairs={{0,2},{1,3},{2,0},{3,1},{4,6},{5,7},{6,4},{7,5},{8,10},{9,11},{10,... | collective-permute-start | bytes 1179656 | tf_op jit(solution)/shard_map/ppermute | solution.py:30
  76.8 13.1 %collective-permute-start.17 = (bf16[384,512]{1,0:T(8,128)(2,1)S(1)}, bf16[384,512]{1,0:T(8,128)(2,1)S(1)}, u32[]{:S(2)}, u32[]{:S(2)}) collective-permute-start(bf16[384,512]{1,0:T(8,128)(2,1)S(1)} %add_convert_fusion.2), channel_id=1, source_target_pairs={{0,2},{1,3},{2,0},{3,1},{4,6},{5,7},{6,4},{7,5},{8,10},{9,11},{10,... | collective-permute-start | bytes 1179656 | tf_op jit(solution)/shard_map/ppermute | solution.py:30
  78.4 11.5 %collective-permute-start.16 = (bf16[384,512]{1,0:T(8,128)(2,1)S(1)}, bf16[384,512]{1,0:T(8,128)(2,1)S(1)}, u32[]{:S(2)}, u32[]{:S(2)}) collective-permute-start(bf16[384,512]{1,0:T(8,128)(2,1)S(1)} %get-tuple-element.85), channel_id=1, source_target_pairs={{0,1},{1,0},{2,3},{3,2},{4,5},{5,4},{6,7},{7,6},{8,9},{9,8},{10,11... | collective-permute-start | bytes 1179656 | tf_op jit(solution)/shard_map/ppermute | solution.py:34
  78.4 12.9 %collective-permute-start.18 = (bf16[384,512]{1,0:T(8,128)(2,1)S(1)}, bf16[384,512]{1,0:T(8,128)(2,1)S(1)}, u32[]{:S(2)}, u32[]{:S(2)}) collective-permute-start(bf16[384,512]{1,0:T(8,128)(2,1)S(1)} %get-tuple-element.87), channel_id=1, source_target_pairs={{0,1},{1,0},{2,3},{3,2},{4,5},{5,4},{6,7},{7,6},{8,9},{9,8},{10,11... | collective-permute-start | bytes 1179656 | tf_op jit(solution)/shard_map/ppermute | solution.py:34
  82.5 9.6 %collective-permute-start.19 = (bf16[384,512]{1,0:T(8,128)(2,1)S(1)}, bf16[384,512]{1,0:T(8,128)(2,1)S(1)}, u32[]{:S(2)}, u32[]{:S(2)}) collective-permute-start(bf16[384,512]{1,0:T(8,128)(2,1)S(1)} %fusion.1), channel_id=1, source_target_pairs={{0,4},{1,5},{2,6},{3,7},{4,0},{5,1},{6,2},{7,3},{8,12},{9,13},{10,... | collective-permute-start | bytes 1179656 | tf_op jit(solution)/shard_map/ppermute | solution.py:30
  90.1 10.4 %collective-permute-start.23 = (bf16[384,512]{1,0:T(8,128)(2,1)S(1)}, bf16[384,512]{1,0:T(8,128)(2,1)S(1)}, u32[]{:S(2)}, u32[]{:S(2)}) collective-permute-start(bf16[384,512]{1,0:T(8,128)(2,1)S(1)} %fusion.6), channel_id=1, source_target_pairs={{0,4},{1,5},{2,6},{3,7},{4,0},{5,1},{6,2},{7,3},{8,12},{9,13},{10,... | collective-permute-start | bytes 1179656 | tf_op jit(solution)/shard_map/ppermute | solution.py:30
  90.7 9.8 %collective-permute-start.22 = (bf16[384,512]{1,0:T(8,128)(2,1)S(1)}, bf16[384,512]{1,0:T(8,128)(2,1)S(1)}, u32[]{:S(2)}, u32[]{:S(2)}) collective-permute-start(bf16[384,512]{1,0:T(8,128)(2,1)S(1)} %get-tuple-element.92), channel_id=1, source_target_pairs={{0,1},{1,0},{2,3},{3,2},{4,5},{5,4},{6,7},{7,6},{8,9},{9,8},{10,11... | collective-permute-start | bytes 1179656 | tf_op jit(solution)/shard_map/ppermute | solution.py:34
  90.7 10.6 %collective-permute-start.20 = (bf16[384,512]{1,0:T(8,128)(2,1)S(1)}, bf16[384,512]{1,0:T(8,128)(2,1)S(1)}, u32[]{:S(2)}, u32[]{:S(2)}) collective-permute-start(bf16[384,512]{1,0:T(8,128)(2,1)S(1)} %get-tuple-element.90), channel_id=1, source_target_pairs={{0,1},{1,0},{2,3},{3,2},{4,5},{5,4},{6,7},{7,6},{8,9},{9,8},{10,11... | collective-permute-start | bytes 1179656 | tf_op jit(solution)/shard_map/ppermute | solution.py:34
  92.3 11.0 %collective-permute-start.21 = (bf16[384,512]{1,0:T(8,128)(2,1)S(1)}, bf16[384,512]{1,0:T(8,128)(2,1)S(1)}, u32[]{:S(2)}, u32[]{:S(2)}) collective-permute-start(bf16[384,512]{1,0:T(8,128)(2,1)S(1)} %fusion.4), channel_id=1, source_target_pairs={{0,2},{1,3},{2,0},{3,1},{4,8},{5,9},{6,10},{7,11},{8,4},{9,5},{10,... | collective-permute-start | bytes 1179656 | tf_op jit(solution)/shard_map/ppermute | solution.py:30
  100.7 10.3 %collective-permute-start.26 = (bf16[384,512]{1,0:T(8,128)(2,1)S(1)}, bf16[384,512]{1,0:T(8,128)(2,1)S(1)}, u32[]{:S(2)}, u32[]{:S(2)}) collective-permute-start(bf16[384,512]{1,0:T(8,128)(2,1)S(1)} %fusion.9), channel_id=1, source_target_pairs={{0,2},{1,3},{2,0},{3,1},{4,8},{5,9},{6,10},{7,11},{8,4},{9,5},{10,... | collective-permute-start | bytes 1179656 | tf_op jit(solution)/shard_map/ppermute | solution.py:30
  101.3 9.7 %collective-permute-start.24 = (bf16[384,512]{1,0:T(8,128)(2,1)S(1)}, bf16[384,512]{1,0:T(8,128)(2,1)S(1)}, u32[]{:S(2)}, u32[]{:S(2)}) collective-permute-start(bf16[384,512]{1,0:T(8,128)(2,1)S(1)} %get-tuple-element.94), channel_id=1, source_target_pairs={{0,1},{1,0},{2,3},{3,2},{4,5},{5,4},{6,7},{7,6},{8,9},{9,8},{10,11... | collective-permute-start | bytes 1179656 | tf_op jit(solution)/shard_map/ppermute | solution.py:34
  103.5 9.6 %collective-permute-start.25 = (bf16[384,512]{1,0:T(8,128)(2,1)S(1)}, bf16[384,512]{1,0:T(8,128)(2,1)S(1)}, u32[]{:S(2)}, u32[]{:S(2)}) collective-permute-start(bf16[384,512]{1,0:T(8,128)(2,1)S(1)} %add_convert_fusion.1), channel_id=1, source_target_pairs={{0,4},{1,5},{2,6},{3,7},{4,0},{5,1},{6,2},{7,3},{8,12},{9,13},{10,... | collective-permute-start | bytes 1179656 | tf_op jit(solution)/shard_map/ppermute | solution.py:30
  (5 other events, 16.6 us)

commit v11 on v10

--- a/solution.py
+++ b/solution.py
@@ -315,22 +315,22 @@
     three, across, their_two, their_in = partials(
         after(hidden, four), (THREE, THREE_ACROSS), (TWO, TWO_IN)
     )
-    across = narrow(across + their_across)
-    got_across = wide(send(across, ACROSS))
     three = narrow(three + their_three + jnp.where(end, got, zero))
     got_three = wide(send(three, ALONG))
+    across = narrow(across + after(their_across, three))
+    got_across = wide(send(across, ACROSS))
     two, two_in, their_one, their_one_in = partials(
         after(hidden, three, across), (TWO, TWO_IN), (ONE, ONE_IN)
     )
-    two = narrow(two + their_two + jnp.where(end, got_across, zero))
-    got_two = wide(send(two, ALONG))
     two_in = narrow(two_in + their_in + jnp.where(end, zero, got) + got_three)
     got_in = wide(send(two_in, INSIDE))
+    two = narrow(two + after(their_two, two_in) + jnp.where(end, got_across, zero))
+    got_two = wide(send(two, ALONG))
     one, one_in, their_own = partials(after(hidden, two, two_in), (ONE, ONE_IN), (OWN,))
-    one_in = narrow(one_in + their_one_in + jnp.where(end, zero, got_across) + got_two)
-    got_one_in = wide(send(one_in, INSIDE))
     one = narrow(one + their_one + got_in)
     got_one = wide(send(one, ALONG))
+    one_in = narrow(one_in + after(their_one_in, one) + jnp.where(end, zero, got_across) + got_two)
+    got_one_in = wide(send(one_in, INSIDE))
     (kept,) = partials(after(hidden, one, one_in), (OWN,), ())
     branch = kept + their_own
     return (resident + branch + got_one + got_one_in).astype(jnp.bfloat16)

time: 114 us -> 114 us (level)
    ppermute x14, waiting for transfers between devices: 24.3 us -> 23.1 us  [send(): return lax.ppermute(x, 'gx', pairs)]
  transfers between devices with their start and end apart: 27 -> 27, of which waited for: 18 -> 17; matrix products, arithmetic and copies ran while one was open for 1% -> 2% of each run, Pallas kernels for 44% -> 44%
where the time goes in v11:
time: 114 us
  Pallas kernels  62.6 us (55%)
  waiting for transfers between devices  27.8 us (24%)
  starting transfers between devices  19.2 us (17%)
  other arithmetic  3.1 us (3%)
    pallas_call x5, Pallas kernels, gate_up(): pl.pallas_call(functools.partial(gate_up_body, count, first, last, rows,...  42 us
    ppermute x14, waiting for transfers between devices, send(): return lax.ppermute(x, 'gx', pairs)  23.1 us
    pallas_call x4, Pallas kernels, down(): pl.pallas_call(functools.partial(down_body, len(kept), len(sent)), grid_s...  18.7 us
    ppermute x14, starting transfers between devices, send(): return lax.ppermute(x, 'gx', pairs)  16.6 us
    ppermute x13, waiting for transfers between devices, swap(): return lax.ppermute(x, 'gx', [(i, i ^ 1) for i in range(4 * LINE)])  4.77 us
    ppermute x13, starting transfers between devices, swap(): return lax.ppermute(x, 'gx', [(i, i ^ 1) for i in range(4 * LINE)])  2.53 us
  transfers between devices with their start and end apart: 27, of which 17 were waited for; matrix products, arithmetic and copies ran while one was open for 2% of the time, Pallas kernels for 44%

profile of v11, /device:TPU:0, one launch (start us, length us, event | category | flops | bytes accessed | tf_op | source)
XLA Modules:
  0.0 114.0 jit_solution(18189844847011902050)
XLA Ops:
  0.0 2.0 %prepare.1.refs_0_ = bf16[1,400,512]{2,1,0:T(8,128)(2,1)} custom-call(bf16[384,512]{1,0:T(8,128)(2,1)} %x_ref, bf16[512]{0:T(512)(128)(2,1)} %gain_ref.1), custom_call_target="tpu_custom_call" | custom-call | tf_op jit(solution)/shard_map/prepare/pallas_call | solution.py:73
  2.4 2.6 %collective-permute-start = (bf16[1,400,512]{2,1,0:T(8,128)(2,1)}, bf16[1,400,512]{2,1,0:T(8,128)(2,1)S(1)}, u32[]{:S(2)}, u32[]{:S(2)}) collective-permute-start(bf16[1,400,512]{2,1,0:T(8,128)(2,1)} %prepare.1.refs_0_), channel_id=1, source_target_pairs={{0,4},{1,5},{2,6},{3,7},{4,0},{5,1},{6,2},{7,3},{8,12},{9,13},{10,... | collective-permute-start | bytes 1228808 | tf_op jit(solution)/shard_map/ppermute | solution.py:30
  5.0 1.5 %collective-permute-start.1 = (bf16[1,400,512]{2,1,0:T(8,128)(2,1)}, bf16[1,400,512]{2,1,0:T(8,128)(2,1)S(1)}, u32[]{:S(2)}, u32[]{:S(2)}) collective-permute-start(bf16[1,400,512]{2,1,0:T(8,128)(2,1)} %prepare.1.refs_0_), channel_id=1, source_target_pairs={{0,2},{1,3},{2,0},{3,1},{4,8},{5,9},{6,10},{7,11},{8,4},{9,5},{10,... | collective-permute-start | bytes 1228808 | tf_op jit(solution)/shard_map/ppermute | solution.py:30
  7.6 5.0 %gate_up.5 = (f32[384,1536]{1,0:T(8,128)S(1)}, f32[384,1536]{1,0:T(8,128)S(1)}, f32[384,256]{1,0:T(8,128)S(1)}, f32[8,512]{1,0:T(8,128)S(1)}) custom-call(s32[1]{0:T(128)} %bitcast.me_ref, bf16[1,400,512]{2,1,0:T(8,128)(2,1)S(1)} %copy-done, bf16[1,400,512]{2,1,0:T(8,128)(2,1)S(1)} %collective-permute-done.2.refs_1_, bf16[8192,1664]{1,0:T(8,128)(2,1)} %refs_2_.3, ...), custom_call_target="tpu_custom_call" | custom-call | flops 327155712 | bytes 851968 | tf_op jit(solution)/shard_map/gate_up/pallas_call | solution.py:187
  12.6 2.8 %collective-permute-done.refs_0_ = bf16[1,400,512]{2,1,0:T(8,128)(2,1)S(1)} collective-permute-done((bf16[1,400,512]{2,1,0:T(8,128)(2,1)}, bf16[1,400,512]{2,1,0:T(8,128)(2,1)S(1)}, u32[]{:S(2)}, u32[]{:S(2)}) %collective-permute-start) | collective-permute-done | bytes 409632 | tf_op jit(solution)/shard_map/ppermute | solution.py:30
  17.0 1.5 %collective-permute-start.3 = (bf16[1,400,512]{2,1,0:T(8,128)(2,1)S(1)}, bf16[1,400,512]{2,1,0:T(8,128)(2,1)S(1)}, u32[]{:S(2)}, u32[]{:S(2)}) collective-permute-start(bf16[1,400,512]{2,1,0:T(8,128)(2,1)S(1)} %collective-permute-done.1.refs_1_), channel_id=1, source_target_pairs={{0,4},{1,5},{2,6},{3,7},{4,0},{5,1},{6,2},{7,3},{8,12},{9,13},{10,... | collective-permute-start | bytes 1228808 | tf_op jit(solution)/shard_map/ppermute | solution.py:30
  18.5 1.5 %collective-permute-start.4 = (bf16[1,400,512]{2,1,0:T(8,128)(2,1)S(1)}, bf16[1,400,512]{2,1,0:T(8,128)(2,1)S(1)}, u32[]{:S(2)}, u32[]{:S(2)}) collective-permute-start(bf16[1,400,512]{2,1,0:T(8,128)(2,1)S(1)} %collective-permute-done.refs_0_), channel_id=1, source_target_pairs={{0,2},{1,3},{2,0},{3,1},{4,8},{5,9},{6,10},{7,11},{8,4},{9,5},{10,... | collective-permute-start | bytes 1228808 | tf_op jit(solution)/shard_map/ppermute | solution.py:30
  20.0 8.6 %gate_up.6 = (f32[384,1536]{1,0:T(8,128)S(1)}, f32[384,1536]{1,0:T(8,128)S(1)}, f32[384,256]{1,0:T(8,128)S(1)}, f32[8,512]{1,0:T(8,128)S(1)}) custom-call(s32[1]{0:T(128)} %bitcast.me_ref, bf16[1,400,512]{2,1,0:T(8,128)(2,1)S(1)} %collective-permute-done.refs_0_, bf16[1,400,512]{2,1,0:T(8,128)(2,1)S(1)} %collective-permute-done.1.refs_1_, ...), custom_call_target="tpu_custom_call" | custom-call | flops 654311424 | bytes 1703936 | tf_op jit(solution)/shard_map/gate_up/pallas_call | solution.py:187
  30.2 1.6 %collective-permute-start.7 = (bf16[1,400,512]{2,1,0:T(8,128)(2,1)S(1)}, bf16[1,400,512]{2,1,0:T(8,128)(2,1)S(1)}, u32[]{:S(2)}, u32[]{:S(2)}) collective-permute-start(bf16[1,400,512]{2,1,0:T(8,128)(2,1)S(1)} %broadcast_select_fusion.1), channel_id=1, source_target_pairs={{0,2},{1,3},{2,0},{3,1},{4,6},{5,7},{6,4},{7,5},{8,10},{9,11},{10,... | collective-permute-start | bytes 1228808 | tf_op jit(solution)/shard_map/ppermute | solution.py:30
  32.5 8.6 %gate_up.7 = (f32[384,1536]{1,0:T(8,128)S(1)}, f32[384,1536]{1,0:T(8,128)S(1)}, f32[384,256]{1,0:T(8,128)S(1)}, f32[8,512]{1,0:T(8,128)S(1)}) custom-call(s32[1]{0:T(128)} %bitcast.me_ref, bf16[1,400,512]{2,1,0:T(8,128)(2,1)S(1)} %collective-permute-done.3.refs_0_, bf16[1,400,512]{2,1,0:T(8,128)(2,1)S(1)} %collective-permute-done.4.refs_1_, ...), custom_call_target="tpu_custom_call" | custom-call | flops 654311424 | bytes 1703936 | tf_op jit(solution)/shard_map/gate_up/pallas_call | solution.py:187
  44.2 1.7 %collective-permute-done.10.refs_2_.refs_3_ = bf16[2,400,512]{2,1,0:T(8,128)(2,1)S(1)} collective-permute-done((bf16[2,400,512]{2,1,0:T(8,128)(2,1)S(1)}, bf16[2,400,512]{2,1,0:T(8,128)(2,1)S(1)}, u32[]{:S(2)}, u32[]{:S(2)}) %collective-permute-start.10) | collective-permute-done | bytes 819232 | tf_op jit(solution)/shard_map/ppermute | solution.py:34
  45.9 8.6 %gate_up.8 = (f32[384,1536]{1,0:T(8,128)S(1)}, f32[384,1536]{1,0:T(8,128)S(1)}, f32[384,256]{1,0:T(8,128)S(1)}, f32[8,512]{1,0:T(8,128)S(1)}) custom-call(s32[1]{0:T(128)} %bitcast.me_ref, bf16[1,400,512]{2,1,0:T(8,128)(2,1)S(1)} %collective-permute-done.6.refs_0_, bf16[1,400,512]{2,1,0:T(8,128)(2,1)S(1)} %collective-permute-done.7.refs_1_, ...), custom_call_target="tpu_custom_call" | custom-call | flops 654311424 | bytes 1703936 | tf_op jit(solution)/shard_map/gate_up/pallas_call | solution.py:187
  55.6 1.7 %collective-permute-done.11.refs_1_ = bf16[1,400,512]{2,1,0:T(8,128)(2,1)S(1)} collective-permute-done((bf16[1,400,512]{2,1,0:T(8,128)(2,1)S(1)}, bf16[1,400,512]{2,1,0:T(8,128)(2,1)S(1)}, u32[]{:S(2)}, u32[]{:S(2)}) %collective-permute-start.11) | collective-permute-done | bytes 409632 | tf_op jit(solution)/shard_map/ppermute | solution.py:34
  57.3 11.0 %gate_up.9 = (bf16[384,1664]{1,0:T(8,128)(2,1)S(1)}, bf16[384,512]{1,0:T(8,128)(2,1)S(1)}, f32[384,512]{1,0:T(8,128)S(1)}, bf16[384,512]{1,0:T(8,128)(2,1)S(1)}, bf16[384,512]{1,0:T(8,128)(2,1)S(1)}) custom-call(s32[1]{0:T(128)} %bitcast.me_ref, bf16[1,400,512]{2,1,0:T(8,128)(2,1)S(1)} %collective-permute-done.9.refs_0_, ...), custom_call_target="tpu_custom_call" | custom-call | flops 327155712 | bytes 851968 | tf_op jit(solution)/shard_map/gate_up/pallas_call | solution.py:187
  70.8 5.8 %down.4 = (f32[384,512]{1,0:T(8,128)S(1)}, f32[384,512]{1,0:T(8,128)S(1)}, bf16[384,512]{1,0:T(8,128)(2,1)S(1)}, bf16[384,512]{1,0:T(8,128)(2,1)S(1)}) custom-call(s32[1]{0:T(128)} %bitcast.me_ref, bf16[384,1664]{1,0:T(8,128)(2,1)S(1)} %get-tuple-element.99.hidden_ref, bf16[1664,8192]{1,0:T(8,128)(2,1)} %weight_ref.7), custom_call_target="tpu_custom_call" | custom-call | flops 327155712 | bytes 851968 | tf_op jit(solution)/shard_map/down/pallas_call | solution.py:240
  77.3 4.2 %collective-permute-done.14 = bf16[384,512]{1,0:T(8,128)(2,1)S(1)} collective-permute-done((bf16[384,512]{1,0:T(8,128)(2,1)S(1)}, bf16[384,512]{1,0:T(8,128)(2,1)S(1)}, u32[]{:S(2)}, u32[]{:S(2)}) %collective-permute-start.14) | collective-permute-done | bytes 393248 | tf_op jit(solution)/shard_map/ppermute | solution.py:30
  83.1 5.8 %down.5 = (f32[384,512]{1,0:T(8,128)S(1)}, f32[384,512]{1,0:T(8,128)S(1)}, bf16[384,512]{1,0:T(8,128)(2,1)S(1)}, bf16[384,512]{1,0:T(8,128)(2,1)S(1)}) custom-call(s32[1]{0:T(128)} %bitcast.me_ref, bf16[384,1664]{1,0:T(8,128)(2,1)S(1)} %get-tuple-element.99.hidden_ref, bf16[1664,8192]{1,0:T(8,128)(2,1)} %weight_ref.7), custom_call_target="tpu_custom_call" | custom-call | flops 327155712 | bytes 851968 | tf_op jit(solution)/shard_map/down/pallas_call | solution.py:240
  89.7 2.4 %collective-permute-done.18 = bf16[384,512]{1,0:T(8,128)(2,1)S(1)} collective-permute-done((bf16[384,512]{1,0:T(8,128)(2,1)S(1)}, bf16[384,512]{1,0:T(8,128)(2,1)S(1)}, u32[]{:S(2)}, u32[]{:S(2)}) %collective-permute-start.18) | collective-permute-done | bytes 393248 | tf_op jit(solution)/shard_map/ppermute | solution.py:30
  93.1 1.7 %collective-permute-start.23 = (bf16[384,512]{1,0:T(8,128)(2,1)S(1)}, bf16[384,512]{1,0:T(8,128)(2,1)S(1)}, u32[]{:S(2)}, u32[]{:S(2)}) collective-permute-start(bf16[384,512]{1,0:T(8,128)(2,1)S(1)} %fusion.6), channel_id=1, source_target_pairs={{0,4},{1,5},{2,6},{3,7},{4,0},{5,1},{6,2},{7,3},{8,12},{9,13},{10,... | collective-permute-start | bytes 1179656 | tf_op jit(solution)/shard_map/ppermute | solution.py:30
  94.9 4.7 %down.6 = (f32[384,512]{1,0:T(8,128)S(1)}, f32[384,512]{1,0:T(8,128)S(1)}, bf16[384,512]{1,0:T(8,128)(2,1)S(1)}) custom-call(s32[1]{0:T(128)} %bitcast.me_ref, bf16[384,1664]{1,0:T(8,128)(2,1)S(1)} %get-tuple-element.99.hidden_ref, bf16[1664,8192]{1,0:T(8,128)(2,1)} %weight_ref.7), custom_call_target="tpu_custom_call" | custom-call | flops 245366784 | bytes 638976 | tf_op jit(solution)/shard_map/down/pallas_call | solution.py:240
  99.8 2.0 %collective-permute-done.21 = bf16[384,512]{1,0:T(8,128)(2,1)S(1)} collective-permute-done((bf16[384,512]{1,0:T(8,128)(2,1)S(1)}, bf16[384,512]{1,0:T(8,128)(2,1)S(1)}, u32[]{:S(2)}, u32[]{:S(2)}) %collective-permute-start.21) | collective-permute-done | bytes 393248 | tf_op jit(solution)/shard_map/ppermute | solution.py:30
  103.0 1.5 %collective-permute-start.26 = (bf16[384,512]{1,0:T(8,128)(2,1)S(1)}, bf16[384,512]{1,0:T(8,128)(2,1)S(1)}, u32[]{:S(2)}, u32[]{:S(2)}) collective-permute-start(bf16[384,512]{1,0:T(8,128)(2,1)S(1)} %fusion.9), channel_id=1, source_target_pairs={{0,2},{1,3},{2,0},{3,1},{4,8},{5,9},{6,10},{7,11},{8,4},{9,5},{10,... | collective-permute-start | bytes 1179656 | tf_op jit(solution)/shard_map/ppermute | solution.py:30
  105.7 2.3 %down.7 = f32[384,512]{1,0:T(8,128)S(1)} custom-call(s32[1]{0:T(128)} %bitcast.me_ref, bf16[384,1664]{1,0:T(8,128)(2,1)S(1)} %get-tuple-element.99.hidden_ref, bf16[1664,8192]{1,0:T(8,128)(2,1)} %weight_ref.7), custom_call_target="tpu_custom_call" | custom-call | flops 81788928 | bytes 212992 | tf_op jit(solution)/shard_map/down/pallas_call | solution.py:240
  108.0 3.9 %collective-permute-done.26 = bf16[384,512]{1,0:T(8,128)(2,1)S(1)} collective-permute-done((bf16[384,512]{1,0:T(8,128)(2,1)S(1)}, bf16[384,512]{1,0:T(8,128)(2,1)S(1)}, u32[]{:S(2)}, u32[]{:S(2)}) %collective-permute-start.26) | collective-permute-done | bytes 393248 | tf_op jit(solution)/shard_map/ppermute | solution.py:30
  (60 shorter events, 20.5 us)
Async XLA Ops:
  2.0 4.5 %collective-permute-start.2 = (bf16[1,400,512]{2,1,0:T(8,128)(2,1)}, bf16[1,400,512]{2,1,0:T(8,128)(2,1)S(1)}, u32[]{:S(2)}, u32[]{:S(2)}) collective-permute-start(bf16[1,400,512]{2,1,0:T(8,128)(2,1)} %prepare.1.refs_0_), channel_id=1, source_target_pairs={{0,1},{1,0},{2,3},{3,2},{4,5},{5,4},{6,7},{7,6},{8,9},{9,8},{10,11... | collective-permute-start | bytes 1228808 | tf_op jit(solution)/shard_map/ppermute | solution.py:34
  2.4 12.9 %collective-permute-start = (bf16[1,400,512]{2,1,0:T(8,128)(2,1)}, bf16[1,400,512]{2,1,0:T(8,128)(2,1)S(1)}, u32[]{:S(2)}, u32[]{:S(2)}) collective-permute-start(bf16[1,400,512]{2,1,0:T(8,128)(2,1)} %prepare.1.refs_0_), channel_id=1, source_target_pairs={{0,4},{1,5},{2,6},{3,7},{4,0},{5,1},{6,2},{7,3},{8,12},{9,13},{10,... | collective-permute-start | bytes 1228808 | tf_op jit(solution)/shard_map/ppermute | solution.py:30
  5.0 11.8 %collective-permute-start.1 = (bf16[1,400,512]{2,1,0:T(8,128)(2,1)}, bf16[1,400,512]{2,1,0:T(8,128)(2,1)S(1)}, u32[]{:S(2)}, u32[]{:S(2)}) collective-permute-start(bf16[1,400,512]{2,1,0:T(8,128)(2,1)} %prepare.1.refs_0_), channel_id=1, source_target_pairs={{0,2},{1,3},{2,0},{3,1},{4,8},{5,9},{6,10},{7,11},{8,4},{9,5},{10,... | collective-permute-start | bytes 1228808 | tf_op jit(solution)/shard_map/ppermute | solution.py:30
  16.9 3.1 %collective-permute-start.5 = (bf16[2,400,512]{2,1,0:T(8,128)(2,1)S(1)}, bf16[2,400,512]{2,1,0:T(8,128)(2,1)S(1)}, u32[]{:S(2)}, u32[]{:S(2)}) collective-permute-start(bf16[2,400,512]{2,1,0:T(8,128)(2,1)S(1)} %pad_maximum_fusion), channel_id=1, source_target_pairs={{0,1},{1,0},{2,3},{3,2},{4,5},{5,4},{6,7},{7,6},{8,9},{9,8},{10,11... | collective-permute-start | bytes 2457608 | tf_op jit(solution)/shard_map/ppermute | solution.py:34
  17.0 11.9 %collective-permute-start.3 = (bf16[1,400,512]{2,1,0:T(8,128)(2,1)S(1)}, bf16[1,400,512]{2,1,0:T(8,128)(2,1)S(1)}, u32[]{:S(2)}, u32[]{:S(2)}) collective-permute-start(bf16[1,400,512]{2,1,0:T(8,128)(2,1)S(1)} %collective-permute-done.1.refs_1_), channel_id=1, source_target_pairs={{0,4},{1,5},{2,6},{3,7},{4,0},{5,1},{6,2},{7,3},{8,12},{9,13},{10,... | collective-permute-start | bytes 1228808 | tf_op jit(solution)/shard_map/ppermute | solution.py:30
  18.5 11.5 %collective-permute-start.4 = (bf16[1,400,512]{2,1,0:T(8,128)(2,1)S(1)}, bf16[1,400,512]{2,1,0:T(8,128)(2,1)S(1)}, u32[]{:S(2)}, u32[]{:S(2)}) collective-permute-start(bf16[1,400,512]{2,1,0:T(8,128)(2,1)S(1)} %collective-permute-done.refs_0_), channel_id=1, source_target_pairs={{0,2},{1,3},{2,0},{3,1},{4,8},{5,9},{6,10},{7,11},{8,4},{9,5},{10,... | collective-permute-start | bytes 1228808 | tf_op jit(solution)/shard_map/ppermute | solution.py:30
  30.1 2.4 %collective-permute-start.8 = (bf16[2,400,512]{2,1,0:T(8,128)(2,1)S(1)}, bf16[2,400,512]{2,1,0:T(8,128)(2,1)S(1)}, u32[]{:S(2)}, u32[]{:S(2)}) collective-permute-start(bf16[2,400,512]{2,1,0:T(8,128)(2,1)S(1)} %pad_maximum_fusion.1), channel_id=1, source_target_pairs={{0,1},{1,0},{2,3},{3,2},{4,5},{5,4},{6,7},{7,6},{8,9},{9,8},{10,11... | collective-permute-start | bytes 2457608 | tf_op jit(solution)/shard_map/ppermute | solution.py:34
  30.2 11.9 %collective-permute-start.7 = (bf16[1,400,512]{2,1,0:T(8,128)(2,1)S(1)}, bf16[1,400,512]{2,1,0:T(8,128)(2,1)S(1)}, u32[]{:S(2)}, u32[]{:S(2)}) collective-permute-start(bf16[1,400,512]{2,1,0:T(8,128)(2,1)S(1)} %broadcast_select_fusion.1), channel_id=1, source_target_pairs={{0,2},{1,3},{2,0},{3,1},{4,6},{5,7},{6,4},{7,5},{8,10},{9,11},{10,... | collective-permute-start | bytes 1228808 | tf_op jit(solution)/shard_map/ppermute | solution.py:30
  31.8 11.6 %collective-permute-start.6 = (bf16[1,400,512]{2,1,0:T(8,128)(2,1)S(1)}, bf16[1,400,512]{2,1,0:T(8,128)(2,1)S(1)}, u32[]{:S(2)}, u32[]{:S(2)}) collective-permute-start(bf16[1,400,512]{2,1,0:T(8,128)(2,1)S(1)} %collective-permute-done.4.refs_1_), channel_id=1, source_target_pairs={{0,4},{1,5},{2,6},{3,7},{4,0},{5,1},{6,2},{7,3},{8,12},{9,13},{10,... | collective-permute-start | bytes 1228808 | tf_op jit(solution)/shard_map/ppermute | solution.py:30
  43.6 11.9 %collective-permute-start.9 = (bf16[1,400,512]{2,1,0:T(8,128)(2,1)S(1)}, bf16[1,400,512]{2,1,0:T(8,128)(2,1)S(1)}, u32[]{:S(2)}, u32[]{:S(2)}) collective-permute-start(bf16[1,400,512]{2,1,0:T(8,128)(2,1)S(1)} %broadcast_select_fusion), channel_id=1, source_target_pairs={{0,2},{1,3},{2,0},{3,1},{4,6},{5,7},{6,4},{7,5},{8,10},{9,11},{10,... | collective-permute-start | bytes 1228808 | tf_op jit(solution)/shard_map/ppermute | solution.py:30
  68.5 8.8 %collective-permute-start.13 = (bf16[384,512]{1,0:T(8,128)(2,1)S(1)}, bf16[384,512]{1,0:T(8,128)(2,1)S(1)}, u32[]{:S(2)}, u32[]{:S(2)}) collective-permute-start(bf16[384,512]{1,0:T(8,128)(2,1)S(1)} %get-tuple-element.83), channel_id=1, source_target_pairs={{0,1},{1,0},{2,3},{3,2},{4,5},{5,4},{6,7},{7,6},{8,9},{9,8},{10,11... | collective-permute-start | bytes 1179656 | tf_op jit(solution)/shard_map/ppermute | solution.py:34
  70.2 11.2 %collective-permute-start.14 = (bf16[384,512]{1,0:T(8,128)(2,1)S(1)}, bf16[384,512]{1,0:T(8,128)(2,1)S(1)}, u32[]{:S(2)}, u32[]{:S(2)}) collective-permute-start(bf16[384,512]{1,0:T(8,128)(2,1)S(1)} %add_convert_fusion.3), channel_id=1, source_target_pairs={{0,2},{1,3},{2,0},{3,1},{4,6},{5,7},{6,4},{7,5},{8,10},{9,11},{10,... | collective-permute-start | bytes 1179656 | tf_op jit(solution)/shard_map/ppermute | solution.py:30
  70.8 11.5 %collective-permute-start.15 = (bf16[384,512]{1,0:T(8,128)(2,1)S(1)}, bf16[384,512]{1,0:T(8,128)(2,1)S(1)}, u32[]{:S(2)}, u32[]{:S(2)}) collective-permute-start(bf16[384,512]{1,0:T(8,128)(2,1)S(1)} %get-tuple-element.85), channel_id=1, source_target_pairs={{0,1},{1,0},{2,3},{3,2},{4,5},{5,4},{6,7},{7,6},{8,9},{9,8},{10,11... | collective-permute-start | bytes 1179656 | tf_op jit(solution)/shard_map/ppermute | solution.py:34
  76.6 13.0 %collective-permute-start.17 = (bf16[384,512]{1,0:T(8,128)(2,1)S(1)}, bf16[384,512]{1,0:T(8,128)(2,1)S(1)}, u32[]{:S(2)}, u32[]{:S(2)}) collective-permute-start(bf16[384,512]{1,0:T(8,128)(2,1)S(1)} %get-tuple-element.91), channel_id=1, source_target_pairs={{0,1},{1,0},{2,3},{3,2},{4,5},{5,4},{6,7},{7,6},{8,9},{9,8},{10,11... | collective-permute-start | bytes 1179656 | tf_op jit(solution)/shard_map/ppermute | solution.py:34
  77.2 11.8 %collective-permute-start.16 = (bf16[384,512]{1,0:T(8,128)(2,1)S(1)}, bf16[384,512]{1,0:T(8,128)(2,1)S(1)}, u32[]{:S(2)}, u32[]{:S(2)}) collective-permute-start(bf16[384,512]{1,0:T(8,128)(2,1)S(1)} %get-tuple-element.89), channel_id=1, source_target_pairs={{0,1},{1,0},{2,3},{3,2},{4,5},{5,4},{6,7},{7,6},{8,9},{9,8},{10,11... | collective-permute-start | bytes 1179656 | tf_op jit(solution)/shard_map/ppermute | solution.py:34
  81.6 10.4 %collective-permute-start.18 = (bf16[384,512]{1,0:T(8,128)(2,1)S(1)}, bf16[384,512]{1,0:T(8,128)(2,1)S(1)}, u32[]{:S(2)}, u32[]{:S(2)}) collective-permute-start(bf16[384,512]{1,0:T(8,128)(2,1)S(1)} %fusion.1), channel_id=1, source_target_pairs={{0,4},{1,5},{2,6},{3,7},{4,0},{5,1},{6,2},{7,3},{8,12},{9,13},{10,... | collective-permute-start | bytes 1179656 | tf_op jit(solution)/shard_map/ppermute | solution.py:30
  82.6 10.3 %collective-permute-start.19 = (bf16[384,512]{1,0:T(8,128)(2,1)S(1)}, bf16[384,512]{1,0:T(8,128)(2,1)S(1)}, u32[]{:S(2)}, u32[]{:S(2)}) collective-permute-start(bf16[384,512]{1,0:T(8,128)(2,1)S(1)} %add_convert_fusion.2), channel_id=1, source_target_pairs={{0,2},{1,3},{2,0},{3,1},{4,6},{5,7},{6,4},{7,5},{8,10},{9,11},{10,... | collective-permute-start | bytes 1179656 | tf_op jit(solution)/shard_map/ppermute | solution.py:30
  89.0 10.8 %collective-permute-start.20 = (bf16[384,512]{1,0:T(8,128)(2,1)S(1)}, bf16[384,512]{1,0:T(8,128)(2,1)S(1)}, u32[]{:S(2)}, u32[]{:S(2)}) collective-permute-start(bf16[384,512]{1,0:T(8,128)(2,1)S(1)} %get-tuple-element.95), channel_id=1, source_target_pairs={{0,1},{1,0},{2,3},{3,2},{4,5},{5,4},{6,7},{7,6},{8,9},{9,8},{10,11... | collective-permute-start | bytes 1179656 | tf_op jit(solution)/shard_map/ppermute | solution.py:34
  89.1 10.6 %collective-permute-start.22 = (bf16[384,512]{1,0:T(8,128)(2,1)S(1)}, bf16[384,512]{1,0:T(8,128)(2,1)S(1)}, u32[]{:S(2)}, u32[]{:S(2)}) collective-permute-start(bf16[384,512]{1,0:T(8,128)(2,1)S(1)} %get-tuple-element.97), channel_id=1, source_target_pairs={{0,1},{1,0},{2,3},{3,2},{4,5},{5,4},{6,7},{7,6},{8,9},{9,8},{10,11... | collective-permute-start | bytes 1179656 | tf_op jit(solution)/shard_map/ppermute | solution.py:34
  92.3 9.5 %collective-permute-start.21 = (bf16[384,512]{1,0:T(8,128)(2,1)S(1)}, bf16[384,512]{1,0:T(8,128)(2,1)S(1)}, u32[]{:S(2)}, u32[]{:S(2)}) collective-permute-start(bf16[384,512]{1,0:T(8,128)(2,1)S(1)} %fusion.4), channel_id=1, source_target_pairs={{0,2},{1,3},{2,0},{3,1},{4,8},{5,9},{6,10},{7,11},{8,4},{9,5},{10,... | collective-permute-start | bytes 1179656 | tf_op jit(solution)/shard_map/ppermute | solution.py:30
  93.1 9.5 %collective-permute-start.23 = (bf16[384,512]{1,0:T(8,128)(2,1)S(1)}, bf16[384,512]{1,0:T(8,128)(2,1)S(1)}, u32[]{:S(2)}, u32[]{:S(2)}) collective-permute-start(bf16[384,512]{1,0:T(8,128)(2,1)S(1)} %fusion.6), channel_id=1, source_target_pairs={{0,4},{1,5},{2,6},{3,7},{4,0},{5,1},{6,2},{7,3},{8,12},{9,13},{10,... | collective-permute-start | bytes 1179656 | tf_op jit(solution)/shard_map/ppermute | solution.py:30
  99.6 8.4 %collective-permute-start.24 = (bf16[384,512]{1,0:T(8,128)(2,1)S(1)}, bf16[384,512]{1,0:T(8,128)(2,1)S(1)}, u32[]{:S(2)}, u32[]{:S(2)}) collective-permute-start(bf16[384,512]{1,0:T(8,128)(2,1)S(1)} %get-tuple-element.100), channel_id=1, source_target_pairs={{0,1},{1,0},{2,3},{3,2},{4,5},{5,4},{6,7},{7,6},{8,9},{9,8},{10,11... | collective-permute-start | bytes 1179656 | tf_op jit(solution)/shard_map/ppermute | solution.py:34
  103.0 8.9 %collective-permute-start.26 = (bf16[384,512]{1,0:T(8,128)(2,1)S(1)}, bf16[384,512]{1,0:T(8,128)(2,1)S(1)}, u32[]{:S(2)}, u32[]{:S(2)}) collective-permute-start(bf16[384,512]{1,0:T(8,128)(2,1)S(1)} %fusion.9), channel_id=1, source_target_pairs={{0,2},{1,3},{2,0},{3,1},{4,8},{5,9},{6,10},{7,11},{8,4},{9,5},{10,... | collective-permute-start | bytes 1179656 | tf_op jit(solution)/shard_map/ppermute | solution.py:30
  104.4 8.5 %collective-permute-start.25 = (bf16[384,512]{1,0:T(8,128)(2,1)S(1)}, bf16[384,512]{1,0:T(8,128)(2,1)S(1)}, u32[]{:S(2)}, u32[]{:S(2)}) collective-permute-start(bf16[384,512]{1,0:T(8,128)(2,1)S(1)} %add_convert_fusion.1), channel_id=1, source_target_pairs={{0,4},{1,5},{2,6},{3,7},{4,0},{5,1},{6,2},{7,3},{8,12},{9,13},{10,... | collective-permute-start | bytes 1179656 | tf_op jit(solution)/shard_map/ppermute | solution.py:30
  (5 other events, 17.0 us)

commit v12 on v11

--- a/solution.py
+++ b/solution.py
@@ -143,13 +143,10 @@
             rem = both.shape[1] // 2
             hidden_ref[:, :main] = act(gate, up)
             hidden_ref[:, main:] = act(both[:, :rem], both[:, rem:])
-            for i in range(0, len(outs), 2):
-                pair = slice(i, i + 2)
-                for copy in copies[pair]:
-                    copy.wait()
-                value = down_block(hidden_ref, buffer_ref.at[:, i * width : (i + 2) * width])
-                for n, out in enumerate(outs[pair]):
-                    out[...] = value[:, n * width : (n + 1) * width].astype(out.dtype)
+            for i, (copy, out) in enumerate(zip(copies, outs)):
+                copy.wait()
+                value = down_block(hidden_ref, buffer_ref.at[:, i * width : (i + 1) * width])
+                out[...] = value.astype(out.dtype)
 
 
 def gate_up(me, jobs, shards, gate_weight, up_weight, acc, last=(), kinds=(), down_weight=None):
@@ -288,13 +285,12 @@
     four = send(jnp.where(end, three, two_in), ACROSS)
     acc = multiply(acc, (THREE, THREE_ACROSS), (three, across))
     four = after(four, acc[3])
-    narrow_kind = jnp.bfloat16
-    hidden, their_four, four, their_three, their_across = multiply(
+    hidden, their_four, four = multiply(
         acc,
         (FOUR,),
         (four,),
-        ((FOUR, 1), (FOUR, 0), (THREE, 1), (THREE_ACROSS, 1)),
-        (narrow_kind, jnp.float32, narrow_kind, narrow_kind),
+        ((FOUR, 1), (FOUR, 0)),
+        (jnp.bfloat16, jnp.float32),
         down_weight,
     )
 
@@ -302,18 +298,22 @@
     wide = lambda x: x.astype(jnp.float32)
     zero = jnp.zeros((), jnp.float32)
 
-    def partials(hidden, kept, sent):
+    def swap_halves(x):
+        half = x.shape[0] // 2
+        return jnp.concatenate([swap(x[:half]), swap(x[half:])])
+
+    def partials(hidden, kept, sent, whole=0):
         kept_jobs, sent_jobs = [(place, 0) for place in kept], [(place, 1) for place in sent]
         outs = down(me, kept_jobs, sent_jobs, hidden, down_weight, width)
-        return [*outs[: len(kept)], *(wide(swap(x)) for x in outs[len(kept) :])]
-
-    their_four, their_three, their_across = (
-        wide(swap(x)) for x in (their_four, their_three, their_across)
-    )
-    four = narrow(four + their_four)
+        cut = len(outs) - whole if whole else len(kept)
+        halved = [wide(swap_halves(x)) for x in outs[len(kept) : cut]]
+        return [*outs[: len(kept)], *halved, *(wide(swap(x)) for x in outs[cut:])]
+
+    four = narrow(four + wide(swap(their_four)))
     got = wide(send(four, ACROSS))
-    three, across, their_two, their_in = partials(
-        after(hidden, four), (THREE, THREE_ACROSS), (TWO, TWO_IN)
+    hidden = after(hidden, four)
+    three, across, their_three, their_across, their_two, their_in = partials(
+        hidden, (THREE, THREE_ACROSS), (THREE, THREE_ACROSS, TWO, TWO_IN), whole=2
     )
     three = narrow(three + their_three + jnp.where(end, got, zero))
     got_three = wide(send(three, ALONG))

time: 114 us -> 114 us (level)
  waiting for transfers between devices: 27.8 us -> 26.5 us
    pallas_call x4, Pallas kernels: 18.7 us -> 21.2 us  [down(): pl.pallas_call(functools.partial(down_body, len(kept), len(sent)), grid_s...]
    pallas_call x5, Pallas kernels: 42 us -> 39.5 us  [gate_up(): pl.pallas_call(functools.partial(gate_up_body, count, first, last, rows,...]
    ppermute x14, waiting for transfers between devices: 23.1 us -> 20.9 us  [send(): return lax.ppermute(x, 'gx', pairs)]
    ppermute x13 -> x15, waiting for transfers between devices: 4.77 us -> 5.61 us  [swap(): return lax.ppermute(x, 'gx', [(i, i ^ 1) for i in range(4 * LINE)])]
    ppermute x13 -> x15, starting transfers between devices: 2.53 us -> 3.02 us  [swap(): return lax.ppermute(x, 'gx', [(i, i ^ 1) for i in range(4 * LINE)])]
  transfers between devices with their start and end apart: 27 -> 29, of which waited for: 17 -> 19; matrix products, arithmetic and copies ran while one was open for 2% -> 2% of each run, Pallas kernels for 44% -> 46%
where the time goes in v12:
time: 114 us; the launch traced here: 113 us
  Pallas kernels  62.6 us (55%)
  waiting for transfers between devices  26.5 us (23%)
  starting transfers between devices  19.8 us (17%)
  other arithmetic  3.12 us (3%)
    pallas_call x5, Pallas kernels, gate_up(): pl.pallas_call(functools.partial(gate_up_body, count, first, last, rows,...  39.5 us
    pallas_call x4, Pallas kernels, down(): pl.pallas_call(functools.partial(down_body, len(kept), len(sent)), grid_s...  21.2 us
    ppermute x14, waiting for transfers between devices, send(): return lax.ppermute(x, 'gx', pairs)  20.9 us
    ppermute x14, starting transfers between devices, send(): return lax.ppermute(x, 'gx', pairs)  16.8 us
    ppermute x15, waiting for transfers between devices, swap(): return lax.ppermute(x, 'gx', [(i, i ^ 1) for i in range(4 * LINE)])  5.61 us
    ppermute x15, starting transfers between devices, swap(): return lax.ppermute(x, 'gx', [(i, i ^ 1) for i in range(4 * LINE)])  3.02 us
  transfers between devices with their start and end apart: 29, of which 19 were waited for; matrix products, arithmetic and copies ran while one was open for 2% of the time, Pallas kernels for 46%

profile of v12, /device:TPU:0, one launch (start us, length us, event | category | flops | bytes accessed | tf_op | source)
XLA Modules:
  0.0 113.4 jit_solution(3625455865926886798)
XLA Ops:
  0.0 2.0 %prepare.1.refs_0_ = bf16[1,400,512]{2,1,0:T(8,128)(2,1)} custom-call(bf16[384,512]{1,0:T(8,128)(2,1)} %x_ref, bf16[512]{0:T(512)(128)(2,1)} %gain_ref.1), custom_call_target="tpu_custom_call" | custom-call | tf_op jit(solution)/shard_map/prepare/pallas_call | solution.py:73
  2.4 2.6 %collective-permute-start = (bf16[1,400,512]{2,1,0:T(8,128)(2,1)}, bf16[1,400,512]{2,1,0:T(8,128)(2,1)S(1)}, u32[]{:S(2)}, u32[]{:S(2)}) collective-permute-start(bf16[1,400,512]{2,1,0:T(8,128)(2,1)} %prepare.1.refs_0_), channel_id=1, source_target_pairs={{0,4},{1,5},{2,6},{3,7},{4,0},{5,1},{6,2},{7,3},{8,12},{9,13},{10,... | collective-permute-start | bytes 1228808 | tf_op jit(solution)/shard_map/ppermute | solution.py:30
  5.0 1.5 %collective-permute-start.1 = (bf16[1,400,512]{2,1,0:T(8,128)(2,1)}, bf16[1,400,512]{2,1,0:T(8,128)(2,1)S(1)}, u32[]{:S(2)}, u32[]{:S(2)}) collective-permute-start(bf16[1,400,512]{2,1,0:T(8,128)(2,1)} %prepare.1.refs_0_), channel_id=1, source_target_pairs={{0,2},{1,3},{2,0},{3,1},{4,8},{5,9},{6,10},{7,11},{8,4},{9,5},{10,... | collective-permute-start | bytes 1228808 | tf_op jit(solution)/shard_map/ppermute | solution.py:30
  7.6 5.0 %gate_up.5 = (f32[384,1536]{1,0:T(8,128)S(1)}, f32[384,1536]{1,0:T(8,128)S(1)}, f32[384,256]{1,0:T(8,128)S(1)}, f32[8,512]{1,0:T(8,128)S(1)}) custom-call(s32[1]{0:T(128)} %bitcast.me_ref, bf16[1,400,512]{2,1,0:T(8,128)(2,1)S(1)} %copy-done, bf16[1,400,512]{2,1,0:T(8,128)(2,1)S(1)} %collective-permute-done.2.refs_1_, bf16[8192,1664]{1,0:T(8,128)(2,1)} %refs_2_.3, ...), custom_call_target="tpu_custom_call" | custom-call | flops 327155712 | bytes 851968 | tf_op jit(solution)/shard_map/gate_up/pallas_call | solution.py:184
  12.6 2.8 %collective-permute-done.refs_0_ = bf16[1,400,512]{2,1,0:T(8,128)(2,1)S(1)} collective-permute-done((bf16[1,400,512]{2,1,0:T(8,128)(2,1)}, bf16[1,400,512]{2,1,0:T(8,128)(2,1)S(1)}, u32[]{:S(2)}, u32[]{:S(2)}) %collective-permute-start) | collective-permute-done | bytes 409632 | tf_op jit(solution)/shard_map/ppermute | solution.py:30
  18.5 1.5 %collective-permute-start.4 = (bf16[1,400,512]{2,1,0:T(8,128)(2,1)S(1)}, bf16[1,400,512]{2,1,0:T(8,128)(2,1)S(1)}, u32[]{:S(2)}, u32[]{:S(2)}) collective-permute-start(bf16[1,400,512]{2,1,0:T(8,128)(2,1)S(1)} %collective-permute-done.refs_0_), channel_id=1, source_target_pairs={{0,2},{1,3},{2,0},{3,1},{4,8},{5,9},{6,10},{7,11},{8,4},{9,5},{10,... | collective-permute-start | bytes 1228808 | tf_op jit(solution)/shard_map/ppermute | solution.py:30
  20.0 8.8 %gate_up.6 = (f32[384,1536]{1,0:T(8,128)S(1)}, f32[384,1536]{1,0:T(8,128)S(1)}, f32[384,256]{1,0:T(8,128)S(1)}, f32[8,512]{1,0:T(8,128)S(1)}) custom-call(s32[1]{0:T(128)} %bitcast.me_ref, bf16[1,400,512]{2,1,0:T(8,128)(2,1)S(1)} %collective-permute-done.refs_0_, bf16[1,400,512]{2,1,0:T(8,128)(2,1)S(1)} %collective-permute-done.1.refs_1_, ...), custom_call_target="tpu_custom_call" | custom-call | flops 654311424 | bytes 1703936 | tf_op jit(solution)/shard_map/gate_up/pallas_call | solution.py:184
  30.2 1.6 %collective-permute-start.7 = (bf16[1,400,512]{2,1,0:T(8,128)(2,1)S(1)}, bf16[1,400,512]{2,1,0:T(8,128)(2,1)S(1)}, u32[]{:S(2)}, u32[]{:S(2)}) collective-permute-start(bf16[1,400,512]{2,1,0:T(8,128)(2,1)S(1)} %broadcast_select_fusion.1), channel_id=1, source_target_pairs={{0,2},{1,3},{2,0},{3,1},{4,6},{5,7},{6,4},{7,5},{8,10},{9,11},{10,... | collective-permute-start | bytes 1228808 | tf_op jit(solution)/shard_map/ppermute | solution.py:30
  32.5 8.6 %gate_up.7 = (f32[384,1536]{1,0:T(8,128)S(1)}, f32[384,1536]{1,0:T(8,128)S(1)}, f32[384,256]{1,0:T(8,128)S(1)}, f32[8,512]{1,0:T(8,128)S(1)}) custom-call(s32[1]{0:T(128)} %bitcast.me_ref, bf16[1,400,512]{2,1,0:T(8,128)(2,1)S(1)} %collective-permute-done.3.refs_0_, bf16[1,400,512]{2,1,0:T(8,128)(2,1)S(1)} %collective-permute-done.4.refs_1_, ...), custom_call_target="tpu_custom_call" | custom-call | flops 654311424 | bytes 1703936 | tf_op jit(solution)/shard_map/gate_up/pallas_call | solution.py:184
  44.2 1.7 %collective-permute-done.10.refs_2_.refs_3_ = bf16[2,400,512]{2,1,0:T(8,128)(2,1)S(1)} collective-permute-done((bf16[2,400,512]{2,1,0:T(8,128)(2,1)S(1)}, bf16[2,400,512]{2,1,0:T(8,128)(2,1)S(1)}, u32[]{:S(2)}, u32[]{:S(2)}) %collective-permute-start.10) | collective-permute-done | bytes 819232 | tf_op jit(solution)/shard_map/ppermute | solution.py:34
  45.9 8.6 %gate_up.8 = (f32[384,1536]{1,0:T(8,128)S(1)}, f32[384,1536]{1,0:T(8,128)S(1)}, f32[384,256]{1,0:T(8,128)S(1)}, f32[8,512]{1,0:T(8,128)S(1)}) custom-call(s32[1]{0:T(128)} %bitcast.me_ref, bf16[1,400,512]{2,1,0:T(8,128)(2,1)S(1)} %collective-permute-done.6.refs_0_, bf16[1,400,512]{2,1,0:T(8,128)(2,1)S(1)} %collective-permute-done.7.refs_1_, ...), custom_call_target="tpu_custom_call" | custom-call | flops 654311424 | bytes 1703936 | tf_op jit(solution)/shard_map/gate_up/pallas_call | solution.py:184
  55.5 1.7 %collective-permute-done.11.refs_1_ = bf16[1,400,512]{2,1,0:T(8,128)(2,1)S(1)} collective-permute-done((bf16[1,400,512]{2,1,0:T(8,128)(2,1)S(1)}, bf16[1,400,512]{2,1,0:T(8,128)(2,1)S(1)}, u32[]{:S(2)}, u32[]{:S(2)}) %collective-permute-start.11) | collective-permute-done | bytes 409632 | tf_op jit(solution)/shard_map/ppermute | solution.py:34
  57.3 8.4 %gate_up.9 = (bf16[384,1664]{1,0:T(8,128)(2,1)S(1)}, bf16[384,512]{1,0:T(8,128)(2,1)S(1)}, f32[384,512]{1,0:T(8,128)S(1)}) custom-call(s32[1]{0:T(128)} %bitcast.me_ref, bf16[1,400,512]{2,1,0:T(8,128)(2,1)S(1)} %collective-permute-done.9.refs_0_, bf16[1,400,512]{2,1,0:T(8,128)(2,1)S(1)} %collective-permute-done.11.refs_1_, bf16[8192,1664]{1,0:T(8,128)(2,1)} %refs_2_.3, ...), custom_call_target="tpu_custom_call" | custom-call | flops 327155712 | bytes 851968 | tf_op jit(solution)/shard_map/gate_up/pallas_call | solution.py:184
  65.9 1.6 %collective-permute-done.12 = bf16[384,512]{1,0:T(8,128)(2,1)S(1)} collective-permute-done((bf16[384,512]{1,0:T(8,128)(2,1)S(1)}, bf16[384,512]{1,0:T(8,128)(2,1)S(1)}, u32[]{:S(2)}, u32[]{:S(2)}) %collective-permute-start.12) | collective-permute-done | bytes 393248 | tf_op jit(solution)/shard_map/ppermute | solution.py:34
  68.2 8.3 %down.4 = (f32[384,512]{1,0:T(8,128)S(1)}, f32[384,512]{1,0:T(8,128)S(1)}, bf16[384,512]{1,0:T(8,128)(2,1)S(1)}, bf16[384,512]{1,0:T(8,128)(2,1)S(1)}, bf16[384,...) custom-call(s32[1]{0:T(128)} %bitcast.me_ref, bf16[384,1664]{1,0:T(8,128)(2,1)S(1)} %get-tuple-element.99.hidden_ref, ...), custom_call_target="tpu_custom_call" | custom-call | flops 490733568 | bytes 1277952 | tf_op jit(solution)/shard_map/down/pallas_call | solution.py:237
  81.3 5.8 %down.5 = (f32[384,512]{1,0:T(8,128)S(1)}, f32[384,512]{1,0:T(8,128)S(1)}, bf16[384,512]{1,0:T(8,128)(2,1)S(1)}, bf16[384,512]{1,0:T(8,128)(2,1)S(1)}) custom-call(s32[1]{0:T(128)} %bitcast.me_ref, bf16[384,1664]{1,0:T(8,128)(2,1)S(1)} %get-tuple-element.99.hidden_ref, bf16[1664,8192]{1,0:T(8,128)(2,1)} %weight_ref.7), custom_call_target="tpu_custom_call" | custom-call | flops 327155712 | bytes 851968 | tf_op jit(solution)/shard_map/down/pallas_call | solution.py:237
  87.8 2.3 %collective-permute-done.20 = bf16[384,512]{1,0:T(8,128)(2,1)S(1)} collective-permute-done((bf16[384,512]{1,0:T(8,128)(2,1)S(1)}, bf16[384,512]{1,0:T(8,128)(2,1)S(1)}, u32[]{:S(2)}, u32[]{:S(2)}) %collective-permute-start.20) | collective-permute-done | bytes 393248 | tf_op jit(solution)/shard_map/ppermute | solution.py:30
  90.4 1.6 %collective-permute-start.23 = (bf16[384,512]{1,0:T(8,128)(2,1)S(1)}, bf16[384,512]{1,0:T(8,128)(2,1)S(1)}, u32[]{:S(2)}, u32[]{:S(2)}) collective-permute-start(bf16[384,512]{1,0:T(8,128)(2,1)S(1)} %fusion.4), channel_id=1, source_target_pairs={{0,2},{1,3},{2,0},{3,1},{4,8},{5,9},{6,10},{7,11},{8,4},{9,5},{10,... | collective-permute-start | bytes 1179656 | tf_op jit(solution)/shard_map/ppermute | solution.py:30
  92.9 4.7 %down.6 = (f32[384,512]{1,0:T(8,128)S(1)}, f32[384,512]{1,0:T(8,128)S(1)}, bf16[384,512]{1,0:T(8,128)(2,1)S(1)}) custom-call(s32[1]{0:T(128)} %bitcast.me_ref, bf16[384,1664]{1,0:T(8,128)(2,1)S(1)} %get-tuple-element.99.hidden_ref, bf16[1664,8192]{1,0:T(8,128)(2,1)} %weight_ref.7), custom_call_target="tpu_custom_call" | custom-call | flops 245366784 | bytes 638976 | tf_op jit(solution)/shard_map/down/pallas_call | solution.py:237
  97.9 2.9 %collective-permute-done.23 = bf16[384,512]{1,0:T(8,128)(2,1)S(1)} collective-permute-done((bf16[384,512]{1,0:T(8,128)(2,1)S(1)}, bf16[384,512]{1,0:T(8,128)(2,1)S(1)}, u32[]{:S(2)}, u32[]{:S(2)}) %collective-permute-start.23) | collective-permute-done | bytes 393248 | tf_op jit(solution)/shard_map/ppermute | solution.py:30
  100.9 1.6 %collective-permute-done.25 = bf16[384,512]{1,0:T(8,128)(2,1)S(1)} collective-permute-done((bf16[384,512]{1,0:T(8,128)(2,1)S(1)}, bf16[384,512]{1,0:T(8,128)(2,1)S(1)}, u32[]{:S(2)}, u32[]{:S(2)}) %collective-permute-start.25) | collective-permute-done | bytes 393248 | tf_op jit(solution)/shard_map/ppermute | solution.py:30
  103.3 1.6 %collective-permute-start.27 = (bf16[384,512]{1,0:T(8,128)(2,1)S(1)}, bf16[384,512]{1,0:T(8,128)(2,1)S(1)}, u32[]{:S(2)}, u32[]{:S(2)}) collective-permute-start(bf16[384,512]{1,0:T(8,128)(2,1)S(1)} %add_convert_fusion.1), channel_id=1, source_target_pairs={{0,4},{1,5},{2,6},{3,7},{4,0},{5,1},{6,2},{7,3},{8,12},{9,13},{10,... | collective-permute-start | bytes 1179656 | tf_op jit(solution)/shard_map/ppermute | solution.py:30
  104.9 2.3 %down.7 = f32[384,512]{1,0:T(8,128)S(1)} custom-call(s32[1]{0:T(128)} %bitcast.me_ref, bf16[384,1664]{1,0:T(8,128)(2,1)S(1)} %get-tuple-element.99.hidden_ref, bf16[1664,8192]{1,0:T(8,128)(2,1)} %weight_ref.7), custom_call_target="tpu_custom_call" | custom-call | flops 81788928 | bytes 212992 | tf_op jit(solution)/shard_map/down/pallas_call | solution.py:237
  107.2 5.0 %collective-permute-done.28 = bf16[384,512]{1,0:T(8,128)(2,1)S(1)} collective-permute-done((bf16[384,512]{1,0:T(8,128)(2,1)S(1)}, bf16[384,512]{1,0:T(8,128)(2,1)S(1)}, u32[]{:S(2)}, u32[]{:S(2)}) %collective-permute-start.28) | collective-permute-done | bytes 393248 | tf_op jit(solution)/shard_map/ppermute | solution.py:30
  (66 shorter events, 20.6 us)
Async XLA Ops:
  2.0 4.5 %collective-permute-start.2 = (bf16[1,400,512]{2,1,0:T(8,128)(2,1)}, bf16[1,400,512]{2,1,0:T(8,128)(2,1)S(1)}, u32[]{:S(2)}, u32[]{:S(2)}) collective-permute-start(bf16[1,400,512]{2,1,0:T(8,128)(2,1)} %prepare.1.refs_0_), channel_id=1, source_target_pairs={{0,1},{1,0},{2,3},{3,2},{4,5},{5,4},{6,7},{7,6},{8,9},{9,8},{10,11... | collective-permute-start | bytes 1228808 | tf_op jit(solution)/shard_map/ppermute | solution.py:34
  2.4 12.9 %collective-permute-start = (bf16[1,400,512]{2,1,0:T(8,128)(2,1)}, bf16[1,400,512]{2,1,0:T(8,128)(2,1)S(1)}, u32[]{:S(2)}, u32[]{:S(2)}) collective-permute-start(bf16[1,400,512]{2,1,0:T(8,128)(2,1)} %prepare.1.refs_0_), channel_id=1, source_target_pairs={{0,4},{1,5},{2,6},{3,7},{4,0},{5,1},{6,2},{7,3},{8,12},{9,13},{10,... | collective-permute-start | bytes 1228808 | tf_op jit(solution)/shard_map/ppermute | solution.py:30
  5.0 11.8 %collective-permute-start.1 = (bf16[1,400,512]{2,1,0:T(8,128)(2,1)}, bf16[1,400,512]{2,1,0:T(8,128)(2,1)S(1)}, u32[]{:S(2)}, u32[]{:S(2)}) collective-permute-start(bf16[1,400,512]{2,1,0:T(8,128)(2,1)} %prepare.1.refs_0_), channel_id=1, source_target_pairs={{0,2},{1,3},{2,0},{3,1},{4,8},{5,9},{6,10},{7,11},{8,4},{9,5},{10,... | collective-permute-start | bytes 1228808 | tf_op jit(solution)/shard_map/ppermute | solution.py:30
  16.9 3.1 %collective-permute-start.5 = (bf16[2,400,512]{2,1,0:T(8,128)(2,1)S(1)}, bf16[2,400,512]{2,1,0:T(8,128)(2,1)S(1)}, u32[]{:S(2)}, u32[]{:S(2)}) collective-permute-start(bf16[2,400,512]{2,1,0:T(8,128)(2,1)S(1)} %pad_maximum_fusion), channel_id=1, source_target_pairs={{0,1},{1,0},{2,3},{3,2},{4,5},{5,4},{6,7},{7,6},{8,9},{9,8},{10,11... | collective-permute-start | bytes 2457608 | tf_op jit(solution)/shard_map/ppermute | solution.py:34
  17.0 11.9 %collective-permute-start.3 = (bf16[1,400,512]{2,1,0:T(8,128)(2,1)S(1)}, bf16[1,400,512]{2,1,0:T(8,128)(2,1)S(1)}, u32[]{:S(2)}, u32[]{:S(2)}) collective-permute-start(bf16[1,400,512]{2,1,0:T(8,128)(2,1)S(1)} %collective-permute-done.1.refs_1_), channel_id=1, source_target_pairs={{0,4},{1,5},{2,6},{3,7},{4,0},{5,1},{6,2},{7,3},{8,12},{9,13},{10,... | collective-permute-start | bytes 1228808 | tf_op jit(solution)/shard_map/ppermute | solution.py:30
  18.5 11.5 %collective-permute-start.4 = (bf16[1,400,512]{2,1,0:T(8,128)(2,1)S(1)}, bf16[1,400,512]{2,1,0:T(8,128)(2,1)S(1)}, u32[]{:S(2)}, u32[]{:S(2)}) collective-permute-start(bf16[1,400,512]{2,1,0:T(8,128)(2,1)S(1)} %collective-permute-done.refs_0_), channel_id=1, source_target_pairs={{0,2},{1,3},{2,0},{3,1},{4,8},{5,9},{6,10},{7,11},{8,4},{9,5},{10,... | collective-permute-start | bytes 1228808 | tf_op jit(solution)/shard_map/ppermute | solution.py:30
  30.1 2.4 %collective-permute-start.8 = (bf16[2,400,512]{2,1,0:T(8,128)(2,1)S(1)}, bf16[2,400,512]{2,1,0:T(8,128)(2,1)S(1)}, u32[]{:S(2)}, u32[]{:S(2)}) collective-permute-start(bf16[2,400,512]{2,1,0:T(8,128)(2,1)S(1)} %pad_maximum_fusion.1), channel_id=1, source_target_pairs={{0,1},{1,0},{2,3},{3,2},{4,5},{5,4},{6,7},{7,6},{8,9},{9,8},{10,11... | collective-permute-start | bytes 2457608 | tf_op jit(solution)/shard_map/ppermute | solution.py:34
  30.2 11.9 %collective-permute-start.7 = (bf16[1,400,512]{2,1,0:T(8,128)(2,1)S(1)}, bf16[1,400,512]{2,1,0:T(8,128)(2,1)S(1)}, u32[]{:S(2)}, u32[]{:S(2)}) collective-permute-start(bf16[1,400,512]{2,1,0:T(8,128)(2,1)S(1)} %broadcast_select_fusion.1), channel_id=1, source_target_pairs={{0,2},{1,3},{2,0},{3,1},{4,6},{5,7},{6,4},{7,5},{8,10},{9,11},{10,... | collective-permute-start | bytes 1228808 | tf_op jit(solution)/shard_map/ppermute | solution.py:30
  31.8 11.6 %collective-permute-start.6 = (bf16[1,400,512]{2,1,0:T(8,128)(2,1)S(1)}, bf16[1,400,512]{2,1,0:T(8,128)(2,1)S(1)}, u32[]{:S(2)}, u32[]{:S(2)}) collective-permute-start(bf16[1,400,512]{2,1,0:T(8,128)(2,1)S(1)} %collective-permute-done.4.refs_1_), channel_id=1, source_target_pairs={{0,4},{1,5},{2,6},{3,7},{4,0},{5,1},{6,2},{7,3},{8,12},{9,13},{10,... | collective-permute-start | bytes 1228808 | tf_op jit(solution)/shard_map/ppermute | solution.py:30
  43.5 2.4 %collective-permute-start.10 = (bf16[2,400,512]{2,1,0:T(8,128)(2,1)S(1)}, bf16[2,400,512]{2,1,0:T(8,128)(2,1)S(1)}, u32[]{:S(2)}, u32[]{:S(2)}) collective-permute-start(bf16[2,400,512]{2,1,0:T(8,128)(2,1)S(1)} %pad_maximum_fusion.2), channel_id=1, source_target_pairs={{0,1},{1,0},{2,3},{3,2},{4,5},{5,4},{6,7},{7,6},{8,9},{9,8},{10,11... | collective-permute-start | bytes 2457608 | tf_op jit(solution)/shard_map/ppermute | solution.py:34
  43.6 11.9 %collective-permute-start.9 = (bf16[1,400,512]{2,1,0:T(8,128)(2,1)S(1)}, bf16[1,400,512]{2,1,0:T(8,128)(2,1)S(1)}, u32[]{:S(2)}, u32[]{:S(2)}) collective-permute-start(bf16[1,400,512]{2,1,0:T(8,128)(2,1)S(1)} %broadcast_select_fusion), channel_id=1, source_target_pairs={{0,2},{1,3},{2,0},{3,1},{4,6},{5,7},{6,4},{7,5},{8,10},{9,11},{10,... | collective-permute-start | bytes 1228808 | tf_op jit(solution)/shard_map/ppermute | solution.py:30
  67.6 11.2 %collective-permute-start.15 = (bf16[384,512]{1,0:T(8,128)(2,1)S(1)}, bf16[384,512]{1,0:T(8,128)(2,1)S(1)}, u32[]{:S(2)}, u32[]{:S(2)}) collective-permute-start(bf16[384,512]{1,0:T(8,128)(2,1)S(1)} %add_convert_fusion.3), channel_id=1, source_target_pairs={{0,2},{1,3},{2,0},{3,1},{4,6},{5,7},{6,4},{7,5},{8,10},{9,11},{10,... | collective-permute-start | bytes 1179656 | tf_op jit(solution)/shard_map/ppermute | solution.py:30
  77.2 2.5 %collective-permute-start.16 = (bf16[192,512]{1,0:T(8,128)(2,1)S(1)}, bf16[192,512]{1,0:T(8,128)(2,1)S(1)}, u32[]{:S(2)}, u32[]{:S(2)}) collective-permute-start(bf16[192,512]{1,0:T(8,128)(2,1)S(1)} %get-tuple-element.103), channel_id=1, source_target_pairs={{0,1},{1,0},{2,3},{3,2},{4,5},{5,4},{6,7},{7,6},{8,9},{9,8},{10,11... | collective-permute-start | bytes 589832 | tf_op jit(solution)/shard_map/ppermute | solution.py:34
  78.1 9.7 %collective-permute-start.19 = (bf16[384,512]{1,0:T(8,128)(2,1)S(1)}, bf16[384,512]{1,0:T(8,128)(2,1)S(1)}, u32[]{:S(2)}, u32[]{:S(2)}) collective-permute-start(bf16[384,512]{1,0:T(8,128)(2,1)S(1)} %get-tuple-element.91), channel_id=1, source_target_pairs={{0,1},{1,0},{2,3},{3,2},{4,5},{5,4},{6,7},{7,6},{8,9},{9,8},{10,11... | collective-permute-start | bytes 1179656 | tf_op jit(solution)/shard_map/ppermute | solution.py:34
  78.3 8.9 %collective-permute-start.18 = (bf16[384,512]{1,0:T(8,128)(2,1)S(1)}, bf16[384,512]{1,0:T(8,128)(2,1)S(1)}, u32[]{:S(2)}, u32[]{:S(2)}) collective-permute-start(bf16[384,512]{1,0:T(8,128)(2,1)S(1)} %get-tuple-element.89), channel_id=1, source_target_pairs={{0,1},{1,0},{2,3},{3,2},{4,5},{5,4},{6,7},{7,6},{8,9},{9,8},{10,11... | collective-permute-start | bytes 1179656 | tf_op jit(solution)/shard_map/ppermute | solution.py:34
  79.0 11.1 %collective-permute-start.20 = (bf16[384,512]{1,0:T(8,128)(2,1)S(1)}, bf16[384,512]{1,0:T(8,128)(2,1)S(1)}, u32[]{:S(2)}, u32[]{:S(2)}) collective-permute-start(bf16[384,512]{1,0:T(8,128)(2,1)S(1)} %fusion.1), channel_id=1, source_target_pairs={{0,4},{1,5},{2,6},{3,7},{4,0},{5,1},{6,2},{7,3},{8,12},{9,13},{10,... | collective-permute-start | bytes 1179656 | tf_op jit(solution)/shard_map/ppermute | solution.py:30
  79.9 12.0 %collective-permute-start.21 = (bf16[384,512]{1,0:T(8,128)(2,1)S(1)}, bf16[384,512]{1,0:T(8,128)(2,1)S(1)}, u32[]{:S(2)}, u32[]{:S(2)}) collective-permute-start(bf16[384,512]{1,0:T(8,128)(2,1)S(1)} %add_convert_fusion.2), channel_id=1, source_target_pairs={{0,2},{1,3},{2,0},{3,1},{4,6},{5,7},{6,4},{7,5},{8,10},{9,11},{10,... | collective-permute-start | bytes 1179656 | tf_op jit(solution)/shard_map/ppermute | solution.py:30
  87.1 10.8 %collective-permute-start.22 = (bf16[384,512]{1,0:T(8,128)(2,1)S(1)}, bf16[384,512]{1,0:T(8,128)(2,1)S(1)}, u32[]{:S(2)}, u32[]{:S(2)}) collective-permute-start(bf16[384,512]{1,0:T(8,128)(2,1)S(1)} %get-tuple-element.95), channel_id=1, source_target_pairs={{0,1},{1,0},{2,3},{3,2},{4,5},{5,4},{6,7},{7,6},{8,9},{9,8},{10,11... | collective-permute-start | bytes 1179656 | tf_op jit(solution)/shard_map/ppermute | solution.py:34
  87.2 10.6 %collective-permute-start.24 = (bf16[384,512]{1,0:T(8,128)(2,1)S(1)}, bf16[384,512]{1,0:T(8,128)(2,1)S(1)}, u32[]{:S(2)}, u32[]{:S(2)}) collective-permute-start(bf16[384,512]{1,0:T(8,128)(2,1)S(1)} %get-tuple-element.97), channel_id=1, source_target_pairs={{0,1},{1,0},{2,3},{3,2},{4,5},{5,4},{6,7},{7,6},{8,9},{9,8},{10,11... | collective-permute-start | bytes 1179656 | tf_op jit(solution)/shard_map/ppermute | solution.py:34
  90.4 10.3 %collective-permute-start.23 = (bf16[384,512]{1,0:T(8,128)(2,1)S(1)}, bf16[384,512]{1,0:T(8,128)(2,1)S(1)}, u32[]{:S(2)}, u32[]{:S(2)}) collective-permute-start(bf16[384,512]{1,0:T(8,128)(2,1)S(1)} %fusion.4), channel_id=1, source_target_pairs={{0,2},{1,3},{2,0},{3,1},{4,8},{5,9},{6,10},{7,11},{8,4},{9,5},{10,... | collective-permute-start | bytes 1179656 | tf_op jit(solution)/shard_map/ppermute | solution.py:30
  92.2 10.3 %collective-permute-start.25 = (bf16[384,512]{1,0:T(8,128)(2,1)S(1)}, bf16[384,512]{1,0:T(8,128)(2,1)S(1)}, u32[]{:S(2)}, u32[]{:S(2)}) collective-permute-start(bf16[384,512]{1,0:T(8,128)(2,1)S(1)} %fusion.6), channel_id=1, source_target_pairs={{0,4},{1,5},{2,6},{3,7},{4,0},{5,1},{6,2},{7,3},{8,12},{9,13},{10,... | collective-permute-start | bytes 1179656 | tf_op jit(solution)/shard_map/ppermute | solution.py:30
  97.7 9.5 %collective-permute-start.26 = (bf16[384,512]{1,0:T(8,128)(2,1)S(1)}, bf16[384,512]{1,0:T(8,128)(2,1)S(1)}, u32[]{:S(2)}, u32[]{:S(2)}) collective-permute-start(bf16[384,512]{1,0:T(8,128)(2,1)S(1)} %get-tuple-element.100), channel_id=1, source_target_pairs={{0,1},{1,0},{2,3},{3,2},{4,5},{5,4},{6,7},{7,6},{8,9},{9,8},{10,11... | collective-permute-start | bytes 1179656 | tf_op jit(solution)/shard_map/ppermute | solution.py:34
  102.8 9.3 %collective-permute-start.28 = (bf16[384,512]{1,0:T(8,128)(2,1)S(1)}, bf16[384,512]{1,0:T(8,128)(2,1)S(1)}, u32[]{:S(2)}, u32[]{:S(2)}) collective-permute-start(bf16[384,512]{1,0:T(8,128)(2,1)S(1)} %fusion.9), channel_id=1, source_target_pairs={{0,2},{1,3},{2,0},{3,1},{4,8},{5,9},{6,10},{7,11},{8,4},{9,5},{10,... | collective-permute-start | bytes 1179656 | tf_op jit(solution)/shard_map/ppermute | solution.py:30
  103.3 9.0 %collective-permute-start.27 = (bf16[384,512]{1,0:T(8,128)(2,1)S(1)}, bf16[384,512]{1,0:T(8,128)(2,1)S(1)}, u32[]{:S(2)}, u32[]{:S(2)}) collective-permute-start(bf16[384,512]{1,0:T(8,128)(2,1)S(1)} %add_convert_fusion.1), channel_id=1, source_target_pairs={{0,4},{1,5},{2,6},{3,7},{4,0},{5,1},{6,2},{7,3},{8,12},{9,13},{10,... | collective-permute-start | bytes 1179656 | tf_op jit(solution)/shard_map/ppermute | solution.py:30
  (7 other events, 19.7 us)

commit v13 on v12

--- a/solution.py
+++ b/solution.py
@@ -12,7 +12,7 @@
 LINE = 4
 EXTRA = 16
 VMEM_LIMIT = 36 * 1024 * 1024
-PREPARE_LIMIT = 60 * 1024 * 1024
+PREPARE_LIMIT = 36 * 1024 * 1024
 
 ALONG = (lambda z, y: (z ^ 1, y),) * 2
 INSIDE = (lambda z, y: (z, y ^ 1), lambda z, y: (z ^ 3, y))
@@ -265,33 +265,45 @@
     resident = activations.astype(jnp.float32)
     OWN, ONE, ONE_IN, TWO, TWO_IN, THREE, THREE_ACROSS, FOUR = range(8)
 
-    def multiply(acc, places, shards, *more):
-        theirs = swap(shards[0] if len(shards) == 1 else jnp.concatenate(shards))
-        jobs = [(place, 0) for place in places] + [(place, 1) for place in places]
-        arrays = [(x, 0) for x in shards] + [(theirs, i) for i in range(len(places))]
-        return gate_up(me, jobs, arrays, gate_weight, up_weight, acc, *more)
+    def multiply(acc, *shards, then=()):
+        jobs = [shard[:2] for shard in shards]
+        arrays = [shard[2:] for shard in shards]
+        return gate_up(me, jobs, arrays, gate_weight, up_weight, acc, *then)
 
     early, end = lax.optimization_barrier((activations, end))
     own = prepare(early, norm_gain)
     one, one_in = send(own, ALONG), send(own, INSIDE)
-    acc = multiply(None, (OWN,), (own,))
-    one, one_in = after((one, one_in), acc[3])
+    theirs = swap(own)
     two, two_in = send(one_in, ALONG), send(one, INSIDE)
-    acc = multiply(acc, (ONE, ONE_IN), (one, one_in))
+    their_ones = swap(jnp.concatenate([one, one_in]))
+    acc = multiply(
+        None, (OWN, 0, own, 0), (OWN, 1, theirs, 0), (ONE, 0, one, 0), (ONE_IN, 0, one_in, 0)
+    )
     two, two_in = after((two, two_in), acc[3])
     three, across = send(two_in, ALONG), send(jnp.where(end, two, one_in), ACROSS)
-    acc = multiply(acc, (TWO, TWO_IN), (two, two_in))
+    their_twos = swap(jnp.concatenate([two, two_in]))
+    acc = multiply(
+        acc,
+        (ONE, 1, their_ones, 0), (ONE_IN, 1, their_ones, 1), (TWO, 0, two, 0), (TWO_IN, 0, two_in, 0),
+    )
     three, across = after((three, across), acc[3])
     four = send(jnp.where(end, three, two_in), ACROSS)
-    acc = multiply(acc, (THREE, THREE_ACROSS), (three, across))
+    their_threes = swap(jnp.concatenate([three, across]))
+    acc = multiply(
+        acc,
+        (TWO, 1, their_twos, 0), (TWO_IN, 1, their_twos, 1),
+        (THREE, 0, three, 0), (THREE_ACROSS, 0, across, 0),
+    )
     four = after(four, acc[3])
+    their_four = swap(four)
+    acc = multiply(
+        acc,
+        (THREE, 1, their_threes, 0), (THREE_ACROSS, 1, their_threes, 1), (FOUR, 0, four, 0),
+    )
     hidden, their_four, four = multiply(
         acc,
-        (FOUR,),
-        (four,),
-        ((FOUR, 1), (FOUR, 0)),
-        (jnp.bfloat16, jnp.float32),
-        down_weight,
+        (FOUR, 1, after(their_four, acc[3]), 0),
+        then=(((FOUR, 1), (FOUR, 0)), (jnp.bfloat16, jnp.float32), down_weight),
     )
 
     narrow = lambda x: x.astype(jnp.bfloat16)

time: 114 us -> 117 us (1.026)
  starting transfers between devices: 19.8 us -> 22.7 us
  waiting for transfers between devices: 26.5 us -> 25.3 us
    ppermute x15, waiting for transfers between devices: 5.61 us -> 1.85 us  [swap(): return lax.ppermute(x, 'gx', [(i, i ^ 1) for i in range(4 * LINE)])]
    ppermute x14, starting transfers between devices: 16.8 us -> 19.8 us  [send(): return lax.ppermute(x, 'gx', pairs)]
    pallas_call x5, Pallas kernels: 39.5 us -> 42.2 us  [gate_up(): pl.pallas_call(functools.partial(gate_up_body, count, first, last, rows,...]
    ppermute x14, waiting for transfers between devices: 20.9 us -> 23.4 us  [send(): return lax.ppermute(x, 'gx', pairs)]
    pallas_call x1, Pallas kernels: 1.99 us -> 0.22 us  [prepare(): pl.pallas_call(prepare_body, out_shape=jax.ShapeDtypeStruct((1, rows + EX...]
  transfers between devices with their start and end apart: 29 -> 29, of which waited for: 19 -> 11; matrix products, arithmetic and copies ran while one was open for 2% -> 2% of each run, Pallas kernels for 46% -> 47%
where the time goes in v13:
time: 117 us
  Pallas kernels  63.7 us (54%)
  waiting for transfers between devices  25.3 us (22%)
  starting transfers between devices  22.7 us (19%)
  other arithmetic  2.92 us (2%)
  local copies, waits for them, and re-layouts  1.73 us (1%)
    pallas_call x5, Pallas kernels, gate_up(): pl.pallas_call(functools.partial(gate_up_body, count, first, last, rows,...  42.2 us
    ppermute x14, waiting for transfers between devices, send(): return lax.ppermute(x, 'gx', pairs)  23.4 us
    pallas_call x4, Pallas kernels, down(): pl.pallas_call(functools.partial(down_body, len(kept), len(sent)), grid_s...  21.3 us
    ppermute x14, starting transfers between devices, send(): return lax.ppermute(x, 'gx', pairs)  19.8 us
    ppermute x15, starting transfers between devices, swap(): return lax.ppermute(x, 'gx', [(i, i ^ 1) for i in range(4 * LINE)])  2.94 us
  transfers between devices with their start and end apart: 29, of which 11 were waited for; matrix products, arithmetic and copies ran while one was open for 2% of the time, Pallas kernels for 47%

profile of v13, /device:TPU:0, one launch (start us, length us, event | category | flops | bytes accessed | tf_op | source)
XLA Modules:
  0.0 116.7 jit_solution(846009346049290982)
XLA Ops:
  1.9 3.0 %collective-permute-start = (bf16[1,400,512]{2,1,0:T(8,128)(2,1)S(1)}, bf16[1,400,512]{2,1,0:T(8,128)(2,1)S(1)}, u32[]{:S(2)}, u32[]{:S(2)}) collective-permute-start(bf16[1,400,512]{2,1,0:T(8,128)(2,1)S(1)} %prepare.1.refs_0_), channel_id=1, source_target_pairs={{0,2},{1,3},{2,0},{3,1},{4,8},{5,9},{6,10},{7,11},{8,4},{9,5},{10,... | collective-permute-start | bytes 1228808 | tf_op jit(solution)/shard_map/ppermute | solution.py:30
  4.9 1.6 %collective-permute-start.2 = (bf16[1,400,512]{2,1,0:T(8,128)(2,1)S(1)}, bf16[1,400,512]{2,1,0:T(8,128)(2,1)S(1)}, u32[]{:S(2)}, u32[]{:S(2)}) collective-permute-start(bf16[1,400,512]{2,1,0:T(8,128)(2,1)S(1)} %prepare.1.refs_0_), channel_id=1, source_target_pairs={{0,4},{1,5},{2,6},{3,7},{4,0},{5,1},{6,2},{7,3},{8,12},{9,13},{10,... | collective-permute-start | bytes 1228808 | tf_op jit(solution)/shard_map/ppermute | solution.py:30
  6.6 7.8 %collective-permute-done.refs_3_ = bf16[1,400,512]{2,1,0:T(8,128)(2,1)S(1)} collective-permute-done((bf16[1,400,512]{2,1,0:T(8,128)(2,1)S(1)}, bf16[1,400,512]{2,1,0:T(8,128)(2,1)S(1)}, u32[]{:S(2)}, u32[]{:S(2)}) %collective-permute-start) | collective-permute-done | bytes 409632 | tf_op jit(solution)/shard_map/ppermute | solution.py:30
  14.4 1.8 %collective-permute-start.1 = (bf16[1,400,512]{2,1,0:T(8,128)(2,1)S(1)}, bf16[1,400,512]{2,1,0:T(8,128)(2,1)S(1)}, u32[]{:S(2)}, u32[]{:S(2)}) collective-permute-start(bf16[1,400,512]{2,1,0:T(8,128)(2,1)S(1)} %collective-permute-done.refs_3_), channel_id=1, source_target_pairs={{0,4},{1,5},{2,6},{3,7},{4,0},{5,1},{6,2},{7,3},{8,12},{9,13},{10,... | collective-permute-start | bytes 1228808 | tf_op jit(solution)/shard_map/ppermute | solution.py:30
  16.2 1.5 %collective-permute-start.3 = (bf16[1,400,512]{2,1,0:T(8,128)(2,1)S(1)}, bf16[1,400,512]{2,1,0:T(8,128)(2,1)S(1)}, u32[]{:S(2)}, u32[]{:S(2)}) collective-permute-start(bf16[1,400,512]{2,1,0:T(8,128)(2,1)S(1)} %collective-permute-done.2.refs_2_), channel_id=1, source_target_pairs={{0,2},{1,3},{2,0},{3,1},{4,8},{5,9},{6,10},{7,11},{8,4},{9,5},{10,... | collective-permute-start | bytes 1228808 | tf_op jit(solution)/shard_map/ppermute | solution.py:30
  17.9 8.8 %gate_up.5 = (f32[384,1536]{1,0:T(8,128)S(1)}, f32[384,1536]{1,0:T(8,128)S(1)}, f32[384,256]{1,0:T(8,128)S(1)}, f32[8,512]{1,0:T(8,128)S(1)}) custom-call(s32[1]{0:T(128)} %bitcast.me_ref, bf16[1,400,512]{2,1,0:T(8,128)(2,1)S(1)} %prepare.1.refs_0_, bf16[1,400,512]{2,1,0:T(8,128)(2,1)S(1)} %collective-permute-done.4.refs_1_, ...), custom_call_target="tpu_custom_call" | custom-call | flops 654311424 | bytes 1703936 | tf_op jit(solution)/shard_map/gate_up/pallas_call | solution.py:184
  26.8 1.7 %collective-permute-start.5 = (bf16[1,400,512]{2,1,0:T(8,128)(2,1)S(1)}, bf16[1,400,512]{2,1,0:T(8,128)(2,1)S(1)}, u32[]{:S(2)}, u32[]{:S(2)}) collective-permute-start(bf16[1,400,512]{2,1,0:T(8,128)(2,1)S(1)} %collective-permute-done.3.refs_3_), channel_id=1, source_target_pairs={{0,4},{1,5},{2,6},{3,7},{4,0},{5,1},{6,2},{7,3},{8,12},{9,13},{10,... | collective-permute-start | bytes 1228808 | tf_op jit(solution)/shard_map/ppermute | solution.py:30
  28.5 1.6 %collective-permute-start.6 = (bf16[1,400,512]{2,1,0:T(8,128)(2,1)S(1)}, bf16[1,400,512]{2,1,0:T(8,128)(2,1)S(1)}, u32[]{:S(2)}, u32[]{:S(2)}) collective-permute-start(bf16[1,400,512]{2,1,0:T(8,128)(2,1)S(1)} %broadcast_select_fusion.1), channel_id=1, source_target_pairs={{0,2},{1,3},{2,0},{3,1},{4,6},{5,7},{6,4},{7,5},{8,10},{9,11},{10,... | collective-permute-start | bytes 1228808 | tf_op jit(solution)/shard_map/ppermute | solution.py:30
  30.3 8.9 %gate_up.6 = (f32[384,1536]{1,0:T(8,128)S(1)}, f32[384,1536]{1,0:T(8,128)S(1)}, f32[384,256]{1,0:T(8,128)S(1)}, f32[8,512]{1,0:T(8,128)S(1)}) custom-call(s32[1]{0:T(128)} %bitcast.me_ref, bf16[2,400,512]{2,1,0:T(8,128)(2,1)S(1)} %collective-permute-done.7.refs_0_.refs_1_, bf16[2,400,512]{2,1,0:T(8,128)(2,1)S(1)} %collective-permute-done.7.refs_0_.refs_1_, ...), custom_call_target="tpu_custom_call" | custom-call | flops 654311424 | bytes 1703936 | tf_op jit(solution)/shard_map/gate_up/pallas_call | solution.py:184
  40.3 1.6 %collective-permute-start.8 = (bf16[1,400,512]{2,1,0:T(8,128)(2,1)S(1)}, bf16[1,400,512]{2,1,0:T(8,128)(2,1)S(1)}, u32[]{:S(2)}, u32[]{:S(2)}) collective-permute-start(bf16[1,400,512]{2,1,0:T(8,128)(2,1)S(1)} %broadcast_select_fusion), channel_id=1, source_target_pairs={{0,2},{1,3},{2,0},{3,1},{4,6},{5,7},{6,4},{7,5},{8,10},{9,11},{10,... | collective-permute-start | bytes 1228808 | tf_op jit(solution)/shard_map/ppermute | solution.py:30
  41.9 8.9 %gate_up.7 = (f32[384,1536]{1,0:T(8,128)S(1)}, f32[384,1536]{1,0:T(8,128)S(1)}, f32[384,256]{1,0:T(8,128)S(1)}, f32[8,512]{1,0:T(8,128)S(1)}) custom-call(s32[1]{0:T(128)} %bitcast.me_ref, bf16[2,400,512]{2,1,0:T(8,128)(2,1)S(1)} %collective-permute-done.9.refs_0_.refs_1_, bf16[2,400,512]{2,1,0:T(8,128)(2,1)S(1)} %collective-permute-done.9.refs_0_.refs_1_, ...), custom_call_target="tpu_custom_call" | custom-call | flops 654311424 | bytes 1703936 | tf_op jit(solution)/shard_map/gate_up/pallas_call | solution.py:184
  50.8 1.5 %collective-permute-done.8.refs_2_ = bf16[1,400,512]{2,1,0:T(8,128)(2,1)S(1)} collective-permute-done((bf16[1,400,512]{2,1,0:T(8,128)(2,1)S(1)}, bf16[1,400,512]{2,1,0:T(8,128)(2,1)S(1)}, u32[]{:S(2)}, u32[]{:S(2)}) %collective-permute-start.8) | collective-permute-done | bytes 409632 | tf_op jit(solution)/shard_map/ppermute | solution.py:30
  52.3 7.2 %gate_up.8 = (f32[384,1536]{1,0:T(8,128)S(1)}, f32[384,1536]{1,0:T(8,128)S(1)}, f32[384,256]{1,0:T(8,128)S(1)}, f32[8,512]{1,0:T(8,128)S(1)}) custom-call(s32[1]{0:T(128)} %bitcast.me_ref, bf16[2,400,512]{2,1,0:T(8,128)(2,1)S(1)} %collective-permute-done.11.refs_0_.refs_1_, bf16[2,400,512]{2,1,0:T(8,128)(2,1)S(1)} %collective-permute-done.11.refs_0_.refs_1_, ...), custom_call_target="tpu_custom_call" | custom-call | flops 490733568 | bytes 1277952 | tf_op jit(solution)/shard_map/gate_up/pallas_call | solution.py:184
  59.4 8.4 %gate_up.9 = (bf16[384,1664]{1,0:T(8,128)(2,1)S(1)}, bf16[384,512]{1,0:T(8,128)(2,1)S(1)}, f32[384,512]{1,0:T(8,128)S(1)}) custom-call(s32[1]{0:T(128)} %bitcast.me_ref, bf16[1,400,512]{2,1,0:T(8,128)(2,1)S(1)} %collective-permute-done.10.refs_0_, bf16[8192,1664]{1,0:T(8,128)(2,1)} %refs_1_.1, bf16[8192,1664]{1,0:T(8,128)(2,1)} %refs_2_.1, ...), custom_call_target="tpu_custom_call" | custom-call | flops 163577856 | bytes 425984 | tf_op jit(solution)/shard_map/gate_up/pallas_call | solution.py:184
  69.9 1.6 %collective-permute-start.15 = (bf16[384,512]{1,0:T(8,128)(2,1)S(1)}, bf16[384,512]{1,0:T(8,128)(2,1)S(1)}, u32[]{:S(2)}, u32[]{:S(2)}) collective-permute-start(bf16[384,512]{1,0:T(8,128)(2,1)S(1)} %add_convert_fusion.3), channel_id=1, source_target_pairs={{0,2},{1,3},{2,0},{3,1},{4,6},{5,7},{6,4},{7,5},{8,10},{9,11},{10,... | collective-permute-start | bytes 1179656 | tf_op jit(solution)/shard_map/ppermute | solution.py:30
  71.5 8.4 %down.4 = (f32[384,512]{1,0:T(8,128)S(1)}, f32[384,512]{1,0:T(8,128)S(1)}, bf16[384,512]{1,0:T(8,128)(2,1)S(1)}, bf16[384,512]{1,0:T(8,128)(2,1)S(1)}, bf16[384,...) custom-call(s32[1]{0:T(128)} %bitcast.me_ref, bf16[384,1664]{1,0:T(8,128)(2,1)S(1)} %get-tuple-element.97.hidden_ref, ...), custom_call_target="tpu_custom_call" | custom-call | flops 490733568 | bytes 1277952 | tf_op jit(solution)/shard_map/down/pallas_call | solution.py:237
  83.8 5.8 %down.5 = (f32[384,512]{1,0:T(8,128)S(1)}, f32[384,512]{1,0:T(8,128)S(1)}, bf16[384,512]{1,0:T(8,128)(2,1)S(1)}, bf16[384,512]{1,0:T(8,128)(2,1)S(1)}) custom-call(s32[1]{0:T(128)} %bitcast.me_ref, bf16[384,1664]{1,0:T(8,128)(2,1)S(1)} %get-tuple-element.97.hidden_ref, bf16[1664,8192]{1,0:T(8,128)(2,1)} %weight_ref.7), custom_call_target="tpu_custom_call" | custom-call | flops 327155712 | bytes 851968 | tf_op jit(solution)/shard_map/down/pallas_call | solution.py:237
  90.3 3.2 %collective-permute-done.20 = bf16[384,512]{1,0:T(8,128)(2,1)S(1)} collective-permute-done((bf16[384,512]{1,0:T(8,128)(2,1)S(1)}, bf16[384,512]{1,0:T(8,128)(2,1)S(1)}, u32[]{:S(2)}, u32[]{:S(2)}) %collective-permute-start.20) | collective-permute-done | bytes 393248 | tf_op jit(solution)/shard_map/ppermute | solution.py:30
  94.5 1.4 %collective-permute-start.25 = (bf16[384,512]{1,0:T(8,128)(2,1)S(1)}, bf16[384,512]{1,0:T(8,128)(2,1)S(1)}, u32[]{:S(2)}, u32[]{:S(2)}) collective-permute-start(bf16[384,512]{1,0:T(8,128)(2,1)S(1)} %fusion.6), channel_id=1, source_target_pairs={{0,4},{1,5},{2,6},{3,7},{4,0},{5,1},{6,2},{7,3},{8,12},{9,13},{10,... | collective-permute-start | bytes 1179656 | tf_op jit(solution)/shard_map/ppermute | solution.py:30
  95.9 4.8 %down.6 = (f32[384,512]{1,0:T(8,128)S(1)}, f32[384,512]{1,0:T(8,128)S(1)}, bf16[384,512]{1,0:T(8,128)(2,1)S(1)}) custom-call(s32[1]{0:T(128)} %bitcast.me_ref, bf16[384,1664]{1,0:T(8,128)(2,1)S(1)} %get-tuple-element.97.hidden_ref, bf16[1664,8192]{1,0:T(8,128)(2,1)} %weight_ref.7), custom_call_target="tpu_custom_call" | custom-call | flops 245366784 | bytes 638976 | tf_op jit(solution)/shard_map/down/pallas_call | solution.py:237
  100.8 3.4 %collective-permute-done.23 = bf16[384,512]{1,0:T(8,128)(2,1)S(1)} collective-permute-done((bf16[384,512]{1,0:T(8,128)(2,1)S(1)}, bf16[384,512]{1,0:T(8,128)(2,1)S(1)}, u32[]{:S(2)}, u32[]{:S(2)}) %collective-permute-start.23) | collective-permute-done | bytes 393248 | tf_op jit(solution)/shard_map/ppermute | solution.py:30
  104.8 1.8 %collective-permute-start.28 = (bf16[384,512]{1,0:T(8,128)(2,1)S(1)}, bf16[384,512]{1,0:T(8,128)(2,1)S(1)}, u32[]{:S(2)}, u32[]{:S(2)}) collective-permute-start(bf16[384,512]{1,0:T(8,128)(2,1)S(1)} %fusion.9), channel_id=1, source_target_pairs={{0,2},{1,3},{2,0},{3,1},{4,8},{5,9},{6,10},{7,11},{8,4},{9,5},{10,... | collective-permute-start | bytes 1179656 | tf_op jit(solution)/shard_map/ppermute | solution.py:30
  106.9 2.3 %down.7 = f32[384,512]{1,0:T(8,128)S(1)} custom-call(s32[1]{0:T(128)} %bitcast.me_ref, bf16[384,1664]{1,0:T(8,128)(2,1)S(1)} %get-tuple-element.97.hidden_ref, bf16[1664,8192]{1,0:T(8,128)(2,1)} %weight_ref.7), custom_call_target="tpu_custom_call" | custom-call | flops 81788928 | bytes 212992 | tf_op jit(solution)/shard_map/down/pallas_call | solution.py:237
  109.3 5.1 %collective-permute-done.28 = bf16[384,512]{1,0:T(8,128)(2,1)S(1)} collective-permute-done((bf16[384,512]{1,0:T(8,128)(2,1)S(1)}, bf16[384,512]{1,0:T(8,128)(2,1)S(1)}, u32[]{:S(2)}, u32[]{:S(2)}) %collective-permute-start.28) | collective-permute-done | bytes 393248 | tf_op jit(solution)/shard_map/ppermute | solution.py:30
  (68 shorter events, 14.3 us)
Async XLA Ops:
  1.9 12.5 %collective-permute-start = (bf16[1,400,512]{2,1,0:T(8,128)(2,1)S(1)}, bf16[1,400,512]{2,1,0:T(8,128)(2,1)S(1)}, u32[]{:S(2)}, u32[]{:S(2)}) collective-permute-start(bf16[1,400,512]{2,1,0:T(8,128)(2,1)S(1)} %prepare.1.refs_0_), channel_id=1, source_target_pairs={{0,2},{1,3},{2,0},{3,1},{4,8},{5,9},{6,10},{7,11},{8,4},{9,5},{10,... | collective-permute-start | bytes 1228808 | tf_op jit(solution)/shard_map/ppermute | solution.py:30
  4.9 11.3 %collective-permute-start.2 = (bf16[1,400,512]{2,1,0:T(8,128)(2,1)S(1)}, bf16[1,400,512]{2,1,0:T(8,128)(2,1)S(1)}, u32[]{:S(2)}, u32[]{:S(2)}) collective-permute-start(bf16[1,400,512]{2,1,0:T(8,128)(2,1)S(1)} %prepare.1.refs_0_), channel_id=1, source_target_pairs={{0,4},{1,5},{2,6},{3,7},{4,0},{5,1},{6,2},{7,3},{8,12},{9,13},{10,... | collective-permute-start | bytes 1228808 | tf_op jit(solution)/shard_map/ppermute | solution.py:30
  6.6 11.3 %collective-permute-start.4 = (bf16[1,400,512]{2,1,0:T(8,128)(2,1)S(1)}, bf16[1,400,512]{2,1,0:T(8,128)(2,1)S(1)}, u32[]{:S(2)}, u32[]{:S(2)}) collective-permute-start(bf16[1,400,512]{2,1,0:T(8,128)(2,1)S(1)} %prepare.1.refs_0_), channel_id=1, source_target_pairs={{0,1},{1,0},{2,3},{3,2},{4,5},{5,4},{6,7},{7,6},{8,9},{9,8},{10,11... | collective-permute-start | bytes 1228808 | tf_op jit(solution)/shard_map/ppermute | solution.py:34
  14.4 12.3 %collective-permute-start.1 = (bf16[1,400,512]{2,1,0:T(8,128)(2,1)S(1)}, bf16[1,400,512]{2,1,0:T(8,128)(2,1)S(1)}, u32[]{:S(2)}, u32[]{:S(2)}) collective-permute-start(bf16[1,400,512]{2,1,0:T(8,128)(2,1)S(1)} %collective-permute-done.refs_3_), channel_id=1, source_target_pairs={{0,4},{1,5},{2,6},{3,7},{4,0},{5,1},{6,2},{7,3},{8,12},{9,13},{10,... | collective-permute-start | bytes 1228808 | tf_op jit(solution)/shard_map/ppermute | solution.py:30
  16.2 10.6 %collective-permute-start.3 = (bf16[1,400,512]{2,1,0:T(8,128)(2,1)S(1)}, bf16[1,400,512]{2,1,0:T(8,128)(2,1)S(1)}, u32[]{:S(2)}, u32[]{:S(2)}) collective-permute-start(bf16[1,400,512]{2,1,0:T(8,128)(2,1)S(1)} %collective-permute-done.2.refs_2_), channel_id=1, source_target_pairs={{0,2},{1,3},{2,0},{3,1},{4,8},{5,9},{6,10},{7,11},{8,4},{9,5},{10,... | collective-permute-start | bytes 1228808 | tf_op jit(solution)/shard_map/ppermute | solution.py:30
  17.8 12.4 %collective-permute-start.7 = (bf16[2,400,512]{2,1,0:T(8,128)(2,1)S(1)}, bf16[2,400,512]{2,1,0:T(8,128)(2,1)S(1)}, u32[]{:S(2)}, u32[]{:S(2)}) collective-permute-start(bf16[2,400,512]{2,1,0:T(8,128)(2,1)S(1)} %pad_maximum_fusion), channel_id=1, source_target_pairs={{0,1},{1,0},{2,3},{3,2},{4,5},{5,4},{6,7},{7,6},{8,9},{9,8},{10,11... | collective-permute-start | bytes 2457608 | tf_op jit(solution)/shard_map/ppermute | solution.py:34
  26.8 12.4 %collective-permute-start.5 = (bf16[1,400,512]{2,1,0:T(8,128)(2,1)S(1)}, bf16[1,400,512]{2,1,0:T(8,128)(2,1)S(1)}, u32[]{:S(2)}, u32[]{:S(2)}) collective-permute-start(bf16[1,400,512]{2,1,0:T(8,128)(2,1)S(1)} %collective-permute-done.3.refs_3_), channel_id=1, source_target_pairs={{0,4},{1,5},{2,6},{3,7},{4,0},{5,1},{6,2},{7,3},{8,12},{9,13},{10,... | collective-permute-start | bytes 1228808 | tf_op jit(solution)/shard_map/ppermute | solution.py:30
  28.5 11.6 %collective-permute-start.6 = (bf16[1,400,512]{2,1,0:T(8,128)(2,1)S(1)}, bf16[1,400,512]{2,1,0:T(8,128)(2,1)S(1)}, u32[]{:S(2)}, u32[]{:S(2)}) collective-permute-start(bf16[1,400,512]{2,1,0:T(8,128)(2,1)S(1)} %broadcast_select_fusion.1), channel_id=1, source_target_pairs={{0,2},{1,3},{2,0},{3,1},{4,6},{5,7},{6,4},{7,5},{8,10},{9,11},{10,... | collective-permute-start | bytes 1228808 | tf_op jit(solution)/shard_map/ppermute | solution.py:30
  30.2 11.8 %collective-permute-start.9 = (bf16[2,400,512]{2,1,0:T(8,128)(2,1)S(1)}, bf16[2,400,512]{2,1,0:T(8,128)(2,1)S(1)}, u32[]{:S(2)}, u32[]{:S(2)}) collective-permute-start(bf16[2,400,512]{2,1,0:T(8,128)(2,1)S(1)} %pad_maximum_fusion.1), channel_id=1, source_target_pairs={{0,1},{1,0},{2,3},{3,2},{4,5},{5,4},{6,7},{7,6},{8,9},{9,8},{10,11... | collective-permute-start | bytes 2457608 | tf_op jit(solution)/shard_map/ppermute | solution.py:34
  40.2 12.1 %collective-permute-start.11 = (bf16[2,400,512]{2,1,0:T(8,128)(2,1)S(1)}, bf16[2,400,512]{2,1,0:T(8,128)(2,1)S(1)}, u32[]{:S(2)}, u32[]{:S(2)}) collective-permute-start(bf16[2,400,512]{2,1,0:T(8,128)(2,1)S(1)} %pad_maximum_fusion.2), channel_id=1, source_target_pairs={{0,1},{1,0},{2,3},{3,2},{4,5},{5,4},{6,7},{7,6},{8,9},{9,8},{10,11... | collective-permute-start | bytes 2457608 | tf_op jit(solution)/shard_map/ppermute | solution.py:34
  40.3 11.9 %collective-permute-start.8 = (bf16[1,400,512]{2,1,0:T(8,128)(2,1)S(1)}, bf16[1,400,512]{2,1,0:T(8,128)(2,1)S(1)}, u32[]{:S(2)}, u32[]{:S(2)}) collective-permute-start(bf16[1,400,512]{2,1,0:T(8,128)(2,1)S(1)} %broadcast_select_fusion), channel_id=1, source_target_pairs={{0,2},{1,3},{2,0},{3,1},{4,6},{5,7},{6,4},{7,5},{8,10},{9,11},{10,... | collective-permute-start | bytes 1228808 | tf_op jit(solution)/shard_map/ppermute | solution.py:30
  52.3 7.2 %collective-permute-start.10 = (bf16[1,400,512]{2,1,0:T(8,128)(2,1)S(1)}, bf16[1,400,512]{2,1,0:T(8,128)(2,1)S(1)}, u32[]{:S(2)}, u32[]{:S(2)}) collective-permute-start(bf16[1,400,512]{2,1,0:T(8,128)(2,1)S(1)} %collective-permute-done.8.refs_2_), channel_id=1, source_target_pairs={{0,1},{1,0},{2,3},{3,2},{4,5},{5,4},{6,7},{7,6},{8,9},{9,8},{10,11... | collective-permute-start | bytes 1228808 | tf_op jit(solution)/shard_map/ppermute | solution.py:34
  69.9 12.0 %collective-permute-start.15 = (bf16[384,512]{1,0:T(8,128)(2,1)S(1)}, bf16[384,512]{1,0:T(8,128)(2,1)S(1)}, u32[]{:S(2)}, u32[]{:S(2)}) collective-permute-start(bf16[384,512]{1,0:T(8,128)(2,1)S(1)} %add_convert_fusion.3), channel_id=1, source_target_pairs={{0,2},{1,3},{2,0},{3,1},{4,6},{5,7},{6,4},{7,5},{8,10},{9,11},{10,... | collective-permute-start | bytes 1179656 | tf_op jit(solution)/shard_map/ppermute | solution.py:30
  81.4 8.3 %collective-permute-start.18 = (bf16[384,512]{1,0:T(8,128)(2,1)S(1)}, bf16[384,512]{1,0:T(8,128)(2,1)S(1)}, u32[]{:S(2)}, u32[]{:S(2)}) collective-permute-start(bf16[384,512]{1,0:T(8,128)(2,1)S(1)} %get-tuple-element.87), channel_id=1, source_target_pairs={{0,1},{1,0},{2,3},{3,2},{4,5},{5,4},{6,7},{7,6},{8,9},{9,8},{10,11... | collective-permute-start | bytes 1179656 | tf_op jit(solution)/shard_map/ppermute | solution.py:34
  81.7 8.6 %collective-permute-start.19 = (bf16[384,512]{1,0:T(8,128)(2,1)S(1)}, bf16[384,512]{1,0:T(8,128)(2,1)S(1)}, u32[]{:S(2)}, u32[]{:S(2)}) collective-permute-start(bf16[384,512]{1,0:T(8,128)(2,1)S(1)} %get-tuple-element.89), channel_id=1, source_target_pairs={{0,1},{1,0},{2,3},{3,2},{4,5},{5,4},{6,7},{7,6},{8,9},{9,8},{10,11... | collective-permute-start | bytes 1179656 | tf_op jit(solution)/shard_map/ppermute | solution.py:34
  82.1 11.4 %collective-permute-start.20 = (bf16[384,512]{1,0:T(8,128)(2,1)S(1)}, bf16[384,512]{1,0:T(8,128)(2,1)S(1)}, u32[]{:S(2)}, u32[]{:S(2)}) collective-permute-start(bf16[384,512]{1,0:T(8,128)(2,1)S(1)} %fusion.1), channel_id=1, source_target_pairs={{0,4},{1,5},{2,6},{3,7},{4,0},{5,1},{6,2},{7,3},{8,12},{9,13},{10,... | collective-permute-start | bytes 1179656 | tf_op jit(solution)/shard_map/ppermute | solution.py:30
  82.8 11.5 %collective-permute-start.21 = (bf16[384,512]{1,0:T(8,128)(2,1)S(1)}, bf16[384,512]{1,0:T(8,128)(2,1)S(1)}, u32[]{:S(2)}, u32[]{:S(2)}) collective-permute-start(bf16[384,512]{1,0:T(8,128)(2,1)S(1)} %add_convert_fusion.2), channel_id=1, source_target_pairs={{0,2},{1,3},{2,0},{3,1},{4,6},{5,7},{6,4},{7,5},{8,10},{9,11},{10,... | collective-permute-start | bytes 1179656 | tf_op jit(solution)/shard_map/ppermute | solution.py:30
  89.6 11.1 %collective-permute-start.24 = (bf16[384,512]{1,0:T(8,128)(2,1)S(1)}, bf16[384,512]{1,0:T(8,128)(2,1)S(1)}, u32[]{:S(2)}, u32[]{:S(2)}) collective-permute-start(bf16[384,512]{1,0:T(8,128)(2,1)S(1)} %get-tuple-element.95), channel_id=1, source_target_pairs={{0,1},{1,0},{2,3},{3,2},{4,5},{5,4},{6,7},{7,6},{8,9},{9,8},{10,11... | collective-permute-start | bytes 1179656 | tf_op jit(solution)/shard_map/ppermute | solution.py:34
  89.7 11.1 %collective-permute-start.22 = (bf16[384,512]{1,0:T(8,128)(2,1)S(1)}, bf16[384,512]{1,0:T(8,128)(2,1)S(1)}, u32[]{:S(2)}, u32[]{:S(2)}) collective-permute-start(bf16[384,512]{1,0:T(8,128)(2,1)S(1)} %get-tuple-element.93), channel_id=1, source_target_pairs={{0,1},{1,0},{2,3},{3,2},{4,5},{5,4},{6,7},{7,6},{8,9},{9,8},{10,11... | collective-permute-start | bytes 1179656 | tf_op jit(solution)/shard_map/ppermute | solution.py:34
  93.7 10.5 %collective-permute-start.23 = (bf16[384,512]{1,0:T(8,128)(2,1)S(1)}, bf16[384,512]{1,0:T(8,128)(2,1)S(1)}, u32[]{:S(2)}, u32[]{:S(2)}) collective-permute-start(bf16[384,512]{1,0:T(8,128)(2,1)S(1)} %fusion.4), channel_id=1, source_target_pairs={{0,2},{1,3},{2,0},{3,1},{4,8},{5,9},{6,10},{7,11},{8,4},{9,5},{10,... | collective-permute-start | bytes 1179656 | tf_op jit(solution)/shard_map/ppermute | solution.py:30
  94.5 10.1 %collective-permute-start.25 = (bf16[384,512]{1,0:T(8,128)(2,1)S(1)}, bf16[384,512]{1,0:T(8,128)(2,1)S(1)}, u32[]{:S(2)}, u32[]{:S(2)}) collective-permute-start(bf16[384,512]{1,0:T(8,128)(2,1)S(1)} %fusion.6), channel_id=1, source_target_pairs={{0,4},{1,5},{2,6},{3,7},{4,0},{5,1},{6,2},{7,3},{8,12},{9,13},{10,... | collective-permute-start | bytes 1179656 | tf_op jit(solution)/shard_map/ppermute | solution.py:30
  100.6 8.6 %collective-permute-start.26 = (bf16[384,512]{1,0:T(8,128)(2,1)S(1)}, bf16[384,512]{1,0:T(8,128)(2,1)S(1)}, u32[]{:S(2)}, u32[]{:S(2)}) collective-permute-start(bf16[384,512]{1,0:T(8,128)(2,1)S(1)} %get-tuple-element.98), channel_id=1, source_target_pairs={{0,1},{1,0},{2,3},{3,2},{4,5},{5,4},{6,7},{7,6},{8,9},{9,8},{10,11... | collective-permute-start | bytes 1179656 | tf_op jit(solution)/shard_map/ppermute | solution.py:34
  104.8 9.5 %collective-permute-start.28 = (bf16[384,512]{1,0:T(8,128)(2,1)S(1)}, bf16[384,512]{1,0:T(8,128)(2,1)S(1)}, u32[]{:S(2)}, u32[]{:S(2)}) collective-permute-start(bf16[384,512]{1,0:T(8,128)(2,1)S(1)} %fusion.9), channel_id=1, source_target_pairs={{0,2},{1,3},{2,0},{3,1},{4,8},{5,9},{6,10},{7,11},{8,4},{9,5},{10,... | collective-permute-start | bytes 1179656 | tf_op jit(solution)/shard_map/ppermute | solution.py:30
  106.6 9.0 %collective-permute-start.27 = (bf16[384,512]{1,0:T(8,128)(2,1)S(1)}, bf16[384,512]{1,0:T(8,128)(2,1)S(1)}, u32[]{:S(2)}, u32[]{:S(2)}) collective-permute-start(bf16[384,512]{1,0:T(8,128)(2,1)S(1)} %add_convert_fusion.1), channel_id=1, source_target_pairs={{0,4},{1,5},{2,6},{3,7},{4,0},{5,1},{6,2},{7,3},{8,12},{9,13},{10,... | collective-permute-start | bytes 1179656 | tf_op jit(solution)/shard_map/ppermute | solution.py:30
  (8 other events, 21.3 us)

commit v14 on v13

--- a/solution.py
+++ b/solution.py
@@ -105,7 +105,7 @@
 
     if last:
 
-        @pl.when(step == 0)
+        @pl.when(step == count - 1)
         def _():
             for copy in copies:
                 copy.start()
@@ -293,16 +293,12 @@
         acc,
         (TWO, 1, their_twos, 0), (TWO_IN, 1, their_twos, 1),
         (THREE, 0, three, 0), (THREE_ACROSS, 0, across, 0),
+        (THREE, 1, their_threes, 0), (THREE_ACROSS, 1, their_threes, 1),
     )
     four = after(four, acc[3])
-    their_four = swap(four)
-    acc = multiply(
-        acc,
-        (THREE, 1, their_threes, 0), (THREE_ACROSS, 1, their_threes, 1), (FOUR, 0, four, 0),
-    )
     hidden, their_four, four = multiply(
         acc,
-        (FOUR, 1, after(their_four, acc[3]), 0),
+        (FOUR, 0, four, 0), (FOUR, 1, swap(four), 0),
         then=(((FOUR, 1), (FOUR, 0)), (jnp.bfloat16, jnp.float32), down_weight),
     )
 

time: 117 us -> 113 us (0.966)
  Pallas kernels: 63.7 us -> 60.4 us
  starting transfers between devices: 22.7 us -> 21.3 us
  waiting for transfers between devices: 25.3 us -> 26.5 us
    ppermute x15, waiting for transfers between devices: 1.85 us -> 5.41 us  [swap(): return lax.ppermute(x, 'gx', [(i, i ^ 1) for i in range(4 * LINE)])]
    pallas_call x5 -> x4, Pallas kernels: 42.2 us -> 38.9 us  [gate_up(): pl.pallas_call(functools.partial(gate_up_body, count, first, last, rows,...]
    ppermute x14, waiting for transfers between devices: 23.4 us -> 21.1 us  [send(): return lax.ppermute(x, 'gx', pairs)]
    ppermute x14, starting transfers between devices: 19.8 us -> 18.5 us  [send(): return lax.ppermute(x, 'gx', pairs)]
  transfers between devices with their start and end apart: 29 -> 29, of which waited for: 11 -> 14; matrix products, arithmetic and copies ran while one was open for 2% -> 2% of each run, Pallas kernels for 47% -> 46%
where the time goes in v14:
time: 113 us
  Pallas kernels  60.4 us (53%)
  waiting for transfers between devices  26.5 us (23%)
  starting transfers between devices  21.3 us (19%)
  other arithmetic  2.92 us (3%)
  local copies, waits for them, and re-layouts  1.73 us (2%)
    pallas_call x4, Pallas kernels, gate_up(): pl.pallas_call(functools.partial(gate_up_body, count, first, last, rows,...  38.9 us
    pallas_call x4, Pallas kernels, down(): pl.pallas_call(functools.partial(down_body, len(kept), len(sent)), grid_s...  21.3 us
    ppermute x14, waiting for transfers between devices, send(): return lax.ppermute(x, 'gx', pairs)  21.1 us
    ppermute x14, starting transfers between devices, send(): return lax.ppermute(x, 'gx', pairs)  18.5 us
    ppermute x15, waiting for transfers between devices, swap(): return lax.ppermute(x, 'gx', [(i, i ^ 1) for i in range(4 * LINE)])  5.41 us
    ppermute x15, starting transfers between devices, swap(): return lax.ppermute(x, 'gx', [(i, i ^ 1) for i in range(4 * LINE)])  2.75 us
  transfers between devices with their start and end apart: 29, of which 14 were waited for; matrix products, arithmetic and copies ran while one was open for 2% of the time, Pallas kernels for 46%

profile of v14, /device:TPU:0, one launch (start us, length us, event | category | flops | bytes accessed | tf_op | source)
XLA Modules:
  0.0 113.1 jit_solution(16471966234268059988)
XLA Ops:
  1.9 3.1 %collective-permute-start.2 = (bf16[1,400,512]{2,1,0:T(8,128)(2,1)S(1)}, bf16[1,400,512]{2,1,0:T(8,128)(2,1)S(1)}, u32[]{:S(2)}, u32[]{:S(2)}) collective-permute-start(bf16[1,400,512]{2,1,0:T(8,128)(2,1)S(1)} %prepare.1.refs_0_), channel_id=1, source_target_pairs={{0,4},{1,5},{2,6},{3,7},{4,0},{5,1},{6,2},{7,3},{8,12},{9,13},{10,... | collective-permute-start | bytes 1228808 | tf_op jit(solution)/shard_map/ppermute | solution.py:30
  5.0 1.5 %collective-permute-start = (bf16[1,400,512]{2,1,0:T(8,128)(2,1)S(1)}, bf16[1,400,512]{2,1,0:T(8,128)(2,1)S(1)}, u32[]{:S(2)}, u32[]{:S(2)}) collective-permute-start(bf16[1,400,512]{2,1,0:T(8,128)(2,1)S(1)} %prepare.1.refs_0_), channel_id=1, source_target_pairs={{0,2},{1,3},{2,0},{3,1},{4,8},{5,9},{6,10},{7,11},{8,4},{9,5},{10,... | collective-permute-start | bytes 1228808 | tf_op jit(solution)/shard_map/ppermute | solution.py:30
  6.5 7.9 %collective-permute-done.2.refs_2_ = bf16[1,400,512]{2,1,0:T(8,128)(2,1)S(1)} collective-permute-done((bf16[1,400,512]{2,1,0:T(8,128)(2,1)S(1)}, bf16[1,400,512]{2,1,0:T(8,128)(2,1)S(1)}, u32[]{:S(2)}, u32[]{:S(2)}) %collective-permute-start.2) | collective-permute-done | bytes 409632 | tf_op jit(solution)/shard_map/ppermute | solution.py:30
  14.5 1.7 %collective-permute-start.3 = (bf16[1,400,512]{2,1,0:T(8,128)(2,1)S(1)}, bf16[1,400,512]{2,1,0:T(8,128)(2,1)S(1)}, u32[]{:S(2)}, u32[]{:S(2)}) collective-permute-start(bf16[1,400,512]{2,1,0:T(8,128)(2,1)S(1)} %collective-permute-done.2.refs_2_), channel_id=1, source_target_pairs={{0,2},{1,3},{2,0},{3,1},{4,8},{5,9},{6,10},{7,11},{8,4},{9,5},{10,... | collective-permute-start | bytes 1228808 | tf_op jit(solution)/shard_map/ppermute | solution.py:30
  16.1 1.6 %collective-permute-start.1 = (bf16[1,400,512]{2,1,0:T(8,128)(2,1)S(1)}, bf16[1,400,512]{2,1,0:T(8,128)(2,1)S(1)}, u32[]{:S(2)}, u32[]{:S(2)}) collective-permute-start(bf16[1,400,512]{2,1,0:T(8,128)(2,1)S(1)} %collective-permute-done.refs_3_), channel_id=1, source_target_pairs={{0,4},{1,5},{2,6},{3,7},{4,0},{5,1},{6,2},{7,3},{8,12},{9,13},{10,... | collective-permute-start | bytes 1228808 | tf_op jit(solution)/shard_map/ppermute | solution.py:30
  18.0 8.8 %gate_up.4 = (f32[384,1536]{1,0:T(8,128)S(1)}, f32[384,1536]{1,0:T(8,128)S(1)}, f32[384,256]{1,0:T(8,128)S(1)}, f32[8,512]{1,0:T(8,128)S(1)}) custom-call(s32[1]{0:T(128)} %bitcast.me_ref, bf16[1,400,512]{2,1,0:T(8,128)(2,1)S(1)} %prepare.1.refs_0_, bf16[1,400,512]{2,1,0:T(8,128)(2,1)S(1)} %collective-permute-done.4.refs_1_, ...), custom_call_target="tpu_custom_call" | custom-call | flops 654311424 | bytes 1703936 | tf_op jit(solution)/shard_map/gate_up/pallas_call | solution.py:184
  26.9 1.6 %collective-permute-start.6 = (bf16[1,400,512]{2,1,0:T(8,128)(2,1)S(1)}, bf16[1,400,512]{2,1,0:T(8,128)(2,1)S(1)}, u32[]{:S(2)}, u32[]{:S(2)}) collective-permute-start(bf16[1,400,512]{2,1,0:T(8,128)(2,1)S(1)} %broadcast_select_fusion.1), channel_id=1, source_target_pairs={{0,2},{1,3},{2,0},{3,1},{4,6},{5,7},{6,4},{7,5},{8,10},{9,11},{10,... | collective-permute-start | bytes 1228808 | tf_op jit(solution)/shard_map/ppermute | solution.py:30
  29.6 8.9 %gate_up.5 = (f32[384,1536]{1,0:T(8,128)S(1)}, f32[384,1536]{1,0:T(8,128)S(1)}, f32[384,256]{1,0:T(8,128)S(1)}, f32[8,512]{1,0:T(8,128)S(1)}) custom-call(s32[1]{0:T(128)} %bitcast.me_ref, bf16[2,400,512]{2,1,0:T(8,128)(2,1)S(1)} %collective-permute-done.7.refs_0_.refs_1_, bf16[2,400,512]{2,1,0:T(8,128)(2,1)S(1)} %collective-permute-done.7.refs_0_.refs_1_, ...), custom_call_target="tpu_custom_call" | custom-call | flops 654311424 | bytes 1703936 | tf_op jit(solution)/shard_map/gate_up/pallas_call | solution.py:184
  40.8 1.7 %collective-permute-done.10.refs_4_.refs_5_ = bf16[2,400,512]{2,1,0:T(8,128)(2,1)S(1)} collective-permute-done((bf16[2,400,512]{2,1,0:T(8,128)(2,1)S(1)}, bf16[2,400,512]{2,1,0:T(8,128)(2,1)S(1)}, u32[]{:S(2)}, u32[]{:S(2)}) %collective-permute-start.10) | collective-permute-done | bytes 819232 | tf_op jit(solution)/shard_map/ppermute | solution.py:34
  42.5 12.5 %gate_up.6 = (f32[384,1536]{1,0:T(8,128)S(1)}, f32[384,1536]{1,0:T(8,128)S(1)}, f32[384,256]{1,0:T(8,128)S(1)}, f32[8,512]{1,0:T(8,128)S(1)}) custom-call(s32[1]{0:T(128)} %bitcast.me_ref, bf16[2,400,512]{2,1,0:T(8,128)(2,1)S(1)} %collective-permute-done.9.refs_0_.refs_1_, bf16[2,400,512]{2,1,0:T(8,128)(2,1)S(1)} %collective-permute-done.9.refs_0_.refs_1_, ...), custom_call_target="tpu_custom_call" | custom-call | flops 981467136 | bytes 2555904 | tf_op jit(solution)/shard_map/gate_up/pallas_call | solution.py:184
  55.2 1.6 %collective-permute-done.11.refs_1_ = bf16[1,400,512]{2,1,0:T(8,128)(2,1)S(1)} collective-permute-done((bf16[1,400,512]{2,1,0:T(8,128)(2,1)S(1)}, bf16[1,400,512]{2,1,0:T(8,128)(2,1)S(1)}, u32[]{:S(2)}, u32[]{:S(2)}) %collective-permute-start.11) | collective-permute-done | bytes 409632 | tf_op jit(solution)/shard_map/ppermute | solution.py:34
  56.9 8.6 %gate_up.7 = (bf16[384,1664]{1,0:T(8,128)(2,1)S(1)}, bf16[384,512]{1,0:T(8,128)(2,1)S(1)}, f32[384,512]{1,0:T(8,128)S(1)}) custom-call(s32[1]{0:T(128)} %bitcast.me_ref, bf16[1,400,512]{2,1,0:T(8,128)(2,1)S(1)} %collective-permute-done.8.refs_0_, bf16[1,400,512]{2,1,0:T(8,128)(2,1)S(1)} %collective-permute-done.11.refs_1_, bf16[8192,1664]{1,0:T(8,128)(2,1)} %refs_2_.1, ...), custom_call_target="tpu_custom_call" | custom-call | flops 327155712 | bytes 851968 | tf_op jit(solution)/shard_map/gate_up/pallas_call | solution.py:184
  65.7 1.6 %collective-permute-done.12 = bf16[384,512]{1,0:T(8,128)(2,1)S(1)} collective-permute-done((bf16[384,512]{1,0:T(8,128)(2,1)S(1)}, bf16[384,512]{1,0:T(8,128)(2,1)S(1)}, u32[]{:S(2)}, u32[]{:S(2)}) %collective-permute-start.12) | collective-permute-done | bytes 393248 | tf_op jit(solution)/shard_map/ppermute | solution.py:34
  68.0 8.4 %down.4 = (f32[384,512]{1,0:T(8,128)S(1)}, f32[384,512]{1,0:T(8,128)S(1)}, bf16[384,512]{1,0:T(8,128)(2,1)S(1)}, bf16[384,512]{1,0:T(8,128)(2,1)S(1)}, bf16[384,...) custom-call(s32[1]{0:T(128)} %bitcast.me_ref, bf16[384,1664]{1,0:T(8,128)(2,1)S(1)} %get-tuple-element.87.hidden_ref, ...), custom_call_target="tpu_custom_call" | custom-call | flops 490733568 | bytes 1277952 | tf_op jit(solution)/shard_map/down/pallas_call | solution.py:237
  80.8 5.8 %down.5 = (f32[384,512]{1,0:T(8,128)S(1)}, f32[384,512]{1,0:T(8,128)S(1)}, bf16[384,512]{1,0:T(8,128)(2,1)S(1)}, bf16[384,512]{1,0:T(8,128)(2,1)S(1)}) custom-call(s32[1]{0:T(128)} %bitcast.me_ref, bf16[384,1664]{1,0:T(8,128)(2,1)S(1)} %get-tuple-element.87.hidden_ref, bf16[1664,8192]{1,0:T(8,128)(2,1)} %weight_ref.7), custom_call_target="tpu_custom_call" | custom-call | flops 327155712 | bytes 851968 | tf_op jit(solution)/shard_map/down/pallas_call | solution.py:237
  87.3 2.6 %collective-permute-done.20 = bf16[384,512]{1,0:T(8,128)(2,1)S(1)} collective-permute-done((bf16[384,512]{1,0:T(8,128)(2,1)S(1)}, bf16[384,512]{1,0:T(8,128)(2,1)S(1)}, u32[]{:S(2)}, u32[]{:S(2)}) %collective-permute-start.20) | collective-permute-done | bytes 393248 | tf_op jit(solution)/shard_map/ppermute | solution.py:30
  90.2 1.6 %collective-permute-start.23 = (bf16[384,512]{1,0:T(8,128)(2,1)S(1)}, bf16[384,512]{1,0:T(8,128)(2,1)S(1)}, u32[]{:S(2)}, u32[]{:S(2)}) collective-permute-start(bf16[384,512]{1,0:T(8,128)(2,1)S(1)} %fusion.4), channel_id=1, source_target_pairs={{0,2},{1,3},{2,0},{3,1},{4,8},{5,9},{6,10},{7,11},{8,4},{9,5},{10,... | collective-permute-start | bytes 1179656 | tf_op jit(solution)/shard_map/ppermute | solution.py:30
  92.0 1.6 %collective-permute-start.25 = (bf16[384,512]{1,0:T(8,128)(2,1)S(1)}, bf16[384,512]{1,0:T(8,128)(2,1)S(1)}, u32[]{:S(2)}, u32[]{:S(2)}) collective-permute-start(bf16[384,512]{1,0:T(8,128)(2,1)S(1)} %fusion.6), channel_id=1, source_target_pairs={{0,4},{1,5},{2,6},{3,7},{4,0},{5,1},{6,2},{7,3},{8,12},{9,13},{10,... | collective-permute-start | bytes 1179656 | tf_op jit(solution)/shard_map/ppermute | solution.py:30
  93.6 4.8 %down.6 = (f32[384,512]{1,0:T(8,128)S(1)}, f32[384,512]{1,0:T(8,128)S(1)}, bf16[384,512]{1,0:T(8,128)(2,1)S(1)}) custom-call(s32[1]{0:T(128)} %bitcast.me_ref, bf16[384,1664]{1,0:T(8,128)(2,1)S(1)} %get-tuple-element.87.hidden_ref, bf16[1664,8192]{1,0:T(8,128)(2,1)} %weight_ref.7), custom_call_target="tpu_custom_call" | custom-call | flops 245366784 | bytes 638976 | tf_op jit(solution)/shard_map/down/pallas_call | solution.py:237
  98.6 1.9 %collective-permute-done.23 = bf16[384,512]{1,0:T(8,128)(2,1)S(1)} collective-permute-done((bf16[384,512]{1,0:T(8,128)(2,1)S(1)}, bf16[384,512]{1,0:T(8,128)(2,1)S(1)}, u32[]{:S(2)}, u32[]{:S(2)}) %collective-permute-start.23) | collective-permute-done | bytes 393248 | tf_op jit(solution)/shard_map/ppermute | solution.py:30
  100.7 1.6 %collective-permute-done.25 = bf16[384,512]{1,0:T(8,128)(2,1)S(1)} collective-permute-done((bf16[384,512]{1,0:T(8,128)(2,1)S(1)}, bf16[384,512]{1,0:T(8,128)(2,1)S(1)}, u32[]{:S(2)}, u32[]{:S(2)}) %collective-permute-start.25) | collective-permute-done | bytes 393248 | tf_op jit(solution)/shard_map/ppermute | solution.py:30
  102.9 1.6 %collective-permute-start.27 = (bf16[384,512]{1,0:T(8,128)(2,1)S(1)}, bf16[384,512]{1,0:T(8,128)(2,1)S(1)}, u32[]{:S(2)}, u32[]{:S(2)}) collective-permute-start(bf16[384,512]{1,0:T(8,128)(2,1)S(1)} %add_convert_fusion.1), channel_id=1, source_target_pairs={{0,4},{1,5},{2,6},{3,7},{4,0},{5,1},{6,2},{7,3},{8,12},{9,13},{10,... | collective-permute-start | bytes 1179656 | tf_op jit(solution)/shard_map/ppermute | solution.py:30
  104.5 2.3 %down.7 = f32[384,512]{1,0:T(8,128)S(1)} custom-call(s32[1]{0:T(128)} %bitcast.me_ref, bf16[384,1664]{1,0:T(8,128)(2,1)S(1)} %get-tuple-element.87.hidden_ref, bf16[1664,8192]{1,0:T(8,128)(2,1)} %weight_ref.7), custom_call_target="tpu_custom_call" | custom-call | flops 81788928 | bytes 212992 | tf_op jit(solution)/shard_map/down/pallas_call | solution.py:237
  106.8 5.1 %collective-permute-done.28 = bf16[384,512]{1,0:T(8,128)(2,1)S(1)} collective-permute-done((bf16[384,512]{1,0:T(8,128)(2,1)S(1)}, bf16[384,512]{1,0:T(8,128)(2,1)S(1)}, u32[]{:S(2)}, u32[]{:S(2)}) %collective-permute-start.28) | collective-permute-done | bytes 393248 | tf_op jit(solution)/shard_map/ppermute | solution.py:30
  (67 shorter events, 14.2 us)
Async XLA Ops:
  1.9 12.6 %collective-permute-start.2 = (bf16[1,400,512]{2,1,0:T(8,128)(2,1)S(1)}, bf16[1,400,512]{2,1,0:T(8,128)(2,1)S(1)}, u32[]{:S(2)}, u32[]{:S(2)}) collective-permute-start(bf16[1,400,512]{2,1,0:T(8,128)(2,1)S(1)} %prepare.1.refs_0_), channel_id=1, source_target_pairs={{0,4},{1,5},{2,6},{3,7},{4,0},{5,1},{6,2},{7,3},{8,12},{9,13},{10,... | collective-permute-start | bytes 1228808 | tf_op jit(solution)/shard_map/ppermute | solution.py:30
  5.0 11.2 %collective-permute-start = (bf16[1,400,512]{2,1,0:T(8,128)(2,1)S(1)}, bf16[1,400,512]{2,1,0:T(8,128)(2,1)S(1)}, u32[]{:S(2)}, u32[]{:S(2)}) collective-permute-start(bf16[1,400,512]{2,1,0:T(8,128)(2,1)S(1)} %prepare.1.refs_0_), channel_id=1, source_target_pairs={{0,2},{1,3},{2,0},{3,1},{4,8},{5,9},{6,10},{7,11},{8,4},{9,5},{10,... | collective-permute-start | bytes 1228808 | tf_op jit(solution)/shard_map/ppermute | solution.py:30
  6.5 11.4 %collective-permute-start.4 = (bf16[1,400,512]{2,1,0:T(8,128)(2,1)S(1)}, bf16[1,400,512]{2,1,0:T(8,128)(2,1)S(1)}, u32[]{:S(2)}, u32[]{:S(2)}) collective-permute-start(bf16[1,400,512]{2,1,0:T(8,128)(2,1)S(1)} %prepare.1.refs_0_), channel_id=1, source_target_pairs={{0,1},{1,0},{2,3},{3,2},{4,5},{5,4},{6,7},{7,6},{8,9},{9,8},{10,11... | collective-permute-start | bytes 1228808 | tf_op jit(solution)/shard_map/ppermute | solution.py:34
  14.5 12.3 %collective-permute-start.3 = (bf16[1,400,512]{2,1,0:T(8,128)(2,1)S(1)}, bf16[1,400,512]{2,1,0:T(8,128)(2,1)S(1)}, u32[]{:S(2)}, u32[]{:S(2)}) collective-permute-start(bf16[1,400,512]{2,1,0:T(8,128)(2,1)S(1)} %collective-permute-done.2.refs_2_), channel_id=1, source_target_pairs={{0,2},{1,3},{2,0},{3,1},{4,8},{5,9},{6,10},{7,11},{8,4},{9,5},{10,... | collective-permute-start | bytes 1228808 | tf_op jit(solution)/shard_map/ppermute | solution.py:30
  16.1 10.7 %collective-permute-start.1 = (bf16[1,400,512]{2,1,0:T(8,128)(2,1)S(1)}, bf16[1,400,512]{2,1,0:T(8,128)(2,1)S(1)}, u32[]{:S(2)}, u32[]{:S(2)}) collective-permute-start(bf16[1,400,512]{2,1,0:T(8,128)(2,1)S(1)} %collective-permute-done.refs_3_), channel_id=1, source_target_pairs={{0,4},{1,5},{2,6},{3,7},{4,0},{5,1},{6,2},{7,3},{8,12},{9,13},{10,... | collective-permute-start | bytes 1228808 | tf_op jit(solution)/shard_map/ppermute | solution.py:30
  17.9 11.8 %collective-permute-start.7 = (bf16[2,400,512]{2,1,0:T(8,128)(2,1)S(1)}, bf16[2,400,512]{2,1,0:T(8,128)(2,1)S(1)}, u32[]{:S(2)}, u32[]{:S(2)}) collective-permute-start(bf16[2,400,512]{2,1,0:T(8,128)(2,1)S(1)} %pad_maximum_fusion), channel_id=1, source_target_pairs={{0,1},{1,0},{2,3},{3,2},{4,5},{5,4},{6,7},{7,6},{8,9},{9,8},{10,11... | collective-permute-start | bytes 2457608 | tf_op jit(solution)/shard_map/ppermute | solution.py:34
  26.9 11.9 %collective-permute-start.6 = (bf16[1,400,512]{2,1,0:T(8,128)(2,1)S(1)}, bf16[1,400,512]{2,1,0:T(8,128)(2,1)S(1)}, u32[]{:S(2)}, u32[]{:S(2)}) collective-permute-start(bf16[1,400,512]{2,1,0:T(8,128)(2,1)S(1)} %broadcast_select_fusion.1), channel_id=1, source_target_pairs={{0,2},{1,3},{2,0},{3,1},{4,6},{5,7},{6,4},{7,5},{8,10},{9,11},{10,... | collective-permute-start | bytes 1228808 | tf_op jit(solution)/shard_map/ppermute | solution.py:30
  28.4 11.6 %collective-permute-start.5 = (bf16[1,400,512]{2,1,0:T(8,128)(2,1)S(1)}, bf16[1,400,512]{2,1,0:T(8,128)(2,1)S(1)}, u32[]{:S(2)}, u32[]{:S(2)}) collective-permute-start(bf16[1,400,512]{2,1,0:T(8,128)(2,1)S(1)} %collective-permute-done.3.refs_3_), channel_id=1, source_target_pairs={{0,4},{1,5},{2,6},{3,7},{4,0},{5,1},{6,2},{7,3},{8,12},{9,13},{10,... | collective-permute-start | bytes 1228808 | tf_op jit(solution)/shard_map/ppermute | solution.py:30
  29.5 11.2 %collective-permute-start.9 = (bf16[2,400,512]{2,1,0:T(8,128)(2,1)S(1)}, bf16[2,400,512]{2,1,0:T(8,128)(2,1)S(1)}, u32[]{:S(2)}, u32[]{:S(2)}) collective-permute-start(bf16[2,400,512]{2,1,0:T(8,128)(2,1)S(1)} %pad_maximum_fusion.1), channel_id=1, source_target_pairs={{0,1},{1,0},{2,3},{3,2},{4,5},{5,4},{6,7},{7,6},{8,9},{9,8},{10,11... | collective-permute-start | bytes 2457608 | tf_op jit(solution)/shard_map/ppermute | solution.py:34
  40.1 2.4 %collective-permute-start.10 = (bf16[2,400,512]{2,1,0:T(8,128)(2,1)S(1)}, bf16[2,400,512]{2,1,0:T(8,128)(2,1)S(1)}, u32[]{:S(2)}, u32[]{:S(2)}) collective-permute-start(bf16[2,400,512]{2,1,0:T(8,128)(2,1)S(1)} %pad_maximum_fusion.2), channel_id=1, source_target_pairs={{0,1},{1,0},{2,3},{3,2},{4,5},{5,4},{6,7},{7,6},{8,9},{9,8},{10,11... | collective-permute-start | bytes 2457608 | tf_op jit(solution)/shard_map/ppermute | solution.py:34
  40.2 14.8 %collective-permute-start.8 = (bf16[1,400,512]{2,1,0:T(8,128)(2,1)S(1)}, bf16[1,400,512]{2,1,0:T(8,128)(2,1)S(1)}, u32[]{:S(2)}, u32[]{:S(2)}) collective-permute-start(bf16[1,400,512]{2,1,0:T(8,128)(2,1)S(1)} %broadcast_select_fusion), channel_id=1, source_target_pairs={{0,2},{1,3},{2,0},{3,1},{4,6},{5,7},{6,4},{7,5},{8,10},{9,11},{10,... | collective-permute-start | bytes 1228808 | tf_op jit(solution)/shard_map/ppermute | solution.py:30
  67.4 11.2 %collective-permute-start.15 = (bf16[384,512]{1,0:T(8,128)(2,1)S(1)}, bf16[384,512]{1,0:T(8,128)(2,1)S(1)}, u32[]{:S(2)}, u32[]{:S(2)}) collective-permute-start(bf16[384,512]{1,0:T(8,128)(2,1)S(1)} %add_convert_fusion.3), channel_id=1, source_target_pairs={{0,2},{1,3},{2,0},{3,1},{4,6},{5,7},{6,4},{7,5},{8,10},{9,11},{10,... | collective-permute-start | bytes 1179656 | tf_op jit(solution)/shard_map/ppermute | solution.py:30
  77.0 2.2 %collective-permute-start.16 = (bf16[192,512]{1,0:T(8,128)(2,1)S(1)}, bf16[192,512]{1,0:T(8,128)(2,1)S(1)}, u32[]{:S(2)}, u32[]{:S(2)}) collective-permute-start(bf16[192,512]{1,0:T(8,128)(2,1)S(1)} %get-tuple-element.91), channel_id=1, source_target_pairs={{0,1},{1,0},{2,3},{3,2},{4,5},{5,4},{6,7},{7,6},{8,9},{9,8},{10,11... | collective-permute-start | bytes 589832 | tf_op jit(solution)/shard_map/ppermute | solution.py:34
  77.9 8.9 %collective-permute-start.18 = (bf16[384,512]{1,0:T(8,128)(2,1)S(1)}, bf16[384,512]{1,0:T(8,128)(2,1)S(1)}, u32[]{:S(2)}, u32[]{:S(2)}) collective-permute-start(bf16[384,512]{1,0:T(8,128)(2,1)S(1)} %get-tuple-element.77), channel_id=1, source_target_pairs={{0,1},{1,0},{2,3},{3,2},{4,5},{5,4},{6,7},{7,6},{8,9},{9,8},{10,11... | collective-permute-start | bytes 1179656 | tf_op jit(solution)/shard_map/ppermute | solution.py:34
  78.2 9.2 %collective-permute-start.19 = (bf16[384,512]{1,0:T(8,128)(2,1)S(1)}, bf16[384,512]{1,0:T(8,128)(2,1)S(1)}, u32[]{:S(2)}, u32[]{:S(2)}) collective-permute-start(bf16[384,512]{1,0:T(8,128)(2,1)S(1)} %get-tuple-element.79), channel_id=1, source_target_pairs={{0,1},{1,0},{2,3},{3,2},{4,5},{5,4},{6,7},{7,6},{8,9},{9,8},{10,11... | collective-permute-start | bytes 1179656 | tf_op jit(solution)/shard_map/ppermute | solution.py:34
  78.8 11.1 %collective-permute-start.20 = (bf16[384,512]{1,0:T(8,128)(2,1)S(1)}, bf16[384,512]{1,0:T(8,128)(2,1)S(1)}, u32[]{:S(2)}, u32[]{:S(2)}) collective-permute-start(bf16[384,512]{1,0:T(8,128)(2,1)S(1)} %fusion.1), channel_id=1, source_target_pairs={{0,4},{1,5},{2,6},{3,7},{4,0},{5,1},{6,2},{7,3},{8,12},{9,13},{10,... | collective-permute-start | bytes 1179656 | tf_op jit(solution)/shard_map/ppermute | solution.py:30
  79.4 12.3 %collective-permute-start.21 = (bf16[384,512]{1,0:T(8,128)(2,1)S(1)}, bf16[384,512]{1,0:T(8,128)(2,1)S(1)}, u32[]{:S(2)}, u32[]{:S(2)}) collective-permute-start(bf16[384,512]{1,0:T(8,128)(2,1)S(1)} %add_convert_fusion.2), channel_id=1, source_target_pairs={{0,2},{1,3},{2,0},{3,1},{4,6},{5,7},{6,4},{7,5},{8,10},{9,11},{10,... | collective-permute-start | bytes 1179656 | tf_op jit(solution)/shard_map/ppermute | solution.py:30
  86.7 11.9 %collective-permute-start.22 = (bf16[384,512]{1,0:T(8,128)(2,1)S(1)}, bf16[384,512]{1,0:T(8,128)(2,1)S(1)}, u32[]{:S(2)}, u32[]{:S(2)}) collective-permute-start(bf16[384,512]{1,0:T(8,128)(2,1)S(1)} %get-tuple-element.83), channel_id=1, source_target_pairs={{0,1},{1,0},{2,3},{3,2},{4,5},{5,4},{6,7},{7,6},{8,9},{9,8},{10,11... | collective-permute-start | bytes 1179656 | tf_op jit(solution)/shard_map/ppermute | solution.py:34
  86.8 11.7 %collective-permute-start.24 = (bf16[384,512]{1,0:T(8,128)(2,1)S(1)}, bf16[384,512]{1,0:T(8,128)(2,1)S(1)}, u32[]{:S(2)}, u32[]{:S(2)}) collective-permute-start(bf16[384,512]{1,0:T(8,128)(2,1)S(1)} %get-tuple-element.85), channel_id=1, source_target_pairs={{0,1},{1,0},{2,3},{3,2},{4,5},{5,4},{6,7},{7,6},{8,9},{9,8},{10,11... | collective-permute-start | bytes 1179656 | tf_op jit(solution)/shard_map/ppermute | solution.py:34
  90.2 10.4 %collective-permute-start.23 = (bf16[384,512]{1,0:T(8,128)(2,1)S(1)}, bf16[384,512]{1,0:T(8,128)(2,1)S(1)}, u32[]{:S(2)}, u32[]{:S(2)}) collective-permute-start(bf16[384,512]{1,0:T(8,128)(2,1)S(1)} %fusion.4), channel_id=1, source_target_pairs={{0,2},{1,3},{2,0},{3,1},{4,8},{5,9},{6,10},{7,11},{8,4},{9,5},{10,... | collective-permute-start | bytes 1179656 | tf_op jit(solution)/shard_map/ppermute | solution.py:30
  92.0 10.3 %collective-permute-start.25 = (bf16[384,512]{1,0:T(8,128)(2,1)S(1)}, bf16[384,512]{1,0:T(8,128)(2,1)S(1)}, u32[]{:S(2)}, u32[]{:S(2)}) collective-permute-start(bf16[384,512]{1,0:T(8,128)(2,1)S(1)} %fusion.6), channel_id=1, source_target_pairs={{0,4},{1,5},{2,6},{3,7},{4,0},{5,1},{6,2},{7,3},{8,12},{9,13},{10,... | collective-permute-start | bytes 1179656 | tf_op jit(solution)/shard_map/ppermute | solution.py:30
  98.4 8.4 %collective-permute-start.26 = (bf16[384,512]{1,0:T(8,128)(2,1)S(1)}, bf16[384,512]{1,0:T(8,128)(2,1)S(1)}, u32[]{:S(2)}, u32[]{:S(2)}) collective-permute-start(bf16[384,512]{1,0:T(8,128)(2,1)S(1)} %get-tuple-element.88), channel_id=1, source_target_pairs={{0,1},{1,0},{2,3},{3,2},{4,5},{5,4},{6,7},{7,6},{8,9},{9,8},{10,11... | collective-permute-start | bytes 1179656 | tf_op jit(solution)/shard_map/ppermute | solution.py:34
  102.5 9.3 %collective-permute-start.28 = (bf16[384,512]{1,0:T(8,128)(2,1)S(1)}, bf16[384,512]{1,0:T(8,128)(2,1)S(1)}, u32[]{:S(2)}, u32[]{:S(2)}) collective-permute-start(bf16[384,512]{1,0:T(8,128)(2,1)S(1)} %fusion.9), channel_id=1, source_target_pairs={{0,2},{1,3},{2,0},{3,1},{4,8},{5,9},{6,10},{7,11},{8,4},{9,5},{10,... | collective-permute-start | bytes 1179656 | tf_op jit(solution)/shard_map/ppermute | solution.py:30
  102.9 9.1 %collective-permute-start.27 = (bf16[384,512]{1,0:T(8,128)(2,1)S(1)}, bf16[384,512]{1,0:T(8,128)(2,1)S(1)}, u32[]{:S(2)}, u32[]{:S(2)}) collective-permute-start(bf16[384,512]{1,0:T(8,128)(2,1)S(1)} %add_convert_fusion.1), channel_id=1, source_target_pairs={{0,4},{1,5},{2,6},{3,7},{4,0},{5,1},{6,2},{7,3},{8,12},{9,13},{10,... | collective-permute-start | bytes 1179656 | tf_op jit(solution)/shard_map/ppermute | solution.py:30
  (8 other events, 20.1 us)

commit v15 on v14

--- a/solution.py
+++ b/solution.py
@@ -293,11 +293,11 @@
         acc,
         (TWO, 1, their_twos, 0), (TWO_IN, 1, their_twos, 1),
         (THREE, 0, three, 0), (THREE_ACROSS, 0, across, 0),
-        (THREE, 1, their_threes, 0), (THREE_ACROSS, 1, their_threes, 1),
     )
     four = after(four, acc[3])
     hidden, their_four, four = multiply(
         acc,
+        (THREE, 1, their_threes, 0), (THREE_ACROSS, 1, their_threes, 1),
         (FOUR, 0, four, 0), (FOUR, 1, swap(four), 0),
         then=(((FOUR, 1), (FOUR, 0)), (jnp.bfloat16, jnp.float32), down_weight),
     )
@@ -315,7 +315,9 @@
         outs = down(me, kept_jobs, sent_jobs, hidden, down_weight, width)
         cut = len(outs) - whole if whole else len(kept)
         halved = [wide(swap_halves(x)) for x in outs[len(kept) : cut]]
-        return [*outs[: len(kept)], *halved, *(wide(swap(x)) for x in outs[cut:])]
+        if whole:
+            return [*outs[: len(kept)], *halved, *outs[cut:]]
+        return [*outs[: len(kept)], *(wide(swap(x)) for x in outs[len(kept) :])]
 
     four = narrow(four + wide(swap(their_four)))
     got = wide(send(four, ACROSS))
@@ -325,6 +327,7 @@
     )
     three = narrow(three + their_three + jnp.where(end, got, zero))
     got_three = wide(send(three, ALONG))
+    their_two, their_in = (wide(swap(x)) for x in after((their_two, their_in), three))
     across = narrow(across + after(their_across, three))
     got_across = wide(send(across, ACROSS))
     two, two_in, their_one, their_one_in = partials(

time: 113 us -> 114 us (level)
    ppermute x14, waiting for transfers between devices: 21.1 us -> 22.6 us  [send(): return lax.ppermute(x, 'gx', pairs)]
    ppermute x15, waiting for transfers between devices: 5.41 us -> 3.96 us  [swap(): return lax.ppermute(x, 'gx', [(i, i ^ 1) for i in range(4 * LINE)])]
  transfers between devices with their start and end apart: 29 -> 29, of which waited for: 14 -> 14; matrix products, arithmetic and copies ran while one was open for 2% -> 2% of each run, Pallas kernels for 46% -> 42%
where the time goes in v15:
time: 114 us
  Pallas kernels  60.6 us (53%)
  waiting for transfers between devices  26.6 us (23%)
  starting transfers between devices  21.5 us (19%)
  other arithmetic  2.9 us (3%)
  local copies, waits for them, and re-layouts  1.73 us (2%)
    pallas_call x4, Pallas kernels, gate_up(): pl.pallas_call(functools.partial(gate_up_body, count, first, last, rows,...  39.1 us
    ppermute x14, waiting for transfers between devices, send(): return lax.ppermute(x, 'gx', pairs)  22.6 us
    pallas_call x4, Pallas kernels, down(): pl.pallas_call(functools.partial(down_body, len(kept), len(sent)), grid_s...  21.3 us
    ppermute x14, starting transfers between devices, send(): return lax.ppermute(x, 'gx', pairs)  18.8 us
    ppermute x15, waiting for transfers between devices, swap(): return lax.ppermute(x, 'gx', [(i, i ^ 1) for i in range(4 * LINE)])  3.96 us
    ppermute x15, starting transfers between devices, swap(): return lax.ppermute(x, 'gx', [(i, i ^ 1) for i in range(4 * LINE)])  2.77 us
  transfers between devices with their start and end apart: 29, of which 14 were waited for; matrix products, arithmetic and copies ran while one was open for 2% of the time, Pallas kernels for 42%

profile of v15, /device:TPU:0, one launch (start us, length us, event | category | flops | bytes accessed | tf_op | source)
XLA Modules:
  0.0 113.7 jit_solution(7276689983301279573)
XLA Ops:
  1.9 3.0 %collective-permute-start = (bf16[1,400,512]{2,1,0:T(8,128)(2,1)S(1)}, bf16[1,400,512]{2,1,0:T(8,128)(2,1)S(1)}, u32[]{:S(2)}, u32[]{:S(2)}) collective-permute-start(bf16[1,400,512]{2,1,0:T(8,128)(2,1)S(1)} %prepare.1.refs_0_), channel_id=1, source_target_pairs={{0,2},{1,3},{2,0},{3,1},{4,8},{5,9},{6,10},{7,11},{8,4},{9,5},{10,... | collective-permute-start | bytes 1228808 | tf_op jit(solution)/shard_map/ppermute | solution.py:30
  4.9 1.6 %collective-permute-start.2 = (bf16[1,400,512]{2,1,0:T(8,128)(2,1)S(1)}, bf16[1,400,512]{2,1,0:T(8,128)(2,1)S(1)}, u32[]{:S(2)}, u32[]{:S(2)}) collective-permute-start(bf16[1,400,512]{2,1,0:T(8,128)(2,1)S(1)} %prepare.1.refs_0_), channel_id=1, source_target_pairs={{0,4},{1,5},{2,6},{3,7},{4,0},{5,1},{6,2},{7,3},{8,12},{9,13},{10,... | collective-permute-start | bytes 1228808 | tf_op jit(solution)/shard_map/ppermute | solution.py:30
  6.6 7.8 %collective-permute-done.refs_3_ = bf16[1,400,512]{2,1,0:T(8,128)(2,1)S(1)} collective-permute-done((bf16[1,400,512]{2,1,0:T(8,128)(2,1)S(1)}, bf16[1,400,512]{2,1,0:T(8,128)(2,1)S(1)}, u32[]{:S(2)}, u32[]{:S(2)}) %collective-permute-start) | collective-permute-done | bytes 409632 | tf_op jit(solution)/shard_map/ppermute | solution.py:30
  14.4 1.8 %collective-permute-start.1 = (bf16[1,400,512]{2,1,0:T(8,128)(2,1)S(1)}, bf16[1,400,512]{2,1,0:T(8,128)(2,1)S(1)}, u32[]{:S(2)}, u32[]{:S(2)}) collective-permute-start(bf16[1,400,512]{2,1,0:T(8,128)(2,1)S(1)} %collective-permute-done.refs_3_), channel_id=1, source_target_pairs={{0,4},{1,5},{2,6},{3,7},{4,0},{5,1},{6,2},{7,3},{8,12},{9,13},{10,... | collective-permute-start | bytes 1228808 | tf_op jit(solution)/shard_map/ppermute | solution.py:30
  16.2 1.5 %collective-permute-start.3 = (bf16[1,400,512]{2,1,0:T(8,128)(2,1)S(1)}, bf16[1,400,512]{2,1,0:T(8,128)(2,1)S(1)}, u32[]{:S(2)}, u32[]{:S(2)}) collective-permute-start(bf16[1,400,512]{2,1,0:T(8,128)(2,1)S(1)} %collective-permute-done.2.refs_2_), channel_id=1, source_target_pairs={{0,2},{1,3},{2,0},{3,1},{4,8},{5,9},{6,10},{7,11},{8,4},{9,5},{10,... | collective-permute-start | bytes 1228808 | tf_op jit(solution)/shard_map/ppermute | solution.py:30
  17.9 8.8 %gate_up.4 = (f32[384,1536]{1,0:T(8,128)S(1)}, f32[384,1536]{1,0:T(8,128)S(1)}, f32[384,256]{1,0:T(8,128)S(1)}, f32[8,512]{1,0:T(8,128)S(1)}) custom-call(s32[1]{0:T(128)} %bitcast.me_ref, bf16[1,400,512]{2,1,0:T(8,128)(2,1)S(1)} %prepare.1.refs_0_, bf16[1,400,512]{2,1,0:T(8,128)(2,1)S(1)} %collective-permute-done.4.refs_1_, ...), custom_call_target="tpu_custom_call" | custom-call | flops 654311424 | bytes 1703936 | tf_op jit(solution)/shard_map/gate_up/pallas_call | solution.py:184
  27.9 2.1 %collective-permute-start.5 = (bf16[1,400,512]{2,1,0:T(8,128)(2,1)S(1)}, bf16[1,400,512]{2,1,0:T(8,128)(2,1)S(1)}, u32[]{:S(2)}, u32[]{:S(2)}) collective-permute-start(bf16[1,400,512]{2,1,0:T(8,128)(2,1)S(1)} %collective-permute-done.3.refs_3_), channel_id=1, source_target_pairs={{0,4},{1,5},{2,6},{3,7},{4,0},{5,1},{6,2},{7,3},{8,12},{9,13},{10,... | collective-permute-start | bytes 1228808 | tf_op jit(solution)/shard_map/ppermute | solution.py:30
  30.2 8.9 %gate_up.5 = (f32[384,1536]{1,0:T(8,128)S(1)}, f32[384,1536]{1,0:T(8,128)S(1)}, f32[384,256]{1,0:T(8,128)S(1)}, f32[8,512]{1,0:T(8,128)S(1)}) custom-call(s32[1]{0:T(128)} %bitcast.me_ref, bf16[2,400,512]{2,1,0:T(8,128)(2,1)S(1)} %collective-permute-done.7.refs_0_.refs_1_, bf16[2,400,512]{2,1,0:T(8,128)(2,1)S(1)} %collective-permute-done.7.refs_0_.refs_1_, ...), custom_call_target="tpu_custom_call" | custom-call | flops 654311424 | bytes 1703936 | tf_op jit(solution)/shard_map/gate_up/pallas_call | solution.py:184
  40.7 9.1 %gate_up.6 = (f32[384,1536]{1,0:T(8,128)S(1)}, f32[384,1536]{1,0:T(8,128)S(1)}, f32[384,256]{1,0:T(8,128)S(1)}, f32[8,512]{1,0:T(8,128)S(1)}) custom-call(s32[1]{0:T(128)} %bitcast.me_ref, bf16[2,400,512]{2,1,0:T(8,128)(2,1)S(1)} %collective-permute-done.10.refs_0_.refs_1_, bf16[2,400,512]{2,1,0:T(8,128)(2,1)S(1)} %collective-permute-done.10.refs_0_.refs_1_, ...), custom_call_target="tpu_custom_call" | custom-call | flops 654311424 | bytes 1703936 | tf_op jit(solution)/shard_map/gate_up/pallas_call | solution.py:184
  49.8 1.2 %collective-permute-done.9.refs_2_ = bf16[1,400,512]{2,1,0:T(8,128)(2,1)S(1)} collective-permute-done((bf16[1,400,512]{2,1,0:T(8,128)(2,1)S(1)}, bf16[1,400,512]{2,1,0:T(8,128)(2,1)S(1)}, u32[]{:S(2)}, u32[]{:S(2)}) %collective-permute-start.9) | collective-permute-done | bytes 409632 | tf_op jit(solution)/shard_map/ppermute | solution.py:30
  51.1 1.7 %collective-permute-done.11.refs_3_ = bf16[1,400,512]{2,1,0:T(8,128)(2,1)S(1)} collective-permute-done((bf16[1,400,512]{2,1,0:T(8,128)(2,1)S(1)}, bf16[1,400,512]{2,1,0:T(8,128)(2,1)S(1)}, u32[]{:S(2)}, u32[]{:S(2)}) %collective-permute-start.11) | collective-permute-done | bytes 409632 | tf_op jit(solution)/shard_map/ppermute | solution.py:34
  52.8 12.3 %gate_up.7 = (bf16[384,1664]{1,0:T(8,128)(2,1)S(1)}, bf16[384,512]{1,0:T(8,128)(2,1)S(1)}, f32[384,512]{1,0:T(8,128)S(1)}) custom-call(s32[1]{0:T(128)} %bitcast.me_ref, bf16[2,400,512]{2,1,0:T(8,128)(2,1)S(1)} %collective-permute-done.8.refs_0_.refs_1_, bf16[2,400,512]{2,1,0:T(8,128)(2,1)S(1)} %collective-permute-done.8.refs_0_.refs_1_, ...), custom_call_target="tpu_custom_call" | custom-call | flops 654311424 | bytes 1703936 | tf_op jit(solution)/shard_map/gate_up/pallas_call | solution.py:184
  65.3 1.6 %collective-permute-done.12 = bf16[384,512]{1,0:T(8,128)(2,1)S(1)} collective-permute-done((bf16[384,512]{1,0:T(8,128)(2,1)S(1)}, bf16[384,512]{1,0:T(8,128)(2,1)S(1)}, u32[]{:S(2)}, u32[]{:S(2)}) %collective-permute-start.12) | collective-permute-done | bytes 393248 | tf_op jit(solution)/shard_map/ppermute | solution.py:34
  67.6 8.4 %down.4 = (f32[384,512]{1,0:T(8,128)S(1)}, f32[384,512]{1,0:T(8,128)S(1)}, bf16[384,512]{1,0:T(8,128)(2,1)S(1)}, bf16[384,512]{1,0:T(8,128)(2,1)S(1)}, bf16[384,...) custom-call(s32[1]{0:T(128)} %bitcast.me_ref, bf16[384,1664]{1,0:T(8,128)(2,1)S(1)} %get-tuple-element.91.hidden_ref, ...), custom_call_target="tpu_custom_call" | custom-call | flops 490733568 | bytes 1277952 | tf_op jit(solution)/shard_map/down/pallas_call | solution.py:237
  78.5 1.4 %collective-permute-start.20 = (bf16[384,512]{1,0:T(8,128)(2,1)S(1)}, bf16[384,512]{1,0:T(8,128)(2,1)S(1)}, u32[]{:S(2)}, u32[]{:S(2)}) collective-permute-start(bf16[384,512]{1,0:T(8,128)(2,1)S(1)} %fusion.1), channel_id=1, source_target_pairs={{0,4},{1,5},{2,6},{3,7},{4,0},{5,1},{6,2},{7,3},{8,12},{9,13},{10,... | collective-permute-start | bytes 1179656 | tf_op jit(solution)/shard_map/ppermute | solution.py:30
  80.7 1.1 %collective-permute-start.21 = (bf16[384,512]{1,0:T(8,128)(2,1)S(1)}, bf16[384,512]{1,0:T(8,128)(2,1)S(1)}, u32[]{:S(2)}, u32[]{:S(2)}) collective-permute-start(bf16[384,512]{1,0:T(8,128)(2,1)S(1)} %add_convert_fusion.2), channel_id=1, source_target_pairs={{0,2},{1,3},{2,0},{3,1},{4,6},{5,7},{6,4},{7,5},{8,10},{9,11},{10,... | collective-permute-start | bytes 1179656 | tf_op jit(solution)/shard_map/ppermute | solution.py:30
  81.9 5.8 %down.5 = (f32[384,512]{1,0:T(8,128)S(1)}, f32[384,512]{1,0:T(8,128)S(1)}, bf16[384,512]{1,0:T(8,128)(2,1)S(1)}, bf16[384,512]{1,0:T(8,128)(2,1)S(1)}) custom-call(s32[1]{0:T(128)} %bitcast.me_ref, bf16[384,1664]{1,0:T(8,128)(2,1)S(1)} %get-tuple-element.91.hidden_ref, bf16[1664,8192]{1,0:T(8,128)(2,1)} %weight_ref.7), custom_call_target="tpu_custom_call" | custom-call | flops 327155712 | bytes 851968 | tf_op jit(solution)/shard_map/down/pallas_call | solution.py:237
  89.6 1.6 %collective-permute-start.23 = (bf16[384,512]{1,0:T(8,128)(2,1)S(1)}, bf16[384,512]{1,0:T(8,128)(2,1)S(1)}, u32[]{:S(2)}, u32[]{:S(2)}) collective-permute-start(bf16[384,512]{1,0:T(8,128)(2,1)S(1)} %fusion.4), channel_id=1, source_target_pairs={{0,2},{1,3},{2,0},{3,1},{4,8},{5,9},{6,10},{7,11},{8,4},{9,5},{10,... | collective-permute-start | bytes 1179656 | tf_op jit(solution)/shard_map/ppermute | solution.py:30
  92.8 4.8 %down.6 = (f32[384,512]{1,0:T(8,128)S(1)}, f32[384,512]{1,0:T(8,128)S(1)}, bf16[384,512]{1,0:T(8,128)(2,1)S(1)}) custom-call(s32[1]{0:T(128)} %bitcast.me_ref, bf16[384,1664]{1,0:T(8,128)(2,1)S(1)} %get-tuple-element.91.hidden_ref, bf16[1664,8192]{1,0:T(8,128)(2,1)} %weight_ref.7), custom_call_target="tpu_custom_call" | custom-call | flops 245366784 | bytes 638976 | tf_op jit(solution)/shard_map/down/pallas_call | solution.py:237
  97.8 2.5 %collective-permute-done.23 = bf16[384,512]{1,0:T(8,128)(2,1)S(1)} collective-permute-done((bf16[384,512]{1,0:T(8,128)(2,1)S(1)}, bf16[384,512]{1,0:T(8,128)(2,1)S(1)}, u32[]{:S(2)}, u32[]{:S(2)}) %collective-permute-start.23) | collective-permute-done | bytes 393248 | tf_op jit(solution)/shard_map/ppermute | solution.py:30
  100.4 1.9 %collective-permute-done.25 = bf16[384,512]{1,0:T(8,128)(2,1)S(1)} collective-permute-done((bf16[384,512]{1,0:T(8,128)(2,1)S(1)}, bf16[384,512]{1,0:T(8,128)(2,1)S(1)}, u32[]{:S(2)}, u32[]{:S(2)}) %collective-permute-start.25) | collective-permute-done | bytes 393248 | tf_op jit(solution)/shard_map/ppermute | solution.py:30
  104.4 2.3 %down.7 = f32[384,512]{1,0:T(8,128)S(1)} custom-call(s32[1]{0:T(128)} %bitcast.me_ref, bf16[384,1664]{1,0:T(8,128)(2,1)S(1)} %get-tuple-element.91.hidden_ref, bf16[1664,8192]{1,0:T(8,128)(2,1)} %weight_ref.7), custom_call_target="tpu_custom_call" | custom-call | flops 81788928 | bytes 212992 | tf_op jit(solution)/shard_map/down/pallas_call | solution.py:237
  106.7 4.8 %collective-permute-done.28 = bf16[384,512]{1,0:T(8,128)(2,1)S(1)} collective-permute-done((bf16[384,512]{1,0:T(8,128)(2,1)S(1)}, bf16[384,512]{1,0:T(8,128)(2,1)S(1)}, u32[]{:S(2)}, u32[]{:S(2)}) %collective-permute-start.28) | collective-permute-done | bytes 393248 | tf_op jit(solution)/shard_map/ppermute | solution.py:30
  111.6 1.2 %collective-permute-done.27 = bf16[384,512]{1,0:T(8,128)(2,1)S(1)} collective-permute-done((bf16[384,512]{1,0:T(8,128)(2,1)S(1)}, bf16[384,512]{1,0:T(8,128)(2,1)S(1)}, u32[]{:S(2)}, u32[]{:S(2)}) %collective-permute-start.27) | collective-permute-done | bytes 393248 | tf_op jit(solution)/shard_map/ppermute | solution.py:30
  (67 shorter events, 15.9 us)
Async XLA Ops:
  1.9 12.5 %collective-permute-start = (bf16[1,400,512]{2,1,0:T(8,128)(2,1)S(1)}, bf16[1,400,512]{2,1,0:T(8,128)(2,1)S(1)}, u32[]{:S(2)}, u32[]{:S(2)}) collective-permute-start(bf16[1,400,512]{2,1,0:T(8,128)(2,1)S(1)} %prepare.1.refs_0_), channel_id=1, source_target_pairs={{0,2},{1,3},{2,0},{3,1},{4,8},{5,9},{6,10},{7,11},{8,4},{9,5},{10,... | collective-permute-start | bytes 1228808 | tf_op jit(solution)/shard_map/ppermute | solution.py:30
  4.9 11.3 %collective-permute-start.2 = (bf16[1,400,512]{2,1,0:T(8,128)(2,1)S(1)}, bf16[1,400,512]{2,1,0:T(8,128)(2,1)S(1)}, u32[]{:S(2)}, u32[]{:S(2)}) collective-permute-start(bf16[1,400,512]{2,1,0:T(8,128)(2,1)S(1)} %prepare.1.refs_0_), channel_id=1, source_target_pairs={{0,4},{1,5},{2,6},{3,7},{4,0},{5,1},{6,2},{7,3},{8,12},{9,13},{10,... | collective-permute-start | bytes 1228808 | tf_op jit(solution)/shard_map/ppermute | solution.py:30
  6.6 11.3 %collective-permute-start.4 = (bf16[1,400,512]{2,1,0:T(8,128)(2,1)S(1)}, bf16[1,400,512]{2,1,0:T(8,128)(2,1)S(1)}, u32[]{:S(2)}, u32[]{:S(2)}) collective-permute-start(bf16[1,400,512]{2,1,0:T(8,128)(2,1)S(1)} %prepare.1.refs_0_), channel_id=1, source_target_pairs={{0,1},{1,0},{2,3},{3,2},{4,5},{5,4},{6,7},{7,6},{8,9},{9,8},{10,11... | collective-permute-start | bytes 1228808 | tf_op jit(solution)/shard_map/ppermute | solution.py:34
  14.4 12.3 %collective-permute-start.1 = (bf16[1,400,512]{2,1,0:T(8,128)(2,1)S(1)}, bf16[1,400,512]{2,1,0:T(8,128)(2,1)S(1)}, u32[]{:S(2)}, u32[]{:S(2)}) collective-permute-start(bf16[1,400,512]{2,1,0:T(8,128)(2,1)S(1)} %collective-permute-done.refs_3_), channel_id=1, source_target_pairs={{0,4},{1,5},{2,6},{3,7},{4,0},{5,1},{6,2},{7,3},{8,12},{9,13},{10,... | collective-permute-start | bytes 1228808 | tf_op jit(solution)/shard_map/ppermute | solution.py:30
  16.2 10.6 %collective-permute-start.3 = (bf16[1,400,512]{2,1,0:T(8,128)(2,1)S(1)}, bf16[1,400,512]{2,1,0:T(8,128)(2,1)S(1)}, u32[]{:S(2)}, u32[]{:S(2)}) collective-permute-start(bf16[1,400,512]{2,1,0:T(8,128)(2,1)S(1)} %collective-permute-done.2.refs_2_), channel_id=1, source_target_pairs={{0,2},{1,3},{2,0},{3,1},{4,8},{5,9},{6,10},{7,11},{8,4},{9,5},{10,... | collective-permute-start | bytes 1228808 | tf_op jit(solution)/shard_map/ppermute | solution.py:30
  17.8 12.4 %collective-permute-start.7 = (bf16[2,400,512]{2,1,0:T(8,128)(2,1)S(1)}, bf16[2,400,512]{2,1,0:T(8,128)(2,1)S(1)}, u32[]{:S(2)}, u32[]{:S(2)}) collective-permute-start(bf16[2,400,512]{2,1,0:T(8,128)(2,1)S(1)} %pad_maximum_fusion), channel_id=1, source_target_pairs={{0,1},{1,0},{2,3},{3,2},{4,5},{5,4},{6,7},{7,6},{8,9},{9,8},{10,11... | collective-permute-start | bytes 2457608 | tf_op jit(solution)/shard_map/ppermute | solution.py:34
  26.8 12.3 %collective-permute-start.6 = (bf16[1,400,512]{2,1,0:T(8,128)(2,1)S(1)}, bf16[1,400,512]{2,1,0:T(8,128)(2,1)S(1)}, u32[]{:S(2)}, u32[]{:S(2)}) collective-permute-start(bf16[1,400,512]{2,1,0:T(8,128)(2,1)S(1)} %broadcast_select_fusion.1), channel_id=1, source_target_pairs={{0,2},{1,3},{2,0},{3,1},{4,6},{5,7},{6,4},{7,5},{8,10},{9,11},{10,... | collective-permute-start | bytes 1228808 | tf_op jit(solution)/shard_map/ppermute | solution.py:30
  27.9 11.9 %collective-permute-start.5 = (bf16[1,400,512]{2,1,0:T(8,128)(2,1)S(1)}, bf16[1,400,512]{2,1,0:T(8,128)(2,1)S(1)}, u32[]{:S(2)}, u32[]{:S(2)}) collective-permute-start(bf16[1,400,512]{2,1,0:T(8,128)(2,1)S(1)} %collective-permute-done.3.refs_3_), channel_id=1, source_target_pairs={{0,4},{1,5},{2,6},{3,7},{4,0},{5,1},{6,2},{7,3},{8,12},{9,13},{10,... | collective-permute-start | bytes 1228808 | tf_op jit(solution)/shard_map/ppermute | solution.py:30
  30.1 10.6 %collective-permute-start.10 = (bf16[2,400,512]{2,1,0:T(8,128)(2,1)S(1)}, bf16[2,400,512]{2,1,0:T(8,128)(2,1)S(1)}, u32[]{:S(2)}, u32[]{:S(2)}) collective-permute-start(bf16[2,400,512]{2,1,0:T(8,128)(2,1)S(1)} %pad_maximum_fusion.2), channel_id=1, source_target_pairs={{0,1},{1,0},{2,3},{3,2},{4,5},{5,4},{6,7},{7,6},{8,9},{9,8},{10,11... | collective-permute-start | bytes 2457608 | tf_op jit(solution)/shard_map/ppermute | solution.py:34
  39.9 11.2 %collective-permute-start.9 = (bf16[1,400,512]{2,1,0:T(8,128)(2,1)S(1)}, bf16[1,400,512]{2,1,0:T(8,128)(2,1)S(1)}, u32[]{:S(2)}, u32[]{:S(2)}) collective-permute-start(bf16[1,400,512]{2,1,0:T(8,128)(2,1)S(1)} %broadcast_select_fusion), channel_id=1, source_target_pairs={{0,2},{1,3},{2,0},{3,1},{4,6},{5,7},{6,4},{7,5},{8,10},{9,11},{10,... | collective-permute-start | bytes 1228808 | tf_op jit(solution)/shard_map/ppermute | solution.py:30
  40.6 12.2 %collective-permute-start.8 = (bf16[2,400,512]{2,1,0:T(8,128)(2,1)S(1)}, bf16[2,400,512]{2,1,0:T(8,128)(2,1)S(1)}, u32[]{:S(2)}, u32[]{:S(2)}) collective-permute-start(bf16[2,400,512]{2,1,0:T(8,128)(2,1)S(1)} %pad_maximum_fusion.1), channel_id=1, source_target_pairs={{0,1},{1,0},{2,3},{3,2},{4,5},{5,4},{6,7},{7,6},{8,9},{9,8},{10,11... | collective-permute-start | bytes 2457608 | tf_op jit(solution)/shard_map/ppermute | solution.py:34
  67.1 11.2 %collective-permute-start.15 = (bf16[384,512]{1,0:T(8,128)(2,1)S(1)}, bf16[384,512]{1,0:T(8,128)(2,1)S(1)}, u32[]{:S(2)}, u32[]{:S(2)}) collective-permute-start(bf16[384,512]{1,0:T(8,128)(2,1)S(1)} %add_convert_fusion.3), channel_id=1, source_target_pairs={{0,2},{1,3},{2,0},{3,1},{4,6},{5,7},{6,4},{7,5},{8,10},{9,11},{10,... | collective-permute-start | bytes 1179656 | tf_op jit(solution)/shard_map/ppermute | solution.py:30
  76.7 3.2 %collective-permute-start.16 = (bf16[192,512]{1,0:T(8,128)(2,1)S(1)}, bf16[192,512]{1,0:T(8,128)(2,1)S(1)}, u32[]{:S(2)}, u32[]{:S(2)}) collective-permute-start(bf16[192,512]{1,0:T(8,128)(2,1)S(1)} %get-tuple-element.95), channel_id=1, source_target_pairs={{0,1},{1,0},{2,3},{3,2},{4,5},{5,4},{6,7},{7,6},{8,9},{9,8},{10,11... | collective-permute-start | bytes 589832 | tf_op jit(solution)/shard_map/ppermute | solution.py:34
  78.5 10.9 %collective-permute-start.20 = (bf16[384,512]{1,0:T(8,128)(2,1)S(1)}, bf16[384,512]{1,0:T(8,128)(2,1)S(1)}, u32[]{:S(2)}, u32[]{:S(2)}) collective-permute-start(bf16[384,512]{1,0:T(8,128)(2,1)S(1)} %fusion.1), channel_id=1, source_target_pairs={{0,4},{1,5},{2,6},{3,7},{4,0},{5,1},{6,2},{7,3},{8,12},{9,13},{10,... | collective-permute-start | bytes 1179656 | tf_op jit(solution)/shard_map/ppermute | solution.py:30
  79.9 7.9 %collective-permute-start.19 = (bf16[384,512]{1,0:T(8,128)(2,1)S(1)}, bf16[384,512]{1,0:T(8,128)(2,1)S(1)}, u32[]{:S(2)}, u32[]{:S(2)}) collective-permute-start(bf16[384,512]{1,0:T(8,128)(2,1)S(1)} %get-tuple-element.83), channel_id=1, source_target_pairs={{0,1},{1,0},{2,3},{3,2},{4,5},{5,4},{6,7},{7,6},{8,9},{9,8},{10,11... | collective-permute-start | bytes 1179656 | tf_op jit(solution)/shard_map/ppermute | solution.py:34
  80.0 11.2 %collective-permute-start.18 = (bf16[384,512]{1,0:T(8,128)(2,1)S(1)}, bf16[384,512]{1,0:T(8,128)(2,1)S(1)}, u32[]{:S(2)}, u32[]{:S(2)}) collective-permute-start(bf16[384,512]{1,0:T(8,128)(2,1)S(1)} %get-tuple-element.81), channel_id=1, source_target_pairs={{0,1},{1,0},{2,3},{3,2},{4,5},{5,4},{6,7},{7,6},{8,9},{9,8},{10,11... | collective-permute-start | bytes 1179656 | tf_op jit(solution)/shard_map/ppermute | solution.py:34
  80.7 11.5 %collective-permute-start.21 = (bf16[384,512]{1,0:T(8,128)(2,1)S(1)}, bf16[384,512]{1,0:T(8,128)(2,1)S(1)}, u32[]{:S(2)}, u32[]{:S(2)}) collective-permute-start(bf16[384,512]{1,0:T(8,128)(2,1)S(1)} %add_convert_fusion.2), channel_id=1, source_target_pairs={{0,2},{1,3},{2,0},{3,1},{4,6},{5,7},{6,4},{7,5},{8,10},{9,11},{10,... | collective-permute-start | bytes 1179656 | tf_op jit(solution)/shard_map/ppermute | solution.py:30
  87.7 10.0 %collective-permute-start.22 = (bf16[384,512]{1,0:T(8,128)(2,1)S(1)}, bf16[384,512]{1,0:T(8,128)(2,1)S(1)}, u32[]{:S(2)}, u32[]{:S(2)}) collective-permute-start(bf16[384,512]{1,0:T(8,128)(2,1)S(1)} %get-tuple-element.87), channel_id=1, source_target_pairs={{0,1},{1,0},{2,3},{3,2},{4,5},{5,4},{6,7},{7,6},{8,9},{9,8},{10,11... | collective-permute-start | bytes 1179656 | tf_op jit(solution)/shard_map/ppermute | solution.py:34
  87.8 9.8 %collective-permute-start.24 = (bf16[384,512]{1,0:T(8,128)(2,1)S(1)}, bf16[384,512]{1,0:T(8,128)(2,1)S(1)}, u32[]{:S(2)}, u32[]{:S(2)}) collective-permute-start(bf16[384,512]{1,0:T(8,128)(2,1)S(1)} %get-tuple-element.89), channel_id=1, source_target_pairs={{0,1},{1,0},{2,3},{3,2},{4,5},{5,4},{6,7},{7,6},{8,9},{9,8},{10,11... | collective-permute-start | bytes 1179656 | tf_op jit(solution)/shard_map/ppermute | solution.py:34
  89.6 10.7 %collective-permute-start.23 = (bf16[384,512]{1,0:T(8,128)(2,1)S(1)}, bf16[384,512]{1,0:T(8,128)(2,1)S(1)}, u32[]{:S(2)}, u32[]{:S(2)}) collective-permute-start(bf16[384,512]{1,0:T(8,128)(2,1)S(1)} %fusion.4), channel_id=1, source_target_pairs={{0,2},{1,3},{2,0},{3,1},{4,8},{5,9},{6,10},{7,11},{8,4},{9,5},{10,... | collective-permute-start | bytes 1179656 | tf_op jit(solution)/shard_map/ppermute | solution.py:30
  92.4 9.9 %collective-permute-start.25 = (bf16[384,512]{1,0:T(8,128)(2,1)S(1)}, bf16[384,512]{1,0:T(8,128)(2,1)S(1)}, u32[]{:S(2)}, u32[]{:S(2)}) collective-permute-start(bf16[384,512]{1,0:T(8,128)(2,1)S(1)} %fusion.6), channel_id=1, source_target_pairs={{0,4},{1,5},{2,6},{3,7},{4,0},{5,1},{6,2},{7,3},{8,12},{9,13},{10,... | collective-permute-start | bytes 1179656 | tf_op jit(solution)/shard_map/ppermute | solution.py:30
  97.6 9.1 %collective-permute-start.26 = (bf16[384,512]{1,0:T(8,128)(2,1)S(1)}, bf16[384,512]{1,0:T(8,128)(2,1)S(1)}, u32[]{:S(2)}, u32[]{:S(2)}) collective-permute-start(bf16[384,512]{1,0:T(8,128)(2,1)S(1)} %get-tuple-element.92), channel_id=1, source_target_pairs={{0,1},{1,0},{2,3},{3,2},{4,5},{5,4},{6,7},{7,6},{8,9},{9,8},{10,11... | collective-permute-start | bytes 1179656 | tf_op jit(solution)/shard_map/ppermute | solution.py:34
  102.6 9.0 %collective-permute-start.28 = (bf16[384,512]{1,0:T(8,128)(2,1)S(1)}, bf16[384,512]{1,0:T(8,128)(2,1)S(1)}, u32[]{:S(2)}, u32[]{:S(2)}) collective-permute-start(bf16[384,512]{1,0:T(8,128)(2,1)S(1)} %fusion.9), channel_id=1, source_target_pairs={{0,2},{1,3},{2,0},{3,1},{4,8},{5,9},{6,10},{7,11},{8,4},{9,5},{10,... | collective-permute-start | bytes 1179656 | tf_op jit(solution)/shard_map/ppermute | solution.py:30
  103.7 9.0 %collective-permute-start.27 = (bf16[384,512]{1,0:T(8,128)(2,1)S(1)}, bf16[384,512]{1,0:T(8,128)(2,1)S(1)}, u32[]{:S(2)}, u32[]{:S(2)}) collective-permute-start(bf16[384,512]{1,0:T(8,128)(2,1)S(1)} %add_convert_fusion.1), channel_id=1, source_target_pairs={{0,4},{1,5},{2,6},{3,7},{4,0},{5,1},{6,2},{7,3},{8,12},{9,13},{10,... | collective-permute-start | bytes 1179656 | tf_op jit(solution)/shard_map/ppermute | solution.py:30
  (8 other events, 21.7 us)

commit v16 on v15

--- a/solution.py
+++ b/solution.py
@@ -295,11 +295,11 @@
         (THREE, 0, three, 0), (THREE_ACROSS, 0, across, 0),
     )
     four = after(four, acc[3])
-    hidden, their_four, four = multiply(
+    hidden, their_four = multiply(
         acc,
         (THREE, 1, their_threes, 0), (THREE_ACROSS, 1, their_threes, 1),
         (FOUR, 0, four, 0), (FOUR, 1, swap(four), 0),
-        then=(((FOUR, 1), (FOUR, 0)), (jnp.bfloat16, jnp.float32), down_weight),
+        then=(((FOUR, 1),), (jnp.bfloat16,), down_weight),
     )
 
     narrow = lambda x: x.astype(jnp.bfloat16)
@@ -319,11 +319,13 @@
             return [*outs[: len(kept)], *halved, *outs[cut:]]
         return [*outs[: len(kept)], *(wide(swap(x)) for x in outs[len(kept) :])]
 
-    four = narrow(four + wide(swap(their_four)))
+    their_four = wide(swap(their_four))
+    four, their_three = partials(hidden, (FOUR,), (THREE,))
+    four = narrow(four + their_four)
     got = wide(send(four, ACROSS))
     hidden = after(hidden, four)
-    three, across, their_three, their_across, their_two, their_in = partials(
-        hidden, (THREE, THREE_ACROSS), (THREE, THREE_ACROSS, TWO, TWO_IN), whole=2
+    three, across, their_across, their_two, their_in = partials(
+        hidden, (THREE, THREE_ACROSS), (THREE_ACROSS, TWO, TWO_IN), whole=2
     )
     three = narrow(three + their_three + jnp.where(end, got, zero))
     got_three = wide(send(three, ALONG))

time: 114 us -> 115 us (level)
  starting transfers between devices: 21.5 us -> 19.9 us
  Pallas kernels: 60.6 us -> 61.9 us
    ppermute x14, waiting for transfers between devices: 22.6 us -> 25.9 us  [send(): return lax.ppermute(x, 'gx', pairs)]
    pallas_call x4 -> x5, Pallas kernels: 21.3 us -> 23.7 us  [down(): pl.pallas_call(functools.partial(down_body, len(kept), len(sent)), grid_s...]
    ppermute x15 -> x14, waiting for transfers between devices: 3.96 us -> 1.78 us  [swap(): return lax.ppermute(x, 'gx', [(i, i ^ 1) for i in range(4 * LINE)])]
    ppermute x14, starting transfers between devices: 18.8 us -> 17.2 us  [send(): return lax.ppermute(x, 'gx', pairs)]
    ppermute x15 -> x14, starting transfers between devices: 2.77 us -> 2.63 us  [swap(): return lax.ppermute(x, 'gx', [(i, i ^ 1) for i in range(4 * LINE)])]
  transfers between devices with their start and end apart: 29 -> 28, of which waited for: 14 -> 11; matrix products, arithmetic and copies ran while one was open for 2% -> 2% of each run, Pallas kernels for 42% -> 44%
where the time goes in v16:
time: 115 us; the launch traced here: 114 us
  Pallas kernels  61.9 us (54%)
  waiting for transfers between devices  27.7 us (24%)
  starting transfers between devices  19.9 us (17%)
  other arithmetic  2.9 us (3%)
  local copies, waits for them, and re-layouts  1.71 us (1%)
    pallas_call x4, Pallas kernels, gate_up(): pl.pallas_call(functools.partial(gate_up_body, count, first, last, rows,...  38.1 us
    ppermute x14, waiting for transfers between devices, send(): return lax.ppermute(x, 'gx', pairs)  25.9 us
    pallas_call x5, Pallas kernels, down(): pl.pallas_call(functools.partial(down_body, len(kept), len(sent)), grid_s...  23.7 us
    ppermute x14, starting transfers between devices, send(): return lax.ppermute(x, 'gx', pairs)  17.2 us
    ppermute x14, starting transfers between devices, swap(): return lax.ppermute(x, 'gx', [(i, i ^ 1) for i in range(4 * LINE)])  2.63 us
  transfers between devices with their start and end apart: 28, of which 11 were waited for; matrix products, arithmetic and copies ran while one was open for 2% of the time, Pallas kernels for 44%

profile of v16, /device:TPU:0, one launch (start us, length us, event | category | flops | bytes accessed | tf_op | source)
XLA Modules:
  0.0 114.4 jit_solution(6146028416643507488)
XLA Ops:
  1.9 3.0 %collective-permute-start = (bf16[1,400,512]{2,1,0:T(8,128)(2,1)S(1)}, bf16[1,400,512]{2,1,0:T(8,128)(2,1)S(1)}, u32[]{:S(2)}, u32[]{:S(2)}) collective-permute-start(bf16[1,400,512]{2,1,0:T(8,128)(2,1)S(1)} %prepare.1.refs_0_), channel_id=1, source_target_pairs={{0,2},{1,3},{2,0},{3,1},{4,8},{5,9},{6,10},{7,11},{8,4},{9,5},{10,... | collective-permute-start | bytes 1228808 | tf_op jit(solution)/shard_map/ppermute | solution.py:30
  4.9 1.6 %collective-permute-start.2 = (bf16[1,400,512]{2,1,0:T(8,128)(2,1)S(1)}, bf16[1,400,512]{2,1,0:T(8,128)(2,1)S(1)}, u32[]{:S(2)}, u32[]{:S(2)}) collective-permute-start(bf16[1,400,512]{2,1,0:T(8,128)(2,1)S(1)} %prepare.1.refs_0_), channel_id=1, source_target_pairs={{0,4},{1,5},{2,6},{3,7},{4,0},{5,1},{6,2},{7,3},{8,12},{9,13},{10,... | collective-permute-start | bytes 1228808 | tf_op jit(solution)/shard_map/ppermute | solution.py:30
  6.6 7.8 %collective-permute-done.refs_3_ = bf16[1,400,512]{2,1,0:T(8,128)(2,1)S(1)} collective-permute-done((bf16[1,400,512]{2,1,0:T(8,128)(2,1)S(1)}, bf16[1,400,512]{2,1,0:T(8,128)(2,1)S(1)}, u32[]{:S(2)}, u32[]{:S(2)}) %collective-permute-start) | collective-permute-done | bytes 409632 | tf_op jit(solution)/shard_map/ppermute | solution.py:30
  14.4 1.8 %collective-permute-start.1 = (bf16[1,400,512]{2,1,0:T(8,128)(2,1)S(1)}, bf16[1,400,512]{2,1,0:T(8,128)(2,1)S(1)}, u32[]{:S(2)}, u32[]{:S(2)}) collective-permute-start(bf16[1,400,512]{2,1,0:T(8,128)(2,1)S(1)} %collective-permute-done.refs_3_), channel_id=1, source_target_pairs={{0,4},{1,5},{2,6},{3,7},{4,0},{5,1},{6,2},{7,3},{8,12},{9,13},{10,... | collective-permute-start | bytes 1228808 | tf_op jit(solution)/shard_map/ppermute | solution.py:30
  16.2 1.5 %collective-permute-start.3 = (bf16[1,400,512]{2,1,0:T(8,128)(2,1)S(1)}, bf16[1,400,512]{2,1,0:T(8,128)(2,1)S(1)}, u32[]{:S(2)}, u32[]{:S(2)}) collective-permute-start(bf16[1,400,512]{2,1,0:T(8,128)(2,1)S(1)} %collective-permute-done.2.refs_2_), channel_id=1, source_target_pairs={{0,2},{1,3},{2,0},{3,1},{4,8},{5,9},{6,10},{7,11},{8,4},{9,5},{10,... | collective-permute-start | bytes 1228808 | tf_op jit(solution)/shard_map/ppermute | solution.py:30
  17.9 8.8 %gate_up.4 = (f32[384,1536]{1,0:T(8,128)S(1)}, f32[384,1536]{1,0:T(8,128)S(1)}, f32[384,256]{1,0:T(8,128)S(1)}, f32[8,512]{1,0:T(8,128)S(1)}) custom-call(s32[1]{0:T(128)} %bitcast.me_ref, bf16[1,400,512]{2,1,0:T(8,128)(2,1)S(1)} %prepare.1.refs_0_, bf16[1,400,512]{2,1,0:T(8,128)(2,1)S(1)} %collective-permute-done.4.refs_1_, ...), custom_call_target="tpu_custom_call" | custom-call | flops 654311424 | bytes 1703936 | tf_op jit(solution)/shard_map/gate_up/pallas_call | solution.py:184
  26.8 1.1 collective-permute-start.6
  27.9 2.1 %collective-permute-start.5 = (bf16[1,400,512]{2,1,0:T(8,128)(2,1)S(1)}, bf16[1,400,512]{2,1,0:T(8,128)(2,1)S(1)}, u32[]{:S(2)}, u32[]{:S(2)}) collective-permute-start(bf16[1,400,512]{2,1,0:T(8,128)(2,1)S(1)} %collective-permute-done.3.refs_3_), channel_id=1, source_target_pairs={{0,4},{1,5},{2,6},{3,7},{4,0},{5,1},{6,2},{7,3},{8,12},{9,13},{10,... | collective-permute-start | bytes 1228808 | tf_op jit(solution)/shard_map/ppermute | solution.py:30
  30.2 8.9 %gate_up.5 = (f32[384,1536]{1,0:T(8,128)S(1)}, f32[384,1536]{1,0:T(8,128)S(1)}, f32[384,256]{1,0:T(8,128)S(1)}, f32[8,512]{1,0:T(8,128)S(1)}) custom-call(s32[1]{0:T(128)} %bitcast.me_ref, bf16[2,400,512]{2,1,0:T(8,128)(2,1)S(1)} %collective-permute-done.7.refs_0_.refs_1_, bf16[2,400,512]{2,1,0:T(8,128)(2,1)S(1)} %collective-permute-done.7.refs_0_.refs_1_, ...), custom_call_target="tpu_custom_call" | custom-call | flops 654311424 | bytes 1703936 | tf_op jit(solution)/shard_map/gate_up/pallas_call | solution.py:184
  40.7 9.1 %gate_up.6 = (f32[384,1536]{1,0:T(8,128)S(1)}, f32[384,1536]{1,0:T(8,128)S(1)}, f32[384,256]{1,0:T(8,128)S(1)}, f32[8,512]{1,0:T(8,128)S(1)}) custom-call(s32[1]{0:T(128)} %bitcast.me_ref, bf16[2,400,512]{2,1,0:T(8,128)(2,1)S(1)} %collective-permute-done.10.refs_0_.refs_1_, bf16[2,400,512]{2,1,0:T(8,128)(2,1)S(1)} %collective-permute-done.10.refs_0_.refs_1_, ...), custom_call_target="tpu_custom_call" | custom-call | flops 654311424 | bytes 1703936 | tf_op jit(solution)/shard_map/gate_up/pallas_call | solution.py:184
  49.8 1.2 %collective-permute-done.9.refs_2_ = bf16[1,400,512]{2,1,0:T(8,128)(2,1)S(1)} collective-permute-done((bf16[1,400,512]{2,1,0:T(8,128)(2,1)S(1)}, bf16[1,400,512]{2,1,0:T(8,128)(2,1)S(1)}, u32[]{:S(2)}, u32[]{:S(2)}) %collective-permute-start.9) | collective-permute-done | bytes 409632 | tf_op jit(solution)/shard_map/ppermute | solution.py:30
  51.1 1.7 %collective-permute-done.11.refs_3_ = bf16[1,400,512]{2,1,0:T(8,128)(2,1)S(1)} collective-permute-done((bf16[1,400,512]{2,1,0:T(8,128)(2,1)S(1)}, bf16[1,400,512]{2,1,0:T(8,128)(2,1)S(1)}, u32[]{:S(2)}, u32[]{:S(2)}) %collective-permute-start.11) | collective-permute-done | bytes 409632 | tf_op jit(solution)/shard_map/ppermute | solution.py:34
  52.8 11.3 %gate_up.7 = (bf16[384,1664]{1,0:T(8,128)(2,1)S(1)}, bf16[384,512]{1,0:T(8,128)(2,1)S(1)}) custom-call(s32[1]{0:T(128)} %bitcast.me_ref, bf16[2,400,512]{2,1,0:T(8,128)(2,1)S(1)} %collective-permute-done.8.refs_0_.refs_1_, bf16[2,400,512]{2,1,0:T(8,128)(2,1)S(1)} %collective-permute-done.8.refs_0_.refs_1_, ...), custom_call_target="tpu_custom_call" | custom-call | flops 654311424 | bytes 1703936 | tf_op jit(solution)/shard_map/gate_up/pallas_call | solution.py:184
  64.3 3.5 %down.5 = (f32[384,512]{1,0:T(8,128)S(1)}, bf16[384,512]{1,0:T(8,128)(2,1)S(1)}) custom-call(s32[1]{0:T(128)} %bitcast.me_ref, bf16[384,1664]{1,0:T(8,128)(2,1)S(1)} %get-tuple-element.91.hidden_ref, bf16[1664,8192]{1,0:T(8,128)(2,1)} %weight_ref.9), custom_call_target="tpu_custom_call" | custom-call | flops 163577856 | bytes 425984 | tf_op jit(solution)/shard_map/down/pallas_call | solution.py:237
  69.0 7.2 %down.6 = (f32[384,512]{1,0:T(8,128)S(1)}, f32[384,512]{1,0:T(8,128)S(1)}, bf16[384,512]{1,0:T(8,128)(2,1)S(1)}, bf16[384,512]{1,0:T(8,128)(2,1)S(1)}, bf16[384,512]{1,0:T(8,128)(2,1)S(1)}) custom-call(s32[1]{0:T(128)} %bitcast.me_ref, bf16[384,1664]{1,0:T(8,128)(2,1)S(1)} %get-tuple-element.91.hidden_ref, bf16[1664,8192]{1,0:T(8,128)(2,1)} %weight_ref.9), custom_call_target="tpu_custom_call" | custom-call | flops 408944640 | bytes 1064960 | tf_op jit(solution)/shard_map/down/pallas_call | solution.py:237
  76.8 2.8 %collective-permute-done.14 = bf16[384,512]{1,0:T(8,128)(2,1)S(1)} collective-permute-done((bf16[384,512]{1,0:T(8,128)(2,1)S(1)}, bf16[384,512]{1,0:T(8,128)(2,1)S(1)}, u32[]{:S(2)}, u32[]{:S(2)}) %collective-permute-start.14) | collective-permute-done | bytes 393248 | tf_op jit(solution)/shard_map/ppermute | solution.py:30
  79.8 1.4 %collective-permute-start.19 = (bf16[384,512]{1,0:T(8,128)(2,1)S(1)}, bf16[384,512]{1,0:T(8,128)(2,1)S(1)}, u32[]{:S(2)}, u32[]{:S(2)}) collective-permute-start(bf16[384,512]{1,0:T(8,128)(2,1)S(1)} %fusion.1), channel_id=1, source_target_pairs={{0,4},{1,5},{2,6},{3,7},{4,0},{5,1},{6,2},{7,3},{8,12},{9,13},{10,... | collective-permute-start | bytes 1179656 | tf_op jit(solution)/shard_map/ppermute | solution.py:30
  82.9 5.8 %down.7 = (f32[384,512]{1,0:T(8,128)S(1)}, f32[384,512]{1,0:T(8,128)S(1)}, bf16[384,512]{1,0:T(8,128)(2,1)S(1)}, bf16[384,512]{1,0:T(8,128)(2,1)S(1)}) custom-call(s32[1]{0:T(128)} %bitcast.me_ref, bf16[384,1664]{1,0:T(8,128)(2,1)S(1)} %get-tuple-element.91.hidden_ref, bf16[1664,8192]{1,0:T(8,128)(2,1)} %weight_ref.9), custom_call_target="tpu_custom_call" | custom-call | flops 327155712 | bytes 851968 | tf_op jit(solution)/shard_map/down/pallas_call | solution.py:237
  91.1 2.8 %collective-permute-done.20 = bf16[384,512]{1,0:T(8,128)(2,1)S(1)} collective-permute-done((bf16[384,512]{1,0:T(8,128)(2,1)S(1)}, bf16[384,512]{1,0:T(8,128)(2,1)S(1)}, u32[]{:S(2)}, u32[]{:S(2)}) %collective-permute-start.20) | collective-permute-done | bytes 393248 | tf_op jit(solution)/shard_map/ppermute | solution.py:30
  94.2 4.8 %down.8 = (f32[384,512]{1,0:T(8,128)S(1)}, f32[384,512]{1,0:T(8,128)S(1)}, bf16[384,512]{1,0:T(8,128)(2,1)S(1)}) custom-call(s32[1]{0:T(128)} %bitcast.me_ref, bf16[384,1664]{1,0:T(8,128)(2,1)S(1)} %get-tuple-element.91.hidden_ref, bf16[1664,8192]{1,0:T(8,128)(2,1)} %weight_ref.9), custom_call_target="tpu_custom_call" | custom-call | flops 245366784 | bytes 638976 | tf_op jit(solution)/shard_map/down/pallas_call | solution.py:237
  99.2 2.4 %collective-permute-done.22 = bf16[384,512]{1,0:T(8,128)(2,1)S(1)} collective-permute-done((bf16[384,512]{1,0:T(8,128)(2,1)S(1)}, bf16[384,512]{1,0:T(8,128)(2,1)S(1)}, u32[]{:S(2)}, u32[]{:S(2)}) %collective-permute-start.22) | collective-permute-done | bytes 393248 | tf_op jit(solution)/shard_map/ppermute | solution.py:30
  101.8 1.9 %collective-permute-done.24 = bf16[384,512]{1,0:T(8,128)(2,1)S(1)} collective-permute-done((bf16[384,512]{1,0:T(8,128)(2,1)S(1)}, bf16[384,512]{1,0:T(8,128)(2,1)S(1)}, u32[]{:S(2)}, u32[]{:S(2)}) %collective-permute-start.24) | collective-permute-done | bytes 393248 | tf_op jit(solution)/shard_map/ppermute | solution.py:30
  105.7 2.3 %down.9 = f32[384,512]{1,0:T(8,128)S(1)} custom-call(s32[1]{0:T(128)} %bitcast.me_ref, bf16[384,1664]{1,0:T(8,128)(2,1)S(1)} %get-tuple-element.91.hidden_ref, bf16[1664,8192]{1,0:T(8,128)(2,1)} %weight_ref.9), custom_call_target="tpu_custom_call" | custom-call | flops 81788928 | bytes 212992 | tf_op jit(solution)/shard_map/down/pallas_call | solution.py:237
  108.0 4.4 %collective-permute-done.27 = bf16[384,512]{1,0:T(8,128)(2,1)S(1)} collective-permute-done((bf16[384,512]{1,0:T(8,128)(2,1)S(1)}, bf16[384,512]{1,0:T(8,128)(2,1)S(1)}, u32[]{:S(2)}, u32[]{:S(2)}) %collective-permute-start.27) | collective-permute-done | bytes 393248 | tf_op jit(solution)/shard_map/ppermute | solution.py:30
  (65 shorter events, 14.7 us)
Async XLA Ops:
  1.9 12.5 %collective-permute-start = (bf16[1,400,512]{2,1,0:T(8,128)(2,1)S(1)}, bf16[1,400,512]{2,1,0:T(8,128)(2,1)S(1)}, u32[]{:S(2)}, u32[]{:S(2)}) collective-permute-start(bf16[1,400,512]{2,1,0:T(8,128)(2,1)S(1)} %prepare.1.refs_0_), channel_id=1, source_target_pairs={{0,2},{1,3},{2,0},{3,1},{4,8},{5,9},{6,10},{7,11},{8,4},{9,5},{10,... | collective-permute-start | bytes 1228808 | tf_op jit(solution)/shard_map/ppermute | solution.py:30
  4.9 11.3 %collective-permute-start.2 = (bf16[1,400,512]{2,1,0:T(8,128)(2,1)S(1)}, bf16[1,400,512]{2,1,0:T(8,128)(2,1)S(1)}, u32[]{:S(2)}, u32[]{:S(2)}) collective-permute-start(bf16[1,400,512]{2,1,0:T(8,128)(2,1)S(1)} %prepare.1.refs_0_), channel_id=1, source_target_pairs={{0,4},{1,5},{2,6},{3,7},{4,0},{5,1},{6,2},{7,3},{8,12},{9,13},{10,... | collective-permute-start | bytes 1228808 | tf_op jit(solution)/shard_map/ppermute | solution.py:30
  6.6 11.3 %collective-permute-start.4 = (bf16[1,400,512]{2,1,0:T(8,128)(2,1)S(1)}, bf16[1,400,512]{2,1,0:T(8,128)(2,1)S(1)}, u32[]{:S(2)}, u32[]{:S(2)}) collective-permute-start(bf16[1,400,512]{2,1,0:T(8,128)(2,1)S(1)} %prepare.1.refs_0_), channel_id=1, source_target_pairs={{0,1},{1,0},{2,3},{3,2},{4,5},{5,4},{6,7},{7,6},{8,9},{9,8},{10,11... | collective-permute-start | bytes 1228808 | tf_op jit(solution)/shard_map/ppermute | solution.py:34
  14.4 12.3 %collective-permute-start.1 = (bf16[1,400,512]{2,1,0:T(8,128)(2,1)S(1)}, bf16[1,400,512]{2,1,0:T(8,128)(2,1)S(1)}, u32[]{:S(2)}, u32[]{:S(2)}) collective-permute-start(bf16[1,400,512]{2,1,0:T(8,128)(2,1)S(1)} %collective-permute-done.refs_3_), channel_id=1, source_target_pairs={{0,4},{1,5},{2,6},{3,7},{4,0},{5,1},{6,2},{7,3},{8,12},{9,13},{10,... | collective-permute-start | bytes 1228808 | tf_op jit(solution)/shard_map/ppermute | solution.py:30
  16.2 10.6 %collective-permute-start.3 = (bf16[1,400,512]{2,1,0:T(8,128)(2,1)S(1)}, bf16[1,400,512]{2,1,0:T(8,128)(2,1)S(1)}, u32[]{:S(2)}, u32[]{:S(2)}) collective-permute-start(bf16[1,400,512]{2,1,0:T(8,128)(2,1)S(1)} %collective-permute-done.2.refs_2_), channel_id=1, source_target_pairs={{0,2},{1,3},{2,0},{3,1},{4,8},{5,9},{6,10},{7,11},{8,4},{9,5},{10,... | collective-permute-start | bytes 1228808 | tf_op jit(solution)/shard_map/ppermute | solution.py:30
  17.8 12.4 %collective-permute-start.7 = (bf16[2,400,512]{2,1,0:T(8,128)(2,1)S(1)}, bf16[2,400,512]{2,1,0:T(8,128)(2,1)S(1)}, u32[]{:S(2)}, u32[]{:S(2)}) collective-permute-start(bf16[2,400,512]{2,1,0:T(8,128)(2,1)S(1)} %pad_maximum_fusion), channel_id=1, source_target_pairs={{0,1},{1,0},{2,3},{3,2},{4,5},{5,4},{6,7},{7,6},{8,9},{9,8},{10,11... | collective-permute-start | bytes 2457608 | tf_op jit(solution)/shard_map/ppermute | solution.py:34
  26.8 12.3 %collective-permute-start.6 = (bf16[1,400,512]{2,1,0:T(8,128)(2,1)S(1)}, bf16[1,400,512]{2,1,0:T(8,128)(2,1)S(1)}, u32[]{:S(2)}, u32[]{:S(2)}) collective-permute-start(bf16[1,400,512]{2,1,0:T(8,128)(2,1)S(1)} %broadcast_select_fusion.1), channel_id=1, source_target_pairs={{0,2},{1,3},{2,0},{3,1},{4,6},{5,7},{6,4},{7,5},{8,10},{9,11},{10,... | collective-permute-start | bytes 1228808 | tf_op jit(solution)/shard_map/ppermute | solution.py:30
  27.9 11.9 %collective-permute-start.5 = (bf16[1,400,512]{2,1,0:T(8,128)(2,1)S(1)}, bf16[1,400,512]{2,1,0:T(8,128)(2,1)S(1)}, u32[]{:S(2)}, u32[]{:S(2)}) collective-permute-start(bf16[1,400,512]{2,1,0:T(8,128)(2,1)S(1)} %collective-permute-done.3.refs_3_), channel_id=1, source_target_pairs={{0,4},{1,5},{2,6},{3,7},{4,0},{5,1},{6,2},{7,3},{8,12},{9,13},{10,... | collective-permute-start | bytes 1228808 | tf_op jit(solution)/shard_map/ppermute | solution.py:30
  30.1 10.6 %collective-permute-start.10 = (bf16[2,400,512]{2,1,0:T(8,128)(2,1)S(1)}, bf16[2,400,512]{2,1,0:T(8,128)(2,1)S(1)}, u32[]{:S(2)}, u32[]{:S(2)}) collective-permute-start(bf16[2,400,512]{2,1,0:T(8,128)(2,1)S(1)} %pad_maximum_fusion.2), channel_id=1, source_target_pairs={{0,1},{1,0},{2,3},{3,2},{4,5},{5,4},{6,7},{7,6},{8,9},{9,8},{10,11... | collective-permute-start | bytes 2457608 | tf_op jit(solution)/shard_map/ppermute | solution.py:34
  39.9 11.2 %collective-permute-start.9 = (bf16[1,400,512]{2,1,0:T(8,128)(2,1)S(1)}, bf16[1,400,512]{2,1,0:T(8,128)(2,1)S(1)}, u32[]{:S(2)}, u32[]{:S(2)}) collective-permute-start(bf16[1,400,512]{2,1,0:T(8,128)(2,1)S(1)} %broadcast_select_fusion), channel_id=1, source_target_pairs={{0,2},{1,3},{2,0},{3,1},{4,6},{5,7},{6,4},{7,5},{8,10},{9,11},{10,... | collective-permute-start | bytes 1228808 | tf_op jit(solution)/shard_map/ppermute | solution.py:30
  40.6 12.2 %collective-permute-start.8 = (bf16[2,400,512]{2,1,0:T(8,128)(2,1)S(1)}, bf16[2,400,512]{2,1,0:T(8,128)(2,1)S(1)}, u32[]{:S(2)}, u32[]{:S(2)}) collective-permute-start(bf16[2,400,512]{2,1,0:T(8,128)(2,1)S(1)} %pad_maximum_fusion.1), channel_id=1, source_target_pairs={{0,1},{1,0},{2,3},{3,2},{4,5},{5,4},{6,7},{7,6},{8,9},{9,8},{10,11... | collective-permute-start | bytes 2457608 | tf_op jit(solution)/shard_map/ppermute | solution.py:34
  67.8 9.0 %collective-permute-start.13 = (bf16[384,512]{1,0:T(8,128)(2,1)S(1)}, bf16[384,512]{1,0:T(8,128)(2,1)S(1)}, u32[]{:S(2)}, u32[]{:S(2)}) collective-permute-start(bf16[384,512]{1,0:T(8,128)(2,1)S(1)} %get-tuple-element.73), channel_id=1, source_target_pairs={{0,1},{1,0},{2,3},{3,2},{4,5},{5,4},{6,7},{7,6},{8,9},{9,8},{10,11... | collective-permute-start | bytes 1179656 | tf_op jit(solution)/shard_map/ppermute | solution.py:34
  68.4 11.2 %collective-permute-start.14 = (bf16[384,512]{1,0:T(8,128)(2,1)S(1)}, bf16[384,512]{1,0:T(8,128)(2,1)S(1)}, u32[]{:S(2)}, u32[]{:S(2)}) collective-permute-start(bf16[384,512]{1,0:T(8,128)(2,1)S(1)} %add_convert_fusion.3), channel_id=1, source_target_pairs={{0,2},{1,3},{2,0},{3,1},{4,6},{5,7},{6,4},{7,5},{8,10},{9,11},{10,... | collective-permute-start | bytes 1179656 | tf_op jit(solution)/shard_map/ppermute | solution.py:30
  79.8 10.4 %collective-permute-start.19 = (bf16[384,512]{1,0:T(8,128)(2,1)S(1)}, bf16[384,512]{1,0:T(8,128)(2,1)S(1)}, u32[]{:S(2)}, u32[]{:S(2)}) collective-permute-start(bf16[384,512]{1,0:T(8,128)(2,1)S(1)} %fusion.1), channel_id=1, source_target_pairs={{0,4},{1,5},{2,6},{3,7},{4,0},{5,1},{6,2},{7,3},{8,12},{9,13},{10,... | collective-permute-start | bytes 1179656 | tf_op jit(solution)/shard_map/ppermute | solution.py:30
  81.2 7.6 %collective-permute-start.18 = (bf16[384,512]{1,0:T(8,128)(2,1)S(1)}, bf16[384,512]{1,0:T(8,128)(2,1)S(1)}, u32[]{:S(2)}, u32[]{:S(2)}) collective-permute-start(bf16[384,512]{1,0:T(8,128)(2,1)S(1)} %get-tuple-element.83), channel_id=1, source_target_pairs={{0,1},{1,0},{2,3},{3,2},{4,5},{5,4},{6,7},{7,6},{8,9},{9,8},{10,11... | collective-permute-start | bytes 1179656 | tf_op jit(solution)/shard_map/ppermute | solution.py:34
  81.3 9.7 %collective-permute-start.17 = (bf16[384,512]{1,0:T(8,128)(2,1)S(1)}, bf16[384,512]{1,0:T(8,128)(2,1)S(1)}, u32[]{:S(2)}, u32[]{:S(2)}) collective-permute-start(bf16[384,512]{1,0:T(8,128)(2,1)S(1)} %get-tuple-element.81), channel_id=1, source_target_pairs={{0,1},{1,0},{2,3},{3,2},{4,5},{5,4},{6,7},{7,6},{8,9},{9,8},{10,11... | collective-permute-start | bytes 1179656 | tf_op jit(solution)/shard_map/ppermute | solution.py:34
  82.1 11.9 %collective-permute-start.20 = (bf16[384,512]{1,0:T(8,128)(2,1)S(1)}, bf16[384,512]{1,0:T(8,128)(2,1)S(1)}, u32[]{:S(2)}, u32[]{:S(2)}) collective-permute-start(bf16[384,512]{1,0:T(8,128)(2,1)S(1)} %add_convert_fusion.2), channel_id=1, source_target_pairs={{0,2},{1,3},{2,0},{3,1},{4,6},{5,7},{6,4},{7,5},{8,10},{9,11},{10,... | collective-permute-start | bytes 1179656 | tf_op jit(solution)/shard_map/ppermute | solution.py:30
  88.8 10.5 %collective-permute-start.21 = (bf16[384,512]{1,0:T(8,128)(2,1)S(1)}, bf16[384,512]{1,0:T(8,128)(2,1)S(1)}, u32[]{:S(2)}, u32[]{:S(2)}) collective-permute-start(bf16[384,512]{1,0:T(8,128)(2,1)S(1)} %get-tuple-element.87), channel_id=1, source_target_pairs={{0,1},{1,0},{2,3},{3,2},{4,5},{5,4},{6,7},{7,6},{8,9},{9,8},{10,11... | collective-permute-start | bytes 1179656 | tf_op jit(solution)/shard_map/ppermute | solution.py:34
  88.8 10.3 %collective-permute-start.23 = (bf16[384,512]{1,0:T(8,128)(2,1)S(1)}, bf16[384,512]{1,0:T(8,128)(2,1)S(1)}, u32[]{:S(2)}, u32[]{:S(2)}) collective-permute-start(bf16[384,512]{1,0:T(8,128)(2,1)S(1)} %get-tuple-element.89), channel_id=1, source_target_pairs={{0,1},{1,0},{2,3},{3,2},{4,5},{5,4},{6,7},{7,6},{8,9},{9,8},{10,11... | collective-permute-start | bytes 1179656 | tf_op jit(solution)/shard_map/ppermute | solution.py:34
  90.4 11.2 %collective-permute-start.22 = (bf16[384,512]{1,0:T(8,128)(2,1)S(1)}, bf16[384,512]{1,0:T(8,128)(2,1)S(1)}, u32[]{:S(2)}, u32[]{:S(2)}) collective-permute-start(bf16[384,512]{1,0:T(8,128)(2,1)S(1)} %fusion.4), channel_id=1, source_target_pairs={{0,2},{1,3},{2,0},{3,1},{4,8},{5,9},{6,10},{7,11},{8,4},{9,5},{10,... | collective-permute-start | bytes 1179656 | tf_op jit(solution)/shard_map/ppermute | solution.py:30
  94.2 9.5 %collective-permute-start.24 = (bf16[384,512]{1,0:T(8,128)(2,1)S(1)}, bf16[384,512]{1,0:T(8,128)(2,1)S(1)}, u32[]{:S(2)}, u32[]{:S(2)}) collective-permute-start(bf16[384,512]{1,0:T(8,128)(2,1)S(1)} %fusion.6), channel_id=1, source_target_pairs={{0,4},{1,5},{2,6},{3,7},{4,0},{5,1},{6,2},{7,3},{8,12},{9,13},{10,... | collective-permute-start | bytes 1179656 | tf_op jit(solution)/shard_map/ppermute | solution.py:30
  99.0 9.0 %collective-permute-start.25 = (bf16[384,512]{1,0:T(8,128)(2,1)S(1)}, bf16[384,512]{1,0:T(8,128)(2,1)S(1)}, u32[]{:S(2)}, u32[]{:S(2)}) collective-permute-start(bf16[384,512]{1,0:T(8,128)(2,1)S(1)} %get-tuple-element.92), channel_id=1, source_target_pairs={{0,1},{1,0},{2,3},{3,2},{4,5},{5,4},{6,7},{7,6},{8,9},{9,8},{10,11... | collective-permute-start | bytes 1179656 | tf_op jit(solution)/shard_map/ppermute | solution.py:34
  103.9 8.6 %collective-permute-start.27 = (bf16[384,512]{1,0:T(8,128)(2,1)S(1)}, bf16[384,512]{1,0:T(8,128)(2,1)S(1)}, u32[]{:S(2)}, u32[]{:S(2)}) collective-permute-start(bf16[384,512]{1,0:T(8,128)(2,1)S(1)} %fusion.9), channel_id=1, source_target_pairs={{0,2},{1,3},{2,0},{3,1},{4,8},{5,9},{6,10},{7,11},{8,4},{9,5},{10,... | collective-permute-start | bytes 1179656 | tf_op jit(solution)/shard_map/ppermute | solution.py:30
  104.7 8.7 %collective-permute-start.26 = (bf16[384,512]{1,0:T(8,128)(2,1)S(1)}, bf16[384,512]{1,0:T(8,128)(2,1)S(1)}, u32[]{:S(2)}, u32[]{:S(2)}) collective-permute-start(bf16[384,512]{1,0:T(8,128)(2,1)S(1)} %add_convert_fusion.1), channel_id=1, source_target_pairs={{0,4},{1,5},{2,6},{3,7},{4,0},{5,1},{6,2},{7,3},{8,12},{9,13},{10,... | collective-permute-start | bytes 1179656 | tf_op jit(solution)/shard_map/ppermute | solution.py:30
  (7 other events, 27.1 us)

commit v17 on v15

--- a/solution.py
+++ b/solution.py
@@ -293,11 +293,11 @@
         acc,
         (TWO, 1, their_twos, 0), (TWO_IN, 1, their_twos, 1),
         (THREE, 0, three, 0), (THREE_ACROSS, 0, across, 0),
+        (THREE, 1, their_threes, 0), (THREE_ACROSS, 1, their_threes, 1),
     )
     four = after(four, acc[3])
     hidden, their_four, four = multiply(
         acc,
-        (THREE, 1, their_threes, 0), (THREE_ACROSS, 1, their_threes, 1),
         (FOUR, 0, four, 0), (FOUR, 1, swap(four), 0),
         then=(((FOUR, 1), (FOUR, 0)), (jnp.bfloat16, jnp.float32), down_weight),
     )

time: 114 us -> 114 us (level)
    ppermute x14, waiting for transfers between devices: 22.6 us -> 20.4 us  [send(): return lax.ppermute(x, 'gx', pairs)]
    ppermute x15, waiting for transfers between devices: 3.96 us -> 5.55 us  [swap(): return lax.ppermute(x, 'gx', [(i, i ^ 1) for i in range(4 * LINE)])]
  transfers between devices with their start and end apart: 29 -> 29, of which waited for: 14 -> 14; matrix products, arithmetic and copies ran while one was open for 2% -> 2% of each run, Pallas kernels for 42% -> 46%
where the time goes in v17:
time: 114 us; the launch traced here: 113 us
  Pallas kernels  60.4 us (53%)
  waiting for transfers between devices  25.9 us (23%)
  starting transfers between devices  21.9 us (19%)
  other arithmetic  2.92 us (3%)
  local copies, waits for them, and re-layouts  1.73 us (2%)
    pallas_call x4, Pallas kernels, gate_up(): pl.pallas_call(functools.partial(gate_up_body, count, first, last, rows,...  38.9 us
    pallas_call x4, Pallas kernels, down(): pl.pallas_call(functools.partial(down_body, len(kept), len(sent)), grid_s...  21.3 us
    ppermute x14, waiting for transfers between devices, send(): return lax.ppermute(x, 'gx', pairs)  20.4 us
    ppermute x14, starting transfers between devices, send(): return lax.ppermute(x, 'gx', pairs)  19 us
    ppermute x15, waiting for transfers between devices, swap(): return lax.ppermute(x, 'gx', [(i, i ^ 1) for i in range(4 * LINE)])  5.55 us
    ppermute x15, starting transfers between devices, swap(): return lax.ppermute(x, 'gx', [(i, i ^ 1) for i in range(4 * LINE)])  2.95 us
  transfers between devices with their start and end apart: 29, of which 14 were waited for; matrix products, arithmetic and copies ran while one was open for 2% of the time, Pallas kernels for 46%

profile of v17, /device:TPU:0, one launch (start us, length us, event | category | flops | bytes accessed | tf_op | source)
XLA Modules:
  0.0 113.2 jit_solution(15512626096859232083)
XLA Ops:
  1.9 3.1 %collective-permute-start.2 = (bf16[1,400,512]{2,1,0:T(8,128)(2,1)S(1)}, bf16[1,400,512]{2,1,0:T(8,128)(2,1)S(1)}, u32[]{:S(2)}, u32[]{:S(2)}) collective-permute-start(bf16[1,400,512]{2,1,0:T(8,128)(2,1)S(1)} %prepare.1.refs_0_), channel_id=1, source_target_pairs={{0,4},{1,5},{2,6},{3,7},{4,0},{5,1},{6,2},{7,3},{8,12},{9,13},{10,... | collective-permute-start | bytes 1228808 | tf_op jit(solution)/shard_map/ppermute | solution.py:30
  5.0 1.5 %collective-permute-start = (bf16[1,400,512]{2,1,0:T(8,128)(2,1)S(1)}, bf16[1,400,512]{2,1,0:T(8,128)(2,1)S(1)}, u32[]{:S(2)}, u32[]{:S(2)}) collective-permute-start(bf16[1,400,512]{2,1,0:T(8,128)(2,1)S(1)} %prepare.1.refs_0_), channel_id=1, source_target_pairs={{0,2},{1,3},{2,0},{3,1},{4,8},{5,9},{6,10},{7,11},{8,4},{9,5},{10,... | collective-permute-start | bytes 1228808 | tf_op jit(solution)/shard_map/ppermute | solution.py:30
  6.5 7.9 %collective-permute-done.2.refs_2_ = bf16[1,400,512]{2,1,0:T(8,128)(2,1)S(1)} collective-permute-done((bf16[1,400,512]{2,1,0:T(8,128)(2,1)S(1)}, bf16[1,400,512]{2,1,0:T(8,128)(2,1)S(1)}, u32[]{:S(2)}, u32[]{:S(2)}) %collective-permute-start.2) | collective-permute-done | bytes 409632 | tf_op jit(solution)/shard_map/ppermute | solution.py:30
  14.5 1.7 %collective-permute-start.3 = (bf16[1,400,512]{2,1,0:T(8,128)(2,1)S(1)}, bf16[1,400,512]{2,1,0:T(8,128)(2,1)S(1)}, u32[]{:S(2)}, u32[]{:S(2)}) collective-permute-start(bf16[1,400,512]{2,1,0:T(8,128)(2,1)S(1)} %collective-permute-done.2.refs_2_), channel_id=1, source_target_pairs={{0,2},{1,3},{2,0},{3,1},{4,8},{5,9},{6,10},{7,11},{8,4},{9,5},{10,... | collective-permute-start | bytes 1228808 | tf_op jit(solution)/shard_map/ppermute | solution.py:30
  16.1 1.6 %collective-permute-start.1 = (bf16[1,400,512]{2,1,0:T(8,128)(2,1)S(1)}, bf16[1,400,512]{2,1,0:T(8,128)(2,1)S(1)}, u32[]{:S(2)}, u32[]{:S(2)}) collective-permute-start(bf16[1,400,512]{2,1,0:T(8,128)(2,1)S(1)} %collective-permute-done.refs_3_), channel_id=1, source_target_pairs={{0,4},{1,5},{2,6},{3,7},{4,0},{5,1},{6,2},{7,3},{8,12},{9,13},{10,... | collective-permute-start | bytes 1228808 | tf_op jit(solution)/shard_map/ppermute | solution.py:30
  18.0 8.8 %gate_up.4 = (f32[384,1536]{1,0:T(8,128)S(1)}, f32[384,1536]{1,0:T(8,128)S(1)}, f32[384,256]{1,0:T(8,128)S(1)}, f32[8,512]{1,0:T(8,128)S(1)}) custom-call(s32[1]{0:T(128)} %bitcast.me_ref, bf16[1,400,512]{2,1,0:T(8,128)(2,1)S(1)} %prepare.1.refs_0_, bf16[1,400,512]{2,1,0:T(8,128)(2,1)S(1)} %collective-permute-done.4.refs_1_, ...), custom_call_target="tpu_custom_call" | custom-call | flops 654311424 | bytes 1703936 | tf_op jit(solution)/shard_map/gate_up/pallas_call | solution.py:184
  26.9 1.6 %collective-permute-start.6 = (bf16[1,400,512]{2,1,0:T(8,128)(2,1)S(1)}, bf16[1,400,512]{2,1,0:T(8,128)(2,1)S(1)}, u32[]{:S(2)}, u32[]{:S(2)}) collective-permute-start(bf16[1,400,512]{2,1,0:T(8,128)(2,1)S(1)} %broadcast_select_fusion.1), channel_id=1, source_target_pairs={{0,2},{1,3},{2,0},{3,1},{4,6},{5,7},{6,4},{7,5},{8,10},{9,11},{10,... | collective-permute-start | bytes 1228808 | tf_op jit(solution)/shard_map/ppermute | solution.py:30
  29.6 8.9 %gate_up.5 = (f32[384,1536]{1,0:T(8,128)S(1)}, f32[384,1536]{1,0:T(8,128)S(1)}, f32[384,256]{1,0:T(8,128)S(1)}, f32[8,512]{1,0:T(8,128)S(1)}) custom-call(s32[1]{0:T(128)} %bitcast.me_ref, bf16[2,400,512]{2,1,0:T(8,128)(2,1)S(1)} %collective-permute-done.7.refs_0_.refs_1_, bf16[2,400,512]{2,1,0:T(8,128)(2,1)S(1)} %collective-permute-done.7.refs_0_.refs_1_, ...), custom_call_target="tpu_custom_call" | custom-call | flops 654311424 | bytes 1703936 | tf_op jit(solution)/shard_map/gate_up/pallas_call | solution.py:184
  40.8 1.7 %collective-permute-done.10.refs_4_.refs_5_ = bf16[2,400,512]{2,1,0:T(8,128)(2,1)S(1)} collective-permute-done((bf16[2,400,512]{2,1,0:T(8,128)(2,1)S(1)}, bf16[2,400,512]{2,1,0:T(8,128)(2,1)S(1)}, u32[]{:S(2)}, u32[]{:S(2)}) %collective-permute-start.10) | collective-permute-done | bytes 819232 | tf_op jit(solution)/shard_map/ppermute | solution.py:34
  42.5 12.5 %gate_up.6 = (f32[384,1536]{1,0:T(8,128)S(1)}, f32[384,1536]{1,0:T(8,128)S(1)}, f32[384,256]{1,0:T(8,128)S(1)}, f32[8,512]{1,0:T(8,128)S(1)}) custom-call(s32[1]{0:T(128)} %bitcast.me_ref, bf16[2,400,512]{2,1,0:T(8,128)(2,1)S(1)} %collective-permute-done.9.refs_0_.refs_1_, bf16[2,400,512]{2,1,0:T(8,128)(2,1)S(1)} %collective-permute-done.9.refs_0_.refs_1_, ...), custom_call_target="tpu_custom_call" | custom-call | flops 981467136 | bytes 2555904 | tf_op jit(solution)/shard_map/gate_up/pallas_call | solution.py:184
  55.2 1.6 %collective-permute-done.11.refs_1_ = bf16[1,400,512]{2,1,0:T(8,128)(2,1)S(1)} collective-permute-done((bf16[1,400,512]{2,1,0:T(8,128)(2,1)S(1)}, bf16[1,400,512]{2,1,0:T(8,128)(2,1)S(1)}, u32[]{:S(2)}, u32[]{:S(2)}) %collective-permute-start.11) | collective-permute-done | bytes 409632 | tf_op jit(solution)/shard_map/ppermute | solution.py:34
  56.9 8.6 %gate_up.7 = (bf16[384,1664]{1,0:T(8,128)(2,1)S(1)}, bf16[384,512]{1,0:T(8,128)(2,1)S(1)}, f32[384,512]{1,0:T(8,128)S(1)}) custom-call(s32[1]{0:T(128)} %bitcast.me_ref, bf16[1,400,512]{2,1,0:T(8,128)(2,1)S(1)} %collective-permute-done.8.refs_0_, bf16[1,400,512]{2,1,0:T(8,128)(2,1)S(1)} %collective-permute-done.11.refs_1_, bf16[8192,1664]{1,0:T(8,128)(2,1)} %refs_2_.1, ...), custom_call_target="tpu_custom_call" | custom-call | flops 327155712 | bytes 851968 | tf_op jit(solution)/shard_map/gate_up/pallas_call | solution.py:184
  65.7 1.6 %collective-permute-done.12 = bf16[384,512]{1,0:T(8,128)(2,1)S(1)} collective-permute-done((bf16[384,512]{1,0:T(8,128)(2,1)S(1)}, bf16[384,512]{1,0:T(8,128)(2,1)S(1)}, u32[]{:S(2)}, u32[]{:S(2)}) %collective-permute-start.12) | collective-permute-done | bytes 393248 | tf_op jit(solution)/shard_map/ppermute | solution.py:34
  68.0 8.4 %down.4 = (f32[384,512]{1,0:T(8,128)S(1)}, f32[384,512]{1,0:T(8,128)S(1)}, bf16[384,512]{1,0:T(8,128)(2,1)S(1)}, bf16[384,512]{1,0:T(8,128)(2,1)S(1)}, bf16[384,...) custom-call(s32[1]{0:T(128)} %bitcast.me_ref, bf16[384,1664]{1,0:T(8,128)(2,1)S(1)} %get-tuple-element.91.hidden_ref, ...), custom_call_target="tpu_custom_call" | custom-call | flops 490733568 | bytes 1277952 | tf_op jit(solution)/shard_map/down/pallas_call | solution.py:237
  81.1 5.8 %down.5 = (f32[384,512]{1,0:T(8,128)S(1)}, f32[384,512]{1,0:T(8,128)S(1)}, bf16[384,512]{1,0:T(8,128)(2,1)S(1)}, bf16[384,512]{1,0:T(8,128)(2,1)S(1)}) custom-call(s32[1]{0:T(128)} %bitcast.me_ref, bf16[384,1664]{1,0:T(8,128)(2,1)S(1)} %get-tuple-element.91.hidden_ref, bf16[1664,8192]{1,0:T(8,128)(2,1)} %weight_ref.7), custom_call_target="tpu_custom_call" | custom-call | flops 327155712 | bytes 851968 | tf_op jit(solution)/shard_map/down/pallas_call | solution.py:237
  87.6 2.1 %collective-permute-done.20 = bf16[384,512]{1,0:T(8,128)(2,1)S(1)} collective-permute-done((bf16[384,512]{1,0:T(8,128)(2,1)S(1)}, bf16[384,512]{1,0:T(8,128)(2,1)S(1)}, u32[]{:S(2)}, u32[]{:S(2)}) %collective-permute-start.20) | collective-permute-done | bytes 393248 | tf_op jit(solution)/shard_map/ppermute | solution.py:30
  89.9 1.6 %collective-permute-start.23 = (bf16[384,512]{1,0:T(8,128)(2,1)S(1)}, bf16[384,512]{1,0:T(8,128)(2,1)S(1)}, u32[]{:S(2)}, u32[]{:S(2)}) collective-permute-start(bf16[384,512]{1,0:T(8,128)(2,1)S(1)} %fusion.4), channel_id=1, source_target_pairs={{0,2},{1,3},{2,0},{3,1},{4,8},{5,9},{6,10},{7,11},{8,4},{9,5},{10,... | collective-permute-start | bytes 1179656 | tf_op jit(solution)/shard_map/ppermute | solution.py:30
  91.8 1.6 %collective-permute-start.25 = (bf16[384,512]{1,0:T(8,128)(2,1)S(1)}, bf16[384,512]{1,0:T(8,128)(2,1)S(1)}, u32[]{:S(2)}, u32[]{:S(2)}) collective-permute-start(bf16[384,512]{1,0:T(8,128)(2,1)S(1)} %fusion.6), channel_id=1, source_target_pairs={{0,4},{1,5},{2,6},{3,7},{4,0},{5,1},{6,2},{7,3},{8,12},{9,13},{10,... | collective-permute-start | bytes 1179656 | tf_op jit(solution)/shard_map/ppermute | solution.py:30
  93.4 4.8 %down.6 = (f32[384,512]{1,0:T(8,128)S(1)}, f32[384,512]{1,0:T(8,128)S(1)}, bf16[384,512]{1,0:T(8,128)(2,1)S(1)}) custom-call(s32[1]{0:T(128)} %bitcast.me_ref, bf16[384,1664]{1,0:T(8,128)(2,1)S(1)} %get-tuple-element.91.hidden_ref, bf16[1664,8192]{1,0:T(8,128)(2,1)} %weight_ref.7), custom_call_target="tpu_custom_call" | custom-call | flops 245366784 | bytes 638976 | tf_op jit(solution)/shard_map/down/pallas_call | solution.py:237
  98.4 1.8 %collective-permute-done.23 = bf16[384,512]{1,0:T(8,128)(2,1)S(1)} collective-permute-done((bf16[384,512]{1,0:T(8,128)(2,1)S(1)}, bf16[384,512]{1,0:T(8,128)(2,1)S(1)}, u32[]{:S(2)}, u32[]{:S(2)}) %collective-permute-start.23) | collective-permute-done | bytes 393248 | tf_op jit(solution)/shard_map/ppermute | solution.py:30
  100.4 1.7 %collective-permute-done.25 = bf16[384,512]{1,0:T(8,128)(2,1)S(1)} collective-permute-done((bf16[384,512]{1,0:T(8,128)(2,1)S(1)}, bf16[384,512]{1,0:T(8,128)(2,1)S(1)}, u32[]{:S(2)}, u32[]{:S(2)}) %collective-permute-start.25) | collective-permute-done | bytes 393248 | tf_op jit(solution)/shard_map/ppermute | solution.py:30
  103.1 1.8 %collective-permute-start.27 = (bf16[384,512]{1,0:T(8,128)(2,1)S(1)}, bf16[384,512]{1,0:T(8,128)(2,1)S(1)}, u32[]{:S(2)}, u32[]{:S(2)}) collective-permute-start(bf16[384,512]{1,0:T(8,128)(2,1)S(1)} %add_convert_fusion.1), channel_id=1, source_target_pairs={{0,4},{1,5},{2,6},{3,7},{4,0},{5,1},{6,2},{7,3},{8,12},{9,13},{10,... | collective-permute-start | bytes 1179656 | tf_op jit(solution)/shard_map/ppermute | solution.py:30
  104.9 2.3 %down.7 = f32[384,512]{1,0:T(8,128)S(1)} custom-call(s32[1]{0:T(128)} %bitcast.me_ref, bf16[384,1664]{1,0:T(8,128)(2,1)S(1)} %get-tuple-element.91.hidden_ref, bf16[1664,8192]{1,0:T(8,128)(2,1)} %weight_ref.7), custom_call_target="tpu_custom_call" | custom-call | flops 81788928 | bytes 212992 | tf_op jit(solution)/shard_map/down/pallas_call | solution.py:237
  107.3 4.3 %collective-permute-done.28 = bf16[384,512]{1,0:T(8,128)(2,1)S(1)} collective-permute-done((bf16[384,512]{1,0:T(8,128)(2,1)S(1)}, bf16[384,512]{1,0:T(8,128)(2,1)S(1)}, u32[]{:S(2)}, u32[]{:S(2)}) %collective-permute-start.28) | collective-permute-done | bytes 393248 | tf_op jit(solution)/shard_map/ppermute | solution.py:30
  (67 shorter events, 15.4 us)
Async XLA Ops:
  1.9 12.6 %collective-permute-start.2 = (bf16[1,400,512]{2,1,0:T(8,128)(2,1)S(1)}, bf16[1,400,512]{2,1,0:T(8,128)(2,1)S(1)}, u32[]{:S(2)}, u32[]{:S(2)}) collective-permute-start(bf16[1,400,512]{2,1,0:T(8,128)(2,1)S(1)} %prepare.1.refs_0_), channel_id=1, source_target_pairs={{0,4},{1,5},{2,6},{3,7},{4,0},{5,1},{6,2},{7,3},{8,12},{9,13},{10,... | collective-permute-start | bytes 1228808 | tf_op jit(solution)/shard_map/ppermute | solution.py:30
  5.0 11.2 %collective-permute-start = (bf16[1,400,512]{2,1,0:T(8,128)(2,1)S(1)}, bf16[1,400,512]{2,1,0:T(8,128)(2,1)S(1)}, u32[]{:S(2)}, u32[]{:S(2)}) collective-permute-start(bf16[1,400,512]{2,1,0:T(8,128)(2,1)S(1)} %prepare.1.refs_0_), channel_id=1, source_target_pairs={{0,2},{1,3},{2,0},{3,1},{4,8},{5,9},{6,10},{7,11},{8,4},{9,5},{10,... | collective-permute-start | bytes 1228808 | tf_op jit(solution)/shard_map/ppermute | solution.py:30
  6.5 11.4 %collective-permute-start.4 = (bf16[1,400,512]{2,1,0:T(8,128)(2,1)S(1)}, bf16[1,400,512]{2,1,0:T(8,128)(2,1)S(1)}, u32[]{:S(2)}, u32[]{:S(2)}) collective-permute-start(bf16[1,400,512]{2,1,0:T(8,128)(2,1)S(1)} %prepare.1.refs_0_), channel_id=1, source_target_pairs={{0,1},{1,0},{2,3},{3,2},{4,5},{5,4},{6,7},{7,6},{8,9},{9,8},{10,11... | collective-permute-start | bytes 1228808 | tf_op jit(solution)/shard_map/ppermute | solution.py:34
  14.5 12.3 %collective-permute-start.3 = (bf16[1,400,512]{2,1,0:T(8,128)(2,1)S(1)}, bf16[1,400,512]{2,1,0:T(8,128)(2,1)S(1)}, u32[]{:S(2)}, u32[]{:S(2)}) collective-permute-start(bf16[1,400,512]{2,1,0:T(8,128)(2,1)S(1)} %collective-permute-done.2.refs_2_), channel_id=1, source_target_pairs={{0,2},{1,3},{2,0},{3,1},{4,8},{5,9},{6,10},{7,11},{8,4},{9,5},{10,... | collective-permute-start | bytes 1228808 | tf_op jit(solution)/shard_map/ppermute | solution.py:30
  16.1 10.7 %collective-permute-start.1 = (bf16[1,400,512]{2,1,0:T(8,128)(2,1)S(1)}, bf16[1,400,512]{2,1,0:T(8,128)(2,1)S(1)}, u32[]{:S(2)}, u32[]{:S(2)}) collective-permute-start(bf16[1,400,512]{2,1,0:T(8,128)(2,1)S(1)} %collective-permute-done.refs_3_), channel_id=1, source_target_pairs={{0,4},{1,5},{2,6},{3,7},{4,0},{5,1},{6,2},{7,3},{8,12},{9,13},{10,... | collective-permute-start | bytes 1228808 | tf_op jit(solution)/shard_map/ppermute | solution.py:30
  17.9 11.8 %collective-permute-start.7 = (bf16[2,400,512]{2,1,0:T(8,128)(2,1)S(1)}, bf16[2,400,512]{2,1,0:T(8,128)(2,1)S(1)}, u32[]{:S(2)}, u32[]{:S(2)}) collective-permute-start(bf16[2,400,512]{2,1,0:T(8,128)(2,1)S(1)} %pad_maximum_fusion), channel_id=1, source_target_pairs={{0,1},{1,0},{2,3},{3,2},{4,5},{5,4},{6,7},{7,6},{8,9},{9,8},{10,11... | collective-permute-start | bytes 2457608 | tf_op jit(solution)/shard_map/ppermute | solution.py:34
  26.9 11.9 %collective-permute-start.6 = (bf16[1,400,512]{2,1,0:T(8,128)(2,1)S(1)}, bf16[1,400,512]{2,1,0:T(8,128)(2,1)S(1)}, u32[]{:S(2)}, u32[]{:S(2)}) collective-permute-start(bf16[1,400,512]{2,1,0:T(8,128)(2,1)S(1)} %broadcast_select_fusion.1), channel_id=1, source_target_pairs={{0,2},{1,3},{2,0},{3,1},{4,6},{5,7},{6,4},{7,5},{8,10},{9,11},{10,... | collective-permute-start | bytes 1228808 | tf_op jit(solution)/shard_map/ppermute | solution.py:30
  28.4 11.6 %collective-permute-start.5 = (bf16[1,400,512]{2,1,0:T(8,128)(2,1)S(1)}, bf16[1,400,512]{2,1,0:T(8,128)(2,1)S(1)}, u32[]{:S(2)}, u32[]{:S(2)}) collective-permute-start(bf16[1,400,512]{2,1,0:T(8,128)(2,1)S(1)} %collective-permute-done.3.refs_3_), channel_id=1, source_target_pairs={{0,4},{1,5},{2,6},{3,7},{4,0},{5,1},{6,2},{7,3},{8,12},{9,13},{10,... | collective-permute-start | bytes 1228808 | tf_op jit(solution)/shard_map/ppermute | solution.py:30
  29.5 11.2 %collective-permute-start.9 = (bf16[2,400,512]{2,1,0:T(8,128)(2,1)S(1)}, bf16[2,400,512]{2,1,0:T(8,128)(2,1)S(1)}, u32[]{:S(2)}, u32[]{:S(2)}) collective-permute-start(bf16[2,400,512]{2,1,0:T(8,128)(2,1)S(1)} %pad_maximum_fusion.1), channel_id=1, source_target_pairs={{0,1},{1,0},{2,3},{3,2},{4,5},{5,4},{6,7},{7,6},{8,9},{9,8},{10,11... | collective-permute-start | bytes 2457608 | tf_op jit(solution)/shard_map/ppermute | solution.py:34
  40.1 2.4 %collective-permute-start.10 = (bf16[2,400,512]{2,1,0:T(8,128)(2,1)S(1)}, bf16[2,400,512]{2,1,0:T(8,128)(2,1)S(1)}, u32[]{:S(2)}, u32[]{:S(2)}) collective-permute-start(bf16[2,400,512]{2,1,0:T(8,128)(2,1)S(1)} %pad_maximum_fusion.2), channel_id=1, source_target_pairs={{0,1},{1,0},{2,3},{3,2},{4,5},{5,4},{6,7},{7,6},{8,9},{9,8},{10,11... | collective-permute-start | bytes 2457608 | tf_op jit(solution)/shard_map/ppermute | solution.py:34
  40.2 14.8 %collective-permute-start.8 = (bf16[1,400,512]{2,1,0:T(8,128)(2,1)S(1)}, bf16[1,400,512]{2,1,0:T(8,128)(2,1)S(1)}, u32[]{:S(2)}, u32[]{:S(2)}) collective-permute-start(bf16[1,400,512]{2,1,0:T(8,128)(2,1)S(1)} %broadcast_select_fusion), channel_id=1, source_target_pairs={{0,2},{1,3},{2,0},{3,1},{4,6},{5,7},{6,4},{7,5},{8,10},{9,11},{10,... | collective-permute-start | bytes 1228808 | tf_op jit(solution)/shard_map/ppermute | solution.py:30
  67.4 11.2 %collective-permute-start.15 = (bf16[384,512]{1,0:T(8,128)(2,1)S(1)}, bf16[384,512]{1,0:T(8,128)(2,1)S(1)}, u32[]{:S(2)}, u32[]{:S(2)}) collective-permute-start(bf16[384,512]{1,0:T(8,128)(2,1)S(1)} %add_convert_fusion.3), channel_id=1, source_target_pairs={{0,2},{1,3},{2,0},{3,1},{4,6},{5,7},{6,4},{7,5},{8,10},{9,11},{10,... | collective-permute-start | bytes 1179656 | tf_op jit(solution)/shard_map/ppermute | solution.py:30
  77.0 2.2 %collective-permute-start.16 = (bf16[192,512]{1,0:T(8,128)(2,1)S(1)}, bf16[192,512]{1,0:T(8,128)(2,1)S(1)}, u32[]{:S(2)}, u32[]{:S(2)}) collective-permute-start(bf16[192,512]{1,0:T(8,128)(2,1)S(1)} %get-tuple-element.95), channel_id=1, source_target_pairs={{0,1},{1,0},{2,3},{3,2},{4,5},{5,4},{6,7},{7,6},{8,9},{9,8},{10,11... | collective-permute-start | bytes 589832 | tf_op jit(solution)/shard_map/ppermute | solution.py:34
  78.8 10.9 %collective-permute-start.20 = (bf16[384,512]{1,0:T(8,128)(2,1)S(1)}, bf16[384,512]{1,0:T(8,128)(2,1)S(1)}, u32[]{:S(2)}, u32[]{:S(2)}) collective-permute-start(bf16[384,512]{1,0:T(8,128)(2,1)S(1)} %fusion.1), channel_id=1, source_target_pairs={{0,4},{1,5},{2,6},{3,7},{4,0},{5,1},{6,2},{7,3},{8,12},{9,13},{10,... | collective-permute-start | bytes 1179656 | tf_op jit(solution)/shard_map/ppermute | solution.py:30
  79.1 7.9 %collective-permute-start.19 = (bf16[384,512]{1,0:T(8,128)(2,1)S(1)}, bf16[384,512]{1,0:T(8,128)(2,1)S(1)}, u32[]{:S(2)}, u32[]{:S(2)}) collective-permute-start(bf16[384,512]{1,0:T(8,128)(2,1)S(1)} %get-tuple-element.83), channel_id=1, source_target_pairs={{0,1},{1,0},{2,3},{3,2},{4,5},{5,4},{6,7},{7,6},{8,9},{9,8},{10,11... | collective-permute-start | bytes 1179656 | tf_op jit(solution)/shard_map/ppermute | solution.py:34
  79.3 12.2 %collective-permute-start.18 = (bf16[384,512]{1,0:T(8,128)(2,1)S(1)}, bf16[384,512]{1,0:T(8,128)(2,1)S(1)}, u32[]{:S(2)}, u32[]{:S(2)}) collective-permute-start(bf16[384,512]{1,0:T(8,128)(2,1)S(1)} %get-tuple-element.81), channel_id=1, source_target_pairs={{0,1},{1,0},{2,3},{3,2},{4,5},{5,4},{6,7},{7,6},{8,9},{9,8},{10,11... | collective-permute-start | bytes 1179656 | tf_op jit(solution)/shard_map/ppermute | solution.py:34
  80.0 11.6 %collective-permute-start.21 = (bf16[384,512]{1,0:T(8,128)(2,1)S(1)}, bf16[384,512]{1,0:T(8,128)(2,1)S(1)}, u32[]{:S(2)}, u32[]{:S(2)}) collective-permute-start(bf16[384,512]{1,0:T(8,128)(2,1)S(1)} %add_convert_fusion.2), channel_id=1, source_target_pairs={{0,2},{1,3},{2,0},{3,1},{4,6},{5,7},{6,4},{7,5},{8,10},{9,11},{10,... | collective-permute-start | bytes 1179656 | tf_op jit(solution)/shard_map/ppermute | solution.py:30
  87.0 11.4 %collective-permute-start.22 = (bf16[384,512]{1,0:T(8,128)(2,1)S(1)}, bf16[384,512]{1,0:T(8,128)(2,1)S(1)}, u32[]{:S(2)}, u32[]{:S(2)}) collective-permute-start(bf16[384,512]{1,0:T(8,128)(2,1)S(1)} %get-tuple-element.87), channel_id=1, source_target_pairs={{0,1},{1,0},{2,3},{3,2},{4,5},{5,4},{6,7},{7,6},{8,9},{9,8},{10,11... | collective-permute-start | bytes 1179656 | tf_op jit(solution)/shard_map/ppermute | solution.py:34
  87.1 11.2 %collective-permute-start.24 = (bf16[384,512]{1,0:T(8,128)(2,1)S(1)}, bf16[384,512]{1,0:T(8,128)(2,1)S(1)}, u32[]{:S(2)}, u32[]{:S(2)}) collective-permute-start(bf16[384,512]{1,0:T(8,128)(2,1)S(1)} %get-tuple-element.89), channel_id=1, source_target_pairs={{0,1},{1,0},{2,3},{3,2},{4,5},{5,4},{6,7},{7,6},{8,9},{9,8},{10,11... | collective-permute-start | bytes 1179656 | tf_op jit(solution)/shard_map/ppermute | solution.py:34
  89.9 10.3 %collective-permute-start.23 = (bf16[384,512]{1,0:T(8,128)(2,1)S(1)}, bf16[384,512]{1,0:T(8,128)(2,1)S(1)}, u32[]{:S(2)}, u32[]{:S(2)}) collective-permute-start(bf16[384,512]{1,0:T(8,128)(2,1)S(1)} %fusion.4), channel_id=1, source_target_pairs={{0,2},{1,3},{2,0},{3,1},{4,8},{5,9},{6,10},{7,11},{8,4},{9,5},{10,... | collective-permute-start | bytes 1179656 | tf_op jit(solution)/shard_map/ppermute | solution.py:30
  91.8 10.2 %collective-permute-start.25 = (bf16[384,512]{1,0:T(8,128)(2,1)S(1)}, bf16[384,512]{1,0:T(8,128)(2,1)S(1)}, u32[]{:S(2)}, u32[]{:S(2)}) collective-permute-start(bf16[384,512]{1,0:T(8,128)(2,1)S(1)} %fusion.6), channel_id=1, source_target_pairs={{0,4},{1,5},{2,6},{3,7},{4,0},{5,1},{6,2},{7,3},{8,12},{9,13},{10,... | collective-permute-start | bytes 1179656 | tf_op jit(solution)/shard_map/ppermute | solution.py:30
  98.2 9.1 %collective-permute-start.26 = (bf16[384,512]{1,0:T(8,128)(2,1)S(1)}, bf16[384,512]{1,0:T(8,128)(2,1)S(1)}, u32[]{:S(2)}, u32[]{:S(2)}) collective-permute-start(bf16[384,512]{1,0:T(8,128)(2,1)S(1)} %get-tuple-element.92), channel_id=1, source_target_pairs={{0,1},{1,0},{2,3},{3,2},{4,5},{5,4},{6,7},{7,6},{8,9},{9,8},{10,11... | collective-permute-start | bytes 1179656 | tf_op jit(solution)/shard_map/ppermute | solution.py:34
  102.3 9.3 %collective-permute-start.28 = (bf16[384,512]{1,0:T(8,128)(2,1)S(1)}, bf16[384,512]{1,0:T(8,128)(2,1)S(1)}, u32[]{:S(2)}, u32[]{:S(2)}) collective-permute-start(bf16[384,512]{1,0:T(8,128)(2,1)S(1)} %fusion.9), channel_id=1, source_target_pairs={{0,2},{1,3},{2,0},{3,1},{4,8},{5,9},{6,10},{7,11},{8,4},{9,5},{10,... | collective-permute-start | bytes 1179656 | tf_op jit(solution)/shard_map/ppermute | solution.py:30
  103.1 9.1 %collective-permute-start.27 = (bf16[384,512]{1,0:T(8,128)(2,1)S(1)}, bf16[384,512]{1,0:T(8,128)(2,1)S(1)}, u32[]{:S(2)}, u32[]{:S(2)}) collective-permute-start(bf16[384,512]{1,0:T(8,128)(2,1)S(1)} %add_convert_fusion.1), channel_id=1, source_target_pairs={{0,4},{1,5},{2,6},{3,7},{4,0},{5,1},{6,2},{7,3},{8,12},{9,13},{10,... | collective-permute-start | bytes 1179656 | tf_op jit(solution)/shard_map/ppermute | solution.py:30
  (8 other events, 20.4 us)

commit v18 on v14

--- a/solution.py
+++ b/solution.py
@@ -275,10 +275,10 @@
     one, one_in = send(own, ALONG), send(own, INSIDE)
     theirs = swap(own)
     two, two_in = send(one_in, ALONG), send(one, INSIDE)
-    their_ones = swap(jnp.concatenate([one, one_in]))
     acc = multiply(
         None, (OWN, 0, own, 0), (OWN, 1, theirs, 0), (ONE, 0, one, 0), (ONE_IN, 0, one_in, 0)
     )
+    their_ones = swap(after(jnp.concatenate([one, one_in]), acc[3]))
     two, two_in = after((two, two_in), acc[3])
     three, across = send(two_in, ALONG), send(jnp.where(end, two, one_in), ACROSS)
     their_twos = swap(jnp.concatenate([two, two_in]))

time: 113 us -> 114 us (level)
  starting transfers between devices: 21.3 us -> 22.6 us
    ppermute x14, starting transfers between devices: 18.5 us -> 19.8 us  [send(): return lax.ppermute(x, 'gx', pairs)]
  transfers between devices with their start and end apart: 29 -> 29, of which waited for: 14 -> 13; matrix products, arithmetic and copies ran while one was open for 2% -> 2% of each run, Pallas kernels for 46% -> 45%
where the time goes in v18:
time: 114 us
  Pallas kernels  60.4 us (53%)
  waiting for transfers between devices  25.9 us (23%)
  starting transfers between devices  22.6 us (20%)
  other arithmetic  2.92 us (3%)
  local copies, waits for them, and re-layouts  1.73 us (2%)
    pallas_call x4, Pallas kernels, gate_up(): pl.pallas_call(functools.partial(gate_up_body, count, first, last, rows,...  38.9 us
    pallas_call x4, Pallas kernels, down(): pl.pallas_call(functools.partial(down_body, len(kept), len(sent)), grid_s...  21.3 us
    ppermute x14, waiting for transfers between devices, send(): return lax.ppermute(x, 'gx', pairs)  20.7 us
    ppermute x14, starting transfers between devices, send(): return lax.ppermute(x, 'gx', pairs)  19.8 us
    ppermute x15, waiting for transfers between devices, swap(): return lax.ppermute(x, 'gx', [(i, i ^ 1) for i in range(4 * LINE)])  5.27 us
    ppermute x15, starting transfers between devices, swap(): return lax.ppermute(x, 'gx', [(i, i ^ 1) for i in range(4 * LINE)])  2.77 us
  transfers between devices with their start and end apart: 29, of which 13 were waited for; matrix products, arithmetic and copies ran while one was open for 2% of the time, Pallas kernels for 45%

profile of v18, /device:TPU:0, one launch (start us, length us, event | category | flops | bytes accessed | tf_op | source)
XLA Modules:
  0.0 113.9 jit_solution(11939919721894426488)
XLA Ops:
  1.9 3.0 %collective-permute-start = (bf16[1,400,512]{2,1,0:T(8,128)(2,1)S(1)}, bf16[1,400,512]{2,1,0:T(8,128)(2,1)S(1)}, u32[]{:S(2)}, u32[]{:S(2)}) collective-permute-start(bf16[1,400,512]{2,1,0:T(8,128)(2,1)S(1)} %prepare.1.refs_0_), channel_id=1, source_target_pairs={{0,2},{1,3},{2,0},{3,1},{4,8},{5,9},{6,10},{7,11},{8,4},{9,5},{10,... | collective-permute-start | bytes 1228808 | tf_op jit(solution)/shard_map/ppermute | solution.py:30
  4.9 1.6 %collective-permute-start.2 = (bf16[1,400,512]{2,1,0:T(8,128)(2,1)S(1)}, bf16[1,400,512]{2,1,0:T(8,128)(2,1)S(1)}, u32[]{:S(2)}, u32[]{:S(2)}) collective-permute-start(bf16[1,400,512]{2,1,0:T(8,128)(2,1)S(1)} %prepare.1.refs_0_), channel_id=1, source_target_pairs={{0,4},{1,5},{2,6},{3,7},{4,0},{5,1},{6,2},{7,3},{8,12},{9,13},{10,... | collective-permute-start | bytes 1228808 | tf_op jit(solution)/shard_map/ppermute | solution.py:30
  6.6 7.8 %collective-permute-done.refs_3_ = bf16[1,400,512]{2,1,0:T(8,128)(2,1)S(1)} collective-permute-done((bf16[1,400,512]{2,1,0:T(8,128)(2,1)S(1)}, bf16[1,400,512]{2,1,0:T(8,128)(2,1)S(1)}, u32[]{:S(2)}, u32[]{:S(2)}) %collective-permute-start) | collective-permute-done | bytes 409632 | tf_op jit(solution)/shard_map/ppermute | solution.py:30
  14.4 1.8 %collective-permute-start.1 = (bf16[1,400,512]{2,1,0:T(8,128)(2,1)S(1)}, bf16[1,400,512]{2,1,0:T(8,128)(2,1)S(1)}, u32[]{:S(2)}, u32[]{:S(2)}) collective-permute-start(bf16[1,400,512]{2,1,0:T(8,128)(2,1)S(1)} %collective-permute-done.refs_3_), channel_id=1, source_target_pairs={{0,4},{1,5},{2,6},{3,7},{4,0},{5,1},{6,2},{7,3},{8,12},{9,13},{10,... | collective-permute-start | bytes 1228808 | tf_op jit(solution)/shard_map/ppermute | solution.py:30
  16.2 1.5 %collective-permute-start.3 = (bf16[1,400,512]{2,1,0:T(8,128)(2,1)S(1)}, bf16[1,400,512]{2,1,0:T(8,128)(2,1)S(1)}, u32[]{:S(2)}, u32[]{:S(2)}) collective-permute-start(bf16[1,400,512]{2,1,0:T(8,128)(2,1)S(1)} %collective-permute-done.2.refs_2_), channel_id=1, source_target_pairs={{0,2},{1,3},{2,0},{3,1},{4,8},{5,9},{6,10},{7,11},{8,4},{9,5},{10,... | collective-permute-start | bytes 1228808 | tf_op jit(solution)/shard_map/ppermute | solution.py:30
  17.7 8.8 %gate_up.4 = (f32[384,1536]{1,0:T(8,128)S(1)}, f32[384,1536]{1,0:T(8,128)S(1)}, f32[384,256]{1,0:T(8,128)S(1)}, f32[8,512]{1,0:T(8,128)S(1)}) custom-call(s32[1]{0:T(128)} %bitcast.me_ref, bf16[1,400,512]{2,1,0:T(8,128)(2,1)S(1)} %prepare.1.refs_0_, bf16[1,400,512]{2,1,0:T(8,128)(2,1)S(1)} %collective-permute-done.4.refs_1_, ...), custom_call_target="tpu_custom_call" | custom-call | flops 654311424 | bytes 1703936 | tf_op jit(solution)/shard_map/gate_up/pallas_call | solution.py:184
  27.9 2.1 %collective-permute-start.5 = (bf16[1,400,512]{2,1,0:T(8,128)(2,1)S(1)}, bf16[1,400,512]{2,1,0:T(8,128)(2,1)S(1)}, u32[]{:S(2)}, u32[]{:S(2)}) collective-permute-start(bf16[1,400,512]{2,1,0:T(8,128)(2,1)S(1)} %collective-permute-done.3.refs_3_), channel_id=1, source_target_pairs={{0,4},{1,5},{2,6},{3,7},{4,0},{5,1},{6,2},{7,3},{8,12},{9,13},{10,... | collective-permute-start | bytes 1228808 | tf_op jit(solution)/shard_map/ppermute | solution.py:30
  30.2 8.9 %gate_up.5 = (f32[384,1536]{1,0:T(8,128)S(1)}, f32[384,1536]{1,0:T(8,128)S(1)}, f32[384,256]{1,0:T(8,128)S(1)}, f32[8,512]{1,0:T(8,128)S(1)}) custom-call(s32[1]{0:T(128)} %bitcast.me_ref, bf16[2,400,512]{2,1,0:T(8,128)(2,1)S(1)} %collective-permute-done.7.refs_0_.refs_1_, bf16[2,400,512]{2,1,0:T(8,128)(2,1)S(1)} %collective-permute-done.7.refs_0_.refs_1_, ...), custom_call_target="tpu_custom_call" | custom-call | flops 654311424 | bytes 1703936 | tf_op jit(solution)/shard_map/gate_up/pallas_call | solution.py:184
  40.7 1.6 %collective-permute-done.10.refs_4_.refs_5_ = bf16[2,400,512]{2,1,0:T(8,128)(2,1)S(1)} collective-permute-done((bf16[2,400,512]{2,1,0:T(8,128)(2,1)S(1)}, bf16[2,400,512]{2,1,0:T(8,128)(2,1)S(1)}, u32[]{:S(2)}, u32[]{:S(2)}) %collective-permute-start.10) | collective-permute-done | bytes 819232 | tf_op jit(solution)/shard_map/ppermute | solution.py:34
  42.3 12.5 %gate_up.6 = (f32[384,1536]{1,0:T(8,128)S(1)}, f32[384,1536]{1,0:T(8,128)S(1)}, f32[384,256]{1,0:T(8,128)S(1)}, f32[8,512]{1,0:T(8,128)S(1)}) custom-call(s32[1]{0:T(128)} %bitcast.me_ref, bf16[2,400,512]{2,1,0:T(8,128)(2,1)S(1)} %collective-permute-done.9.refs_0_.refs_1_, bf16[2,400,512]{2,1,0:T(8,128)(2,1)S(1)} %collective-permute-done.9.refs_0_.refs_1_, ...), custom_call_target="tpu_custom_call" | custom-call | flops 981467136 | bytes 2555904 | tf_op jit(solution)/shard_map/gate_up/pallas_call | solution.py:184
  55.1 1.6 %collective-permute-done.11.refs_1_ = bf16[1,400,512]{2,1,0:T(8,128)(2,1)S(1)} collective-permute-done((bf16[1,400,512]{2,1,0:T(8,128)(2,1)S(1)}, bf16[1,400,512]{2,1,0:T(8,128)(2,1)S(1)}, u32[]{:S(2)}, u32[]{:S(2)}) %collective-permute-start.11) | collective-permute-done | bytes 409632 | tf_op jit(solution)/shard_map/ppermute | solution.py:34
  56.7 8.6 %gate_up.7 = (bf16[384,1664]{1,0:T(8,128)(2,1)S(1)}, bf16[384,512]{1,0:T(8,128)(2,1)S(1)}, f32[384,512]{1,0:T(8,128)S(1)}) custom-call(s32[1]{0:T(128)} %bitcast.me_ref, bf16[1,400,512]{2,1,0:T(8,128)(2,1)S(1)} %collective-permute-done.8.refs_0_, bf16[1,400,512]{2,1,0:T(8,128)(2,1)S(1)} %collective-permute-done.11.refs_1_, bf16[8192,1664]{1,0:T(8,128)(2,1)} %refs_2_.1, ...), custom_call_target="tpu_custom_call" | custom-call | flops 327155712 | bytes 851968 | tf_op jit(solution)/shard_map/gate_up/pallas_call | solution.py:184
  65.5 1.6 %collective-permute-done.12 = bf16[384,512]{1,0:T(8,128)(2,1)S(1)} collective-permute-done((bf16[384,512]{1,0:T(8,128)(2,1)S(1)}, bf16[384,512]{1,0:T(8,128)(2,1)S(1)}, u32[]{:S(2)}, u32[]{:S(2)}) %collective-permute-start.12) | collective-permute-done | bytes 393248 | tf_op jit(solution)/shard_map/ppermute | solution.py:34
  67.9 8.4 %down.4 = (f32[384,512]{1,0:T(8,128)S(1)}, f32[384,512]{1,0:T(8,128)S(1)}, bf16[384,512]{1,0:T(8,128)(2,1)S(1)}, bf16[384,512]{1,0:T(8,128)(2,1)S(1)}, bf16[384,...) custom-call(s32[1]{0:T(128)} %bitcast.me_ref, bf16[384,1664]{1,0:T(8,128)(2,1)S(1)} %get-tuple-element.89.hidden_ref, ...), custom_call_target="tpu_custom_call" | custom-call | flops 490733568 | bytes 1277952 | tf_op jit(solution)/shard_map/down/pallas_call | solution.py:237
  78.6 1.8 %collective-permute-start.20 = (bf16[384,512]{1,0:T(8,128)(2,1)S(1)}, bf16[384,512]{1,0:T(8,128)(2,1)S(1)}, u32[]{:S(2)}, u32[]{:S(2)}) collective-permute-start(bf16[384,512]{1,0:T(8,128)(2,1)S(1)} %fusion.1), channel_id=1, source_target_pairs={{0,4},{1,5},{2,6},{3,7},{4,0},{5,1},{6,2},{7,3},{8,12},{9,13},{10,... | collective-permute-start | bytes 1179656 | tf_op jit(solution)/shard_map/ppermute | solution.py:30
  80.7 1.4 %collective-permute-start.21 = (bf16[384,512]{1,0:T(8,128)(2,1)S(1)}, bf16[384,512]{1,0:T(8,128)(2,1)S(1)}, u32[]{:S(2)}, u32[]{:S(2)}) collective-permute-start(bf16[384,512]{1,0:T(8,128)(2,1)S(1)} %add_convert_fusion.2), channel_id=1, source_target_pairs={{0,2},{1,3},{2,0},{3,1},{4,6},{5,7},{6,4},{7,5},{8,10},{9,11},{10,... | collective-permute-start | bytes 1179656 | tf_op jit(solution)/shard_map/ppermute | solution.py:30
  82.1 5.8 %down.5 = (f32[384,512]{1,0:T(8,128)S(1)}, f32[384,512]{1,0:T(8,128)S(1)}, bf16[384,512]{1,0:T(8,128)(2,1)S(1)}, bf16[384,512]{1,0:T(8,128)(2,1)S(1)}) custom-call(s32[1]{0:T(128)} %bitcast.me_ref, bf16[384,1664]{1,0:T(8,128)(2,1)S(1)} %get-tuple-element.89.hidden_ref, bf16[1664,8192]{1,0:T(8,128)(2,1)} %weight_ref.7), custom_call_target="tpu_custom_call" | custom-call | flops 327155712 | bytes 851968 | tf_op jit(solution)/shard_map/down/pallas_call | solution.py:237
  90.1 1.5 %collective-permute-start.23 = (bf16[384,512]{1,0:T(8,128)(2,1)S(1)}, bf16[384,512]{1,0:T(8,128)(2,1)S(1)}, u32[]{:S(2)}, u32[]{:S(2)}) collective-permute-start(bf16[384,512]{1,0:T(8,128)(2,1)S(1)} %fusion.4), channel_id=1, source_target_pairs={{0,2},{1,3},{2,0},{3,1},{4,8},{5,9},{6,10},{7,11},{8,4},{9,5},{10,... | collective-permute-start | bytes 1179656 | tf_op jit(solution)/shard_map/ppermute | solution.py:30
  92.3 4.8 %down.6 = (f32[384,512]{1,0:T(8,128)S(1)}, f32[384,512]{1,0:T(8,128)S(1)}, bf16[384,512]{1,0:T(8,128)(2,1)S(1)}) custom-call(s32[1]{0:T(128)} %bitcast.me_ref, bf16[384,1664]{1,0:T(8,128)(2,1)S(1)} %get-tuple-element.89.hidden_ref, bf16[1664,8192]{1,0:T(8,128)(2,1)} %weight_ref.7), custom_call_target="tpu_custom_call" | custom-call | flops 245366784 | bytes 638976 | tf_op jit(solution)/shard_map/down/pallas_call | solution.py:237
  97.3 3.3 %collective-permute-done.23 = bf16[384,512]{1,0:T(8,128)(2,1)S(1)} collective-permute-done((bf16[384,512]{1,0:T(8,128)(2,1)S(1)}, bf16[384,512]{1,0:T(8,128)(2,1)S(1)}, u32[]{:S(2)}, u32[]{:S(2)}) %collective-permute-start.23) | collective-permute-done | bytes 393248 | tf_op jit(solution)/shard_map/ppermute | solution.py:30
  100.7 1.4 %collective-permute-done.25 = bf16[384,512]{1,0:T(8,128)(2,1)S(1)} collective-permute-done((bf16[384,512]{1,0:T(8,128)(2,1)S(1)}, bf16[384,512]{1,0:T(8,128)(2,1)S(1)}, u32[]{:S(2)}, u32[]{:S(2)}) %collective-permute-start.25) | collective-permute-done | bytes 393248 | tf_op jit(solution)/shard_map/ppermute | solution.py:30
  102.4 1.5 %collective-permute-start.28 = (bf16[384,512]{1,0:T(8,128)(2,1)S(1)}, bf16[384,512]{1,0:T(8,128)(2,1)S(1)}, u32[]{:S(2)}, u32[]{:S(2)}) collective-permute-start(bf16[384,512]{1,0:T(8,128)(2,1)S(1)} %fusion.9), channel_id=1, source_target_pairs={{0,2},{1,3},{2,0},{3,1},{4,8},{5,9},{6,10},{7,11},{8,4},{9,5},{10,... | collective-permute-start | bytes 1179656 | tf_op jit(solution)/shard_map/ppermute | solution.py:30
  104.4 2.3 %down.7 = f32[384,512]{1,0:T(8,128)S(1)} custom-call(s32[1]{0:T(128)} %bitcast.me_ref, bf16[384,1664]{1,0:T(8,128)(2,1)S(1)} %get-tuple-element.89.hidden_ref, bf16[1664,8192]{1,0:T(8,128)(2,1)} %weight_ref.7), custom_call_target="tpu_custom_call" | custom-call | flops 81788928 | bytes 212992 | tf_op jit(solution)/shard_map/down/pallas_call | solution.py:237
  106.8 4.9 %collective-permute-done.28 = bf16[384,512]{1,0:T(8,128)(2,1)S(1)} collective-permute-done((bf16[384,512]{1,0:T(8,128)(2,1)S(1)}, bf16[384,512]{1,0:T(8,128)(2,1)S(1)}, u32[]{:S(2)}, u32[]{:S(2)}) %collective-permute-start.28) | collective-permute-done | bytes 393248 | tf_op jit(solution)/shard_map/ppermute | solution.py:30
  (67 shorter events, 14.9 us)
Async XLA Ops:
  1.9 12.5 %collective-permute-start = (bf16[1,400,512]{2,1,0:T(8,128)(2,1)S(1)}, bf16[1,400,512]{2,1,0:T(8,128)(2,1)S(1)}, u32[]{:S(2)}, u32[]{:S(2)}) collective-permute-start(bf16[1,400,512]{2,1,0:T(8,128)(2,1)S(1)} %prepare.1.refs_0_), channel_id=1, source_target_pairs={{0,2},{1,3},{2,0},{3,1},{4,8},{5,9},{6,10},{7,11},{8,4},{9,5},{10,... | collective-permute-start | bytes 1228808 | tf_op jit(solution)/shard_map/ppermute | solution.py:30
  4.9 11.3 %collective-permute-start.2 = (bf16[1,400,512]{2,1,0:T(8,128)(2,1)S(1)}, bf16[1,400,512]{2,1,0:T(8,128)(2,1)S(1)}, u32[]{:S(2)}, u32[]{:S(2)}) collective-permute-start(bf16[1,400,512]{2,1,0:T(8,128)(2,1)S(1)} %prepare.1.refs_0_), channel_id=1, source_target_pairs={{0,4},{1,5},{2,6},{3,7},{4,0},{5,1},{6,2},{7,3},{8,12},{9,13},{10,... | collective-permute-start | bytes 1228808 | tf_op jit(solution)/shard_map/ppermute | solution.py:30
  6.6 11.2 %collective-permute-start.4 = (bf16[1,400,512]{2,1,0:T(8,128)(2,1)S(1)}, bf16[1,400,512]{2,1,0:T(8,128)(2,1)S(1)}, u32[]{:S(2)}, u32[]{:S(2)}) collective-permute-start(bf16[1,400,512]{2,1,0:T(8,128)(2,1)S(1)} %prepare.1.refs_0_), channel_id=1, source_target_pairs={{0,1},{1,0},{2,3},{3,2},{4,5},{5,4},{6,7},{7,6},{8,9},{9,8},{10,11... | collective-permute-start | bytes 1228808 | tf_op jit(solution)/shard_map/ppermute | solution.py:34
  14.4 12.3 %collective-permute-start.1 = (bf16[1,400,512]{2,1,0:T(8,128)(2,1)S(1)}, bf16[1,400,512]{2,1,0:T(8,128)(2,1)S(1)}, u32[]{:S(2)}, u32[]{:S(2)}) collective-permute-start(bf16[1,400,512]{2,1,0:T(8,128)(2,1)S(1)} %collective-permute-done.refs_3_), channel_id=1, source_target_pairs={{0,4},{1,5},{2,6},{3,7},{4,0},{5,1},{6,2},{7,3},{8,12},{9,13},{10,... | collective-permute-start | bytes 1228808 | tf_op jit(solution)/shard_map/ppermute | solution.py:30
  16.2 10.5 %collective-permute-start.3 = (bf16[1,400,512]{2,1,0:T(8,128)(2,1)S(1)}, bf16[1,400,512]{2,1,0:T(8,128)(2,1)S(1)}, u32[]{:S(2)}, u32[]{:S(2)}) collective-permute-start(bf16[1,400,512]{2,1,0:T(8,128)(2,1)S(1)} %collective-permute-done.2.refs_2_), channel_id=1, source_target_pairs={{0,2},{1,3},{2,0},{3,1},{4,8},{5,9},{6,10},{7,11},{8,4},{9,5},{10,... | collective-permute-start | bytes 1228808 | tf_op jit(solution)/shard_map/ppermute | solution.py:30
  26.7 3.5 %collective-permute-start.7 = (bf16[2,400,512]{2,1,0:T(8,128)(2,1)S(1)}, bf16[2,400,512]{2,1,0:T(8,128)(2,1)S(1)}, u32[]{:S(2)}, u32[]{:S(2)}) collective-permute-start(bf16[2,400,512]{2,1,0:T(8,128)(2,1)S(1)} %pad_maximum_fusion), channel_id=1, source_target_pairs={{0,1},{1,0},{2,3},{3,2},{4,5},{5,4},{6,7},{7,6},{8,9},{9,8},{10,11... | collective-permute-start | bytes 2457608 | tf_op jit(solution)/shard_map/ppermute | solution.py:34
  26.8 12.3 %collective-permute-start.6 = (bf16[1,400,512]{2,1,0:T(8,128)(2,1)S(1)}, bf16[1,400,512]{2,1,0:T(8,128)(2,1)S(1)}, u32[]{:S(2)}, u32[]{:S(2)}) collective-permute-start(bf16[1,400,512]{2,1,0:T(8,128)(2,1)S(1)} %broadcast_select_fusion.1), channel_id=1, source_target_pairs={{0,2},{1,3},{2,0},{3,1},{4,6},{5,7},{6,4},{7,5},{8,10},{9,11},{10,... | collective-permute-start | bytes 1228808 | tf_op jit(solution)/shard_map/ppermute | solution.py:30
  27.9 12.0 %collective-permute-start.5 = (bf16[1,400,512]{2,1,0:T(8,128)(2,1)S(1)}, bf16[1,400,512]{2,1,0:T(8,128)(2,1)S(1)}, u32[]{:S(2)}, u32[]{:S(2)}) collective-permute-start(bf16[1,400,512]{2,1,0:T(8,128)(2,1)S(1)} %collective-permute-done.3.refs_3_), channel_id=1, source_target_pairs={{0,4},{1,5},{2,6},{3,7},{4,0},{5,1},{6,2},{7,3},{8,12},{9,13},{10,... | collective-permute-start | bytes 1228808 | tf_op jit(solution)/shard_map/ppermute | solution.py:30
  30.1 10.6 %collective-permute-start.9 = (bf16[2,400,512]{2,1,0:T(8,128)(2,1)S(1)}, bf16[2,400,512]{2,1,0:T(8,128)(2,1)S(1)}, u32[]{:S(2)}, u32[]{:S(2)}) collective-permute-start(bf16[2,400,512]{2,1,0:T(8,128)(2,1)S(1)} %pad_maximum_fusion.1), channel_id=1, source_target_pairs={{0,1},{1,0},{2,3},{3,2},{4,5},{5,4},{6,7},{7,6},{8,9},{9,8},{10,11... | collective-permute-start | bytes 2457608 | tf_op jit(solution)/shard_map/ppermute | solution.py:34
  40.1 14.8 %collective-permute-start.8 = (bf16[1,400,512]{2,1,0:T(8,128)(2,1)S(1)}, bf16[1,400,512]{2,1,0:T(8,128)(2,1)S(1)}, u32[]{:S(2)}, u32[]{:S(2)}) collective-permute-start(bf16[1,400,512]{2,1,0:T(8,128)(2,1)S(1)} %broadcast_select_fusion), channel_id=1, source_target_pairs={{0,2},{1,3},{2,0},{3,1},{4,6},{5,7},{6,4},{7,5},{8,10},{9,11},{10,... | collective-permute-start | bytes 1228808 | tf_op jit(solution)/shard_map/ppermute | solution.py:30
  67.2 11.2 %collective-permute-start.15 = (bf16[384,512]{1,0:T(8,128)(2,1)S(1)}, bf16[384,512]{1,0:T(8,128)(2,1)S(1)}, u32[]{:S(2)}, u32[]{:S(2)}) collective-permute-start(bf16[384,512]{1,0:T(8,128)(2,1)S(1)} %add_convert_fusion.3), channel_id=1, source_target_pairs={{0,2},{1,3},{2,0},{3,1},{4,6},{5,7},{6,4},{7,5},{8,10},{9,11},{10,... | collective-permute-start | bytes 1179656 | tf_op jit(solution)/shard_map/ppermute | solution.py:30
  76.9 3.5 %collective-permute-start.16 = (bf16[192,512]{1,0:T(8,128)(2,1)S(1)}, bf16[192,512]{1,0:T(8,128)(2,1)S(1)}, u32[]{:S(2)}, u32[]{:S(2)}) collective-permute-start(bf16[192,512]{1,0:T(8,128)(2,1)S(1)} %get-tuple-element.93), channel_id=1, source_target_pairs={{0,1},{1,0},{2,3},{3,2},{4,5},{5,4},{6,7},{7,6},{8,9},{9,8},{10,11... | collective-permute-start | bytes 589832 | tf_op jit(solution)/shard_map/ppermute | solution.py:34
  77.1 3.4 %collective-permute-start.17 = (bf16[192,512]{1,0:T(8,128)(2,1)S(1)}, bf16[192,512]{1,0:T(8,128)(2,1)S(1)}, u32[]{:S(2)}, u32[]{:S(2)}) collective-permute-start(bf16[192,512]{1,0:T(8,128)(2,1)S(1)} %get-tuple-element.94), channel_id=1, source_target_pairs={{0,1},{1,0},{2,3},{3,2},{4,5},{5,4},{6,7},{7,6},{8,9},{9,8},{10,11... | collective-permute-start | bytes 589832 | tf_op jit(solution)/shard_map/ppermute | solution.py:34
  77.8 10.8 %collective-permute-start.19 = (bf16[384,512]{1,0:T(8,128)(2,1)S(1)}, bf16[384,512]{1,0:T(8,128)(2,1)S(1)}, u32[]{:S(2)}, u32[]{:S(2)}) collective-permute-start(bf16[384,512]{1,0:T(8,128)(2,1)S(1)} %get-tuple-element.81), channel_id=1, source_target_pairs={{0,1},{1,0},{2,3},{3,2},{4,5},{5,4},{6,7},{7,6},{8,9},{9,8},{10,11... | collective-permute-start | bytes 1179656 | tf_op jit(solution)/shard_map/ppermute | solution.py:34
  78.1 9.9 %collective-permute-start.18 = (bf16[384,512]{1,0:T(8,128)(2,1)S(1)}, bf16[384,512]{1,0:T(8,128)(2,1)S(1)}, u32[]{:S(2)}, u32[]{:S(2)}) collective-permute-start(bf16[384,512]{1,0:T(8,128)(2,1)S(1)} %get-tuple-element.79), channel_id=1, source_target_pairs={{0,1},{1,0},{2,3},{3,2},{4,5},{5,4},{6,7},{7,6},{8,9},{9,8},{10,11... | collective-permute-start | bytes 1179656 | tf_op jit(solution)/shard_map/ppermute | solution.py:34
  78.6 11.3 %collective-permute-start.20 = (bf16[384,512]{1,0:T(8,128)(2,1)S(1)}, bf16[384,512]{1,0:T(8,128)(2,1)S(1)}, u32[]{:S(2)}, u32[]{:S(2)}) collective-permute-start(bf16[384,512]{1,0:T(8,128)(2,1)S(1)} %fusion.1), channel_id=1, source_target_pairs={{0,4},{1,5},{2,6},{3,7},{4,0},{5,1},{6,2},{7,3},{8,12},{9,13},{10,... | collective-permute-start | bytes 1179656 | tf_op jit(solution)/shard_map/ppermute | solution.py:30
  80.7 10.9 %collective-permute-start.21 = (bf16[384,512]{1,0:T(8,128)(2,1)S(1)}, bf16[384,512]{1,0:T(8,128)(2,1)S(1)}, u32[]{:S(2)}, u32[]{:S(2)}) collective-permute-start(bf16[384,512]{1,0:T(8,128)(2,1)S(1)} %add_convert_fusion.2), channel_id=1, source_target_pairs={{0,2},{1,3},{2,0},{3,1},{4,6},{5,7},{6,4},{7,5},{8,10},{9,11},{10,... | collective-permute-start | bytes 1179656 | tf_op jit(solution)/shard_map/ppermute | solution.py:30
  88.0 9.3 %collective-permute-start.22 = (bf16[384,512]{1,0:T(8,128)(2,1)S(1)}, bf16[384,512]{1,0:T(8,128)(2,1)S(1)}, u32[]{:S(2)}, u32[]{:S(2)}) collective-permute-start(bf16[384,512]{1,0:T(8,128)(2,1)S(1)} %get-tuple-element.85), channel_id=1, source_target_pairs={{0,1},{1,0},{2,3},{3,2},{4,5},{5,4},{6,7},{7,6},{8,9},{9,8},{10,11... | collective-permute-start | bytes 1179656 | tf_op jit(solution)/shard_map/ppermute | solution.py:34
  88.1 9.1 %collective-permute-start.24 = (bf16[384,512]{1,0:T(8,128)(2,1)S(1)}, bf16[384,512]{1,0:T(8,128)(2,1)S(1)}, u32[]{:S(2)}, u32[]{:S(2)}) collective-permute-start(bf16[384,512]{1,0:T(8,128)(2,1)S(1)} %get-tuple-element.87), channel_id=1, source_target_pairs={{0,1},{1,0},{2,3},{3,2},{4,5},{5,4},{6,7},{7,6},{8,9},{9,8},{10,11... | collective-permute-start | bytes 1179656 | tf_op jit(solution)/shard_map/ppermute | solution.py:34
  90.1 10.4 %collective-permute-start.23 = (bf16[384,512]{1,0:T(8,128)(2,1)S(1)}, bf16[384,512]{1,0:T(8,128)(2,1)S(1)}, u32[]{:S(2)}, u32[]{:S(2)}) collective-permute-start(bf16[384,512]{1,0:T(8,128)(2,1)S(1)} %fusion.4), channel_id=1, source_target_pairs={{0,2},{1,3},{2,0},{3,1},{4,8},{5,9},{6,10},{7,11},{8,4},{9,5},{10,... | collective-permute-start | bytes 1179656 | tf_op jit(solution)/shard_map/ppermute | solution.py:30
  91.8 10.3 %collective-permute-start.25 = (bf16[384,512]{1,0:T(8,128)(2,1)S(1)}, bf16[384,512]{1,0:T(8,128)(2,1)S(1)}, u32[]{:S(2)}, u32[]{:S(2)}) collective-permute-start(bf16[384,512]{1,0:T(8,128)(2,1)S(1)} %fusion.6), channel_id=1, source_target_pairs={{0,4},{1,5},{2,6},{3,7},{4,0},{5,1},{6,2},{7,3},{8,12},{9,13},{10,... | collective-permute-start | bytes 1179656 | tf_op jit(solution)/shard_map/ppermute | solution.py:30
  97.1 9.7 %collective-permute-start.26 = (bf16[384,512]{1,0:T(8,128)(2,1)S(1)}, bf16[384,512]{1,0:T(8,128)(2,1)S(1)}, u32[]{:S(2)}, u32[]{:S(2)}) collective-permute-start(bf16[384,512]{1,0:T(8,128)(2,1)S(1)} %get-tuple-element.90), channel_id=1, source_target_pairs={{0,1},{1,0},{2,3},{3,2},{4,5},{5,4},{6,7},{7,6},{8,9},{9,8},{10,11... | collective-permute-start | bytes 1179656 | tf_op jit(solution)/shard_map/ppermute | solution.py:34
  102.4 9.4 %collective-permute-start.28 = (bf16[384,512]{1,0:T(8,128)(2,1)S(1)}, bf16[384,512]{1,0:T(8,128)(2,1)S(1)}, u32[]{:S(2)}, u32[]{:S(2)}) collective-permute-start(bf16[384,512]{1,0:T(8,128)(2,1)S(1)} %fusion.9), channel_id=1, source_target_pairs={{0,2},{1,3},{2,0},{3,1},{4,8},{5,9},{6,10},{7,11},{8,4},{9,5},{10,... | collective-permute-start | bytes 1179656 | tf_op jit(solution)/shard_map/ppermute | solution.py:30
  103.9 9.0 %collective-permute-start.27 = (bf16[384,512]{1,0:T(8,128)(2,1)S(1)}, bf16[384,512]{1,0:T(8,128)(2,1)S(1)}, u32[]{:S(2)}, u32[]{:S(2)}) collective-permute-start(bf16[384,512]{1,0:T(8,128)(2,1)S(1)} %add_convert_fusion.1), channel_id=1, source_target_pairs={{0,4},{1,5},{2,6},{3,7},{4,0},{5,1},{6,2},{7,3},{8,12},{9,13},{10,... | collective-permute-start | bytes 1179656 | tf_op jit(solution)/shard_map/ppermute | solution.py:30
  (8 other events, 21.4 us)
